TPU v7x, 128 devices: a whole 4x4x4 slice. The times are simulated.
128 devices in a mesh: row: 16 (over x, z), col: 8 (over y, core).
Axes of the slice: x: 4, y: 4, z: 4, core: 2. Of those that a mesh axis runs over, the one named last changes fastest.
Arguments:
- features: bfloat16 [262144, 128], P(('col', 'row')), may hold values from -6 to 6
- weight: bfloat16 [128, 256], replicated, may hold values from -0.5 to 0.5
- offset: float32 [256], replicated, may hold values from -3 to 3
- tile_values: bfloat16 [16, 8, 64, 128, 128], P('row', 'col'), may hold values from -0.25 to 0.25
- tile_rows: int32 [16, 8, 64], P('row', 'col'), may hold values from 0 to 127
- tile_cols: int32 [16, 8, 64], P('row', 'col'), may hold values from 0 to 255
- live_tiles: int32 [16, 8], P('row', 'col'), may hold values from 16 to 64, as said below
- grad_hidden: bfloat16 [262144, 256], P(('row', 'col')), may hold values from -6 to 6
Outputs:
- hidden: bfloat16 [262144, 256], P(('row', 'col'))
- grad_features: float32 [262144, 128], P(('col', 'row'))
- grad_weight: float32 [128, 256], replicated
- grad_offset: float32 [256], replicated
Inputs may be any that keep to these rules, and one draw needn't show every extreme that they name: Only the first live_tiles[r, c] slots of block pair (r, c) are used; some block pair uses all 64 slots and some uses only 16; none uses fewer than 16.
All inputs are finite; a program needn't handle non-finite values.
Results may differ from a plain program's by a relative error of at most 0.0075.
Values may be sent and summed in bfloat16 or wider, within the bound.
No kernel may reach another device: no remote copies, remote signals or barrier semaphores. Data moves between devices by JAX's collectives and lax.ppermute only.
A program may use at most 192 MiB of HBM per device.

v0:
```python
import functools
import math

import jax
import jax.numpy as jnp
from jax import lax
from jax.experimental import pallas as pl
from jax.experimental.pallas import tpu as pltpu
from jax.sharding import PartitionSpec as P

T = 128
F32, BF16, I32 = jnp.float32, jnp.bfloat16, jnp.int32
VMEM_BYTES = 56 * 1024 * 1024
GROUP = 4
HALF = 8 * T
META = 16
CAP = 16
SMEM = pl.BlockSpec(memory_space=pltpu.SMEM)
VMEM = pl.BlockSpec(memory_space=pltpu.VMEM)
ANY = pl.BlockSpec(memory_space=pl.ANY)
PARAMS = pltpu.CompilerParams(vmem_limit_bytes=VMEM_BYTES)


def along_x(value, step):
    pairs = [(x * 4 + z, (x + step) % 4 * 4 + z) for x in range(4) for z in range(4)]
    return lax.ppermute(value, "row", pairs)


def along_z(value, step):
    pairs = [(x * 4 + z, x * 4 + (z + step) % 4) for x in range(4) for z in range(4)]
    return lax.ppermute(value, "row", pairs)


def along_y(value, step):
    pairs = [(y * 2 + k, (y + step) % 4 * 2 + k) for y in range(4) for k in range(2)]
    return lax.ppermute(value, "col", pairs)


def other_core(value):
    pairs = [(y * 2 + k, y * 2 + 1 - k) for y in range(4) for k in range(2)]
    return lax.ppermute(value, "col", pairs)


def ring_gather(value, along):
    return [value, along(value, -1), along(value, 2), along(value, 1)]


def ring_send(pieces, along):
    return [pieces[0], along(pieces[3], -1), along(pieces[2], 2), along(pieces[1], 1)]


def ring_sum(value, along):
    a, b, c, d = ring_gather(value, along)
    return a + b + c + d


def total_of(pieces):
    return sum(piece.astype(F32) for piece in pieces)


def block(place):
    return pl.ds(pl.multiple_of(place * T, T), T)


def places(rows, cols, live, at_row, at_col):
    x, z, y, core = at_row // 4, at_row % 4, at_col // 2, at_col % 2
    owner = rows // 16
    same_core = (owner % 2 == core).astype(I32)
    row_place = (same_core * 4 + (owner // 2 - y) % 4) * 16 + rows % 16

    owner = cols // 16
    dx, dz = (owner // 4 - x) % 4, (owner % 4 - z) % 4
    half = cols % 16 // 8
    outer, inner = jnp.where(half == 0, dz, dx), jnp.where(half == 0, dx, dz)
    group, code = half * 4 + outer, inner * 8 + cols % 8
    dense_place = group * 32 + code

    slot = jnp.arange(cols.shape[0], dtype=I32)
    valid = slot < live
    same = cols[:, None] == cols[None, :]
    earlier = slot[None, :] < slot[:, None]
    first = valid & ~jnp.any(same & earlier, axis=1)
    ahead = earlier & first[None, :] & (group[:, None] == group[None, :])
    rank = jnp.sum(ahead.astype(I32), axis=1)
    overflow = jnp.any(first & (outer != 0) & (rank >= CAP))
    far = 64 + (half * 3 + outer - 1) * CAP + jnp.minimum(rank, CAP - 1)
    place = jnp.where(outer == 0, half * 32 + code, far)
    place = jnp.sum(jnp.where(same & first[None, :], place[None, :], 0), axis=1)
    place = jnp.where(valid, place, 0)
    return row_place, place, dense_place, jnp.where(first, cols, -1), overflow


def products_kernel(live, in_place, out_place, tiles_ref, *refs, spans, outs, contract):
    n = len(spans)
    sources, out_refs, (tiles, held, total, sems) = refs[:n], refs[n:-4], refs[-4:]
    copies = [pltpu.make_async_copy(tiles_ref, tiles, sems.at[n])]
    start = 0
    for k, (ref, rows) in enumerate(zip(sources, spans)):
        copies.append(
            pltpu.make_async_copy(
                ref.at[pl.ds(0, rows)], held.at[pl.ds(start, rows)], sems.at[k]
            )
        )
        start += rows
    for copy in copies:
        copy.start()

    zeros = jnp.zeros((4, T, T), F32)

    def clear(k, carry):
        total[pl.ds(k * 4, 4)] = zeros
        return carry

    lax.fori_loop(0, total.shape[0] // 4, clear, 0)
    for copy in copies:
        copy.wait()

    def group(number, carry):
        products = []
        for k in range(GROUP):
            slot = number * GROUP + k
            product = lax.dot_general(
                tiles[slot],
                held[block(in_place[slot])],
                ((contract, (0,)), ((), ())),
                preferred_element_type=F32,
            )
            products.append(jnp.where(slot < live[0], product, 0.0))
        for k, product in enumerate(products):
            total[out_place[number * GROUP + k]] += product
        return carry

    lax.fori_loop(0, (live[0] + GROUP - 1) // GROUP, group, 0)
    start = 0
    for ref, blocks in zip(out_refs, outs):

        def out(k, carry, ref=ref, start=start):
            ref[block(k)] = total[start + k].astype(BF16)
            return carry

        lax.fori_loop(0, blocks, out, 0)
        start += blocks


def products(live, in_place, out_place, tiles, sources, spans, outs, contract):
    return pl.pallas_call(
        functools.partial(products_kernel, spans=spans, outs=outs, contract=contract),
        out_shape=[jax.ShapeDtypeStruct((n * T, T), BF16) for n in outs],
        in_specs=[SMEM] * 3 + [ANY] * (1 + len(sources)),
        out_specs=[VMEM] * len(outs),
        scratch_shapes=[
            pltpu.VMEM(tiles.shape, BF16),
            pltpu.VMEM((sum(spans), T), BF16),
            pltpu.VMEM((sum(outs), T, T), F32),
            pltpu.SemaphoreType.DMA((len(spans) + 1,)),
        ],
        compiler_params=PARAMS,
    )(live, in_place, out_place, tiles, *sources)


def pack_kernel(at_row, *refs):
    pieces, sends, (lists, counts), (held, words, table, sems) = (
        refs[:8],
        refs[8:14],
        refs[14:16],
        refs[16:],
    )
    copies = [pltpu.make_async_copy(p, held.at[k], sems.at[k]) for k, p in enumerate(pieces)]
    for copy in copies:
        copy.start()
    for copy in copies:
        copy.wait()
    for n in range(6):
        piece = n + 5 if n < 3 else n - 2
        words[pl.ds(n * 8, 8)] = held[piece, pl.ds(HALF, META)].astype(F32)[:8].astype(I32)
    copy = pltpu.make_async_copy(words, table, sems.at[0])
    copy.start()
    copy.wait()
    x, z = at_row[0] // 4, lax.rem(at_row[0], 4)
    for n in range(6):

        def step(slot, count, n=n):
            col = table[n * 8, slot]
            if n < 3:
                match = (col >= 0) & ((col & 0x38) == z * 16)
                inner = ((col >> 6) - x) & 3
                piece = inner
            else:
                match = (col >= 0) & ((col & 0xC8) == x * 64 + 8)
                inner = ((col >> 4) - z) & 3
                piece = 4 + inner
            match = match & (count < CAP)

            @pl.when(match)
            def _():
                lists[n * CAP + count] = inner * 8 + (col & 7)
                sends[n][block(count)] = held[piece, block(col & 7)]

            return count + jnp.where(match, 1, 0)

        counts[n] = lax.fori_loop(0, table[n * 8, 65], step, 0)


def pack(at_row, pieces):
    return pl.pallas_call(
        pack_kernel,
        out_shape=[jax.ShapeDtypeStruct((CAP * T, T), BF16)] * 6
        + [jax.ShapeDtypeStruct((6 * CAP,), I32), jax.ShapeDtypeStruct((6,), I32)],
        in_specs=[SMEM] + [ANY] * 8,
        out_specs=[VMEM] * 6 + [SMEM] * 2,
        scratch_shapes=[
            pltpu.VMEM((8, HALF + META, T), BF16),
            pltpu.VMEM((48, T), I32),
            pltpu.SMEM((48, T), I32),
            pltpu.SemaphoreType.DMA((8,)),
        ],
        compiler_params=PARAMS,
    )(at_row, *pieces)


def combine_kernel(lists, counts, own, *refs):
    parts, outs, (total,) = refs[:6], refs[6:14], refs[14:]

    def widen(k, carry):
        total[k] = own[block(k)].astype(F32)
        return carry

    lax.fori_loop(0, 64, widen, 0)
    for n, part in enumerate(parts):

        def add(k, carry, n=n, part=part):
            total[lists[n * CAP + k] + n // 3 * 32] += part[block(k)].astype(F32)
            return carry

        lax.fori_loop(0, counts[n], add, 0)
    for n, ref in enumerate(outs):

        def out(k, carry, n=n, ref=ref):
            ref[block(k)] = total[n * 8 + k].astype(ref.dtype)
            return carry

        lax.fori_loop(0, 8, out, 0)


def combine(lists, counts, own, parts):
    return pl.pallas_call(
        combine_kernel,
        out_shape=[
            jax.ShapeDtypeStruct((HALF, T), BF16 if d else F32) for _ in range(2) for d in range(4)
        ],
        in_specs=[SMEM] * 2 + [VMEM] * 7,
        out_specs=[VMEM] * 8,
        scratch_shapes=[pltpu.VMEM((64, T, T), F32)],
        compiler_params=PARAMS,
    )(lists, counts, own, *parts)


def dense_kernel(m0, m1, m2, m3, grad, weight, offset, hidden, projected, sums):
    @pl.when(pl.program_id(0) == 0)
    def _():
        sums[...] = jnp.zeros_like(sums)

    mixed = m0[...].astype(F32) + m1[...].astype(F32) + m2[...].astype(F32) + m3[...].astype(F32)
    high = mixed.astype(BF16)
    low = (mixed - high.astype(F32)).astype(BF16)
    w = weight[...]
    pre = jnp.dot(high, w, preferred_element_type=F32)
    pre = pre + jnp.dot(low, w, preferred_element_type=F32) + offset[...]
    s = jax.nn.sigmoid(pre)
    hidden[...] = (pre * s).astype(BF16)
    slope = (grad[...].astype(F32) * s * (1.0 + pre * (1.0 - s))).astype(BF16)
    projected[...] = lax.dot_general(
        slope, w, (((1,), (1,)), ((), ())), preferred_element_type=F32
    ).astype(BF16)
    over_rows = (((0,), (0,)), ((), ()))
    sums[:T] += lax.dot_general(
        high, slope, over_rows, preferred_element_type=F32
    ) + lax.dot_general(low, slope, over_rows, preferred_element_type=F32)
    sums[T:] += jnp.sum(slope.astype(F32).reshape(-1, 8, slope.shape[1]), axis=0)


def dense(parts, grad, weight, offset):
    rows, width = parts[0].shape[0], weight.shape[1]
    step = 512
    half = pl.BlockSpec((step, T), lambda i: (i, 0))
    full = pl.BlockSpec((step, width), lambda i: (i, 0))
    return pl.pallas_call(
        dense_kernel,
        grid=(rows // step,),
        out_shape=[
            jax.ShapeDtypeStruct((rows, width), BF16),
            jax.ShapeDtypeStruct((rows, T), BF16),
            jax.ShapeDtypeStruct((T + 8, width), F32),
        ],
        in_specs=[half] * 4
        + [
            full,
            pl.BlockSpec((T, width), lambda i: (0, 0)),
            pl.BlockSpec((1, width), lambda i: (0, 0)),
        ],
        out_specs=[full, half, pl.BlockSpec((T + 8, width), lambda i: (0, 0))],
        compiler_params=PARAMS,
    )(*parts, grad, weight, offset)


def on_device(features, weight, offset, tile_values, tile_rows, tile_cols, live_tiles, grad_hidden):
    tiles = tile_values.reshape(tile_values.shape[2:])
    nodes_here = features.shape[0]
    scaling = 1.0 / math.sqrt(nodes_here * lax.axis_size("row") * lax.axis_size("col"))
    at_row, at_col = lax.axis_index("row"), lax.axis_index("col")
    live, cols = live_tiles.reshape(1), tile_cols.reshape(-1)
    row_place, col_place, dense_place, named, overflow = places(
        tile_rows.reshape(-1), cols, live, at_row, at_col
    )

    meta = jnp.concatenate([named, overflow.astype(I32)[None], live, jnp.zeros(62, I32)])
    meta = jnp.broadcast_to(meta.astype(BF16), (META, T))
    first = ring_gather(jnp.concatenate([features[:HALF], meta]), along_x)
    second = ring_gather(jnp.concatenate([features[HALF:], meta]), along_z)
    *sends, lists, counts = pack(at_row.reshape(1), first + second)
    named_blocks = (
        ring_send([None] + sends[:3], along_z)[1:] + ring_send([None] + sends[3:], along_x)[1:]
    )
    full = functools.reduce(jnp.maximum, [piece[HALF, 64] for piece in first])
    full = jnp.broadcast_to(full.astype(F32), (8, T))
    for along in (along_z, along_y):
        full = functools.reduce(jnp.maximum, ring_gather(full, along))
    full = jnp.maximum(full, other_core(full))[0, 0] > 0.5

    def forward_all(first, second, named_blocks):
        whole = [jnp.concatenate([p[:HALF] for p in half]) for half in (first, second)]
        whole = ring_gather(whole[0], along_z) + ring_gather(whole[1], along_x)
        return products(
            live, dense_place, row_place, tiles, whole, (4 * HALF,) * 8, (64, 64), (1,)
        )

    def forward_named(first, second, named_blocks):
        return products(
            live,
            col_place,
            row_place,
            tiles,
            first + second + named_blocks,
            (HALF,) * 8 + (CAP * T,) * 6,
            (64, 64),
            (1,),
        )

    send, keep = lax.cond(full, forward_all, forward_named, first, second, named_blocks)

    both = keep.astype(F32) + other_core(send).astype(F32)
    both = both.reshape(4, nodes_here, T)
    mixed_parts = ring_send([both[d].astype(BF16) for d in range(4)], along_y)
    hidden, projected, sums = dense(mixed_parts, grad_hidden, weight, offset.reshape(1, -1))

    own = ring_gather(projected, along_y)
    gathered = [other_core(piece) for piece in own] + own

    for along in (along_x, along_z, along_y):
        sums = ring_sum(sums, along)
    sums = (sums + other_core(sums)) * scaling

    here, *parts = products(
        live,
        row_place,
        col_place,
        tiles,
        gathered,
        (nodes_here,) * 8,
        (64,) + (CAP,) * 6,
        (0,),
    )
    parts = (
        ring_send([None] + parts[:3], along_z)[1:] + ring_send([None] + parts[3:], along_x)[1:]
    )

    def backward_all(here, parts, gathered):
        outs = products(
            live, row_place, dense_place, tiles, gathered, (nodes_here,) * 8, (32,) * 8, (0,)
        )
        result = []
        for pieces, along in ((outs[:4], along_z), (outs[4:], along_x)):
            mine = total_of(ring_send(pieces, along)).reshape(4, HALF, T)
            result += [mine[0]] + [mine[d].astype(BF16) for d in (1, 2, 3)]
        return result

    def backward_named(here, parts, gathered):
        return list(combine(lists, counts, here, parts))

    outs = lax.cond(full, backward_all, backward_named, here, parts, gathered)
    first = total_of(ring_send(outs[:4], along_x))
    second = total_of(ring_send(outs[4:], along_z))
    grad_features = jnp.concatenate([first, second])
    return (hidden, grad_features, sums[:T], jnp.sum(sums[T:], axis=0))


def solution(mesh):
    in_specs = (
        P(("col", "row"), None),
        P(),
        P(),
        P("row", "col", None, None, None),
        P("row", "col", None),
        P("row", "col", None),
        P("row", "col"),
        P(("row", "col"), None),
    )
    out_specs = (P(("row", "col"), None), P(("col", "row"), None), P(), P())
    return jax.shard_map(
        on_device, mesh=mesh, in_specs=in_specs, out_specs=out_specs, check_vma=False
    )
```

profile of v0, /device:TPU:0, one launch (start us, length us, event | category | flops | bytes accessed | tf_op | source)
XLA Modules:
  0.0 264.0 jit_solution(1703816500487672366)
XLA Ops:
  9.1 3.6 %collective-permute-start.23 = (bf16[1040,128]{1,0:T(8,128)(2,1)S(1)}, bf16[1040,128]{1,0:T(8,128)(2,1)S(1)}, u32[]{:S(2)}, u32[]{:S(2)}) collective-permute-start(bf16[1040,128]{1,0:T(8,128)(2,1)S(1)} %get-tuple-element.269.refs_4_), channel_id=1, source_target_pairs={{0,16},{8,24},{16,0},{24,8},{32,48},{40,56},{48,32},{56,40},{64,80... | collective-permute-start | bytes 798728 | tf_op jit(solution)/shard_map/ppermute | solution.py:31
  20.4 4.1 %collective-permute-done.23.refs_6_ = bf16[1040,128]{1,0:T(8,128)(2,1)S(1)} collective-permute-done((bf16[1040,128]{1,0:T(8,128)(2,1)S(1)}, bf16[1040,128]{1,0:T(8,128)(2,1)S(1)}, u32[]{:S(2)}, u32[]{:S(2)}) %collective-permute-start.23) | collective-permute-done | bytes 266272 | tf_op jit(solution)/shard_map/ppermute | solution.py:31
  24.5 4.4 %collective-permute-done.13.refs_2_ = bf16[1040,128]{1,0:T(8,128)(2,1)S(1)} collective-permute-done((bf16[1040,128]{1,0:T(8,128)(2,1)S(1)}, bf16[1040,128]{1,0:T(8,128)(2,1)S(1)}, u32[]{:S(2)}, u32[]{:S(2)}) %collective-permute-start.13) | collective-permute-done | bytes 266272 | tf_op jit(solution)/shard_map/ppermute | solution.py:26
  28.9 7.1 %shard_map.111 = (bf16[2048,128]{1,0:T(8,128)(2,1)}, bf16[2048,128]{1,0:T(8,128)(2,1)}, bf16[2048,128]{1,0:T(8,128)(2,1)}, bf16[2048,128]{1,0:T(8,128)(2,1)}, bf...) custom-call(s32[1]{0:T(128)} %bitcast.10.at_row, ...), custom_call_target="tpu_custom_call" | custom-call | tf_op jit(solution)/shard_map/pallas_call | solution.py:205
  67.4 7.4 %collective-permute-done.26 = bf16[2048,128]{1,0:T(8,128)(2,1)S(1)} collective-permute-done((bf16[2048,128]{1,0:T(8,128)(2,1)}, bf16[2048,128]{1,0:T(8,128)(2,1)S(1)}, u32[]{:S(2)}, u32[]{:S(2)}) %collective-permute-start.26) | collective-permute-done | bytes 524320 | tf_op jit(solution)/shard_map/ppermute | solution.py:31
  74.7 10.7 %collective-permute-done.27 = bf16[2048,128]{1,0:T(8,128)(2,1)S(1)} collective-permute-done((bf16[2048,128]{1,0:T(8,128)(2,1)}, bf16[2048,128]{1,0:T(8,128)(2,1)S(1)}, u32[]{:S(2)}, u32[]{:S(2)}) %collective-permute-start.27) | collective-permute-done | bytes 524320 | tf_op jit(solution)/shard_map/ppermute | solution.py:31
  87.7 3.6 %collective-permute-done.30 = bf16[2048,128]{1,0:T(8,128)(2,1)S(1)} collective-permute-done((bf16[2048,128]{1,0:T(8,128)(2,1)}, bf16[2048,128]{1,0:T(8,128)(2,1)S(1)}, u32[]{:S(2)}, u32[]{:S(2)}) %collective-permute-start.30) | collective-permute-done | bytes 524320 | tf_op jit(solution)/shard_map/ppermute | solution.py:26
  91.2 8.7 %conditional.11 = ((bf16[8192,128]{1,0:T(8,128)(2,1)}, bf16[8192,128]{1,0:T(8,128)(2,1)})) conditional(s32[]{:T(128)} %bitcast.7, (s32[1]{0:T(128)}, s32[64]{0:T(128)S(1)}, s32[64]{0:T(128)S(1)}, bf16[64,128,128]{2,1,0:T(8,128)(2,1)S(1)}, bf16[1040,128]{1,0:T(8,128)(2,1)S(1)}, /*index=5*/bf16[1040,128]{1,0:T(8,128)(2,1)}, ...), branch_computations={%region_4.5_spmd, %region_5.6_spmd} | conditional | flops 8388608 | bytes 70304328
  91.2 8.7 %branch_0_fun.2 = (bf16[8192,128]{1,0:T(8,128)(2,1)}, bf16[8192,128]{1,0:T(8,128)(2,1)}) custom-call(s32[1]{0:T(128)} %get-tuple-element.118.live, s32[64]{0:T(128)S(1)} %get-tuple-element.119.in_place, s32[64]{0:T(128)S(1)} %get-tuple-element.120.out_place, bf16[64,128,128]{2,1,0:T(8,128)(2,1)S(1)} %get-tuple-element.121.tiles_ref, ...), custom_call_target="tpu_custom_call" | custom-call | tf_op jit(solution)/shard_map/cond/branch_0_fun/pallas_call | solution.py:146
  100.0 4.4 %collective-permute-done.31 = bf16[8192,128]{1,0:T(8,128)(2,1)S(1)} collective-permute-done((bf16[8192,128]{1,0:T(8,128)(2,1)}, bf16[8192,128]{1,0:T(8,128)(2,1)S(1)}, u32[]{:S(2)}, u32[]{:S(2)}) %collective-permute-start.31) | collective-permute-done | bytes 2097184 | tf_op jit(solution)/shard_map/ppermute | solution.py:41
  111.0 11.9 %collective-permute-done.34.m3 = bf16[2048,128]{1,0:T(8,128)(2,1)S(1)} collective-permute-done((bf16[2048,128]{1,0:T(8,128)(2,1)S(1)}, bf16[2048,128]{1,0:T(8,128)(2,1)S(1)}, u32[]{:S(2)}, u32[]{:S(2)}) %collective-permute-start.34) | collective-permute-done | bytes 524320 | tf_op jit(solution)/shard_map/ppermute | solution.py:36
  122.9 11.3 %collective-permute-done.33.m2 = bf16[2048,128]{1,0:T(8,128)(2,1)S(1)} collective-permute-done((bf16[2048,128]{1,0:T(8,128)(2,1)S(1)}, bf16[2048,128]{1,0:T(8,128)(2,1)S(1)}, u32[]{:S(2)}, u32[]{:S(2)}) %collective-permute-start.33) | collective-permute-done | bytes 524320 | tf_op jit(solution)/shard_map/ppermute | solution.py:36
  135.3 5.5 %shard_map.112 = (bf16[2048,256]{1,0:T(8,128)(2,1)}, bf16[2048,128]{1,0:T(8,128)(2,1)S(1)}, f32[136,256]{1,0:T(8,128)}) custom-call(bf16[2048,128]{1,0:T(8,128)(2,1)} %get-tuple-element.266.m0, bf16[2048,128]{1,0:T(8,128)(2,1)} %copy-done.22, bf16[2048,128]{1,0:T(8,128)(2,1)} %copy-done.21, bf16[2048,128]{1,0:T(8,128)(2,1)} %copy-done.20, ...), custom_call_target="tpu_custom_call" | custom-call | tf_op jit(solution)/shard_map/pallas_call | solution.py:287
  144.8 10.6 %collective-permute-done.40.refs_7_ = bf16[2048,128]{1,0:T(8,128)(2,1)S(1)} collective-permute-done((bf16[2048,128]{1,0:T(8,128)(2,1)S(1)}, bf16[2048,128]{1,0:T(8,128)(2,1)S(1)}, u32[]{:S(2)}, u32[]{:S(2)}) %collective-permute-start.40) | collective-permute-done | bytes 524320 | tf_op jit(solution)/shard_map/ppermute | solution.py:36
  155.5 12.4 %collective-permute-done.38.refs_6_ = bf16[2048,128]{1,0:T(8,128)(2,1)S(1)} collective-permute-done((bf16[2048,128]{1,0:T(8,128)(2,1)S(1)}, bf16[2048,128]{1,0:T(8,128)(2,1)S(1)}, u32[]{:S(2)}, u32[]{:S(2)}) %collective-permute-start.38) | collective-permute-done | bytes 524320 | tf_op jit(solution)/shard_map/ppermute | solution.py:36
  172.5 8.1 %shard_map.113 = (bf16[8192,128]{1,0:T(8,128)(2,1)S(1)}, bf16[2048,128]{1,0:T(8,128)(2,1)}, bf16[2048,128]{1,0:T(8,128)(2,1)}, bf16[2048,128]{1,0:T(8,128)(2,1)}...) custom-call(s32[1]{0:T(128)} %bitcast.44.live, ...), custom_call_target="tpu_custom_call" | custom-call | tf_op jit(solution)/shard_map/pallas_call | solution.py:146
  186.6 4.0 %collective-permute-done.59 = f32[136,256]{1,0:T(8,128)S(1)} collective-permute-done((f32[136,256]{1,0:T(8,128)S(1)}, f32[136,256]{1,0:T(8,128)S(1)}, u32[]{:S(2)}, u32[]{:S(2)}) %collective-permute-start.59) | collective-permute-done | bytes 139296 | tf_op jit(solution)/shard_map/ppermute | solution.py:31
  190.7 8.5 %collective-permute-done.57 = f32[136,256]{1,0:T(8,128)S(1)} collective-permute-done((f32[136,256]{1,0:T(8,128)S(1)}, f32[136,256]{1,0:T(8,128)S(1)}, u32[]{:S(2)}, u32[]{:S(2)}) %collective-permute-start.57) | collective-permute-done | bytes 139296 | tf_op jit(solution)/shard_map/ppermute | solution.py:31
  212.3 7.0 %collective-permute-done.43 = bf16[2048,128]{1,0:T(8,128)(2,1)S(1)} collective-permute-done((bf16[2048,128]{1,0:T(8,128)(2,1)}, bf16[2048,128]{1,0:T(8,128)(2,1)S(1)}, u32[]{:S(2)}, u32[]{:S(2)}) %collective-permute-start.43) | collective-permute-done | bytes 524320 | tf_op jit(solution)/shard_map/ppermute | solution.py:31
  219.3 9.7 %collective-permute-done.44 = bf16[2048,128]{1,0:T(8,128)(2,1)S(1)} collective-permute-done((bf16[2048,128]{1,0:T(8,128)(2,1)}, bf16[2048,128]{1,0:T(8,128)(2,1)S(1)}, u32[]{:S(2)}, u32[]{:S(2)}) %collective-permute-start.44) | collective-permute-done | bytes 524320 | tf_op jit(solution)/shard_map/ppermute | solution.py:31
  229.1 6.4 %collective-permute-done.47 = bf16[2048,128]{1,0:T(8,128)(2,1)S(1)} collective-permute-done((bf16[2048,128]{1,0:T(8,128)(2,1)}, bf16[2048,128]{1,0:T(8,128)(2,1)S(1)}, u32[]{:S(2)}, u32[]{:S(2)}) %collective-permute-start.47) | collective-permute-done | bytes 524320 | tf_op jit(solution)/shard_map/ppermute | solution.py:26
  235.4 5.0 %conditional.10 = ((f32[1024,128]{1,0:T(8,128)S(1)}, bf16[1024,128]{1,0:T(8,128)(2,1)S(1)}, bf16[1024,128]{1,0:T(8,128)(2,1)S(1)}, bf16[1024,128]{1,0:T(8,128)(2...) conditional(s32[]{:T(128)} %bitcast.7, (s32[96]{0:T(128)S(1)}, ...), branch_computations={%region_6.7_spmd, %region_7.8_spmd} | conditional | flops 8388608 | bytes 49283412 | solution.py:390
  252.5 4.8 %collective-permute-done.50 = bf16[1024,128]{1,0:T(8,128)(2,1)S(1)} collective-permute-done((bf16[1024,128]{1,0:T(8,128)(2,1)S(1)}, bf16[1024,128]{1,0:T(8,128)(2,1)S(1)}, u32[]{:S(2)}, u32[]{:S(2)}) %collective-permute-start.50) | collective-permute-done | bytes 262176 | tf_op jit(solution)/shard_map/ppermute | solution.py:26
  259.2 3.7 %collective-permute-done.53 = bf16[1024,128]{1,0:T(8,128)(2,1)S(1)} collective-permute-done((bf16[1024,128]{1,0:T(8,128)(2,1)S(1)}, bf16[1024,128]{1,0:T(8,128)(2,1)S(1)}, u32[]{:S(2)}, u32[]{:S(2)}) %collective-permute-start.53) | collective-permute-done | bytes 262176 | tf_op jit(solution)/shard_map/ppermute | solution.py:31
  (157 shorter events, 101.2 us)
Async XLA Ops:
  9.1 15.4 %collective-permute-start.23 = (bf16[1040,128]{1,0:T(8,128)(2,1)S(1)}, bf16[1040,128]{1,0:T(8,128)(2,1)S(1)}, u32[]{:S(2)}, u32[]{:S(2)}) collective-permute-start(bf16[1040,128]{1,0:T(8,128)(2,1)S(1)} %get-tuple-element.269.refs_4_), channel_id=1, source_target_pairs={{0,16},{8,24},{16,0},{24,8},{32,48},{40,56},{48,32},{56,40},{64,80... | collective-permute-start | bytes 798728 | tf_op jit(solution)/shard_map/ppermute | solution.py:31
  36.0 29.9 %collective-permute-start.25 = (bf16[2048,128]{1,0:T(8,128)(2,1)}, bf16[2048,128]{1,0:T(8,128)(2,1)}, u32[]{:S(2)}, u32[]{:S(2)}) collective-permute-start(bf16[2048,128]{1,0:T(8,128)(2,1)} %get-tuple-element.209), channel_id=1, source_target_pairs={{0,24},{8,0},{16,8},{24,16},{32,56},{40,32},{48,40},{56,48},{64,88... | collective-permute-start | bytes 1572872 | tf_op jit(solution)/shard_map/ppermute | solution.py:31
  58.2 16.6 %collective-permute-start.26 = (bf16[2048,128]{1,0:T(8,128)(2,1)}, bf16[2048,128]{1,0:T(8,128)(2,1)S(1)}, u32[]{:S(2)}, u32[]{:S(2)}) collective-permute-start(bf16[2048,128]{1,0:T(8,128)(2,1)} %get-tuple-element.210), channel_id=1, source_target_pairs={{0,16},{8,24},{16,0},{24,8},{32,48},{40,56},{48,32},{56,40},{64,80... | collective-permute-start | bytes 1572872 | tf_op jit(solution)/shard_map/ppermute | solution.py:31
  59.6 25.8 %collective-permute-start.27 = (bf16[2048,128]{1,0:T(8,128)(2,1)}, bf16[2048,128]{1,0:T(8,128)(2,1)S(1)}, u32[]{:S(2)}, u32[]{:S(2)}) collective-permute-start(bf16[2048,128]{1,0:T(8,128)(2,1)} %get-tuple-element.211), channel_id=1, source_target_pairs={{0,8},{8,16},{16,24},{24,0},{32,40},{40,48},{48,56},{56,32},{64,72... | collective-permute-start | bytes 1572872 | tf_op jit(solution)/shard_map/ppermute | solution.py:31
  62.3 25.4 %collective-permute-start.28 = (bf16[2048,128]{1,0:T(8,128)(2,1)}, bf16[2048,128]{1,0:T(8,128)(2,1)S(1)}, u32[]{:S(2)}, u32[]{:S(2)}) collective-permute-start(bf16[2048,128]{1,0:T(8,128)(2,1)} %get-tuple-element.212), channel_id=1, source_target_pairs={{0,96},{8,104},{16,112},{24,120},{32,0},{40,8},{48,16},{56,24},{64... | collective-permute-start | bytes 1572872 | tf_op jit(solution)/shard_map/ppermute | solution.py:26
  64.9 22.8 %collective-permute-start.29 = (bf16[2048,128]{1,0:T(8,128)(2,1)}, bf16[2048,128]{1,0:T(8,128)(2,1)S(1)}, u32[]{:S(2)}, u32[]{:S(2)}) collective-permute-start(bf16[2048,128]{1,0:T(8,128)(2,1)} %get-tuple-element.213), channel_id=1, source_target_pairs={{0,64},{8,72},{16,80},{24,88},{32,96},{40,104},{48,112},{56,120},{... | collective-permute-start | bytes 1572872 | tf_op jit(solution)/shard_map/ppermute | solution.py:26
  65.9 25.3 %collective-permute-start.30 = (bf16[2048,128]{1,0:T(8,128)(2,1)}, bf16[2048,128]{1,0:T(8,128)(2,1)S(1)}, u32[]{:S(2)}, u32[]{:S(2)}) collective-permute-start(bf16[2048,128]{1,0:T(8,128)(2,1)} %get-tuple-element.214), channel_id=1, source_target_pairs={{0,32},{8,40},{16,48},{24,56},{32,64},{40,72},{48,80},{56,88},{64,... | collective-permute-start | bytes 1572872 | tf_op jit(solution)/shard_map/ppermute | solution.py:26
  107.4 15.4 %collective-permute-start.34 = (bf16[2048,128]{1,0:T(8,128)(2,1)S(1)}, bf16[2048,128]{1,0:T(8,128)(2,1)S(1)}, u32[]{:S(2)}, u32[]{:S(2)}) collective-permute-start(bf16[2048,128]{1,0:T(8,128)(2,1)S(1)} %get-tuple-element.263), channel_id=1, source_target_pairs={{0,2},{1,3},{2,4},{3,5},{4,6},{5,7},{6,0},{7,1},{8,10},{9,11},{10,... | collective-permute-start | bytes 1572872 | tf_op jit(solution)/shard_map/ppermute | solution.py:36
  108.3 25.8 %collective-permute-start.33 = (bf16[2048,128]{1,0:T(8,128)(2,1)S(1)}, bf16[2048,128]{1,0:T(8,128)(2,1)S(1)}, u32[]{:S(2)}, u32[]{:S(2)}) collective-permute-start(bf16[2048,128]{1,0:T(8,128)(2,1)S(1)} %get-tuple-element.264), channel_id=1, source_target_pairs={{0,4},{1,5},{2,6},{3,7},{4,0},{5,1},{6,2},{7,3},{8,12},{9,13},{10,... | collective-permute-start | bytes 1572872 | tf_op jit(solution)/shard_map/ppermute | solution.py:36
  110.7 23.7 %collective-permute-start.32 = (bf16[2048,128]{1,0:T(8,128)(2,1)S(1)}, bf16[2048,128]{1,0:T(8,128)(2,1)S(1)}, u32[]{:S(2)}, u32[]{:S(2)}) collective-permute-start(bf16[2048,128]{1,0:T(8,128)(2,1)S(1)} %get-tuple-element.265), channel_id=1, source_target_pairs={{0,6},{1,7},{2,0},{3,1},{4,2},{5,3},{6,4},{7,5},{8,14},{9,15},{10,... | collective-permute-start | bytes 1572872 | tf_op jit(solution)/shard_map/ppermute | solution.py:36
  140.7 14.7 %collective-permute-start.40 = (bf16[2048,128]{1,0:T(8,128)(2,1)S(1)}, bf16[2048,128]{1,0:T(8,128)(2,1)S(1)}, u32[]{:S(2)}, u32[]{:S(2)}) collective-permute-start(bf16[2048,128]{1,0:T(8,128)(2,1)S(1)} %get-tuple-element.220.refs_4_), channel_id=1, source_target_pairs={{0,2},{1,3},{2,4},{3,5},{4,6},{5,7},{6,0},{7,1},{8,10},{9,11},{10,... | collective-permute-start | bytes 1572872 | tf_op jit(solution)/shard_map/ppermute | solution.py:36
  141.3 26.6 %collective-permute-start.38 = (bf16[2048,128]{1,0:T(8,128)(2,1)S(1)}, bf16[2048,128]{1,0:T(8,128)(2,1)S(1)}, u32[]{:S(2)}, u32[]{:S(2)}) collective-permute-start(bf16[2048,128]{1,0:T(8,128)(2,1)S(1)} %get-tuple-element.220.refs_4_), channel_id=1, source_target_pairs={{0,4},{1,5},{2,6},{3,7},{4,0},{5,1},{6,2},{7,3},{8,12},{9,13},{10,... | collective-permute-start | bytes 1572872 | tf_op jit(solution)/shard_map/ppermute | solution.py:36
  144.8 23.1 %collective-permute-start.36 = (bf16[2048,128]{1,0:T(8,128)(2,1)S(1)}, bf16[2048,128]{1,0:T(8,128)(2,1)S(1)}, u32[]{:S(2)}, u32[]{:S(2)}) collective-permute-start(bf16[2048,128]{1,0:T(8,128)(2,1)S(1)} %get-tuple-element.220.refs_4_), channel_id=1, source_target_pairs={{0,6},{1,7},{2,0},{3,1},{4,2},{5,3},{6,4},{7,5},{8,14},{9,15},{10,... | collective-permute-start | bytes 1572872 | tf_op jit(solution)/shard_map/ppermute | solution.py:36
  144.8 23.6 %collective-permute-start.35 = (bf16[2048,128]{1,0:T(8,128)(2,1)S(1)}, bf16[2048,128]{1,0:T(8,128)(2,1)S(1)}, u32[]{:S(2)}, u32[]{:S(2)}) collective-permute-start(bf16[2048,128]{1,0:T(8,128)(2,1)S(1)} %get-tuple-element.220.refs_4_), channel_id=1, source_target_pairs={{0,1},{1,0},{2,3},{3,2},{4,5},{5,4},{6,7},{7,6},{8,9},{9,8},{10,11... | collective-permute-start | bytes 1572872 | tf_op jit(solution)/shard_map/ppermute | solution.py:41
  155.4 14.3 %collective-permute-start.41 = (bf16[2048,128]{1,0:T(8,128)(2,1)S(1)}, bf16[2048,128]{1,0:T(8,128)(2,1)S(1)}, u32[]{:S(2)}, u32[]{:S(2)}) collective-permute-start(bf16[2048,128]{1,0:T(8,128)(2,1)S(1)} %collective-permute-done.40.refs_7_), channel_id=1, source_target_pairs={{0,1},{1,0},{2,3},{3,2},{4,5},{5,4},{6,7},{7,6},{8,9},{9,8},{10,11... | collective-permute-start | bytes 1572872 | tf_op jit(solution)/shard_map/ppermute | solution.py:41
  180.7 30.8 %collective-permute-start.42 = (bf16[2048,128]{1,0:T(8,128)(2,1)}, bf16[2048,128]{1,0:T(8,128)(2,1)S(1)}, u32[]{:S(2)}, u32[]{:S(2)}) collective-permute-start(bf16[2048,128]{1,0:T(8,128)(2,1)} %get-tuple-element.222), channel_id=1, source_target_pairs={{0,24},{8,0},{16,8},{24,16},{32,56},{40,32},{48,40},{56,48},{64,88... | collective-permute-start | bytes 1572872 | tf_op jit(solution)/shard_map/ppermute | solution.py:31
  183.9 15.2 %collective-permute-start.57 = (f32[136,256]{1,0:T(8,128)S(1)}, f32[136,256]{1,0:T(8,128)S(1)}, u32[]{:S(2)}, u32[]{:S(2)}) collective-permute-start(f32[136,256]{1,0:T(8,128)S(1)} %add_add_fusion.2), channel_id=1, source_target_pairs={{0,24},{8,0},{16,8},{24,16},{32,56},{40,32},{48,40},{56,48},{64,88... | collective-permute-start | bytes 417800 | tf_op jit(solution)/shard_map/ppermute | solution.py:31
  202.7 16.6 %collective-permute-start.43 = (bf16[2048,128]{1,0:T(8,128)(2,1)}, bf16[2048,128]{1,0:T(8,128)(2,1)S(1)}, u32[]{:S(2)}, u32[]{:S(2)}) collective-permute-start(bf16[2048,128]{1,0:T(8,128)(2,1)} %get-tuple-element.223), channel_id=1, source_target_pairs={{0,16},{8,24},{16,0},{24,8},{32,48},{40,56},{48,32},{56,40},{64,80... | collective-permute-start | bytes 1572872 | tf_op jit(solution)/shard_map/ppermute | solution.py:31
  205.5 23.5 %collective-permute-start.44 = (bf16[2048,128]{1,0:T(8,128)(2,1)}, bf16[2048,128]{1,0:T(8,128)(2,1)S(1)}, u32[]{:S(2)}, u32[]{:S(2)}) collective-permute-start(bf16[2048,128]{1,0:T(8,128)(2,1)} %get-tuple-element.224), channel_id=1, source_target_pairs={{0,8},{8,16},{16,24},{24,0},{32,40},{40,48},{48,56},{56,32},{64,72... | collective-permute-start | bytes 1572872 | tf_op jit(solution)/shard_map/ppermute | solution.py:31
  209.4 19.7 %collective-permute-start.45 = (bf16[2048,128]{1,0:T(8,128)(2,1)}, bf16[2048,128]{1,0:T(8,128)(2,1)S(1)}, u32[]{:S(2)}, u32[]{:S(2)}) collective-permute-start(bf16[2048,128]{1,0:T(8,128)(2,1)} %get-tuple-element.225), channel_id=1, source_target_pairs={{0,96},{8,104},{16,112},{24,120},{32,0},{40,8},{48,16},{56,24},{64... | collective-permute-start | bytes 1572872 | tf_op jit(solution)/shard_map/ppermute | solution.py:26
  209.4 19.7 %collective-permute-start.46 = (bf16[2048,128]{1,0:T(8,128)(2,1)}, bf16[2048,128]{1,0:T(8,128)(2,1)S(1)}, u32[]{:S(2)}, u32[]{:S(2)}) collective-permute-start(bf16[2048,128]{1,0:T(8,128)(2,1)} %get-tuple-element.226), channel_id=1, source_target_pairs={{0,64},{8,72},{16,80},{24,88},{32,96},{40,104},{48,112},{56,120},{... | collective-permute-start | bytes 1572872 | tf_op jit(solution)/shard_map/ppermute | solution.py:26
  211.5 24.0 %collective-permute-start.47 = (bf16[2048,128]{1,0:T(8,128)(2,1)}, bf16[2048,128]{1,0:T(8,128)(2,1)S(1)}, u32[]{:S(2)}, u32[]{:S(2)}) collective-permute-start(bf16[2048,128]{1,0:T(8,128)(2,1)} %get-tuple-element.227), channel_id=1, source_target_pairs={{0,32},{8,40},{16,48},{24,56},{32,64},{40,72},{48,80},{56,88},{64,... | collective-permute-start | bytes 1572872 | tf_op jit(solution)/shard_map/ppermute | solution.py:26
  242.5 14.8 %collective-permute-start.50 = (bf16[1024,128]{1,0:T(8,128)(2,1)S(1)}, bf16[1024,128]{1,0:T(8,128)(2,1)S(1)}, u32[]{:S(2)}, u32[]{:S(2)}) collective-permute-start(bf16[1024,128]{1,0:T(8,128)(2,1)S(1)} %get-tuple-element.231), channel_id=1, source_target_pairs={{0,32},{8,40},{16,48},{24,56},{32,64},{40,72},{48,80},{56,88},{64,... | collective-permute-start | bytes 786440 | tf_op jit(solution)/shard_map/ppermute | solution.py:26
  244.5 14.7 %collective-permute-start.51 = (bf16[1024,128]{1,0:T(8,128)(2,1)S(1)}, bf16[1024,128]{1,0:T(8,128)(2,1)S(1)}, u32[]{:S(2)}, u32[]{:S(2)}) collective-permute-start(bf16[1024,128]{1,0:T(8,128)(2,1)S(1)} %get-tuple-element.233), channel_id=1, source_target_pairs={{0,24},{8,0},{16,8},{24,16},{32,56},{40,32},{48,40},{56,48},{64,88... | collective-permute-start | bytes 786440 | tf_op jit(solution)/shard_map/ppermute | solution.py:31
  (47 other events, 487.7 us)
where the time goes:
time: 266 us; the launch traced here: 264 us
  waiting for transfers between devices  139 us (52%)
  starting transfers between devices  68.2 us (26%)
  Pallas kernels  32.4 us (12%)
  local copies, waits for them, and re-layouts  10.3 us (4%)
  other arithmetic  8.52 us (3%)
  between operations  4.91 us (2%)
    ppermute x18, waiting for transfers between devices, along_z(): return lax.ppermute(value, 'row', pairs)  58.5 us
    ppermute x12, waiting for transfers between devices, along_y(): return lax.ppermute(value, 'col', pairs)  52.2 us
    ppermute x18, starting transfers between devices, along_z(): return lax.ppermute(value, 'row', pairs)  31.9 us
    ppermute x15, waiting for transfers between devices, along_x(): return lax.ppermute(value, 'row', pairs)  24.4 us
    ppermute x15, starting transfers between devices, along_x(): return lax.ppermute(value, 'row', pairs)  19.3 us
    pallas_call x2, Pallas kernels, products(): pl.pallas_call(functools.partial(products_kernel, spans=spans, outs=outs,...  16.8 us
    ppermute x12, starting transfers between devices, along_y(): return lax.ppermute(value, 'col', pairs)  16.3 us
    pallas_call x1, Pallas kernels, pack(): pl.pallas_call(pack_kernel, out_shape=[jax.ShapeDtypeStruct((CAP * T, T),...  7.06 us
  transfers between devices with their start and end apart: 52, of which 27 were waited for; matrix products, arithmetic and copies ran while one was open for 2% of the time, Pallas kernels for 3%

commit v1 on v0

v1 whole, which is shorter than its diff:
```python
import functools
import math

import jax
import jax.numpy as jnp
from jax import lax
from jax.experimental import pallas as pl
from jax.experimental.pallas import tpu as pltpu
from jax.sharding import PartitionSpec as P

T = 128
F32, BF16, I32 = jnp.float32, jnp.bfloat16, jnp.int32
VMEM_BYTES = 56 * 1024 * 1024
GROUP = 4
HALF = 8 * T
META = 16
CAP = 16
FLAG_LANE = 64
SMEM = pl.BlockSpec(memory_space=pltpu.SMEM)
VMEM = pl.BlockSpec(memory_space=pltpu.VMEM)
ANY = pl.BlockSpec(memory_space=pl.ANY)
PARAMS = pltpu.CompilerParams(vmem_limit_bytes=VMEM_BYTES)


def along_x(value, to):
    pairs = [(x * 4 + z, to(x) % 4 * 4 + z) for x in range(4) for z in range(4)]
    return lax.ppermute(value, "row", pairs)


def along_z(value, to):
    pairs = [(x * 4 + z, x * 4 + to(z) % 4) for x in range(4) for z in range(4)]
    return lax.ppermute(value, "row", pairs)


def along_y(value, to):
    pairs = [(y * 2 + k, to(y) % 4 * 2 + k) for y in range(4) for k in range(2)]
    return lax.ppermute(value, "col", pairs)


def other_core(value):
    pairs = [(y * 2 + k, y * 2 + 1 - k) for y in range(4) for k in range(2)]
    return lax.ppermute(value, "col", pairs)


def ahead(step):
    return lambda at: at + step


def ring_gather(value, along):
    return [value, along(value, ahead(-1)), along(value, ahead(2)), along(value, ahead(1))]


def ring_swap(pieces, along):
    return [
        pieces[0],
        along(pieces[3], ahead(-1)),
        along(pieces[2], ahead(2)),
        along(pieces[1], ahead(1)),
    ]


def swap_pairs(value, along, bit):
    return along(value, lambda at: at ^ bit)


def total_of(pieces):
    return sum(piece.astype(F32) for piece in pieces)


def block(place):
    return pl.ds(pl.multiple_of(place * T, T), T)


def prepare_kernel(at_row, at_col, live_ref, rows_ref, cols_ref, features, first_out, second_out, tables, sems):
    outs = (first_out, second_out)
    copies = [
        pltpu.make_async_copy(
            features.at[pl.ds(k * HALF, HALF)], outs[k].at[pl.ds(0, HALF)], sems.at[k]
        )
        for k in range(2)
    ]
    for copy in copies:
        copy.start()
    live = live_ref[0]
    x, z = at_row[0] >> 2, at_row[0] & 3
    y, core = at_col[0] >> 1, at_col[0] & 1
    rows, cols = rows_ref[...], cols_ref[...]
    slots = cols.shape[1]

    same_core = jnp.where(((rows >> 4) & 1) == core, 64, 0)
    row_place = same_core + (((rows >> 5) - y) & 3) * 16 + (rows & 15)
    dx, dz = ((cols >> 6) - x) & 3, ((cols >> 4) - z) & 3
    half = (cols >> 3) & 1
    outer, inner = jnp.where(half == 0, dz, dx), jnp.where(half == 0, dx, dz)
    group, code = half * 4 + outer, inner * 8 + (cols & 7)
    dense_place = group * 32 + code

    t = lax.broadcasted_iota(I32, (slots, slots), 0)
    s = lax.broadcasted_iota(I32, (slots, slots), 1)
    lane = lax.broadcasted_iota(I32, (slots, T), 1).astype(F32)

    def column(row):
        return jnp.sum(jnp.where(t == s, row, 0.0), axis=1, keepdims=True)

    def count(mask, value=1.0):
        return jnp.sum(jnp.where(mask, value, 0.0), axis=0, keepdims=True)

    valid = lax.broadcasted_iota(I32, (1, slots), 1) < live
    cols_f, group_f = cols.astype(F32), group.astype(F32)
    same = column(cols_f) == cols_f
    first = valid & (count(same & (t < s)) == 0.0)
    first_c = column(jnp.where(first, 1.0, 0.0)) > 0.0
    group_c = column(group_f)
    rank = count((t < s) & first_c & (group_c == group_f))
    over = jnp.where(first & (outer != 0) & (rank >= CAP), 1.0, 0.0)
    over = jnp.max(over, axis=1, keepdims=True)
    far = (64 + (half * 3 + outer - 1) * CAP).astype(F32) + jnp.minimum(rank, CAP - 1.0)
    place = jnp.where(outer == 0, (half * 32 + code).astype(F32), far)
    place = count(same & first_c, column(place))
    place = jnp.where(valid, place, 0.0).astype(I32)
    pad = jnp.zeros((5, slots), I32)
    tables[...] = jnp.concatenate([row_place, place, dense_place, pad], axis=0)

    key = column(jnp.where(first & (rank < CAP), group_f * CAP + rank, -1.0))
    wanted = count(key == lane, column(code.astype(F32)))
    amounts = jnp.minimum(count((group_c == lane) & first_c), 1.0 * CAP)
    line = lax.broadcasted_iota(I32, (META, T), 0)
    amounts = jnp.where(lax.broadcasted_iota(I32, (1, T), 1) == FLAG_LANE, over, amounts)
    meta = jnp.where(line == 0, wanted, jnp.where(line == 1, amounts, 0.0)).astype(BF16)
    for ref in outs:
        ref[pl.ds(HALF, META)] = meta
    for copy in copies:
        copy.wait()


def prepare(at_row, at_col, live, rows, cols, features):
    slots = cols.shape[-1]
    return pl.pallas_call(
        prepare_kernel,
        out_shape=[jax.ShapeDtypeStruct((HALF + META, T), BF16)] * 2
        + [jax.ShapeDtypeStruct((8, slots), I32)],
        in_specs=[SMEM] * 3 + [VMEM] * 2 + [ANY],
        out_specs=[VMEM] * 3,
        scratch_shapes=[pltpu.SemaphoreType.DMA((2,))],
        compiler_params=PARAMS,
    )(at_row, at_col, live, rows.reshape(1, slots), cols.reshape(1, slots), features)


def products_kernel(live, tables, tiles_ref, *refs, spans, outs, contract, in_row, out_row):
    n = len(spans)
    sources, out_refs, (tiles, held, total, sems) = refs[:n], refs[n:-4], refs[-4:]
    copies = [pltpu.make_async_copy(tiles_ref, tiles, sems.at[n])]
    start = 0
    for k, (ref, rows) in enumerate(zip(sources, spans)):
        copies.append(
            pltpu.make_async_copy(
                ref.at[pl.ds(0, rows)], held.at[pl.ds(start, rows)], sems.at[k]
            )
        )
        start += rows
    if len(out_refs) > len(outs):
        sources, passed = out_refs[0], out_refs[-1]
        out_refs = out_refs[1:-1]
        copies.append(pltpu.make_async_copy(sources, passed, sems.at[n + 1]))
    for copy in copies:
        copy.start()

    zeros = jnp.zeros((4, T, T), F32)

    def clear(k, carry):
        total[pl.ds(k * 4, 4)] = zeros
        return carry

    lax.fori_loop(0, total.shape[0] // 4, clear, 0)
    for copy in copies:
        copy.wait()

    def group(number, carry):
        products = []
        for k in range(GROUP):
            slot = number * GROUP + k
            product = lax.dot_general(
                tiles[slot],
                held[block(tables[in_row, slot])],
                ((contract, (0,)), ((), ())),
                preferred_element_type=F32,
            )
            products.append(jnp.where(slot < live[0], product, 0.0))
        for k, product in enumerate(products):
            total[tables[out_row, number * GROUP + k]] += product
        return carry

    lax.fori_loop(0, (live[0] + GROUP - 1) // GROUP, group, 0)
    start = 0
    for ref, blocks in zip(out_refs, outs):

        def out(k, carry, ref=ref, start=start):
            ref[block(k)] = total[start + k].astype(BF16)
            return carry

        lax.fori_loop(0, blocks, out, 0)
        start += blocks


def products(live, tables, in_row, out_row, tiles, sources, spans, outs, contract, passed=()):
    kernel = functools.partial(
        products_kernel,
        spans=spans,
        outs=outs,
        contract=contract,
        in_row=in_row,
        out_row=out_row,
    )
    return pl.pallas_call(
        kernel,
        out_shape=[jax.ShapeDtypeStruct((n * T, T), BF16) for n in outs]
        + [jax.ShapeDtypeStruct(p.shape, p.dtype) for p in passed],
        in_specs=[SMEM] * 2 + [ANY] * (1 + len(sources) + len(passed)),
        out_specs=[VMEM] * len(outs) + [ANY] * len(passed),
        scratch_shapes=[
            pltpu.VMEM(tiles.shape, BF16),
            pltpu.VMEM((sum(spans), T), BF16),
            pltpu.VMEM((sum(outs), T, T), F32),
            pltpu.SemaphoreType.DMA((len(spans) + 2,)),
        ],
        compiler_params=PARAMS,
    )(live, tables, tiles, *sources, *passed)


def pack_kernel(*refs):
    pieces, sends, (lists, counts), (held, words, table, sems) = (
        refs[:8],
        refs[8:14],
        refs[14:16],
        refs[16:],
    )
    copies = [pltpu.make_async_copy(p, held.at[k], sems.at[k]) for k, p in enumerate(pieces)]
    for copy in copies:
        copy.start()
    for copy in copies:
        copy.wait()
    metas = [held[k, pl.ds(HALF, META)].astype(F32) for k in range(8)]
    for n in range(6):
        words[pl.ds(n * 8, 8)] = metas[n + 5 if n < 3 else n - 2][:8].astype(I32)
    copy = pltpu.make_async_copy(words, table, sems.at[0])
    copy.start()
    flags = functools.reduce(jnp.maximum, metas[:4]).astype(BF16)
    for n in range(3):
        sends[n][pl.ds(CAP * T, META)] = flags
    copy.wait()
    for n in range(6):
        group = 3 - n if n < 3 else 10 - n
        amount = table[n * 8 + 1, group]
        counts[n] = amount

        def step(k, carry, n=n, group=group):
            code = table[n * 8, group * CAP + k]
            lists[n * CAP + k] = code
            sends[n][block(k)] = held[n // 3 * 4 + (code >> 3), block(code & 7)]
            return carry

        lax.fori_loop(0, amount, step, 0)


def pack(pieces):
    return pl.pallas_call(
        pack_kernel,
        out_shape=[
            jax.ShapeDtypeStruct((CAP * T + (META if n < 3 else 0), T), BF16) for n in range(6)
        ]
        + [jax.ShapeDtypeStruct((6 * CAP,), I32), jax.ShapeDtypeStruct((6,), I32)],
        in_specs=[ANY] * 8,
        out_specs=[VMEM] * 6 + [SMEM] * 2,
        scratch_shapes=[
            pltpu.VMEM((8, HALF + META, T), BF16),
            pltpu.VMEM((48, T), I32),
            pltpu.SMEM((48, T), I32),
            pltpu.SemaphoreType.DMA((8,)),
        ],
        compiler_params=PARAMS,
    )(*pieces)


def combine_kernel(lists, counts, own, *refs):
    parts, outs, (total,) = refs[:6], refs[6:14], refs[14:]

    def widen(k, carry):
        total[k] = own[block(k)].astype(F32)
        return carry

    lax.fori_loop(0, 64, widen, 0)
    for n, part in enumerate(parts):

        def add(k, carry, n=n, part=part):
            total[lists[n * CAP + k] + n // 3 * 32] += part[block(k)].astype(F32)
            return carry

        lax.fori_loop(0, counts[n], add, 0)
    for n, ref in enumerate(outs):

        def out(k, carry, n=n, ref=ref):
            ref[block(k)] = total[n * 8 + k].astype(ref.dtype)
            return carry

        lax.fori_loop(0, 8, out, 0)


def combine(lists, counts, own, parts):
    return pl.pallas_call(
        combine_kernel,
        out_shape=[
            jax.ShapeDtypeStruct((HALF, T), BF16 if d else F32) for _ in range(2) for d in range(4)
        ],
        in_specs=[SMEM] * 2 + [VMEM] * 7,
        out_specs=[VMEM] * 8,
        scratch_shapes=[pltpu.VMEM((64, T, T), F32)],
        compiler_params=PARAMS,
    )(lists, counts, own, *parts)


def dense_kernel(m0, m1, m2, m3, grad, weight, offset, hidden, projected, sums):
    @pl.when(pl.program_id(0) == 0)
    def _():
        sums[...] = jnp.zeros_like(sums)

    mixed = m0[...].astype(F32) + m1[...].astype(F32) + m2[...].astype(F32) + m3[...].astype(F32)
    high = mixed.astype(BF16)
    low = (mixed - high.astype(F32)).astype(BF16)
    w = weight[...]
    pre = jnp.dot(high, w, preferred_element_type=F32)
    pre = pre + jnp.dot(low, w, preferred_element_type=F32) + offset[...]
    s = jax.nn.sigmoid(pre)
    hidden[...] = (pre * s).astype(BF16)
    slope = (grad[...].astype(F32) * s * (1.0 + pre * (1.0 - s))).astype(BF16)
    projected[...] = lax.dot_general(
        slope, w, (((1,), (1,)), ((), ())), preferred_element_type=F32
    ).astype(BF16)
    over_rows = (((0,), (0,)), ((), ()))
    sums[:T] += lax.dot_general(
        high, slope, over_rows, preferred_element_type=F32
    ) + lax.dot_general(low, slope, over_rows, preferred_element_type=F32)
    sums[T:] += jnp.sum(slope.astype(F32).reshape(-1, 8, slope.shape[1]), axis=0)


def dense(parts, grad, weight, offset):
    rows, width = parts[0].shape[0], weight.shape[1]
    step = 512
    half = pl.BlockSpec((step, T), lambda i: (i, 0))
    full = pl.BlockSpec((step, width), lambda i: (i, 0))
    return pl.pallas_call(
        dense_kernel,
        grid=(rows // step,),
        out_shape=[
            jax.ShapeDtypeStruct((rows, width), BF16),
            jax.ShapeDtypeStruct((rows, T), BF16),
            jax.ShapeDtypeStruct((T + 8, width), F32),
        ],
        in_specs=[half] * 4
        + [
            full,
            pl.BlockSpec((T, width), lambda i: (0, 0)),
            pl.BlockSpec((1, width), lambda i: (0, 0)),
        ],
        out_specs=[full, half, pl.BlockSpec((T + 8, width), lambda i: (0, 0))],
        compiler_params=PARAMS,
    )(*parts, grad, weight, offset)


def on_device(features, weight, offset, tile_values, tile_rows, tile_cols, live_tiles, grad_hidden):
    tiles = tile_values.reshape(tile_values.shape[2:])
    nodes_here = features.shape[0]
    scaling = 1.0 / math.sqrt(nodes_here * lax.axis_size("row") * lax.axis_size("col"))
    at_row, at_col = lax.axis_index("row"), lax.axis_index("col")
    live = live_tiles.reshape(1)
    first, second, tables = prepare(
        at_row.reshape(1), at_col.reshape(1), live, tile_rows, tile_cols, features
    )

    first, second = ring_gather(first, along_x), ring_gather(second, along_z)
    *sends, lists, counts = pack(first + second)
    named = (
        ring_swap([None] + sends[:3], along_z)[1:] + ring_swap([None] + sends[3:], along_x)[1:]
    )
    flags = [sends[0]] + named[:3]
    full = functools.reduce(jnp.maximum, [f[CAP * T + 1, FLAG_LANE] for f in flags]) > 0.5

    def forward_all(first, second, named):
        whole = [jnp.concatenate([p[:HALF] for p in half]) for half in (first, second)]
        whole = ring_gather(whole[0], along_z) + ring_gather(whole[1], along_x)
        return products(live, tables, 2, 0, tiles, whole, (4 * HALF,) * 8, (64, 64), (1,))

    def forward_named(first, second, named):
        spans = (HALF,) * 8 + (CAP * T,) * 6
        return products(
            live, tables, 1, 0, tiles, first + second + named, spans, (64, 64), (1,)
        )

    send, keep = lax.cond(full, forward_all, forward_named, first, second, named)

    both = keep.astype(F32) + other_core(send).astype(F32)
    both = both.reshape(4, nodes_here, T)
    mixed_parts = ring_swap([both[d].astype(BF16) for d in range(4)], along_y)
    hidden, projected, sums = dense(mixed_parts, grad_hidden, weight, offset.reshape(1, -1))

    own = ring_gather(projected, along_y)
    gathered = [other_core(piece) for piece in own] + own

    for along in (along_x, along_z):
        sums = sums + swap_pairs(sums, along, 1)
        sums = sums + swap_pairs(sums, along, 2)

    here, *parts, sums = products(
        live,
        tables,
        0,
        1,
        tiles,
        gathered,
        (nodes_here,) * 8,
        (64,) + (CAP,) * 6,
        (0,),
        (sums,),
    )
    sums = sums + swap_pairs(sums, along_y, 1)
    sums = sums + swap_pairs(sums, along_y, 2)
    sums = (sums + other_core(sums)) * scaling

    parts = (
        ring_swap([None] + parts[:3], along_z)[1:] + ring_swap([None] + parts[3:], along_x)[1:]
    )

    def backward_all(here, parts, gathered):
        outs = products(
            live, tables, 0, 2, tiles, gathered, (nodes_here,) * 8, (32,) * 8, (0,)
        )
        result = []
        for pieces, along in ((outs[:4], along_z), (outs[4:], along_x)):
            mine = total_of(ring_swap(pieces, along)).reshape(4, HALF, T)
            result += [mine[0]] + [mine[d].astype(BF16) for d in (1, 2, 3)]
        return result

    def backward_named(here, parts, gathered):
        return list(combine(lists, counts, here, parts))

    outs = lax.cond(full, backward_all, backward_named, here, parts, gathered)
    first = total_of(ring_swap(outs[:4], along_x))
    second = total_of(ring_swap(outs[4:], along_z))
    grad_features = jnp.concatenate([first, second])
    return (hidden, grad_features, sums[:T], jnp.sum(sums[T:], axis=0))


def solution(mesh):
    in_specs = (
        P(("col", "row"), None),
        P(),
        P(),
        P("row", "col", None, None, None),
        P("row", "col", None),
        P("row", "col", None),
        P("row", "col"),
        P(("row", "col"), None),
    )
    out_specs = (P(("row", "col"), None), P(("col", "row"), None), P(), P())
    return jax.shard_map(
        on_device, mesh=mesh, in_specs=in_specs, out_specs=out_specs, check_vma=False
    )
```

time: 266 us -> 244 us (0.917)
  waiting for transfers between devices: 139 us -> 123 us
    ppermute x15 -> x14, waiting for transfers between devices: 24.4 us -> 16.9 us  [along_x(): return lax.ppermute(value, 'row', pairs)]
    ppermute x12 -> x8, waiting for transfers between devices: 52.2 us -> 46.3 us  [along_y(): return lax.ppermute(value, 'col', pairs)]
    ppermute x18 -> x14, waiting for transfers between devices: 58.5 us -> 55.1 us  [along_z(): return lax.ppermute(value, 'row', pairs)]
    slice x6 -> x5, local copies, waits for them, and re-layouts: 5.69 us -> 3.94 us  [the longest x4 3.01 us: on_device(): f[CAP * T + 1, FLAG_LANE]]
    ppermute x12 -> x8, starting transfers between devices: 16.3 us -> 15.1 us  [along_y(): return lax.ppermute(value, 'col', pairs)]
    ppermute x18 -> x14, starting transfers between devices: 31.9 us -> 30.9 us  [along_z(): return lax.ppermute(value, 'row', pairs)]
    ppermute x15 -> x14, starting transfers between devices: 19.3 us -> 20 us  [along_x(): return lax.ppermute(value, 'row', pairs)]
    pallas_call x3 -> x4, Pallas kernels: 23.8 us -> 23.5 us  [the longest x2 18.6 us: products(): pl.pallas_call(kernel, out_shape=[jax.ShapeDtypeStruct((n * T, T), BF16)...]
  transfers between devices with their start and end apart: 52 -> 42, of which waited for: 27 -> 25; matrix products, arithmetic and copies ran while one was open for 2% -> 3% of each run, Pallas kernels for 3% -> 0%
where the time goes in v1:
time: 244 us; the launch traced here: 242 us
  waiting for transfers between devices  123 us (50%)
  starting transfers between devices  66.7 us (27%)
  Pallas kernels  33.2 us (14%)
  local copies, waits for them, and re-layouts  8.8 us (4%)
  other arithmetic  6.57 us (3%)
  between operations  4.23 us (2%)
    ppermute x14, waiting for transfers between devices, along_z(): return lax.ppermute(value, 'row', pairs)  55.1 us
    ppermute x8, waiting for transfers between devices, along_y(): return lax.ppermute(value, 'col', pairs)  46.3 us
    ppermute x14, starting transfers between devices, along_z(): return lax.ppermute(value, 'row', pairs)  30.9 us
    ppermute x14, starting transfers between devices, along_x(): return lax.ppermute(value, 'row', pairs)  20 us
    pallas_call x2, Pallas kernels, products(): pl.pallas_call(kernel, out_shape=[jax.ShapeDtypeStruct((n * T, T), BF16)...  18.6 us
    ppermute x14, waiting for transfers between devices, along_x(): return lax.ppermute(value, 'row', pairs)  16.9 us
    ppermute x8, starting transfers between devices, along_y(): return lax.ppermute(value, 'col', pairs)  15.1 us
    pallas_call x1, Pallas kernels, dense(): pl.pallas_call(dense_kernel, grid=(rows // step,), out_shape=[jax.ShapeDt...  5.48 us
  transfers between devices with their start and end apart: 42, of which 25 were waited for; matrix products, arithmetic and copies ran while one was open for 3% of the time, Pallas kernels for 0%

profile of v1, /device:TPU:0, one launch (start us, length us, event | category | flops | bytes accessed | tf_op | source)
XLA Modules:
  0.0 242.2 jit_solution(16302702801382600795)
XLA Ops:
  10.9 3.6 %collective-permute-start.16 = (bf16[1040,128]{1,0:T(8,128)(2,1)S(1)}, bf16[1040,128]{1,0:T(8,128)(2,1)S(1)}, u32[]{:S(2)}, u32[]{:S(2)}) collective-permute-start(bf16[1040,128]{1,0:T(8,128)(2,1)S(1)} %get-tuple-element.205.refs_4_), channel_id=1, source_target_pairs={{0,16},{8,24},{16,0},{24,8},{32,48},{40,56},{48,32},{56,40},{64,80... | collective-permute-start | bytes 798728 | tf_op jit(solution)/shard_map/ppermute | solution.py:32
  19.4 6.0 %collective-permute-done.16.refs_6_ = bf16[1040,128]{1,0:T(8,128)(2,1)S(1)} collective-permute-done((bf16[1040,128]{1,0:T(8,128)(2,1)S(1)}, bf16[1040,128]{1,0:T(8,128)(2,1)S(1)}, u32[]{:S(2)}, u32[]{:S(2)}) %collective-permute-start.16) | collective-permute-done | bytes 266272 | tf_op jit(solution)/shard_map/ppermute | solution.py:32
  35.0 8.9 %collective-permute-done.18 = bf16[2064,128]{1,0:T(8,128)(2,1)S(1)} collective-permute-done((bf16[2064,128]{1,0:T(8,128)(2,1)}, bf16[2064,128]{1,0:T(8,128)(2,1)S(1)}, u32[]{:S(2)}, u32[]{:S(2)}) %collective-permute-start.18) | collective-permute-done | bytes 528416 | tf_op jit(solution)/shard_map/ppermute | solution.py:32
  48.9 7.8 %collective-permute-done.20 = bf16[2064,128]{1,0:T(8,128)(2,1)S(1)} collective-permute-done((bf16[2064,128]{1,0:T(8,128)(2,1)}, bf16[2064,128]{1,0:T(8,128)(2,1)S(1)}, u32[]{:S(2)}, u32[]{:S(2)}) %collective-permute-start.20) | collective-permute-done | bytes 528416 | tf_op jit(solution)/shard_map/ppermute | solution.py:32
  58.8 6.9 %conditional.11 = ((bf16[8192,128]{1,0:T(8,128)(2,1)}, bf16[8192,128]{1,0:T(8,128)(2,1)})) conditional(s32[]{:T(128)} %bitcast.5, (s32[1]{0:T(128)}, s32[8,64]{1,0:T(8,128)S(1)}, bf16[64,128,128]{2,1,0:T(8,128)(2,1)S(1)}, bf16[1040,128]{1,0:T(8,128)(2,1)S(1)}, bf16[1040,128]{1,0:T(8,128)(2,1)S(1)}, /*index=5*/bf16[1040,128]{1,0:T(8,128)(2,1)S(1)}, ...), branch_computations={%region_0.0_spmd, %region_1.0_spmd} | conditional | flops 8388608 | bytes 67109336
  58.8 6.9 %branch_0_fun.2 = (bf16[8192,128]{1,0:T(8,128)(2,1)}, bf16[8192,128]{1,0:T(8,128)(2,1)}) custom-call(s32[1]{0:T(128)} %get-tuple-element.112.live, s32[8,64]{1,0:T(8,128)S(1)} %get-tuple-element.113.tables, bf16[64,128,128]{2,1,0:T(8,128)(2,1)S(1)} %get-tuple-element.114.tiles_ref, bf16[1040,128]{1,0:T(8,128)(2,1)S(1)} %get-tuple-element.115.refs_0_, ...), custom_call_target="tpu_custom_call" | custom-call | tf_op jit(solution)/shard_map/cond/branch_0_fun/pallas_call | solution.py:214
  65.8 4.4 %collective-permute-done.24 = bf16[8192,128]{1,0:T(8,128)(2,1)S(1)} collective-permute-done((bf16[8192,128]{1,0:T(8,128)(2,1)}, bf16[8192,128]{1,0:T(8,128)(2,1)S(1)}, u32[]{:S(2)}, u32[]{:S(2)}) %collective-permute-start.24) | collective-permute-done | bytes 2097184 | tf_op jit(solution)/shard_map/ppermute | solution.py:42
  79.7 9.2 %collective-permute-done.27.m3 = bf16[2048,128]{1,0:T(8,128)(2,1)S(1)} collective-permute-done((bf16[2048,128]{1,0:T(8,128)(2,1)S(1)}, bf16[2048,128]{1,0:T(8,128)(2,1)S(1)}, u32[]{:S(2)}, u32[]{:S(2)}) %collective-permute-start.27) | collective-permute-done | bytes 524320 | tf_op jit(solution)/shard_map/ppermute | solution.py:37
  88.8 12.4 %collective-permute-done.26.m2 = bf16[2048,128]{1,0:T(8,128)(2,1)S(1)} collective-permute-done((bf16[2048,128]{1,0:T(8,128)(2,1)S(1)}, bf16[2048,128]{1,0:T(8,128)(2,1)S(1)}, u32[]{:S(2)}, u32[]{:S(2)}) %collective-permute-start.26) | collective-permute-done | bytes 524320 | tf_op jit(solution)/shard_map/ppermute | solution.py:37
  102.2 5.5 %shard_map.113 = (bf16[2048,256]{1,0:T(8,128)(2,1)}, bf16[2048,128]{1,0:T(8,128)(2,1)S(1)}, f32[136,256]{1,0:T(8,128)}) custom-call(bf16[2048,128]{1,0:T(8,128)(2,1)} %get-tuple-element.257.m0, bf16[2048,128]{1,0:T(8,128)(2,1)} %copy-done.12, bf16[2048,128]{1,0:T(8,128)(2,1)} %copy-done.11, bf16[2048,128]{1,0:T(8,128)(2,1)} %copy-done.10, ...), custom_call_target="tpu_custom_call" | custom-call | tf_op jit(solution)/shard_map/pallas_call | solution.py:350
  115.4 7.3 %collective-permute-done.33.refs_7_ = bf16[2048,128]{1,0:T(8,128)(2,1)S(1)} collective-permute-done((bf16[2048,128]{1,0:T(8,128)(2,1)S(1)}, bf16[2048,128]{1,0:T(8,128)(2,1)S(1)}, u32[]{:S(2)}, u32[]{:S(2)}) %collective-permute-start.33) | collective-permute-done | bytes 524320 | tf_op jit(solution)/shard_map/ppermute | solution.py:37
  122.7 11.4 %collective-permute-done.31.refs_6_ = bf16[2048,128]{1,0:T(8,128)(2,1)S(1)} collective-permute-done((bf16[2048,128]{1,0:T(8,128)(2,1)S(1)}, bf16[2048,128]{1,0:T(8,128)(2,1)S(1)}, u32[]{:S(2)}, u32[]{:S(2)}) %collective-permute-start.31) | collective-permute-done | bytes 524320 | tf_op jit(solution)/shard_map/ppermute | solution.py:37
  135.5 4.7 %collective-permute-start.36 = (f32[136,256]{1,0:T(8,128)S(1)}, f32[136,256]{1,0:T(8,128)S(1)}, u32[]{:S(2)}, u32[]{:S(2)}) collective-permute-start(f32[136,256]{1,0:T(8,128)S(1)} %add.61), channel_id=1, source_target_pairs={{0,64},{8,72},{16,80},{24,88},{32,96},{40,104},{48,112},{56,120},{... | collective-permute-start | bytes 417800 | tf_op jit(solution)/shard_map/ppermute | solution.py:27
  140.2 3.8 %collective-permute-done.36 = f32[136,256]{1,0:T(8,128)S(1)} collective-permute-done((f32[136,256]{1,0:T(8,128)S(1)}, f32[136,256]{1,0:T(8,128)S(1)}, u32[]{:S(2)}, u32[]{:S(2)}) %collective-permute-start.36) | collective-permute-done | bytes 139296 | tf_op jit(solution)/shard_map/ppermute | solution.py:27
  144.1 10.3 %collective-permute-start.37 = (f32[136,256]{1,0:T(8,128)S(1)}, f32[136,256]{1,0:T(8,128)S(1)}, u32[]{:S(2)}, u32[]{:S(2)}) collective-permute-start(f32[136,256]{1,0:T(8,128)S(1)} %add.62), channel_id=1, source_target_pairs={{0,8},{8,0},{16,24},{24,16},{32,40},{40,32},{48,56},{56,48},{64,72... | collective-permute-start | bytes 417800 | tf_op jit(solution)/shard_map/ppermute | solution.py:32
  157.9 6.5 %collective-permute-done.38 = f32[136,256]{1,0:T(8,128)S(1)} collective-permute-done((f32[136,256]{1,0:T(8,128)S(1)}, f32[136,256]{1,0:T(8,128)S(1)}, u32[]{:S(2)}, u32[]{:S(2)}) %collective-permute-start.38) | collective-permute-done | bytes 139296 | tf_op jit(solution)/shard_map/ppermute | solution.py:32
  165.1 11.6 %shard_map.114 = (bf16[8192,128]{1,0:T(8,128)(2,1)}, bf16[2048,128]{1,0:T(8,128)(2,1)}, bf16[2048,128]{1,0:T(8,128)(2,1)}, bf16[2048,128]{1,0:T(8,128)(2,1)}, bf...) custom-call(s32[1]{0:T(128)} %bitcast.9.live, ...), custom_call_target="tpu_custom_call" | custom-call | tf_op jit(solution)/shard_map/pallas_call | solution.py:214
  180.5 3.7 %collective-permute-done.51 = f32[136,256]{1,0:T(8,128)S(1)} collective-permute-done((f32[136,256]{1,0:T(8,128)}, f32[136,256]{1,0:T(8,128)S(1)}, u32[]{:S(2)}, u32[]{:S(2)}) %collective-permute-start.51) | collective-permute-done | bytes 139296 | tf_op jit(solution)/shard_map/ppermute | solution.py:37
  192.5 11.1 %collective-permute-done.40 = bf16[2048,128]{1,0:T(8,128)(2,1)S(1)} collective-permute-done((bf16[2048,128]{1,0:T(8,128)(2,1)}, bf16[2048,128]{1,0:T(8,128)(2,1)S(1)}, u32[]{:S(2)}, u32[]{:S(2)}) %collective-permute-start.40) | collective-permute-done | bytes 524320 | tf_op jit(solution)/shard_map/ppermute | solution.py:32
  203.6 6.9 %collective-permute-done.41 = bf16[2048,128]{1,0:T(8,128)(2,1)S(1)} collective-permute-done((bf16[2048,128]{1,0:T(8,128)(2,1)}, bf16[2048,128]{1,0:T(8,128)(2,1)S(1)}, u32[]{:S(2)}, u32[]{:S(2)}) %collective-permute-start.41) | collective-permute-done | bytes 524320 | tf_op jit(solution)/shard_map/ppermute | solution.py:32
  213.1 5.3 %conditional.10 = ((f32[1024,128]{1,0:T(8,128)S(1)}, bf16[1024,128]{1,0:T(8,128)(2,1)}, bf16[1024,128]{1,0:T(8,128)(2,1)}, bf16[1024,128]{1,0:T(8,128)(2,1)}, f3...) conditional(s32[]{:T(128)} %bitcast.5, (s32[96]{0:T(128)S(1)}, ...), branch_computations={%region_2.0_spmd, %region_3.0_spmd} | conditional | flops 8388608 | bytes 49283412 | solution.py:445
  214.2 4.2 %branch_0_fun.3 = (f32[1024,128]{1,0:T(8,128)S(1)}, bf16[1024,128]{1,0:T(8,128)(2,1)}, bf16[1024,128]{1,0:T(8,128)(2,1)}, bf16[1024,128]{1,0:T(8,128)(2,1)}, f32...) custom-call(s32[96]{0:T(128)S(1)} %get-tuple-element.140.lists, ...), custom_call_target="tpu_custom_call" | custom-call | tf_op jit(solution)/shard_map/cond/branch_0_fun/pallas_call | solution.py:309
  232.4 4.1 %collective-permute-done.47 = bf16[1024,128]{1,0:T(8,128)(2,1)S(1)} collective-permute-done((bf16[1024,128]{1,0:T(8,128)(2,1)}, bf16[1024,128]{1,0:T(8,128)(2,1)S(1)}, u32[]{:S(2)}, u32[]{:S(2)}) %collective-permute-start.47) | collective-permute-done | bytes 262176 | tf_op jit(solution)/shard_map/ppermute | solution.py:27
  237.7 3.4 %collective-permute-done.50 = bf16[1024,128]{1,0:T(8,128)(2,1)S(1)} collective-permute-done((bf16[1024,128]{1,0:T(8,128)(2,1)}, bf16[1024,128]{1,0:T(8,128)(2,1)S(1)}, u32[]{:S(2)}, u32[]{:S(2)}) %collective-permute-start.50) | collective-permute-done | bytes 262176 | tf_op jit(solution)/shard_map/ppermute | solution.py:32
  (106 shorter events, 84.2 us)
Async XLA Ops:
  10.9 14.6 %collective-permute-start.16 = (bf16[1040,128]{1,0:T(8,128)(2,1)S(1)}, bf16[1040,128]{1,0:T(8,128)(2,1)S(1)}, u32[]{:S(2)}, u32[]{:S(2)}) collective-permute-start(bf16[1040,128]{1,0:T(8,128)(2,1)S(1)} %get-tuple-element.205.refs_4_), channel_id=1, source_target_pairs={{0,16},{8,24},{16,0},{24,8},{32,48},{40,56},{48,32},{56,40},{64,80... | collective-permute-start | bytes 798728 | tf_op jit(solution)/shard_map/ppermute | solution.py:32
  28.7 15.2 %collective-permute-start.18 = (bf16[2064,128]{1,0:T(8,128)(2,1)}, bf16[2064,128]{1,0:T(8,128)(2,1)S(1)}, u32[]{:S(2)}, u32[]{:S(2)}) collective-permute-start(bf16[2064,128]{1,0:T(8,128)(2,1)} %get-tuple-element.207), channel_id=1, source_target_pairs={{0,24},{8,0},{16,8},{24,16},{32,56},{40,32},{48,40},{56,48},{64,88... | collective-permute-start | bytes 1585160 | tf_op jit(solution)/shard_map/ppermute | solution.py:32
  30.8 16.9 %collective-permute-start.19 = (bf16[2064,128]{1,0:T(8,128)(2,1)}, bf16[2064,128]{1,0:T(8,128)(2,1)S(1)}, u32[]{:S(2)}, u32[]{:S(2)}) collective-permute-start(bf16[2064,128]{1,0:T(8,128)(2,1)} %get-tuple-element.208), channel_id=1, source_target_pairs={{0,16},{8,24},{16,0},{24,8},{32,48},{40,56},{48,32},{56,40},{64,80... | collective-permute-start | bytes 1585160 | tf_op jit(solution)/shard_map/ppermute | solution.py:32
  32.3 24.4 %collective-permute-start.20 = (bf16[2064,128]{1,0:T(8,128)(2,1)}, bf16[2064,128]{1,0:T(8,128)(2,1)S(1)}, u32[]{:S(2)}, u32[]{:S(2)}) collective-permute-start(bf16[2064,128]{1,0:T(8,128)(2,1)} %get-tuple-element.206), channel_id=1, source_target_pairs={{0,8},{8,16},{16,24},{24,0},{32,40},{40,48},{48,56},{56,32},{64,72... | collective-permute-start | bytes 1585160 | tf_op jit(solution)/shard_map/ppermute | solution.py:32
  32.4 25.6 %collective-permute-start.21 = (bf16[2048,128]{1,0:T(8,128)(2,1)}, bf16[2048,128]{1,0:T(8,128)(2,1)S(1)}, u32[]{:S(2)}, u32[]{:S(2)}) collective-permute-start(bf16[2048,128]{1,0:T(8,128)(2,1)} %get-tuple-element.210), channel_id=1, source_target_pairs={{0,96},{8,104},{16,112},{24,120},{32,0},{40,8},{48,16},{56,24},{64... | collective-permute-start | bytes 1572872 | tf_op jit(solution)/shard_map/ppermute | solution.py:27
  32.7 25.3 %collective-permute-start.22 = (bf16[2048,128]{1,0:T(8,128)(2,1)}, bf16[2048,128]{1,0:T(8,128)(2,1)S(1)}, u32[]{:S(2)}, u32[]{:S(2)}) collective-permute-start(bf16[2048,128]{1,0:T(8,128)(2,1)} %get-tuple-element.211), channel_id=1, source_target_pairs={{0,64},{8,72},{16,80},{24,88},{32,96},{40,104},{48,112},{56,120},{... | collective-permute-start | bytes 1572872 | tf_op jit(solution)/shard_map/ppermute | solution.py:27
  43.9 14.9 %collective-permute-start.23 = (bf16[2048,128]{1,0:T(8,128)(2,1)}, bf16[2048,128]{1,0:T(8,128)(2,1)S(1)}, u32[]{:S(2)}, u32[]{:S(2)}) collective-permute-start(bf16[2048,128]{1,0:T(8,128)(2,1)} %get-tuple-element.212), channel_id=1, source_target_pairs={{0,32},{8,40},{16,48},{24,56},{32,64},{40,72},{48,80},{56,88},{64,... | collective-permute-start | bytes 1572872 | tf_op jit(solution)/shard_map/ppermute | solution.py:27
  73.2 15.6 %collective-permute-start.27 = (bf16[2048,128]{1,0:T(8,128)(2,1)S(1)}, bf16[2048,128]{1,0:T(8,128)(2,1)S(1)}, u32[]{:S(2)}, u32[]{:S(2)}) collective-permute-start(bf16[2048,128]{1,0:T(8,128)(2,1)S(1)} %get-tuple-element.254), channel_id=1, source_target_pairs={{0,2},{1,3},{2,4},{3,5},{4,6},{5,7},{6,0},{7,1},{8,10},{9,11},{10,... | collective-permute-start | bytes 1572872 | tf_op jit(solution)/shard_map/ppermute | solution.py:37
  75.6 25.6 %collective-permute-start.26 = (bf16[2048,128]{1,0:T(8,128)(2,1)S(1)}, bf16[2048,128]{1,0:T(8,128)(2,1)S(1)}, u32[]{:S(2)}, u32[]{:S(2)}) collective-permute-start(bf16[2048,128]{1,0:T(8,128)(2,1)S(1)} %get-tuple-element.255), channel_id=1, source_target_pairs={{0,4},{1,5},{2,6},{3,7},{4,0},{5,1},{6,2},{7,3},{8,12},{9,13},{10,... | collective-permute-start | bytes 1572872 | tf_op jit(solution)/shard_map/ppermute | solution.py:37
  77.8 23.4 %collective-permute-start.25 = (bf16[2048,128]{1,0:T(8,128)(2,1)S(1)}, bf16[2048,128]{1,0:T(8,128)(2,1)S(1)}, u32[]{:S(2)}, u32[]{:S(2)}) collective-permute-start(bf16[2048,128]{1,0:T(8,128)(2,1)S(1)} %get-tuple-element.256), channel_id=1, source_target_pairs={{0,6},{1,7},{2,0},{3,1},{4,2},{5,3},{6,4},{7,5},{8,14},{9,15},{10,... | collective-permute-start | bytes 1572872 | tf_op jit(solution)/shard_map/ppermute | solution.py:37
  107.7 15.0 %collective-permute-start.33 = (bf16[2048,128]{1,0:T(8,128)(2,1)S(1)}, bf16[2048,128]{1,0:T(8,128)(2,1)S(1)}, u32[]{:S(2)}, u32[]{:S(2)}) collective-permute-start(bf16[2048,128]{1,0:T(8,128)(2,1)S(1)} %get-tuple-element.218.refs_4_), channel_id=1, source_target_pairs={{0,2},{1,3},{2,4},{3,5},{4,6},{5,7},{6,0},{7,1},{8,10},{9,11},{10,... | collective-permute-start | bytes 1572872 | tf_op jit(solution)/shard_map/ppermute | solution.py:37
  108.7 25.4 %collective-permute-start.31 = (bf16[2048,128]{1,0:T(8,128)(2,1)S(1)}, bf16[2048,128]{1,0:T(8,128)(2,1)S(1)}, u32[]{:S(2)}, u32[]{:S(2)}) collective-permute-start(bf16[2048,128]{1,0:T(8,128)(2,1)S(1)} %get-tuple-element.218.refs_4_), channel_id=1, source_target_pairs={{0,4},{1,5},{2,6},{3,7},{4,0},{5,1},{6,2},{7,3},{8,12},{9,13},{10,... | collective-permute-start | bytes 1572872 | tf_op jit(solution)/shard_map/ppermute | solution.py:37
  111.0 23.1 %collective-permute-start.29 = (bf16[2048,128]{1,0:T(8,128)(2,1)S(1)}, bf16[2048,128]{1,0:T(8,128)(2,1)S(1)}, u32[]{:S(2)}, u32[]{:S(2)}) collective-permute-start(bf16[2048,128]{1,0:T(8,128)(2,1)S(1)} %get-tuple-element.218.refs_4_), channel_id=1, source_target_pairs={{0,6},{1,7},{2,0},{3,1},{4,2},{5,3},{6,4},{7,5},{8,14},{9,15},{10,... | collective-permute-start | bytes 1572872 | tf_op jit(solution)/shard_map/ppermute | solution.py:37
  113.0 21.7 %collective-permute-start.35 = (f32[136,256]{1,0:T(8,128)}, f32[136,256]{1,0:T(8,128)S(1)}, u32[]{:S(2)}, u32[]{:S(2)}) collective-permute-start(f32[136,256]{1,0:T(8,128)} %get-tuple-element.219), channel_id=1, source_target_pairs={{0,32},{8,40},{16,48},{24,56},{32,0},{40,8},{48,16},{56,24},{64,96... | collective-permute-start | bytes 417800 | tf_op jit(solution)/shard_map/ppermute | solution.py:27
  115.4 49.7 %collective-permute-start.28 = (bf16[2048,128]{1,0:T(8,128)(2,1)S(1)}, bf16[2048,128]{1,0:T(8,128)(2,1)S(1)}, u32[]{:S(2)}, u32[]{:S(2)}) collective-permute-start(bf16[2048,128]{1,0:T(8,128)(2,1)S(1)} %get-tuple-element.218.refs_4_), channel_id=1, source_target_pairs={{0,1},{1,0},{2,3},{3,2},{4,5},{5,4},{6,7},{7,6},{8,9},{9,8},{10,11... | collective-permute-start | bytes 1572872 | tf_op jit(solution)/shard_map/ppermute | solution.py:42
  122.7 42.4 %collective-permute-start.34 = (bf16[2048,128]{1,0:T(8,128)(2,1)S(1)}, bf16[2048,128]{1,0:T(8,128)(2,1)S(1)}, u32[]{:S(2)}, u32[]{:S(2)}) collective-permute-start(bf16[2048,128]{1,0:T(8,128)(2,1)S(1)} %collective-permute-done.33.refs_7_), channel_id=1, source_target_pairs={{0,1},{1,0},{2,3},{3,2},{4,5},{5,4},{6,7},{7,6},{8,9},{9,8},{10,11... | collective-permute-start | bytes 1572872 | tf_op jit(solution)/shard_map/ppermute | solution.py:42
  134.1 31.0 %collective-permute-start.32 = (bf16[2048,128]{1,0:T(8,128)(2,1)S(1)}, bf16[2048,128]{1,0:T(8,128)(2,1)S(1)}, u32[]{:S(2)}, u32[]{:S(2)}) collective-permute-start(bf16[2048,128]{1,0:T(8,128)(2,1)S(1)} %collective-permute-done.31.refs_6_), channel_id=1, source_target_pairs={{0,1},{1,0},{2,3},{3,2},{4,5},{5,4},{6,7},{7,6},{8,9},{9,8},{10,11... | collective-permute-start | bytes 1572872 | tf_op jit(solution)/shard_map/ppermute | solution.py:42
  134.1 31.0 %collective-permute-start.30 = (bf16[2048,128]{1,0:T(8,128)(2,1)S(1)}, bf16[2048,128]{1,0:T(8,128)(2,1)S(1)}, u32[]{:S(2)}, u32[]{:S(2)}) collective-permute-start(bf16[2048,128]{1,0:T(8,128)(2,1)S(1)} %collective-permute-done.29.refs_5_), channel_id=1, source_target_pairs={{0,1},{1,0},{2,3},{3,2},{4,5},{5,4},{6,7},{7,6},{8,9},{9,8},{10,11... | collective-permute-start | bytes 1572872 | tf_op jit(solution)/shard_map/ppermute | solution.py:42
  176.8 15.5 %collective-permute-start.39 = (bf16[2048,128]{1,0:T(8,128)(2,1)}, bf16[2048,128]{1,0:T(8,128)(2,1)S(1)}, u32[]{:S(2)}, u32[]{:S(2)}) collective-permute-start(bf16[2048,128]{1,0:T(8,128)(2,1)} %get-tuple-element.221), channel_id=1, source_target_pairs={{0,24},{8,0},{16,8},{24,16},{32,56},{40,32},{48,40},{56,48},{64,88... | collective-permute-start | bytes 1572872 | tf_op jit(solution)/shard_map/ppermute | solution.py:32
  187.0 16.6 %collective-permute-start.40 = (bf16[2048,128]{1,0:T(8,128)(2,1)}, bf16[2048,128]{1,0:T(8,128)(2,1)S(1)}, u32[]{:S(2)}, u32[]{:S(2)}) collective-permute-start(bf16[2048,128]{1,0:T(8,128)(2,1)} %get-tuple-element.222), channel_id=1, source_target_pairs={{0,16},{8,24},{16,0},{24,8},{32,48},{40,56},{48,32},{56,40},{64,80... | collective-permute-start | bytes 1572872 | tf_op jit(solution)/shard_map/ppermute | solution.py:32
  189.5 21.0 %collective-permute-start.41 = (bf16[2048,128]{1,0:T(8,128)(2,1)}, bf16[2048,128]{1,0:T(8,128)(2,1)S(1)}, u32[]{:S(2)}, u32[]{:S(2)}) collective-permute-start(bf16[2048,128]{1,0:T(8,128)(2,1)} %get-tuple-element.223), channel_id=1, source_target_pairs={{0,8},{8,16},{16,24},{24,0},{32,40},{40,48},{48,56},{56,32},{64,72... | collective-permute-start | bytes 1572872 | tf_op jit(solution)/shard_map/ppermute | solution.py:32
  189.5 21.0 %collective-permute-start.42 = (bf16[2048,128]{1,0:T(8,128)(2,1)}, bf16[2048,128]{1,0:T(8,128)(2,1)S(1)}, u32[]{:S(2)}, u32[]{:S(2)}) collective-permute-start(bf16[2048,128]{1,0:T(8,128)(2,1)} %get-tuple-element.224), channel_id=1, source_target_pairs={{0,96},{8,104},{16,112},{24,120},{32,0},{40,8},{48,16},{56,24},{64... | collective-permute-start | bytes 1572872 | tf_op jit(solution)/shard_map/ppermute | solution.py:27
  191.7 18.7 %collective-permute-start.43 = (bf16[2048,128]{1,0:T(8,128)(2,1)}, bf16[2048,128]{1,0:T(8,128)(2,1)S(1)}, u32[]{:S(2)}, u32[]{:S(2)}) collective-permute-start(bf16[2048,128]{1,0:T(8,128)(2,1)} %get-tuple-element.225), channel_id=1, source_target_pairs={{0,64},{8,72},{16,80},{24,88},{32,96},{40,104},{48,112},{56,120},{... | collective-permute-start | bytes 1572872 | tf_op jit(solution)/shard_map/ppermute | solution.py:27
  192.2 20.9 %collective-permute-start.44 = (bf16[2048,128]{1,0:T(8,128)(2,1)}, bf16[2048,128]{1,0:T(8,128)(2,1)S(1)}, u32[]{:S(2)}, u32[]{:S(2)}) collective-permute-start(bf16[2048,128]{1,0:T(8,128)(2,1)} %get-tuple-element.226), channel_id=1, source_target_pairs={{0,32},{8,40},{16,48},{24,56},{32,64},{40,72},{48,80},{56,88},{64,... | collective-permute-start | bytes 1572872 | tf_op jit(solution)/shard_map/ppermute | solution.py:27
  (28 other events, 254.0 us)

commit v2 on v1

--- a/solution.py
+++ b/solution.py
@@ -57,10 +57,6 @@
         along(pieces[2], ahead(2)),
         along(pieces[1], ahead(1)),
     ]
-
-
-def swap_pairs(value, along, bit):
-    return along(value, lambda at: at ^ bit)
 
 
 def total_of(pieces):
@@ -158,10 +154,6 @@
             )
         )
         start += rows
-    if len(out_refs) > len(outs):
-        sources, passed = out_refs[0], out_refs[-1]
-        out_refs = out_refs[1:-1]
-        copies.append(pltpu.make_async_copy(sources, passed, sems.at[n + 1]))
     for copy in copies:
         copy.start()
 
@@ -202,7 +194,7 @@
         start += blocks
 
 
-def products(live, tables, in_row, out_row, tiles, sources, spans, outs, contract, passed=()):
+def products(live, tables, in_row, out_row, tiles, sources, spans, outs, contract):
     kernel = functools.partial(
         products_kernel,
         spans=spans,
@@ -213,18 +205,17 @@
     )
     return pl.pallas_call(
         kernel,
-        out_shape=[jax.ShapeDtypeStruct((n * T, T), BF16) for n in outs]
-        + [jax.ShapeDtypeStruct(p.shape, p.dtype) for p in passed],
-        in_specs=[SMEM] * 2 + [ANY] * (1 + len(sources) + len(passed)),
-        out_specs=[VMEM] * len(outs) + [ANY] * len(passed),
+        out_shape=[jax.ShapeDtypeStruct((n * T, T), BF16) for n in outs],
+        in_specs=[SMEM] * 2 + [ANY] * (1 + len(sources)),
+        out_specs=[VMEM] * len(outs),
         scratch_shapes=[
             pltpu.VMEM(tiles.shape, BF16),
             pltpu.VMEM((sum(spans), T), BF16),
             pltpu.VMEM((sum(outs), T, T), F32),
-            pltpu.SemaphoreType.DMA((len(spans) + 2,)),
-        ],
-        compiler_params=PARAMS,
-    )(live, tables, tiles, *sources, *passed)
+            pltpu.SemaphoreType.DMA((len(spans) + 1,)),
+        ],
+        compiler_params=PARAMS,
+    )(live, tables, tiles, *sources)
 
 
 def pack_kernel(*refs):
@@ -316,6 +307,44 @@
         scratch_shapes=[pltpu.VMEM((64, T, T), F32)],
         compiler_params=PARAMS,
     )(lists, counts, own, *parts)
+
+
+def add_up_kernel(sums, _, out):
+    out[...] = jnp.sum(sums[...], axis=0)
+
+
+def add_up(sums, after):
+    return pl.pallas_call(
+        add_up_kernel,
+        out_shape=jax.ShapeDtypeStruct(sums.shape[1:], F32),
+        in_specs=[VMEM, ANY],
+        out_specs=VMEM,
+        compiler_params=PARAMS,
+    )(sums, after)
+
+
+def finish_kernel(*refs, scaling):
+    pieces, sums, (nodes, weight, offset) = refs[:8], refs[8], refs[9:]
+    for k in range(2):
+        nodes[pl.ds(k * HALF, HALF)] = total_of([ref[...] for ref in pieces[4 * k : 4 * k + 4]])
+    total = jnp.sum(sums[...], axis=0) * scaling
+    weight[...] = total[:T]
+    offset[...] = jnp.sum(total[T:], axis=0, keepdims=True)
+
+
+def finish(pieces, sums, scaling):
+    width = sums.shape[-1]
+    return pl.pallas_call(
+        functools.partial(finish_kernel, scaling=scaling),
+        out_shape=[
+            jax.ShapeDtypeStruct((2 * HALF, T), F32),
+            jax.ShapeDtypeStruct((T, width), F32),
+            jax.ShapeDtypeStruct((1, width), F32),
+        ],
+        in_specs=[VMEM] * 9,
+        out_specs=[VMEM] * 3,
+        compiler_params=PARAMS,
+    )(*pieces, sums)
 
 
 def dense_kernel(m0, m1, m2, m3, grad, weight, offset, hidden, projected, sums):
@@ -405,26 +434,11 @@
     own = ring_gather(projected, along_y)
     gathered = [other_core(piece) for piece in own] + own
 
-    for along in (along_x, along_z):
-        sums = sums + swap_pairs(sums, along, 1)
-        sums = sums + swap_pairs(sums, along, 2)
-
-    here, *parts, sums = products(
-        live,
-        tables,
-        0,
-        1,
-        tiles,
-        gathered,
-        (nodes_here,) * 8,
-        (64,) + (CAP,) * 6,
-        (0,),
-        (sums,),
-    )
-    sums = sums + swap_pairs(sums, along_y, 1)
-    sums = sums + swap_pairs(sums, along_y, 2)
-    sums = (sums + other_core(sums)) * scaling
-
+    sums = lax.all_gather(sums, "row", axis=0)
+
+    spans, outs = (nodes_here,) * 8, (64,) + (CAP,) * 6
+    here, *parts = products(live, tables, 0, 1, tiles, gathered, spans, outs, (0,))
+    sums = lax.all_gather(add_up(sums, here), "col", axis=0)
     parts = (
         ring_swap([None] + parts[:3], along_z)[1:] + ring_swap([None] + parts[3:], along_x)[1:]
     )
@@ -443,10 +457,9 @@
         return list(combine(lists, counts, here, parts))
 
     outs = lax.cond(full, backward_all, backward_named, here, parts, gathered)
-    first = total_of(ring_swap(outs[:4], along_x))
-    second = total_of(ring_swap(outs[4:], along_z))
-    grad_features = jnp.concatenate([first, second])
-    return (hidden, grad_features, sums[:T], jnp.sum(sums[T:], axis=0))
+    pieces = ring_swap(outs[:4], along_x) + ring_swap(outs[4:], along_z)
+    grad_features, grad_weight, grad_offset = finish(pieces, sums, scaling)
+    return (hidden, grad_features, grad_weight, grad_offset.reshape(-1))
 
 
 def solution(mesh):

time: 244 us -> 240 us (0.984)
  starting transfers between devices: 66.7 us -> 41.3 us
  between operations: 4.23 us -> 17.7 us
  waiting for transfers between devices: 123 us -> 136 us
  other arithmetic: 6.57 us -> 2.13 us
  local copies, waits for them, and re-layouts: 8.8 us -> 6.25 us
    all_gather x0 -> x2, waiting for transfers between devices: none -> 9.88 us  [the longest x1 9.88 us: on_device(): sums = lax.all_gather(sums, 'row', axis=0)]
    ppermute x14 -> x12, starting transfers between devices: 30.9 us -> 21.2 us  [along_z(): return lax.ppermute(value, 'row', pairs)]
    ppermute x8 -> x6, starting transfers between devices: 15.1 us -> 6.11 us  [along_y(): return lax.ppermute(value, 'col', pairs)]
    ppermute x14 -> x12, starting transfers between devices: 20 us -> 13.9 us  [along_x(): return lax.ppermute(value, 'row', pairs)]
    pallas_call x0 -> x2, Pallas kernels: none -> 5.66 us  [the longest x1 3.27 us: finish(): pl.pallas_call(functools.partial(finish_kernel, scaling=scaling), out_sha...]
    ppermute x14 -> x12, waiting for transfers between devices: 55.1 us -> 50.9 us  [along_z(): return lax.ppermute(value, 'row', pairs)]
    pallas_call x2, Pallas kernels: 18.6 us -> 15.2 us  [products(): pl.pallas_call(kernel, out_shape=[jax.ShapeDtypeStruct((n * T, T), BF16)...]
    ppermute x8 -> x6, waiting for transfers between devices: 46.3 us -> 49.4 us  [along_y(): return lax.ppermute(value, 'col', pairs)]
  transfers between devices with their start and end apart: 42 -> 37, of which waited for: 25 -> 21; matrix products, arithmetic and copies ran while one was open for 3% -> 1% of each run, Pallas kernels for 0% -> 5%
where the time goes in v2:
time: 240 us; the launch traced here: 238 us
  waiting for transfers between devices  136 us (57%)
  starting transfers between devices  41.3 us (17%)
  Pallas kernels  35.1 us (15%)
  between operations  17.7 us (7%)
  local copies, waits for them, and re-layouts  6.25 us (3%)
    ppermute x12, waiting for transfers between devices, along_z(): return lax.ppermute(value, 'row', pairs)  50.9 us
    ppermute x6, waiting for transfers between devices, along_y(): return lax.ppermute(value, 'col', pairs)  49.4 us
    ppermute x12, starting transfers between devices, along_z(): return lax.ppermute(value, 'row', pairs)  21.2 us
    ppermute x12, waiting for transfers between devices, along_x(): return lax.ppermute(value, 'row', pairs)  19.4 us
    pallas_call x2, Pallas kernels, products(): pl.pallas_call(kernel, out_shape=[jax.ShapeDtypeStruct((n * T, T), BF16)...  15.2 us
    ppermute x12, starting transfers between devices, along_x(): return lax.ppermute(value, 'row', pairs)  13.9 us
    all_gather x1, waiting for transfers between devices, on_device(): sums = lax.all_gather(sums, 'row', axis=0)  9.88 us
    ppermute x5, waiting for transfers between devices, other_core(): return lax.ppermute(value, 'col', pairs)  6.22 us
  transfers between devices with their start and end apart: 37, of which 21 were waited for; matrix products, arithmetic and copies ran while one was open for 1% of the time, Pallas kernels for 5%

profile of v2, /device:TPU:0, one launch (start us, length us, event | category | flops | bytes accessed | tf_op | source)
XLA Modules:
  0.0 238.4 jit_solution(7022383284422852989)
XLA Ops:
  14.3 4.0 %collective-permute-start.15 = (bf16[1040,128]{1,0:T(8,128)(2,1)S(1)}, bf16[1040,128]{1,0:T(8,128)(2,1)S(1)}, u32[]{:S(2)}, u32[]{:S(2)}) collective-permute-start(bf16[1040,128]{1,0:T(8,128)(2,1)S(1)} %get-tuple-element.207.refs_4_), channel_id=1, source_target_pairs={{0,24},{8,0},{16,8},{24,16},{32,56},{40,32},{48,40},{56,48},{64,88... | collective-permute-start | bytes 798728 | tf_op jit(solution)/shard_map/ppermute | solution.py:32
  18.4 5.6 %collective-permute-done.12.refs_1_ = bf16[1040,128]{1,0:T(8,128)(2,1)S(1)} collective-permute-done((bf16[1040,128]{1,0:T(8,128)(2,1)S(1)}, bf16[1040,128]{1,0:T(8,128)(2,1)S(1)}, u32[]{:S(2)}, u32[]{:S(2)}) %collective-permute-start.12) | collective-permute-done | bytes 266272 | tf_op jit(solution)/shard_map/ppermute | solution.py:27
  29.2 3.4 %collective-permute-done.17.refs_7_ = bf16[1040,128]{1,0:T(8,128)(2,1)S(1)} collective-permute-done((bf16[1040,128]{1,0:T(8,128)(2,1)S(1)}, bf16[1040,128]{1,0:T(8,128)(2,1)S(1)}, u32[]{:S(2)}, u32[]{:S(2)}) %collective-permute-start.17) | collective-permute-done | bytes 266272 | tf_op jit(solution)/shard_map/ppermute | solution.py:32
  39.1 4.4 %collective-permute-start.21 = (bf16[2048,128]{1,0:T(8,128)(2,1)}, bf16[2048,128]{1,0:T(8,128)(2,1)S(1)}, u32[]{:S(2)}, u32[]{:S(2)}) collective-permute-start(bf16[2048,128]{1,0:T(8,128)(2,1)} %get-tuple-element.212), channel_id=1, source_target_pairs={{0,96},{8,104},{16,112},{24,120},{32,0},{40,8},{48,16},{56,24},{64... | collective-permute-start | bytes 1572872 | tf_op jit(solution)/shard_map/ppermute | solution.py:27
  43.5 14.8 %collective-permute-done.18 = bf16[2064,128]{1,0:T(8,128)(2,1)S(1)} collective-permute-done((bf16[2064,128]{1,0:T(8,128)(2,1)}, bf16[2064,128]{1,0:T(8,128)(2,1)S(1)}, u32[]{:S(2)}, u32[]{:S(2)}) %collective-permute-start.18) | collective-permute-done | bytes 528416 | tf_op jit(solution)/shard_map/ppermute | solution.py:32
  64.0 4.9 %collective-permute-done.23 = bf16[2048,128]{1,0:T(8,128)(2,1)S(1)} collective-permute-done((bf16[2048,128]{1,0:T(8,128)(2,1)}, bf16[2048,128]{1,0:T(8,128)(2,1)S(1)}, u32[]{:S(2)}, u32[]{:S(2)}) %collective-permute-start.23) | collective-permute-done | bytes 524320 | tf_op jit(solution)/shard_map/ppermute | solution.py:27
  68.9 7.5 %conditional.11 = ((bf16[8192,128]{1,0:T(8,128)(2,1)}, bf16[8192,128]{1,0:T(8,128)(2,1)})) conditional(s32[]{:T(128)} %bitcast.5, (s32[1]{0:T(128)}, s32[8,64]{1,0:T(8,128)S(1)}, bf16[64,128,128]{2,1,0:T(8,128)(2,1)S(1)}, bf16[1040,128]{1,0:T(8,128)(2,1)S(1)}, bf16[1040,128]{1,0:T(8,128)(2,1)S(1)}, /*index=5*/bf16[1040,128]{1,0:T(8,128)(2,1)S(1)}, ...), branch_computations={%region_0.0_spmd, %region_1.0_spmd} | conditional | flops 8388608 | bytes 73499264
  68.9 7.4 %branch_0_fun.2 = (bf16[8192,128]{1,0:T(8,128)(2,1)}, bf16[8192,128]{1,0:T(8,128)(2,1)}) custom-call(s32[1]{0:T(128)} %get-tuple-element.112.live, s32[8,64]{1,0:T(8,128)S(1)} %get-tuple-element.113.tables, bf16[64,128,128]{2,1,0:T(8,128)(2,1)S(1)} %get-tuple-element.114.tiles_ref, bf16[1040,128]{1,0:T(8,128)(2,1)S(1)} %get-tuple-element.115.refs_0_, ...), custom_call_target="tpu_custom_call" | custom-call | tf_op jit(solution)/shard_map/cond/branch_0_fun/pallas_call | solution.py:206
  76.4 4.4 %collective-permute-done.24 = bf16[8192,128]{1,0:T(8,128)(2,1)S(1)} collective-permute-done((bf16[8192,128]{1,0:T(8,128)(2,1)}, bf16[8192,128]{1,0:T(8,128)(2,1)S(1)}, u32[]{:S(2)}, u32[]{:S(2)}) %collective-permute-start.24) | collective-permute-done | bytes 2097184 | tf_op jit(solution)/shard_map/ppermute | solution.py:42
  87.9 21.7 %collective-permute-done.25.m1 = bf16[2048,128]{1,0:T(8,128)(2,1)S(1)} collective-permute-done((bf16[2048,128]{1,0:T(8,128)(2,1)S(1)}, bf16[2048,128]{1,0:T(8,128)(2,1)S(1)}, u32[]{:S(2)}, u32[]{:S(2)}) %collective-permute-start.25) | collective-permute-done | bytes 524320 | tf_op jit(solution)/shard_map/ppermute | solution.py:37
  109.5 3.4 %collective-permute-done.27.m3 = bf16[2048,128]{1,0:T(8,128)(2,1)S(1)} collective-permute-done((bf16[2048,128]{1,0:T(8,128)(2,1)S(1)}, bf16[2048,128]{1,0:T(8,128)(2,1)S(1)}, u32[]{:S(2)}, u32[]{:S(2)}) %collective-permute-start.27) | collective-permute-done | bytes 524320 | tf_op jit(solution)/shard_map/ppermute | solution.py:37
  113.8 5.5 %shard_map.113 = (bf16[2048,256]{1,0:T(8,128)(2,1)}, bf16[2048,128]{1,0:T(8,128)(2,1)S(1)}, f32[136,256]{1,0:T(8,128)}) custom-call(bf16[2048,128]{1,0:T(8,128)(2,1)} %get-tuple-element.261.m0, bf16[2048,128]{1,0:T(8,128)(2,1)} %copy-done.22, bf16[2048,128]{1,0:T(8,128)(2,1)} %copy-done.23, bf16[2048,128]{1,0:T(8,128)(2,1)} %copy-done.24, ...), custom_call_target="tpu_custom_call" | custom-call | tf_op jit(solution)/shard_map/pallas_call | solution.py:379
  121.4 12.8 %collective-permute-done.29.refs_5_ = bf16[2048,128]{1,0:T(8,128)(2,1)S(1)} collective-permute-done((bf16[2048,128]{1,0:T(8,128)(2,1)S(1)}, bf16[2048,128]{1,0:T(8,128)(2,1)S(1)}, u32[]{:S(2)}, u32[]{:S(2)}) %collective-permute-start.29) | collective-permute-done | bytes 524320 | tf_op jit(solution)/shard_map/ppermute | solution.py:37
  136.7 9.1 %collective-permute-done.33.refs_7_ = bf16[2048,128]{1,0:T(8,128)(2,1)S(1)} collective-permute-done((bf16[2048,128]{1,0:T(8,128)(2,1)S(1)}, bf16[2048,128]{1,0:T(8,128)(2,1)S(1)}, u32[]{:S(2)}, u32[]{:S(2)}) %collective-permute-start.33) | collective-permute-done | bytes 524320 | tf_op jit(solution)/shard_map/ppermute | solution.py:37
  148.5 7.7 %shard_map.114 = (bf16[8192,128]{1,0:T(8,128)(2,1)}, bf16[2048,128]{1,0:T(8,128)(2,1)}, bf16[2048,128]{1,0:T(8,128)(2,1)}, bf16[2048,128]{1,0:T(8,128)(2,1)}, bf...) custom-call(s32[1]{0:T(128)} %bitcast.12.live, ...), custom_call_target="tpu_custom_call" | custom-call | tf_op jit(solution)/shard_map/pallas_call | solution.py:206
  156.2 9.9 %all-gather.5.cloned.1.call-done = f32[2176,256]{1,0:T(8,128)} async-done(((f32[136,256]{1,0:T(8,128)}), f32[2176,256]{1,0:T(8,128)}) %all-gather.5.cloned.1.call-update) | async-done | bytes 2228240 | tf_op jit(solution)/shard_map/all_gather | solution.py:437
  174.6 17.9 %collective-permute-done.35 = bf16[2048,128]{1,0:T(8,128)(2,1)S(1)} collective-permute-done((bf16[2048,128]{1,0:T(8,128)(2,1)}, bf16[2048,128]{1,0:T(8,128)(2,1)S(1)}, u32[]{:S(2)}, u32[]{:S(2)}) %collective-permute-start.35) | collective-permute-done | bytes 524320 | tf_op jit(solution)/shard_map/ppermute | solution.py:32
  192.6 3.6 %collective-permute-done.37 = bf16[2048,128]{1,0:T(8,128)(2,1)S(1)} collective-permute-done((bf16[2048,128]{1,0:T(8,128)(2,1)}, bf16[2048,128]{1,0:T(8,128)(2,1)S(1)}, u32[]{:S(2)}, u32[]{:S(2)}) %collective-permute-start.37) | collective-permute-done | bytes 524320 | tf_op jit(solution)/shard_map/ppermute | solution.py:32
  196.1 7.0 %collective-permute-done.40 = bf16[2048,128]{1,0:T(8,128)(2,1)S(1)} collective-permute-done((bf16[2048,128]{1,0:T(8,128)(2,1)}, bf16[2048,128]{1,0:T(8,128)(2,1)S(1)}, u32[]{:S(2)}, u32[]{:S(2)}) %collective-permute-start.40) | collective-permute-done | bytes 524320 | tf_op jit(solution)/shard_map/ppermute | solution.py:27
  203.2 3.9 %conditional.10 = ((f32[1024,128]{1,0:T(8,128)}, bf16[1024,128]{1,0:T(8,128)(2,1)S(1)}, bf16[1024,128]{1,0:T(8,128)(2,1)S(1)}, bf16[1024,128]{1,0:T(8,128)(2,1)S...) conditional(s32[]{:T(128)} %bitcast.5, (s32[96]{0:T(128)S(1)}, ...), branch_computations={%region_2.0_spmd, %region_3.0_spmd} | conditional | flops 8388608 | bytes 49283412 | solution.py:459
  203.2 3.9 %branch_0_fun.3 = (f32[1024,128]{1,0:T(8,128)}, bf16[1024,128]{1,0:T(8,128)(2,1)S(1)}, bf16[1024,128]{1,0:T(8,128)(2,1)S(1)}, bf16[1024,128]{1,0:T(8,128)(2,1)S(...) custom-call(s32[96]{0:T(128)S(1)} %get-tuple-element.140.lists, ...), custom_call_target="tpu_custom_call" | custom-call | tf_op jit(solution)/shard_map/cond/branch_0_fun/pallas_call | solution.py:300
  209.1 7.8 %collective-permute-start.44 = (bf16[1024,128]{1,0:T(8,128)(2,1)}, bf16[1024,128]{1,0:T(8,128)(2,1)S(1)}, u32[]{:S(2)}, u32[]{:S(2)}) collective-permute-start(bf16[1024,128]{1,0:T(8,128)(2,1)} %get-tuple-element.233), channel_id=1, source_target_pairs={{0,24},{8,0},{16,8},{24,16},{32,56},{40,32},{48,40},{56,48},{64,88... | collective-permute-start | bytes 786440 | tf_op jit(solution)/shard_map/ppermute | solution.py:32
  217.8 6.1 %collective-permute-done.44.refs_5_ = bf16[1024,128]{1,0:T(8,128)(2,1)S(1)} collective-permute-done((bf16[1024,128]{1,0:T(8,128)(2,1)}, bf16[1024,128]{1,0:T(8,128)(2,1)S(1)}, u32[]{:S(2)}, u32[]{:S(2)}) %collective-permute-start.44) | collective-permute-done | bytes 262176 | tf_op jit(solution)/shard_map/ppermute | solution.py:32
  228.2 3.3 %shard_map.116 = (f32[2048,128]{1,0:T(8,128)}, f32[128,256]{1,0:T(8,128)}, f32[1,256]{1,0:T(1,128)}) custom-call(f32[1024,128]{1,0:T(8,128)} %get-tuple-element.228.refs_0_, bf16[1024,128]{1,0:T(8,128)(2,1)} %copy-done.25, bf16[1024,128]{1,0:T(8,128)(2,1)} %copy-done.26, bf16[1024,128]{1,0:T(8,128)(2,1)} %copy-done.27, ...), custom_call_target="tpu_custom_call" | custom-call | tf_op jit(solution)/shard_map/pallas_call | solution.py:337
  (100 shorter events, 52.3 us)
Async XLA Ops:
  7.2 158.9 %all-gather.5.cloned.1.call-start = ((), (), s32[]{:S(2)}) async-start(), calls=%async_computation | async-start | bytes 2367488 | tf_op jit(solution)/shard_map/all_gather | solution.py:437
  9.7 14.3 %collective-permute-start.12 = (bf16[1040,128]{1,0:T(8,128)(2,1)S(1)}, bf16[1040,128]{1,0:T(8,128)(2,1)S(1)}, u32[]{:S(2)}, u32[]{:S(2)}) collective-permute-start(bf16[1040,128]{1,0:T(8,128)(2,1)S(1)} %get-tuple-element.206.refs_0_), channel_id=1, source_target_pairs={{0,96},{8,104},{16,112},{24,120},{32,0},{40,8},{48,16},{56,24},{64... | collective-permute-start | bytes 798728 | tf_op jit(solution)/shard_map/ppermute | solution.py:27
  12.7 13.3 %collective-permute-start.13 = (bf16[1040,128]{1,0:T(8,128)(2,1)S(1)}, bf16[1040,128]{1,0:T(8,128)(2,1)S(1)}, u32[]{:S(2)}, u32[]{:S(2)}) collective-permute-start(bf16[1040,128]{1,0:T(8,128)(2,1)S(1)} %get-tuple-element.206.refs_0_), channel_id=1, source_target_pairs={{0,64},{8,72},{16,80},{24,88},{32,96},{40,104},{48,112},{56,120},{... | collective-permute-start | bytes 798728 | tf_op jit(solution)/shard_map/ppermute | solution.py:27
  13.5 14.3 %collective-permute-start.14 = (bf16[1040,128]{1,0:T(8,128)(2,1)S(1)}, bf16[1040,128]{1,0:T(8,128)(2,1)S(1)}, u32[]{:S(2)}, u32[]{:S(2)}) collective-permute-start(bf16[1040,128]{1,0:T(8,128)(2,1)S(1)} %get-tuple-element.206.refs_0_), channel_id=1, source_target_pairs={{0,32},{8,40},{16,48},{24,56},{32,64},{40,72},{48,80},{56,88},{64,... | collective-permute-start | bytes 798728 | tf_op jit(solution)/shard_map/ppermute | solution.py:27
  14.3 14.6 %collective-permute-start.15 = (bf16[1040,128]{1,0:T(8,128)(2,1)S(1)}, bf16[1040,128]{1,0:T(8,128)(2,1)S(1)}, u32[]{:S(2)}, u32[]{:S(2)}) collective-permute-start(bf16[1040,128]{1,0:T(8,128)(2,1)S(1)} %get-tuple-element.207.refs_4_), channel_id=1, source_target_pairs={{0,24},{8,0},{16,8},{24,16},{32,56},{40,32},{48,40},{56,48},{64,88... | collective-permute-start | bytes 798728 | tf_op jit(solution)/shard_map/ppermute | solution.py:32
  35.8 22.4 %collective-permute-start.18 = (bf16[2064,128]{1,0:T(8,128)(2,1)}, bf16[2064,128]{1,0:T(8,128)(2,1)S(1)}, u32[]{:S(2)}, u32[]{:S(2)}) collective-permute-start(bf16[2064,128]{1,0:T(8,128)(2,1)} %get-tuple-element.209), channel_id=1, source_target_pairs={{0,24},{8,0},{16,8},{24,16},{32,56},{40,32},{48,40},{56,48},{64,88... | collective-permute-start | bytes 1585160 | tf_op jit(solution)/shard_map/ppermute | solution.py:32
  37.9 23.6 %collective-permute-start.19 = (bf16[2064,128]{1,0:T(8,128)(2,1)}, bf16[2064,128]{1,0:T(8,128)(2,1)S(1)}, u32[]{:S(2)}, u32[]{:S(2)}) collective-permute-start(bf16[2064,128]{1,0:T(8,128)(2,1)} %get-tuple-element.210), channel_id=1, source_target_pairs={{0,16},{8,24},{16,0},{24,8},{32,48},{40,56},{48,32},{56,40},{64,80... | collective-permute-start | bytes 1585160 | tf_op jit(solution)/shard_map/ppermute | solution.py:32
  37.9 24.8 %collective-permute-start.20 = (bf16[2064,128]{1,0:T(8,128)(2,1)}, bf16[2064,128]{1,0:T(8,128)(2,1)S(1)}, u32[]{:S(2)}, u32[]{:S(2)}) collective-permute-start(bf16[2064,128]{1,0:T(8,128)(2,1)} %get-tuple-element.208), channel_id=1, source_target_pairs={{0,8},{8,16},{16,24},{24,0},{32,40},{40,48},{48,56},{56,32},{64,72... | collective-permute-start | bytes 1585160 | tf_op jit(solution)/shard_map/ppermute | solution.py:32
  39.1 24.8 %collective-permute-start.21 = (bf16[2048,128]{1,0:T(8,128)(2,1)}, bf16[2048,128]{1,0:T(8,128)(2,1)S(1)}, u32[]{:S(2)}, u32[]{:S(2)}) collective-permute-start(bf16[2048,128]{1,0:T(8,128)(2,1)} %get-tuple-element.212), channel_id=1, source_target_pairs={{0,96},{8,104},{16,112},{24,120},{32,0},{40,8},{48,16},{56,24},{64... | collective-permute-start | bytes 1572872 | tf_op jit(solution)/shard_map/ppermute | solution.py:27
  43.5 20.5 %collective-permute-start.22 = (bf16[2048,128]{1,0:T(8,128)(2,1)}, bf16[2048,128]{1,0:T(8,128)(2,1)S(1)}, u32[]{:S(2)}, u32[]{:S(2)}) collective-permute-start(bf16[2048,128]{1,0:T(8,128)(2,1)} %get-tuple-element.213), channel_id=1, source_target_pairs={{0,64},{8,72},{16,80},{24,88},{32,96},{40,104},{48,112},{56,120},{... | collective-permute-start | bytes 1572872 | tf_op jit(solution)/shard_map/ppermute | solution.py:27
  83.9 25.7 %collective-permute-start.25 = (bf16[2048,128]{1,0:T(8,128)(2,1)S(1)}, bf16[2048,128]{1,0:T(8,128)(2,1)S(1)}, u32[]{:S(2)}, u32[]{:S(2)}) collective-permute-start(bf16[2048,128]{1,0:T(8,128)(2,1)S(1)} %get-tuple-element.260), channel_id=1, source_target_pairs={{0,6},{1,7},{2,0},{3,1},{4,2},{5,3},{6,4},{7,5},{8,14},{9,15},{10,... | collective-permute-start | bytes 1572872 | tf_op jit(solution)/shard_map/ppermute | solution.py:37
  86.8 22.7 %collective-permute-start.26 = (bf16[2048,128]{1,0:T(8,128)(2,1)S(1)}, bf16[2048,128]{1,0:T(8,128)(2,1)S(1)}, u32[]{:S(2)}, u32[]{:S(2)}) collective-permute-start(bf16[2048,128]{1,0:T(8,128)(2,1)S(1)} %get-tuple-element.259), channel_id=1, source_target_pairs={{0,4},{1,5},{2,6},{3,7},{4,0},{5,1},{6,2},{7,3},{8,12},{9,13},{10,... | collective-permute-start | bytes 1572872 | tf_op jit(solution)/shard_map/ppermute | solution.py:37
  86.8 26.1 %collective-permute-start.27 = (bf16[2048,128]{1,0:T(8,128)(2,1)S(1)}, bf16[2048,128]{1,0:T(8,128)(2,1)S(1)}, u32[]{:S(2)}, u32[]{:S(2)}) collective-permute-start(bf16[2048,128]{1,0:T(8,128)(2,1)S(1)} %get-tuple-element.258), channel_id=1, source_target_pairs={{0,2},{1,3},{2,4},{3,5},{4,6},{5,7},{6,0},{7,1},{8,10},{9,11},{10,... | collective-permute-start | bytes 1572872 | tf_op jit(solution)/shard_map/ppermute | solution.py:37
  119.3 108.3 %all-gather.7.cloned.1.call-start = ((), (), s32[]{:S(2)}) async-start(), calls=%async_computation.1 | async-start | bytes 1253376 | tf_op jit(solution)/shard_map/all_gather | solution.py:441
  119.3 14.9 %collective-permute-start.29 = (bf16[2048,128]{1,0:T(8,128)(2,1)S(1)}, bf16[2048,128]{1,0:T(8,128)(2,1)S(1)}, u32[]{:S(2)}, u32[]{:S(2)}) collective-permute-start(bf16[2048,128]{1,0:T(8,128)(2,1)S(1)} %get-tuple-element.220.refs_4_), channel_id=1, source_target_pairs={{0,6},{1,7},{2,0},{3,1},{4,2},{5,3},{6,4},{7,5},{8,14},{9,15},{10,... | collective-permute-start | bytes 1572872 | tf_op jit(solution)/shard_map/ppermute | solution.py:37
  120.3 16.4 %collective-permute-start.31 = (bf16[2048,128]{1,0:T(8,128)(2,1)S(1)}, bf16[2048,128]{1,0:T(8,128)(2,1)S(1)}, u32[]{:S(2)}, u32[]{:S(2)}) collective-permute-start(bf16[2048,128]{1,0:T(8,128)(2,1)S(1)} %get-tuple-element.220.refs_4_), channel_id=1, source_target_pairs={{0,4},{1,5},{2,6},{3,7},{4,0},{5,1},{6,2},{7,3},{8,12},{9,13},{10,... | collective-permute-start | bytes 1572872 | tf_op jit(solution)/shard_map/ppermute | solution.py:37
  120.6 25.2 %collective-permute-start.33 = (bf16[2048,128]{1,0:T(8,128)(2,1)S(1)}, bf16[2048,128]{1,0:T(8,128)(2,1)S(1)}, u32[]{:S(2)}, u32[]{:S(2)}) collective-permute-start(bf16[2048,128]{1,0:T(8,128)(2,1)S(1)} %get-tuple-element.220.refs_4_), channel_id=1, source_target_pairs={{0,2},{1,3},{2,4},{3,5},{4,6},{5,7},{6,0},{7,1},{8,10},{9,11},{10,... | collective-permute-start | bytes 1572872 | tf_op jit(solution)/shard_map/ppermute | solution.py:37
  121.4 24.4 %collective-permute-start.28 = (bf16[2048,128]{1,0:T(8,128)(2,1)S(1)}, bf16[2048,128]{1,0:T(8,128)(2,1)S(1)}, u32[]{:S(2)}, u32[]{:S(2)}) collective-permute-start(bf16[2048,128]{1,0:T(8,128)(2,1)S(1)} %get-tuple-element.220.refs_4_), channel_id=1, source_target_pairs={{0,1},{1,0},{2,3},{3,2},{4,5},{5,4},{6,7},{7,6},{8,9},{9,8},{10,11... | collective-permute-start | bytes 1572872 | tf_op jit(solution)/shard_map/ppermute | solution.py:42
  168.5 24.0 %collective-permute-start.35 = (bf16[2048,128]{1,0:T(8,128)(2,1)}, bf16[2048,128]{1,0:T(8,128)(2,1)S(1)}, u32[]{:S(2)}, u32[]{:S(2)}) collective-permute-start(bf16[2048,128]{1,0:T(8,128)(2,1)} %get-tuple-element.222), channel_id=1, source_target_pairs={{0,24},{8,0},{16,8},{24,16},{32,56},{40,32},{48,40},{56,48},{64,88... | collective-permute-start | bytes 1572872 | tf_op jit(solution)/shard_map/ppermute | solution.py:32
  170.8 21.7 %collective-permute-start.36 = (bf16[2048,128]{1,0:T(8,128)(2,1)}, bf16[2048,128]{1,0:T(8,128)(2,1)S(1)}, u32[]{:S(2)}, u32[]{:S(2)}) collective-permute-start(bf16[2048,128]{1,0:T(8,128)(2,1)} %get-tuple-element.223), channel_id=1, source_target_pairs={{0,16},{8,24},{16,0},{24,8},{32,48},{40,56},{48,32},{56,40},{64,80... | collective-permute-start | bytes 1572872 | tf_op jit(solution)/shard_map/ppermute | solution.py:32
  171.7 24.5 %collective-permute-start.37 = (bf16[2048,128]{1,0:T(8,128)(2,1)}, bf16[2048,128]{1,0:T(8,128)(2,1)S(1)}, u32[]{:S(2)}, u32[]{:S(2)}) collective-permute-start(bf16[2048,128]{1,0:T(8,128)(2,1)} %get-tuple-element.224), channel_id=1, source_target_pairs={{0,8},{8,16},{16,24},{24,0},{32,40},{40,48},{48,56},{56,32},{64,72... | collective-permute-start | bytes 1572872 | tf_op jit(solution)/shard_map/ppermute | solution.py:32
  171.8 24.4 %collective-permute-start.38 = (bf16[2048,128]{1,0:T(8,128)(2,1)}, bf16[2048,128]{1,0:T(8,128)(2,1)S(1)}, u32[]{:S(2)}, u32[]{:S(2)}) collective-permute-start(bf16[2048,128]{1,0:T(8,128)(2,1)} %get-tuple-element.225), channel_id=1, source_target_pairs={{0,96},{8,104},{16,112},{24,120},{32,0},{40,8},{48,16},{56,24},{64... | collective-permute-start | bytes 1572872 | tf_op jit(solution)/shard_map/ppermute | solution.py:27
  173.8 22.3 %collective-permute-start.39 = (bf16[2048,128]{1,0:T(8,128)(2,1)}, bf16[2048,128]{1,0:T(8,128)(2,1)S(1)}, u32[]{:S(2)}, u32[]{:S(2)}) collective-permute-start(bf16[2048,128]{1,0:T(8,128)(2,1)} %get-tuple-element.226), channel_id=1, source_target_pairs={{0,64},{8,72},{16,80},{24,88},{32,96},{40,104},{48,112},{56,120},{... | collective-permute-start | bytes 1572872 | tf_op jit(solution)/shard_map/ppermute | solution.py:27
  209.1 14.8 %collective-permute-start.44 = (bf16[1024,128]{1,0:T(8,128)(2,1)}, bf16[1024,128]{1,0:T(8,128)(2,1)S(1)}, u32[]{:S(2)}, u32[]{:S(2)}) collective-permute-start(bf16[1024,128]{1,0:T(8,128)(2,1)} %get-tuple-element.233), channel_id=1, source_target_pairs={{0,24},{8,0},{16,8},{24,16},{32,56},{40,32},{48,40},{56,48},{64,88... | collective-permute-start | bytes 786440 | tf_op jit(solution)/shard_map/ppermute | solution.py:32
  (29 other events, 242.9 us)
Sparse Core Ops, SparseCore 0:
  119.4 46.6 all-gather.4
  168.6 22.8 all-gather.6

commit v3 on v2

v3 whole, which is shorter than its diff:
```python
import functools
import itertools
import math

import jax
import jax.numpy as jnp
from jax import lax
from jax.experimental import pallas as pl
from jax.experimental.pallas import tpu as pltpu
from jax.sharding import PartitionSpec as P

T = 128
F32, BF16, I32 = jnp.float32, jnp.bfloat16, jnp.int32
VMEM_BYTES = 56 * 1024 * 1024
GROUP = 4
META = 16
CAP = 26
LANES = 32
SMEM = pl.BlockSpec(memory_space=pltpu.SMEM)
VMEM = pl.BlockSpec(memory_space=pltpu.VMEM)
ANY = pl.BlockSpec(memory_space=pl.ANY)
PARAMS = pltpu.CompilerParams(vmem_limit_bytes=VMEM_BYTES)


def along_xz(value, to, x_core):
    pairs = []
    for x, z, y, core in itertools.product(range(4), range(4), range(4), range(2)):
        far = (to(x) % 4, z) if core == x_core else (x, to(z) % 4)
        pairs.append(((x * 4 + z) * 8 + y * 2 + core, (far[0] * 4 + far[1]) * 8 + y * 2 + core))
    return lax.ppermute(value, ("row", "col"), pairs)


def along_inner(value, to):
    return along_xz(value, to, 0)


def along_outer(value, to):
    return along_xz(value, to, 1)


def along_y(value, to):
    pairs = [(y * 2 + k, to(y) % 4 * 2 + k) for y in range(4) for k in range(2)]
    return lax.ppermute(value, "col", pairs)


def other_core(value):
    pairs = [(y * 2 + k, y * 2 + 1 - k) for y in range(4) for k in range(2)]
    return lax.ppermute(value, "col", pairs)


def ahead(step):
    return lambda at: at + step


def ring_gather(value, along):
    return [value, along(value, ahead(-1)), along(value, ahead(2)), along(value, ahead(1))]


def ring_swap(pieces, along):
    return [
        pieces[0],
        along(pieces[3], ahead(-1)),
        along(pieces[2], ahead(2)),
        along(pieces[1], ahead(1)),
    ]


def total_of(pieces):
    return sum(piece.astype(F32) for piece in pieces)


def block(place):
    return pl.ds(pl.multiple_of(place * T, T), T)


def prepare_kernel(
    at_row, at_col, live_ref, rows_ref, cols_ref, features, payload, meta, tables, sem
):
    nodes = features.shape[0]
    copy = pltpu.make_async_copy(features, payload.at[pl.ds(0, nodes)], sem)
    copy.start()
    live = live_ref[0]
    x, z = at_row[0] >> 2, at_row[0] & 3
    y, core = at_col[0] >> 1, at_col[0] & 1
    rows, cols = rows_ref[...], cols_ref[...]
    slots = cols.shape[1]

    same_core = jnp.where(((rows >> 4) & 1) == core, 64, 0)
    row_place = same_core + (((rows >> 5) - y) & 3) * 16 + (rows & 15)
    dx, dz = ((cols >> 6) - x) & 3, ((cols >> 4) - z) & 3
    outer, inner = jnp.where(core == 0, dz, dx), jnp.where(core == 0, dx, dz)
    code = inner * 16 + (cols & 15)
    dense_place = outer * 64 + code

    t = lax.broadcasted_iota(I32, (slots, slots), 0)
    s = lax.broadcasted_iota(I32, (slots, slots), 1)
    lane = lax.broadcasted_iota(I32, (slots, T), 1).astype(F32)

    def column(row):
        return jnp.sum(jnp.where(t == s, row, 0.0), axis=1, keepdims=True)

    def count(mask, value=1.0):
        return jnp.sum(jnp.where(mask, value, 0.0), axis=0, keepdims=True)

    valid = lax.broadcasted_iota(I32, (1, slots), 1) < live
    cols_f, outer_f = cols.astype(F32), outer.astype(F32)
    same = column(cols_f) == cols_f
    first = valid & (count(same & (t < s)) == 0.0)
    first_c = column(jnp.where(first, 1.0, 0.0)) > 0.0
    outer_c = column(outer_f)
    rank = count((t < s) & first_c & (outer_c == outer_f))
    over = jnp.where(first & (outer != 0) & (rank >= CAP), 1.0, 0.0)
    over = jnp.max(over, axis=1, keepdims=True)
    far = (64 + (outer - 1) * CAP).astype(F32) + jnp.minimum(rank, CAP - 1.0)
    place = jnp.where(outer == 0, code.astype(F32), far)
    place = count(same & first_c, column(place))
    place = jnp.where(valid, place, 0.0).astype(I32)
    pad = jnp.zeros((5, slots), I32)
    tables[...] = jnp.concatenate([row_place, place, dense_place, pad], axis=0)

    key = column(jnp.where(first & (rank < CAP), outer_f * LANES + rank, -1.0))
    wanted = count(key == lane, column(code.astype(F32)))
    amounts = jnp.minimum(count((outer_c == lane) & first_c), 1.0 * CAP)
    line = lax.broadcasted_iota(I32, (META, T), 0)
    lines = [wanted, amounts, jnp.broadcast_to(over, (1, T)), jnp.zeros((META - 3, T), F32)]
    meta[...] = jnp.concatenate(lines, axis=0).astype(BF16)
    payload[pl.ds(nodes, META)] = meta[...]
    copy.wait()


def prepare(at_row, at_col, live, rows, cols, features):
    slots = cols.shape[-1]
    return pl.pallas_call(
        prepare_kernel,
        out_shape=[
            jax.ShapeDtypeStruct((features.shape[0] + META, T), BF16),
            jax.ShapeDtypeStruct((META, T), BF16),
            jax.ShapeDtypeStruct((8, slots), I32),
        ],
        in_specs=[SMEM] * 3 + [VMEM] * 2 + [ANY],
        out_specs=[VMEM] * 3,
        scratch_shapes=[pltpu.SemaphoreType.DMA],
        compiler_params=PARAMS,
    )(at_row, at_col, live, rows.reshape(1, slots), cols.reshape(1, slots), features)


def products_kernel(live, tables, tiles_ref, *refs, spans, outs, contract, in_row, out_row):
    n = len(spans)
    sources, out_refs, (tiles, held, total, sems) = refs[:n], refs[n:-4], refs[-4:]
    copies = [pltpu.make_async_copy(tiles_ref, tiles, sems.at[n])]
    start = 0
    for k, (ref, rows) in enumerate(zip(sources, spans)):
        copies.append(
            pltpu.make_async_copy(
                ref.at[pl.ds(0, rows)], held.at[pl.ds(start, rows)], sems.at[k]
            )
        )
        start += rows
    for copy in copies:
        copy.start()

    zeros = jnp.zeros((4, T, T), F32)

    def clear(k, carry):
        total[pl.ds(k * 4, 4)] = zeros
        return carry

    lax.fori_loop(0, total.shape[0] // 4, clear, 0)
    for copy in copies:
        copy.wait()

    def group(number, carry):
        products = []
        for k in range(GROUP):
            slot = number * GROUP + k
            product = lax.dot_general(
                tiles[slot],
                held[block(tables[in_row, slot])],
                ((contract, (0,)), ((), ())),
                preferred_element_type=F32,
            )
            products.append(jnp.where(slot < live[0], product, 0.0))
        for k, product in enumerate(products):
            total[tables[out_row, number * GROUP + k]] += product
        return carry

    lax.fori_loop(0, (live[0] + GROUP - 1) // GROUP, group, 0)
    start = 0
    for ref, blocks in zip(out_refs, outs):

        def out(k, carry, ref=ref, start=start):
            ref[block(k)] = total[start + k].astype(BF16)
            return carry

        lax.fori_loop(0, blocks, out, 0)
        start += blocks


def products(live, tables, in_row, out_row, tiles, sources, spans, outs, contract):
    kernel = functools.partial(
        products_kernel,
        spans=spans,
        outs=outs,
        contract=contract,
        in_row=in_row,
        out_row=out_row,
    )
    return pl.pallas_call(
        kernel,
        out_shape=[jax.ShapeDtypeStruct((n * T, T), BF16) for n in outs],
        in_specs=[SMEM] * 2 + [ANY] * (1 + len(sources)),
        out_specs=[VMEM] * len(outs),
        scratch_shapes=[
            pltpu.VMEM(tiles.shape, BF16),
            pltpu.VMEM((sum(spans), T), BF16),
            pltpu.VMEM((sum(outs), T, T), F32),
            pltpu.SemaphoreType.DMA((len(spans) + 1,)),
        ],
        compiler_params=PARAMS,
    )(live, tables, tiles, *sources)


def pack_kernel(*refs):
    pieces, metas, sends, (lists, counts), (held, words, table, sems) = (
        refs[:4],
        refs[4:7],
        refs[7:10],
        refs[10:12],
        refs[12:],
    )
    nodes = held.shape[1] - META
    copies = [pltpu.make_async_copy(p, held.at[k], sems.at[k]) for k, p in enumerate(pieces)]
    for copy in copies:
        copy.start()
    for n in range(3):
        words[pl.ds(n * 8, 8)] = metas[n][...].astype(F32)[:8].astype(I32)
    fetch = pltpu.make_async_copy(words, table, sems.at[4])
    fetch.start()
    fetch.wait()
    for copy in copies:
        copy.wait()
    said = [held[k, pl.ds(nodes, META)].astype(F32) for k in range(4)]
    said = functools.reduce(jnp.maximum, said).astype(BF16)
    for n in range(3):
        sends[n][pl.ds(CAP * T, META)] = said
        group = 3 - n
        amount = table[n * 8 + 1, group]
        counts[n] = amount

        def step(k, carry, n=n, group=group):
            code = table[n * 8, group * LANES + k]
            lists[n * CAP + k] = code
            sends[n][block(k)] = held[code >> 4, block(code & 15)]
            return carry

        lax.fori_loop(0, amount, step, 0)


def pack(pieces, metas):
    return pl.pallas_call(
        pack_kernel,
        out_shape=[jax.ShapeDtypeStruct((CAP * T + META, T), BF16)] * 3
        + [jax.ShapeDtypeStruct((3 * CAP,), I32), jax.ShapeDtypeStruct((3,), I32)],
        in_specs=[ANY] * 4 + [VMEM] * 3,
        out_specs=[VMEM] * 3 + [SMEM] * 2,
        scratch_shapes=[
            pltpu.VMEM((4,) + pieces[0].shape, BF16),
            pltpu.VMEM((24, T), I32),
            pltpu.SMEM((24, T), I32),
            pltpu.SemaphoreType.DMA((5,)),
        ],
        compiler_params=PARAMS,
    )(*pieces, *metas)


def combine_kernel(lists, counts, own, sums, *refs):
    parts, outs, (total,) = refs[:3], refs[3:7], refs[7:]

    def widen(k, carry):
        total[k] = own[block(k)].astype(F32)
        return carry

    lax.fori_loop(0, 64, widen, 0)
    for n, part in enumerate(parts):

        def add(k, carry, n=n, part=part):
            total[lists[n * CAP + k]] += part[block(k)].astype(F32)
            return carry

        lax.fori_loop(0, counts[n], add, 0)
    for n, ref in enumerate(outs):

        def out(k, carry, n=n, ref=ref):
            ref[block(k)] = total[n * 16 + k].astype(ref.dtype)
            return carry

        lax.fori_loop(0, 16, out, 0)
        if n:
            ref[pl.ds(16 * T, sums.shape[0])] = sums[...]


def combine(lists, counts, own, sums, parts):
    rows = 16 * T
    return pl.pallas_call(
        combine_kernel,
        out_shape=[jax.ShapeDtypeStruct((rows, T), F32)]
        + [jax.ShapeDtypeStruct((rows + sums.shape[0], T), BF16)] * 3,
        in_specs=[SMEM] * 2 + [VMEM] * 5,
        out_specs=[VMEM] * 4,
        scratch_shapes=[pltpu.VMEM((64, T, T), F32)],
        compiler_params=PARAMS,
    )(lists, counts, own, sums, *parts)


def finish_kernel(*refs, scaling):
    pieces, sums, (nodes, weight, offset) = refs[:4], refs[4], refs[5:]
    rows = nodes.shape[0]
    nodes[...] = total_of([ref[pl.ds(0, rows)] for ref in pieces])
    lines = sums.shape[0]
    for k in range(2):
        part = pl.ds(k * T, T)
        total = sums[:, part]
        for ref in pieces[1:]:
            total = total + ref[pl.ds(rows + k * lines, lines)].astype(F32)
        total = total * scaling
        weight[:, part] = total[:T]
        offset[:, part] = jnp.sum(total[T:], axis=0, keepdims=True)


def finish(pieces, sums, scaling):
    width = sums.shape[-1]
    return pl.pallas_call(
        functools.partial(finish_kernel, scaling=scaling),
        out_shape=[
            jax.ShapeDtypeStruct(pieces[0].shape, F32),
            jax.ShapeDtypeStruct((T, width), F32),
            jax.ShapeDtypeStruct((1, width), F32),
        ],
        in_specs=[VMEM] * 5,
        out_specs=[VMEM] * 3,
        compiler_params=PARAMS,
    )(*pieces, sums)


def dense_kernel(m0, m1, m2, m3, grad, weight, offset, hidden, projected, sums):
    @pl.when(pl.program_id(0) == 0)
    def _():
        sums[...] = jnp.zeros_like(sums)

    mixed = m0[...].astype(F32) + m1[...].astype(F32) + m2[...].astype(F32) + m3[...].astype(F32)
    high = mixed.astype(BF16)
    low = (mixed - high.astype(F32)).astype(BF16)
    w = weight[...]
    pre = jnp.dot(high, w, preferred_element_type=F32)
    pre = pre + jnp.dot(low, w, preferred_element_type=F32) + offset[...]
    s = jax.nn.sigmoid(pre)
    hidden[...] = (pre * s).astype(BF16)
    slope = (grad[...].astype(F32) * s * (1.0 + pre * (1.0 - s))).astype(BF16)
    projected[...] = lax.dot_general(
        slope, w, (((1,), (1,)), ((), ())), preferred_element_type=F32
    ).astype(BF16)
    over_rows = (((0,), (0,)), ((), ()))
    sums[:T] += lax.dot_general(
        high, slope, over_rows, preferred_element_type=F32
    ) + lax.dot_general(low, slope, over_rows, preferred_element_type=F32)
    sums[T:] += jnp.sum(slope.astype(F32).reshape(-1, 8, slope.shape[1]), axis=0)


def dense(parts, grad, weight, offset):
    rows, width = parts[0].shape[0], weight.shape[1]
    step = 512
    half = pl.BlockSpec((step, T), lambda i: (i, 0))
    full = pl.BlockSpec((step, width), lambda i: (i, 0))
    return pl.pallas_call(
        dense_kernel,
        grid=(rows // step,),
        out_shape=[
            jax.ShapeDtypeStruct((rows, width), BF16),
            jax.ShapeDtypeStruct((rows, T), BF16),
            jax.ShapeDtypeStruct((T + 8, width), F32),
        ],
        in_specs=[half] * 4
        + [
            full,
            pl.BlockSpec((T, width), lambda i: (0, 0)),
            pl.BlockSpec((1, width), lambda i: (0, 0)),
        ],
        out_specs=[full, half, pl.BlockSpec((T + 8, width), lambda i: (0, 0))],
        compiler_params=PARAMS,
    )(*parts, grad, weight, offset)


def on_device(features, weight, offset, tile_values, tile_rows, tile_cols, live_tiles, grad_hidden):
    tiles = tile_values.reshape(tile_values.shape[2:])
    nodes_here = features.shape[0]
    scaling = 1.0 / math.sqrt(nodes_here * lax.axis_size("row") * lax.axis_size("col"))
    at_row, at_col = lax.axis_index("row"), lax.axis_index("col")
    live = live_tiles.reshape(1)
    payload, meta, tables = prepare(
        at_row.reshape(1), at_col.reshape(1), live, tile_rows, tile_cols, features
    )

    pieces = ring_gather(payload, along_inner)
    *sends, lists, counts = pack(pieces, ring_gather(meta, along_outer)[1:])
    named = ring_swap([None] + sends, along_outer)[1:]
    flags = [sends[0]] + named
    full = functools.reduce(jnp.maximum, [f[CAP * T + 2, 0] for f in flags]) > 0.5

    def forward_all(pieces, named):
        whole = jnp.concatenate([p[:nodes_here] for p in pieces])
        whole = ring_gather(whole, along_outer)
        spans = (4 * nodes_here,) * 4
        return products(live, tables, 2, 0, tiles, whole, spans, (64, 64), (1,))

    def forward_named(pieces, named):
        spans = (nodes_here,) * 4 + (CAP * T,) * 3
        return products(live, tables, 1, 0, tiles, pieces + named, spans, (64, 64), (1,))

    send, keep = lax.cond(full, forward_all, forward_named, pieces, named)

    both = keep.astype(F32) + other_core(send).astype(F32)
    both = both.reshape(4, nodes_here, T)
    mixed_parts = ring_swap([both[d].astype(BF16) for d in range(4)], along_y)
    hidden, projected, sums = dense(mixed_parts, grad_hidden, weight, offset.reshape(1, -1))

    own = ring_gather(projected, along_y)
    gathered = [other_core(piece) for piece in own] + own

    sums = sums + other_core(sums)
    for along in (along_outer, along_y):
        sums = total_of(ring_gather(sums, along))
    rounded = jnp.concatenate([sums[:, :T], sums[:, T:]]).astype(BF16)

    spans, outs = (nodes_here,) * 8, (64,) + (CAP,) * 3
    here, *parts = products(live, tables, 0, 1, tiles, gathered, spans, outs, (0,))
    parts = ring_swap([None] + parts, along_outer)[1:]

    def backward_all(here, rounded, parts, gathered):
        outs = products(live, tables, 0, 2, tiles, gathered, spans, (64,) * 4, (0,))
        mine = total_of(ring_swap(outs, along_outer)).reshape(4, nodes_here, T)
        far = [jnp.concatenate([mine[d].astype(BF16), rounded]) for d in (1, 2, 3)]
        return [mine[0]] + far

    def backward_named(here, rounded, parts, gathered):
        return list(combine(lists, counts, here, rounded, parts))

    outs = lax.cond(full, backward_all, backward_named, here, rounded, parts, gathered)
    outs = ring_swap(outs, along_inner)
    grad_features, grad_weight, grad_offset = finish(outs, sums, scaling)
    return (hidden, grad_features, grad_weight, grad_offset.reshape(-1))


def solution(mesh):
    in_specs = (
        P(("col", "row"), None),
        P(),
        P(),
        P("row", "col", None, None, None),
        P("row", "col", None),
        P("row", "col", None),
        P("row", "col"),
        P(("row", "col"), None),
    )
    out_specs = (P(("row", "col"), None), P(("col", "row"), None), P(), P())
    return jax.shard_map(
        on_device, mesh=mesh, in_specs=in_specs, out_specs=out_specs, check_vma=False
    )
```

time: 240 us -> 201 us (0.84)
  waiting for transfers between devices: 136 us -> 101 us
  between operations: 17.7 us -> 4.21 us
  starting transfers between devices: 41.3 us -> 52.2 us
  Pallas kernels: 35.1 us -> 31.2 us
    ppermute x24 -> x18, waiting for transfers between devices: 70.3 us -> 52.2 us  [along_xz(): return lax.ppermute(value, ('row', 'col'), pairs)]
    all_gather x2 -> x0, waiting for transfers between devices: 9.88 us -> none  [the longest x1 9.88 us: on_device(): sums = lax.all_gather(sums, 'row', axis=0)]
    ppermute x6 -> x9, starting transfers between devices: 6.11 us -> 12.9 us  [along_y(): return lax.ppermute(value, 'col', pairs)]
    ppermute x6 -> x9, waiting for transfers between devices: 49.4 us -> 42.9 us  [along_y(): return lax.ppermute(value, 'col', pairs)]
    ppermute x24 -> x18, starting transfers between devices: 35 us -> 38.7 us  [along_xz(): return lax.ppermute(value, ('row', 'col'), pairs)]
    pallas_call x4 -> x3, Pallas kernels: 11.2 us -> 10.2 us  [the longest x1 4.34 us: combine(): pl.pallas_call(combine_kernel, out_shape=[jax.ShapeDtypeStruct((rows, T),...]
    ppermute x5 -> x6, waiting for transfers between devices: 6.22 us -> 5.94 us  [other_core(): return lax.ppermute(value, 'col', pairs)]
  transfers between devices with their start and end apart: 37 -> 33, of which waited for: 21 -> 20; matrix products, arithmetic and copies ran while one was open for 1% -> 2% of each run, Pallas kernels for 5% -> 3%
where the time goes in v3:
time: 201 us; the launch traced here: 199 us
  waiting for transfers between devices  101 us (50%)
  starting transfers between devices  52.2 us (26%)
  Pallas kernels  31.2 us (16%)
  local copies, waits for them, and re-layouts  6.44 us (3%)
  between operations  4.21 us (2%)
  other arithmetic  3.82 us (2%)
    ppermute x18, waiting for transfers between devices, along_xz(): return lax.ppermute(value, ('row', 'col'), pairs)  52.2 us
    ppermute x9, waiting for transfers between devices, along_y(): return lax.ppermute(value, 'col', pairs)  42.9 us
    ppermute x18, starting transfers between devices, along_xz(): return lax.ppermute(value, ('row', 'col'), pairs)  38.7 us
    ppermute x9, starting transfers between devices, along_y(): return lax.ppermute(value, 'col', pairs)  12.9 us
    pallas_call x2, Pallas kernels, products(): pl.pallas_call(kernel, out_shape=[jax.ShapeDtypeStruct((n * T, T), BF16)...  12.9 us
    ppermute x6, waiting for transfers between devices, other_core(): return lax.ppermute(value, 'col', pairs)  5.94 us
    pallas_call x1, Pallas kernels, dense(): pl.pallas_call(dense_kernel, grid=(rows // step,), out_shape=[jax.ShapeDt...  5.48 us
    pallas_call x1, Pallas kernels, combine(): pl.pallas_call(combine_kernel, out_shape=[jax.ShapeDtypeStruct((rows, T),...  4.34 us
  transfers between devices with their start and end apart: 33, of which 20 were waited for; matrix products, arithmetic and copies ran while one was open for 2% of the time, Pallas kernels for 3%

profile of v3, /device:TPU:0, one launch (start us, length us, event | category | flops | bytes accessed | tf_op | source)
XLA Modules:
  0.0 199.0 jit_solution(1021907880919014076)
XLA Ops:
  11.5 3.6 %collective-permute-start.10 = (bf16[16,128]{1,0:T(8,128)(2,1)}, bf16[16,128]{1,0:T(8,128)(2,1)S(1)}, u32[]{:S(2)}, u32[]{:S(2)}) collective-permute-start(bf16[16,128]{1,0:T(8,128)(2,1)} %get-tuple-element.157), channel_id=1, source_target_pairs={{0,16},{1,65},{2,18},{3,67},{4,20},{5,69},{6,22},{7,71},{8,24},{9,... | collective-permute-start | bytes 12296 | tf_op jit(solution)/shard_map/ppermute | solution.py:30
  21.1 3.5 %shard_map.112 = (bf16[3344,128]{1,0:T(8,128)(2,1)}, bf16[3344,128]{1,0:T(8,128)(2,1)}, bf16[3344,128]{1,0:T(8,128)(2,1)}, s32[78]{0:T(128)S(1)}, s32[3]{0:T(128)S(1)}) custom-call(bf16[2064,128]{1,0:T(8,128)(2,1)S(1)} %get-tuple-element.156.refs_0_, bf16[2064,128]{1,0:T(8,128)(2,1)S(1)} %collective-permute-done.6.refs_1_, ...), custom_call_target="tpu_custom_call" | custom-call | tf_op jit(solution)/shard_map/pallas_call | solution.py:260
  24.7 4.0 %collective-permute-start.12 = (bf16[3344,128]{1,0:T(8,128)(2,1)}, bf16[3344,128]{1,0:T(8,128)(2,1)S(1)}, u32[]{:S(2)}, u32[]{:S(2)}) collective-permute-start(bf16[3344,128]{1,0:T(8,128)(2,1)} %get-tuple-element.159), channel_id=1, source_target_pairs={{0,24},{1,97},{2,26},{3,99},{4,28},{5,101},{6,30},{7,103},{8,0},{9... | collective-permute-start | bytes 2568200 | tf_op jit(solution)/shard_map/ppermute | solution.py:30
  32.1 16.4 %collective-permute-done.12 = bf16[3344,128]{1,0:T(8,128)(2,1)S(1)} collective-permute-done((bf16[3344,128]{1,0:T(8,128)(2,1)}, bf16[3344,128]{1,0:T(8,128)(2,1)S(1)}, u32[]{:S(2)}, u32[]{:S(2)}) %collective-permute-start.12) | collective-permute-done | bytes 856096 | tf_op jit(solution)/shard_map/ppermute | solution.py:30
  53.5 6.7 %conditional.11 = ((bf16[8192,128]{1,0:T(8,128)(2,1)}, bf16[8192,128]{1,0:T(8,128)(2,1)})) conditional(s32[]{:T(128)} %bitcast.5, (s32[1]{0:T(128)}, s32[8,64]{1,0:T(8,128)S(1)}, bf16[64,128,128]{2,1,0:T(8,128)(2,1)S(1)}, bf16[2064,128]{1,0:T(8,128)(2,1)S(1)}, bf16[2064,128]{1,0:T(8,128)(2,1)S(1)}, /*index=5*/bf16[2064,128]{1,0:T(8,128)(2,1)S(1)}, ...), branch_computations={%region_0.0_spmd, %region_1.0_spmd} | conditional | flops 8388608 | bytes 67109104
  53.5 6.7 %branch_0_fun.2 = (bf16[8192,128]{1,0:T(8,128)(2,1)}, bf16[8192,128]{1,0:T(8,128)(2,1)}) custom-call(s32[1]{0:T(128)} %get-tuple-element.88.live, s32[8,64]{1,0:T(8,128)S(1)} %get-tuple-element.89.tables, bf16[64,128,128]{2,1,0:T(8,128)(2,1)S(1)} %get-tuple-element.90.tiles_ref, bf16[2064,128]{1,0:T(8,128)(2,1)S(1)} %get-tuple-element.91.refs_0_, ...), custom_call_target="tpu_custom_call" | custom-call | tf_op jit(solution)/shard_map/cond/branch_0_fun/pallas_call | solution.py:208
  60.3 4.4 %collective-permute-done.15 = bf16[8192,128]{1,0:T(8,128)(2,1)S(1)} collective-permute-done((bf16[8192,128]{1,0:T(8,128)(2,1)}, bf16[8192,128]{1,0:T(8,128)(2,1)S(1)}, u32[]{:S(2)}, u32[]{:S(2)}) %collective-permute-start.15) | collective-permute-done | bytes 2097184 | tf_op jit(solution)/shard_map/ppermute | solution.py:48
  70.5 2.8 %collective-permute-start.17 = (bf16[2048,128]{1,0:T(8,128)(2,1)S(1)}, bf16[2048,128]{1,0:T(8,128)(2,1)S(1)}, u32[]{:S(2)}, u32[]{:S(2)}) collective-permute-start(bf16[2048,128]{1,0:T(8,128)(2,1)S(1)} %get-tuple-element.199), channel_id=1, source_target_pairs={{0,4},{1,5},{2,6},{3,7},{4,0},{5,1},{6,2},{7,3},{8,12},{9,13},{10,... | collective-permute-start | bytes 1572872 | tf_op jit(solution)/shard_map/ppermute | solution.py:43
  73.3 10.8 %collective-permute-done.18.m3 = bf16[2048,128]{1,0:T(8,128)(2,1)S(1)} collective-permute-done((bf16[2048,128]{1,0:T(8,128)(2,1)S(1)}, bf16[2048,128]{1,0:T(8,128)(2,1)S(1)}, u32[]{:S(2)}, u32[]{:S(2)}) %collective-permute-start.18) | collective-permute-done | bytes 524320 | tf_op jit(solution)/shard_map/ppermute | solution.py:43
  84.1 12.4 %collective-permute-done.17.m2 = bf16[2048,128]{1,0:T(8,128)(2,1)S(1)} collective-permute-done((bf16[2048,128]{1,0:T(8,128)(2,1)S(1)}, bf16[2048,128]{1,0:T(8,128)(2,1)S(1)}, u32[]{:S(2)}, u32[]{:S(2)}) %collective-permute-start.17) | collective-permute-done | bytes 524320 | tf_op jit(solution)/shard_map/ppermute | solution.py:43
  97.5 5.5 %shard_map.113 = (bf16[2048,256]{1,0:T(8,128)(2,1)}, bf16[2048,128]{1,0:T(8,128)(2,1)S(1)}, f32[136,256]{1,0:T(8,128)}) custom-call(bf16[2048,128]{1,0:T(8,128)(2,1)} %get-tuple-element.201.m0, bf16[2048,128]{1,0:T(8,128)(2,1)} %copy-done.11, bf16[2048,128]{1,0:T(8,128)(2,1)} %copy-done.10, bf16[2048,128]{1,0:T(8,128)(2,1)} %copy-done.9, ...), custom_call_target="tpu_custom_call" | custom-call | tf_op jit(solution)/shard_map/pallas_call | solution.py:374
  109.8 3.4 %collective-permute-start.28 = (f32[136,256]{1,0:T(8,128)S(1)}, f32[136,256]{1,0:T(8,128)S(1)}, u32[]{:S(2)}, u32[]{:S(2)}) collective-permute-start(f32[136,256]{1,0:T(8,128)S(1)} %add.34), channel_id=1, source_target_pairs={{0,16},{1,65},{2,18},{3,67},{4,20},{5,69},{6,22},{7,71},{8,24},{9,... | collective-permute-start | bytes 417800 | tf_op jit(solution)/shard_map/ppermute | solution.py:30
  117.5 11.9 %collective-permute-done.22.refs_6_ = bf16[2048,128]{1,0:T(8,128)(2,1)S(1)} collective-permute-done((bf16[2048,128]{1,0:T(8,128)(2,1)S(1)}, bf16[2048,128]{1,0:T(8,128)(2,1)S(1)}, u32[]{:S(2)}, u32[]{:S(2)}) %collective-permute-start.22) | collective-permute-done | bytes 524320 | tf_op jit(solution)/shard_map/ppermute | solution.py:43
  135.6 6.2 %shard_map.114 = (bf16[8192,128]{1,0:T(8,128)(2,1)}, bf16[3328,128]{1,0:T(8,128)(2,1)}, bf16[3328,128]{1,0:T(8,128)(2,1)}, bf16[3328,128]{1,0:T(8,128)(2,1)}) custom-call(s32[1]{0:T(128)} %bitcast.10.live, s32[8,64]{1,0:T(8,128)S(1)} %get-tuple-element.161.tables, bf16[64,128,128]{2,1,0:T(8,128)(2,1)S(1)} %bitcast.13, ...), custom_call_target="tpu_custom_call" | custom-call | tf_op jit(solution)/shard_map/pallas_call | solution.py:208
  141.8 4.8 %collective-permute-start.33 = (bf16[3328,128]{1,0:T(8,128)(2,1)}, bf16[3328,128]{1,0:T(8,128)(2,1)S(1)}, u32[]{:S(2)}, u32[]{:S(2)}) collective-permute-start(bf16[3328,128]{1,0:T(8,128)(2,1)} %get-tuple-element.170), channel_id=1, source_target_pairs={{0,24},{1,97},{2,26},{3,99},{4,28},{5,101},{6,30},{7,103},{8,0},{9... | collective-permute-start | bytes 2555912 | tf_op jit(solution)/shard_map/ppermute | solution.py:30
  150.6 3.7 %collective-permute-done.31 = f32[136,256]{1,0:T(8,128)S(1)} collective-permute-done((f32[136,256]{1,0:T(8,128)S(1)}, f32[136,256]{1,0:T(8,128)S(1)}, u32[]{:S(2)}, u32[]{:S(2)}) %collective-permute-start.31) | collective-permute-done | bytes 139296 | tf_op jit(solution)/shard_map/ppermute | solution.py:43
  157.3 8.9 %collective-permute-done.33 = bf16[3328,128]{1,0:T(8,128)(2,1)S(1)} collective-permute-done((bf16[3328,128]{1,0:T(8,128)(2,1)}, bf16[3328,128]{1,0:T(8,128)(2,1)S(1)}, u32[]{:S(2)}, u32[]{:S(2)}) %collective-permute-start.33) | collective-permute-done | bytes 852000 | tf_op jit(solution)/shard_map/ppermute | solution.py:30
  166.3 3.6 %collective-permute-done.35 = bf16[3328,128]{1,0:T(8,128)(2,1)S(1)} collective-permute-done((bf16[3328,128]{1,0:T(8,128)(2,1)}, bf16[3328,128]{1,0:T(8,128)(2,1)S(1)}, u32[]{:S(2)}, u32[]{:S(2)}) %collective-permute-start.35) | collective-permute-done | bytes 852000 | tf_op jit(solution)/shard_map/ppermute | solution.py:30
  169.8 5.2 %conditional.10 = ((f32[2048,128]{1,0:T(8,128)S(1)}, bf16[2320,128]{1,0:T(8,128)(2,1)}, bf16[2320,128]{1,0:T(8,128)(2,1)}, bf16[2320,128]{1,0:T(8,128)(2,1)})) conditional(s32[]{:T(128)} %bitcast.5, (s32[78]{0:T(128)S(1)}, s32[3]{0:T(128)S(1)}, bf16[8192,128]{1,0:T(8,128)(2,1)}, bf16[272,128]{1,0:T(8,128)(2,1)S(1)}, bf16[3328,128]{1,0:T(8,128)(2,1)S(1)}, ...), branch_computations={%region_2.0_spmd, %region_3.0_spmd} | conditional | flops 11358208 | bytes 48513184 | solution.py:447
  170.7 4.3 %branch_0_fun.3 = (f32[2048,128]{1,0:T(8,128)S(1)}, bf16[2320,128]{1,0:T(8,128)(2,1)}, bf16[2320,128]{1,0:T(8,128)(2,1)}, bf16[2320,128]{1,0:T(8,128)(2,1)}) custom-call(s32[78]{0:T(128)S(1)} %get-tuple-element.105.lists, s32[3]{0:T(128)S(1)} %get-tuple-element.106.counts, bf16[8192,128]{1,0:T(8,128)(2,1)} %get-tuple-element.107.own, ...), custom_call_target="tpu_custom_call" | custom-call | tf_op jit(solution)/shard_map/cond/branch_0_fun/pallas_call | solution.py:304
  177.5 3.1 %collective-permute-start.37 = (bf16[2320,128]{1,0:T(8,128)(2,1)}, bf16[2320,128]{1,0:T(8,128)(2,1)S(1)}, u32[]{:S(2)}, u32[]{:S(2)}) collective-permute-start(bf16[2320,128]{1,0:T(8,128)(2,1)} %get-tuple-element.175), channel_id=1, source_target_pairs={{0,64},{1,17},{2,66},{3,19},{4,68},{5,21},{6,70},{7,23},{8,72},{9,... | collective-permute-start | bytes 1781768 | tf_op jit(solution)/shard_map/ppermute | solution.py:30
  182.0 3.9 %collective-permute-done.36.refs_1_ = bf16[2320,128]{1,0:T(8,128)(2,1)S(1)} collective-permute-done((bf16[2320,128]{1,0:T(8,128)(2,1)}, bf16[2320,128]{1,0:T(8,128)(2,1)S(1)}, u32[]{:S(2)}, u32[]{:S(2)}) %collective-permute-start.36) | collective-permute-done | bytes 593952 | tf_op jit(solution)/shard_map/ppermute | solution.py:30
  185.9 3.3 %collective-permute-done.37.refs_2_ = bf16[2320,128]{1,0:T(8,128)(2,1)S(1)} collective-permute-done((bf16[2320,128]{1,0:T(8,128)(2,1)}, bf16[2320,128]{1,0:T(8,128)(2,1)S(1)}, u32[]{:S(2)}, u32[]{:S(2)}) %collective-permute-start.37) | collective-permute-done | bytes 593952 | tf_op jit(solution)/shard_map/ppermute | solution.py:30
  189.3 6.3 %collective-permute-done.38.refs_3_ = bf16[2320,128]{1,0:T(8,128)(2,1)S(1)} collective-permute-done((bf16[2320,128]{1,0:T(8,128)(2,1)}, bf16[2320,128]{1,0:T(8,128)(2,1)S(1)}, u32[]{:S(2)}, u32[]{:S(2)}) %collective-permute-start.38) | collective-permute-done | bytes 593952 | tf_op jit(solution)/shard_map/ppermute | solution.py:30
  (84 shorter events, 61.3 us)
Async XLA Ops:
  3.8 15.6 %collective-permute-start.8 = (bf16[2064,128]{1,0:T(8,128)(2,1)S(1)}, bf16[2064,128]{1,0:T(8,128)(2,1)S(1)}, u32[]{:S(2)}, u32[]{:S(2)}) collective-permute-start(bf16[2064,128]{1,0:T(8,128)(2,1)S(1)} %get-tuple-element.156.refs_0_), channel_id=1, source_target_pairs={{0,32},{1,9},{2,34},{3,11},{4,36},{5,13},{6,38},{7,15},{8,40},{9,1... | collective-permute-start | bytes 1585160 | tf_op jit(solution)/shard_map/ppermute | solution.py:30
  5.4 15.7 %collective-permute-start.7 = (bf16[2064,128]{1,0:T(8,128)(2,1)S(1)}, bf16[2064,128]{1,0:T(8,128)(2,1)S(1)}, u32[]{:S(2)}, u32[]{:S(2)}) collective-permute-start(bf16[2064,128]{1,0:T(8,128)(2,1)S(1)} %get-tuple-element.156.refs_0_), channel_id=1, source_target_pairs={{0,64},{1,17},{2,66},{3,19},{4,68},{5,21},{6,70},{7,23},{8,72},{9,... | collective-permute-start | bytes 1585160 | tf_op jit(solution)/shard_map/ppermute | solution.py:30
  8.1 13.0 %collective-permute-start.6 = (bf16[2064,128]{1,0:T(8,128)(2,1)S(1)}, bf16[2064,128]{1,0:T(8,128)(2,1)S(1)}, u32[]{:S(2)}, u32[]{:S(2)}) collective-permute-start(bf16[2064,128]{1,0:T(8,128)(2,1)S(1)} %get-tuple-element.156.refs_0_), channel_id=1, source_target_pairs={{0,96},{1,25},{2,98},{3,27},{4,100},{5,29},{6,102},{7,31},{8,104},... | collective-permute-start | bytes 1585160 | tf_op jit(solution)/shard_map/ppermute | solution.py:30
  24.7 23.8 %collective-permute-start.12 = (bf16[3344,128]{1,0:T(8,128)(2,1)}, bf16[3344,128]{1,0:T(8,128)(2,1)S(1)}, u32[]{:S(2)}, u32[]{:S(2)}) collective-permute-start(bf16[3344,128]{1,0:T(8,128)(2,1)} %get-tuple-element.159), channel_id=1, source_target_pairs={{0,24},{1,97},{2,26},{3,99},{4,28},{5,101},{6,30},{7,103},{8,0},{9... | collective-permute-start | bytes 2568200 | tf_op jit(solution)/shard_map/ppermute | solution.py:30
  28.7 21.6 %collective-permute-start.13 = (bf16[3344,128]{1,0:T(8,128)(2,1)}, bf16[3344,128]{1,0:T(8,128)(2,1)S(1)}, u32[]{:S(2)}, u32[]{:S(2)}) collective-permute-start(bf16[3344,128]{1,0:T(8,128)(2,1)} %get-tuple-element.160), channel_id=1, source_target_pairs={{0,16},{1,65},{2,18},{3,67},{4,20},{5,69},{6,22},{7,71},{8,24},{9,... | collective-permute-start | bytes 2568200 | tf_op jit(solution)/shard_map/ppermute | solution.py:30
  29.5 22.8 %collective-permute-start.14 = (bf16[3344,128]{1,0:T(8,128)(2,1)}, bf16[3344,128]{1,0:T(8,128)(2,1)S(1)}, u32[]{:S(2)}, u32[]{:S(2)}) collective-permute-start(bf16[3344,128]{1,0:T(8,128)(2,1)} %get-tuple-element.158), channel_id=1, source_target_pairs={{0,8},{1,33},{2,10},{3,35},{4,12},{5,37},{6,14},{7,39},{8,16},{9,4... | collective-permute-start | bytes 2568200 | tf_op jit(solution)/shard_map/ppermute | solution.py:30
  67.7 16.3 %collective-permute-start.18 = (bf16[2048,128]{1,0:T(8,128)(2,1)S(1)}, bf16[2048,128]{1,0:T(8,128)(2,1)S(1)}, u32[]{:S(2)}, u32[]{:S(2)}) collective-permute-start(bf16[2048,128]{1,0:T(8,128)(2,1)S(1)} %get-tuple-element.198), channel_id=1, source_target_pairs={{0,2},{1,3},{2,4},{3,5},{4,6},{5,7},{6,0},{7,1},{8,10},{9,11},{10,... | collective-permute-start | bytes 1572872 | tf_op jit(solution)/shard_map/ppermute | solution.py:43
  70.5 26.0 %collective-permute-start.17 = (bf16[2048,128]{1,0:T(8,128)(2,1)S(1)}, bf16[2048,128]{1,0:T(8,128)(2,1)S(1)}, u32[]{:S(2)}, u32[]{:S(2)}) collective-permute-start(bf16[2048,128]{1,0:T(8,128)(2,1)S(1)} %get-tuple-element.199), channel_id=1, source_target_pairs={{0,4},{1,5},{2,6},{3,7},{4,0},{5,1},{6,2},{7,3},{8,12},{9,13},{10,... | collective-permute-start | bytes 1572872 | tf_op jit(solution)/shard_map/ppermute | solution.py:43
  73.3 23.2 %collective-permute-start.16 = (bf16[2048,128]{1,0:T(8,128)(2,1)S(1)}, bf16[2048,128]{1,0:T(8,128)(2,1)S(1)}, u32[]{:S(2)}, u32[]{:S(2)}) collective-permute-start(bf16[2048,128]{1,0:T(8,128)(2,1)S(1)} %get-tuple-element.200), channel_id=1, source_target_pairs={{0,6},{1,7},{2,0},{3,1},{4,2},{5,3},{6,4},{7,5},{8,14},{9,15},{10,... | collective-permute-start | bytes 1572872 | tf_op jit(solution)/shard_map/ppermute | solution.py:43
  103.0 14.5 %collective-permute-start.24 = (bf16[2048,128]{1,0:T(8,128)(2,1)S(1)}, bf16[2048,128]{1,0:T(8,128)(2,1)S(1)}, u32[]{:S(2)}, u32[]{:S(2)}) collective-permute-start(bf16[2048,128]{1,0:T(8,128)(2,1)S(1)} %get-tuple-element.167.refs_4_), channel_id=1, source_target_pairs={{0,2},{1,3},{2,4},{3,5},{4,6},{5,7},{6,0},{7,1},{8,10},{9,11},{10,... | collective-permute-start | bytes 1572872 | tf_op jit(solution)/shard_map/ppermute | solution.py:43
  103.5 25.9 %collective-permute-start.22 = (bf16[2048,128]{1,0:T(8,128)(2,1)S(1)}, bf16[2048,128]{1,0:T(8,128)(2,1)S(1)}, u32[]{:S(2)}, u32[]{:S(2)}) collective-permute-start(bf16[2048,128]{1,0:T(8,128)(2,1)S(1)} %get-tuple-element.167.refs_4_), channel_id=1, source_target_pairs={{0,4},{1,5},{2,6},{3,7},{4,0},{5,1},{6,2},{7,3},{8,12},{9,13},{10,... | collective-permute-start | bytes 1572872 | tf_op jit(solution)/shard_map/ppermute | solution.py:43
  106.3 23.1 %collective-permute-start.20 = (bf16[2048,128]{1,0:T(8,128)(2,1)S(1)}, bf16[2048,128]{1,0:T(8,128)(2,1)S(1)}, u32[]{:S(2)}, u32[]{:S(2)}) collective-permute-start(bf16[2048,128]{1,0:T(8,128)(2,1)S(1)} %get-tuple-element.167.refs_4_), channel_id=1, source_target_pairs={{0,6},{1,7},{2,0},{3,1},{4,2},{5,3},{6,4},{7,5},{8,14},{9,15},{10,... | collective-permute-start | bytes 1572872 | tf_op jit(solution)/shard_map/ppermute | solution.py:43
  109.8 20.1 %collective-permute-start.28 = (f32[136,256]{1,0:T(8,128)S(1)}, f32[136,256]{1,0:T(8,128)S(1)}, u32[]{:S(2)}, u32[]{:S(2)}) collective-permute-start(f32[136,256]{1,0:T(8,128)S(1)} %add.34), channel_id=1, source_target_pairs={{0,16},{1,65},{2,18},{3,67},{4,20},{5,69},{6,22},{7,71},{8,24},{9,... | collective-permute-start | bytes 417800 | tf_op jit(solution)/shard_map/ppermute | solution.py:30
  115.6 19.9 %collective-permute-start.19 = (bf16[2048,128]{1,0:T(8,128)(2,1)S(1)}, bf16[2048,128]{1,0:T(8,128)(2,1)S(1)}, u32[]{:S(2)}, u32[]{:S(2)}) collective-permute-start(bf16[2048,128]{1,0:T(8,128)(2,1)S(1)} %get-tuple-element.167.refs_4_), channel_id=1, source_target_pairs={{0,1},{1,0},{2,3},{3,2},{4,5},{5,4},{6,7},{7,6},{8,9},{9,8},{10,11... | collective-permute-start | bytes 1572872 | tf_op jit(solution)/shard_map/ppermute | solution.py:48
  117.5 18.1 %collective-permute-start.25 = (bf16[2048,128]{1,0:T(8,128)(2,1)S(1)}, bf16[2048,128]{1,0:T(8,128)(2,1)S(1)}, u32[]{:S(2)}, u32[]{:S(2)}) collective-permute-start(bf16[2048,128]{1,0:T(8,128)(2,1)S(1)} %collective-permute-done.24.refs_7_), channel_id=1, source_target_pairs={{0,1},{1,0},{2,3},{3,2},{4,5},{5,4},{6,7},{7,6},{8,9},{9,8},{10,11... | collective-permute-start | bytes 1572872 | tf_op jit(solution)/shard_map/ppermute | solution.py:48
  135.1 13.9 %collective-permute-start.32 = (f32[136,256]{1,0:T(8,128)S(1)}, f32[136,256]{1,0:T(8,128)S(1)}, u32[]{:S(2)}, u32[]{:S(2)}) collective-permute-start(f32[136,256]{1,0:T(8,128)S(1)} %add_add_fusion.1), channel_id=1, source_target_pairs={{0,2},{1,3},{2,4},{3,5},{4,6},{5,7},{6,0},{7,1},{8,10},{9,11},{10,... | collective-permute-start | bytes 417800 | tf_op jit(solution)/shard_map/ppermute | solution.py:43
  141.8 24.4 %collective-permute-start.33 = (bf16[3328,128]{1,0:T(8,128)(2,1)}, bf16[3328,128]{1,0:T(8,128)(2,1)S(1)}, u32[]{:S(2)}, u32[]{:S(2)}) collective-permute-start(bf16[3328,128]{1,0:T(8,128)(2,1)} %get-tuple-element.170), channel_id=1, source_target_pairs={{0,24},{1,97},{2,26},{3,99},{4,28},{5,101},{6,30},{7,103},{8,0},{9... | collective-permute-start | bytes 2555912 | tf_op jit(solution)/shard_map/ppermute | solution.py:30
  146.6 19.7 %collective-permute-start.34 = (bf16[3328,128]{1,0:T(8,128)(2,1)}, bf16[3328,128]{1,0:T(8,128)(2,1)S(1)}, u32[]{:S(2)}, u32[]{:S(2)}) collective-permute-start(bf16[3328,128]{1,0:T(8,128)(2,1)} %get-tuple-element.171), channel_id=1, source_target_pairs={{0,16},{1,65},{2,18},{3,67},{4,20},{5,69},{6,22},{7,71},{8,24},{9,... | collective-permute-start | bytes 2555912 | tf_op jit(solution)/shard_map/ppermute | solution.py:30
  146.6 23.2 %collective-permute-start.35 = (bf16[3328,128]{1,0:T(8,128)(2,1)}, bf16[3328,128]{1,0:T(8,128)(2,1)S(1)}, u32[]{:S(2)}, u32[]{:S(2)}) collective-permute-start(bf16[3328,128]{1,0:T(8,128)(2,1)} %get-tuple-element.172), channel_id=1, source_target_pairs={{0,8},{1,33},{2,10},{3,35},{4,12},{5,37},{6,14},{7,39},{8,16},{9,4... | collective-permute-start | bytes 2555912 | tf_op jit(solution)/shard_map/ppermute | solution.py:30
  147.5 6.7 %collective-permute-start.31 = (f32[136,256]{1,0:T(8,128)S(1)}, f32[136,256]{1,0:T(8,128)S(1)}, u32[]{:S(2)}, u32[]{:S(2)}) collective-permute-start(f32[136,256]{1,0:T(8,128)S(1)} %add_add_fusion.1), channel_id=1, source_target_pairs={{0,4},{1,5},{2,6},{3,7},{4,0},{5,1},{6,2},{7,3},{8,12},{9,13},{10,... | collective-permute-start | bytes 417800 | tf_op jit(solution)/shard_map/ppermute | solution.py:43
  148.9 7.7 %collective-permute-start.30 = (f32[136,256]{1,0:T(8,128)S(1)}, f32[136,256]{1,0:T(8,128)S(1)}, u32[]{:S(2)}, u32[]{:S(2)}) collective-permute-start(f32[136,256]{1,0:T(8,128)S(1)} %add_add_fusion.1), channel_id=1, source_target_pairs={{0,6},{1,7},{2,0},{3,1},{4,2},{5,3},{6,4},{7,5},{8,14},{9,15},{10,... | collective-permute-start | bytes 417800 | tf_op jit(solution)/shard_map/ppermute | solution.py:43
  175.1 10.8 %collective-permute-start.36 = (bf16[2320,128]{1,0:T(8,128)(2,1)}, bf16[2320,128]{1,0:T(8,128)(2,1)S(1)}, u32[]{:S(2)}, u32[]{:S(2)}) collective-permute-start(bf16[2320,128]{1,0:T(8,128)(2,1)} %get-tuple-element.174), channel_id=1, source_target_pairs={{0,96},{1,25},{2,98},{3,27},{4,100},{5,29},{6,102},{7,31},{8,104},... | collective-permute-start | bytes 1781768 | tf_op jit(solution)/shard_map/ppermute | solution.py:30
  177.5 11.7 %collective-permute-start.37 = (bf16[2320,128]{1,0:T(8,128)(2,1)}, bf16[2320,128]{1,0:T(8,128)(2,1)S(1)}, u32[]{:S(2)}, u32[]{:S(2)}) collective-permute-start(bf16[2320,128]{1,0:T(8,128)(2,1)} %get-tuple-element.175), channel_id=1, source_target_pairs={{0,64},{1,17},{2,66},{3,19},{4,68},{5,21},{6,70},{7,23},{8,72},{9,... | collective-permute-start | bytes 1781768 | tf_op jit(solution)/shard_map/ppermute | solution.py:30
  180.6 15.0 %collective-permute-start.38 = (bf16[2320,128]{1,0:T(8,128)(2,1)}, bf16[2320,128]{1,0:T(8,128)(2,1)S(1)}, u32[]{:S(2)}, u32[]{:S(2)}) collective-permute-start(bf16[2320,128]{1,0:T(8,128)(2,1)} %get-tuple-element.176), channel_id=1, source_target_pairs={{0,32},{1,9},{2,34},{3,11},{4,36},{5,13},{6,38},{7,15},{8,40},{9,1... | collective-permute-start | bytes 1781768 | tf_op jit(solution)/shard_map/ppermute | solution.py:30
  (20 other events, 141.3 us)

commit v4 on v3

--- a/solution.py
+++ b/solution.py
@@ -86,7 +86,7 @@
     slots = cols.shape[1]
 
     same_core = jnp.where(((rows >> 4) & 1) == core, 64, 0)
-    row_place = same_core + (((rows >> 5) - y) & 3) * 16 + (rows & 15)
+    row_place = same_core + ((rows >> 3) & 1) * 32 + (((rows >> 5) - y) & 3) * 8 + (rows & 7)
     dx, dz = ((cols >> 6) - x) & 3, ((cols >> 4) - z) & 3
     outer, inner = jnp.where(core == 0, dz, dx), jnp.where(core == 0, dx, dz)
     code = inner * 16 + (cols & 15)
@@ -147,6 +147,9 @@
 def products_kernel(live, tables, tiles_ref, *refs, spans, outs, contract, in_row, out_row):
     n = len(spans)
     sources, out_refs, (tiles, held, total, sems) = refs[:n], refs[n:-4], refs[-4:]
+    if len(out_refs) > len(outs):
+        out_refs[-1][...] = out_refs[0][...]
+        out_refs = out_refs[1:-1]
     copies = [pltpu.make_async_copy(tiles_ref, tiles, sems.at[n])]
     start = 0
     for k, (ref, rows) in enumerate(zip(sources, spans)):
@@ -196,7 +199,7 @@
         start += blocks
 
 
-def products(live, tables, in_row, out_row, tiles, sources, spans, outs, contract):
+def products(live, tables, in_row, out_row, tiles, sources, spans, outs, contract, passed=()):
     kernel = functools.partial(
         products_kernel,
         spans=spans,
@@ -207,9 +210,10 @@
     )
     return pl.pallas_call(
         kernel,
-        out_shape=[jax.ShapeDtypeStruct((n * T, T), BF16) for n in outs],
-        in_specs=[SMEM] * 2 + [ANY] * (1 + len(sources)),
-        out_specs=[VMEM] * len(outs),
+        out_shape=[jax.ShapeDtypeStruct((n * T, T), BF16) for n in outs]
+        + [jax.ShapeDtypeStruct(p.shape, p.dtype) for p in passed],
+        in_specs=[SMEM] * 2 + [ANY] * (1 + len(sources)) + [VMEM] * len(passed),
+        out_specs=[VMEM] * (len(outs) + len(passed)),
         scratch_shapes=[
             pltpu.VMEM(tiles.shape, BF16),
             pltpu.VMEM((sum(spans), T), BF16),
@@ -217,7 +221,7 @@
             pltpu.SemaphoreType.DMA((len(spans) + 1,)),
         ],
         compiler_params=PARAMS,
-    )(live, tables, tiles, *sources)
+    )(live, tables, tiles, *sources, *passed)
 
 
 def pack_kernel(*refs):
@@ -273,6 +277,31 @@
     )(*pieces, *metas)
 
 
+def flag_kernel(*refs):
+    sources, out, held, sems = refs[:4], refs[4], refs[5], refs[6]
+    copies = [
+        pltpu.make_async_copy(ref.at[pl.ds(CAP * T, META)], held.at[k], sems.at[k])
+        for k, ref in enumerate(sources)
+    ]
+    for copy in copies:
+        copy.start()
+    for copy in copies:
+        copy.wait()
+    said = functools.reduce(jnp.maximum, [held[k].astype(F32) for k in range(4)])
+    out[0] = jnp.max(said[2:3]).astype(I32)
+
+
+def overflow(sources):
+    return pl.pallas_call(
+        flag_kernel,
+        out_shape=jax.ShapeDtypeStruct((1,), I32),
+        in_specs=[ANY] * 4,
+        out_specs=SMEM,
+        scratch_shapes=[pltpu.VMEM((4, META, T), BF16), pltpu.SemaphoreType.DMA((4,))],
+        compiler_params=PARAMS,
+    )(*sources)
+
+
 def combine_kernel(lists, counts, own, sums, *refs):
     parts, outs, (total,) = refs[:3], refs[3:7], refs[7:]
 
@@ -342,12 +371,14 @@
     )(*pieces, sums)
 
 
-def dense_kernel(m0, m1, m2, m3, grad, weight, offset, hidden, projected, sums):
+def dense_kernel(*refs):
+    parts, (grad, weight, offset), (hidden, projected, sums) = refs[:5], refs[5:8], refs[-3:]
+
     @pl.when(pl.program_id(0) == 0)
     def _():
-        sums[...] = jnp.zeros_like(sums)
-
-    mixed = m0[...].astype(F32) + m1[...].astype(F32) + m2[...].astype(F32) + m3[...].astype(F32)
+        sums[...] = refs[9][...] if len(refs) > 11 else jnp.zeros_like(sums)
+
+    mixed = total_of([ref[...] for ref in parts])
     high = mixed.astype(BF16)
     low = (mixed - high.astype(F32)).astype(BF16)
     w = weight[...]
@@ -366,28 +397,33 @@
     sums[T:] += jnp.sum(slope.astype(F32).reshape(-1, 8, slope.shape[1]), axis=0)
 
 
-def dense(parts, grad, weight, offset):
-    rows, width = parts[0].shape[0], weight.shape[1]
+def dense(parts, grad, weight, offset, part, before):
+    width, rows = weight.shape[1], grad.shape[0]
     step = 512
+    steps = rows // 2 // step
+    shift = part * steps
     half = pl.BlockSpec((step, T), lambda i: (i, 0))
-    full = pl.BlockSpec((step, width), lambda i: (i, 0))
+    full = pl.BlockSpec((step, width), lambda i: (i + shift, 0))
+    whole = pl.BlockSpec((T + 8, width), lambda i: (0, 0))
     return pl.pallas_call(
         dense_kernel,
-        grid=(rows // step,),
+        grid=(steps,),
         out_shape=[
             jax.ShapeDtypeStruct((rows, width), BF16),
-            jax.ShapeDtypeStruct((rows, T), BF16),
+            jax.ShapeDtypeStruct((rows // 2, T), BF16),
             jax.ShapeDtypeStruct((T + 8, width), F32),
         ],
-        in_specs=[half] * 4
+        in_specs=[half] * 5
         + [
             full,
             pl.BlockSpec((T, width), lambda i: (0, 0)),
             pl.BlockSpec((1, width), lambda i: (0, 0)),
-        ],
-        out_specs=[full, half, pl.BlockSpec((T + 8, width), lambda i: (0, 0))],
-        compiler_params=PARAMS,
-    )(*parts, grad, weight, offset)
+        ]
+        + ([ANY, whole] + [ANY] * (len(before) - 2) if before else []),
+        out_specs=[full, half, whole],
+        input_output_aliases={8: 0} if before else {},
+        compiler_params=PARAMS,
+    )(*parts, grad, weight, offset, *before)
 
 
 def on_device(features, weight, offset, tile_values, tile_rows, tile_cols, live_tiles, grad_hidden):
@@ -404,35 +440,47 @@
     *sends, lists, counts = pack(pieces, ring_gather(meta, along_outer)[1:])
     named = ring_swap([None] + sends, along_outer)[1:]
     flags = [sends[0]] + named
-    full = functools.reduce(jnp.maximum, [f[CAP * T + 2, 0] for f in flags]) > 0.5
+    full = overflow(flags)[0] > 0
 
     def forward_all(pieces, named):
         whole = jnp.concatenate([p[:nodes_here] for p in pieces])
         whole = ring_gather(whole, along_outer)
         spans = (4 * nodes_here,) * 4
-        return products(live, tables, 2, 0, tiles, whole, spans, (64, 64), (1,))
+        return products(live, tables, 2, 0, tiles, whole, spans, (32,) * 4, (1,))
 
     def forward_named(pieces, named):
         spans = (nodes_here,) * 4 + (CAP * T,) * 3
-        return products(live, tables, 1, 0, tiles, pieces + named, spans, (64, 64), (1,))
-
-    send, keep = lax.cond(full, forward_all, forward_named, pieces, named)
-
-    both = keep.astype(F32) + other_core(send).astype(F32)
-    both = both.reshape(4, nodes_here, T)
-    mixed_parts = ring_swap([both[d].astype(BF16) for d in range(4)], along_y)
-    hidden, projected, sums = dense(mixed_parts, grad_hidden, weight, offset.reshape(1, -1))
-
-    own = ring_gather(projected, along_y)
-    gathered = [other_core(piece) for piece in own] + own
-
-    sums = sums + other_core(sums)
-    for along in (along_outer, along_y):
-        sums = total_of(ring_gather(sums, along))
+        return products(live, tables, 1, 0, tiles, pieces + named, spans, (32,) * 4, (1,))
+
+    outs = lax.cond(full, forward_all, forward_named, pieces, named)
+
+    part_rows = nodes_here // 2
+    halves = []
+    for send, keep in zip(outs[:2], outs[2:]):
+        got = other_core(send)
+        far = []
+        for d in (1, 2, 3):
+            at = slice(d * part_rows, (d + 1) * part_rows)
+            far.append((keep[at].astype(F32) + got[at].astype(F32)).astype(BF16))
+        halves.append([keep, got] + ring_swap([None] + far, along_y)[1:])
+    before, own, others = (), [], []
+    for part, parts in enumerate(halves):
+        hidden, projected, sums = dense(
+            parts, grad_hidden, weight, offset.reshape(1, -1), part, before
+        )
+        here = ring_gather(projected, along_y)
+        before = (hidden, sums, *here[1:])
+        own += here
+        others += [other_core(piece) for piece in here]
+
+    sums = total_of(ring_gather(sums + other_core(sums), along_outer))
+
+    gathered, spans, outs = others + own, (part_rows,) * 16, (64,) + (CAP,) * 3
+    here, *parts, sums = products(
+        live, tables, 0, 1, tiles, gathered, spans, outs, (0,), (sums,)
+    )
+    sums = total_of(ring_gather(sums, along_y))
     rounded = jnp.concatenate([sums[:, :T], sums[:, T:]]).astype(BF16)
-
-    spans, outs = (nodes_here,) * 8, (64,) + (CAP,) * 3
-    here, *parts = products(live, tables, 0, 1, tiles, gathered, spans, outs, (0,))
     parts = ring_swap([None] + parts, along_outer)[1:]
 
     def backward_all(here, rounded, parts, gathered):

time: 201 us -> 193 us (0.960)
  Pallas kernels: 31.2 us -> 37.8 us
  waiting for transfers between devices: 101 us -> 95 us
  starting transfers between devices: 52.2 us -> 48.9 us
  local copies, waits for them, and re-layouts: 6.44 us -> 4.36 us
  between operations: 4.21 us -> 2.16 us
    ppermute x18, starting transfers between devices: 38.7 us -> 29.7 us  [along_xz(): return lax.ppermute(value, ('row', 'col'), pairs)]
    ppermute x9 -> x15, starting transfers between devices: 12.9 us -> 16.9 us  [along_y(): return lax.ppermute(value, 'col', pairs)]
    slice x5 -> x0, local copies, waits for them, and re-layouts: 3.7 us -> none  [the longest x4 2.77 us: on_device(): f[CAP * T + 2, 0]]
    pallas_call x2, Pallas kernels: 12.9 us -> 16 us  [products(): pl.pallas_call(kernel, out_shape=[jax.ShapeDtypeStruct((n * T, T), BF16)...]
    pallas_call x1 -> x3, Pallas kernels: 5.48 us -> 8.49 us  [the longest x2 7.12 us: dense(): pl.pallas_call(dense_kernel, grid=(steps,), out_shape=[jax.ShapeDtypeStru...]
    ppermute x9 -> x15, waiting for transfers between devices: 42.9 us -> 40.5 us  [along_y(): return lax.ppermute(value, 'col', pairs)]
    ppermute x6 -> x11, waiting for transfers between devices: 5.94 us -> 3.59 us  [other_core(): return lax.ppermute(value, 'col', pairs)]
  transfers between devices with their start and end apart: 33 -> 44, of which waited for: 20 -> 26; matrix products, arithmetic and copies ran while one was open for 2% -> 2% of each run, Pallas kernels for 3% -> 4%
where the time goes in v4:
time: 193 us; the launch traced here: 192 us
  waiting for transfers between devices  95 us (49%)
  starting transfers between devices  48.9 us (25%)
  Pallas kernels  37.8 us (20%)
  local copies, waits for them, and re-layouts  4.36 us (2%)
  other arithmetic  3.65 us (2%)
  between operations  2.16 us (1%)
    ppermute x18, waiting for transfers between devices, along_xz(): return lax.ppermute(value, ('row', 'col'), pairs)  50.9 us
    ppermute x15, waiting for transfers between devices, along_y(): return lax.ppermute(value, 'col', pairs)  40.5 us
    ppermute x18, starting transfers between devices, along_xz(): return lax.ppermute(value, ('row', 'col'), pairs)  29.7 us
    ppermute x15, starting transfers between devices, along_y(): return lax.ppermute(value, 'col', pairs)  16.9 us
    pallas_call x2, Pallas kernels, products(): pl.pallas_call(kernel, out_shape=[jax.ShapeDtypeStruct((n * T, T), BF16)...  16 us
    pallas_call x2, Pallas kernels, dense(): pl.pallas_call(dense_kernel, grid=(steps,), out_shape=[jax.ShapeDtypeStru...  7.12 us
    pallas_call x1, Pallas kernels, combine(): pl.pallas_call(combine_kernel, out_shape=[jax.ShapeDtypeStruct((rows, T),...  4.54 us
  transfers between devices with their start and end apart: 44, of which 26 were waited for; matrix products, arithmetic and copies ran while one was open for 2% of the time, Pallas kernels for 4%

profile of v4, /device:TPU:0, one launch (start us, length us, event | category | flops | bytes accessed | tf_op | source)
XLA Modules:
  0.0 191.9 jit_solution(774184026197381718)
XLA Ops:
  11.3 3.6 %collective-permute-start.10 = (bf16[16,128]{1,0:T(8,128)(2,1)}, bf16[16,128]{1,0:T(8,128)(2,1)S(1)}, u32[]{:S(2)}, u32[]{:S(2)}) collective-permute-start(bf16[16,128]{1,0:T(8,128)(2,1)} %get-tuple-element.171), channel_id=1, source_target_pairs={{0,16},{1,65},{2,18},{3,67},{4,20},{5,69},{6,22},{7,71},{8,24},{9,... | collective-permute-start | bytes 12296 | tf_op jit(solution)/shard_map/ppermute | solution.py:30
  20.9 3.5 %shard_map.112 = (bf16[3344,128]{1,0:T(8,128)(2,1)}, bf16[3344,128]{1,0:T(8,128)(2,1)}, bf16[3344,128]{1,0:T(8,128)(2,1)}, s32[78]{0:T(128)S(1)}, s32[3]{0:T(128)S(1)}) custom-call(bf16[2064,128]{1,0:T(8,128)(2,1)S(1)} %get-tuple-element.170.refs_0_, bf16[2064,128]{1,0:T(8,128)(2,1)S(1)} %collective-permute-done.6.refs_1_, ...), custom_call_target="tpu_custom_call" | custom-call | tf_op jit(solution)/shard_map/pallas_call | solution.py:264
  24.4 4.1 %collective-permute-start.12 = (bf16[3344,128]{1,0:T(8,128)(2,1)}, bf16[3344,128]{1,0:T(8,128)(2,1)S(1)}, u32[]{:S(2)}, u32[]{:S(2)}) collective-permute-start(bf16[3344,128]{1,0:T(8,128)(2,1)} %get-tuple-element.173), channel_id=1, source_target_pairs={{0,24},{1,97},{2,26},{3,99},{4,28},{5,101},{6,30},{7,103},{8,0},{9... | collective-permute-start | bytes 2568200 | tf_op jit(solution)/shard_map/ppermute | solution.py:30
  30.7 17.6 %collective-permute-done.12.refs_1_ = bf16[3344,128]{1,0:T(8,128)(2,1)S(1)} collective-permute-done((bf16[3344,128]{1,0:T(8,128)(2,1)}, bf16[3344,128]{1,0:T(8,128)(2,1)S(1)}, u32[]{:S(2)}, u32[]{:S(2)}) %collective-permute-start.12) | collective-permute-done | bytes 856096 | tf_op jit(solution)/shard_map/ppermute | solution.py:30
  48.3 3.9 %collective-permute-done.14.refs_3_ = bf16[3344,128]{1,0:T(8,128)(2,1)S(1)} collective-permute-done((bf16[3344,128]{1,0:T(8,128)(2,1)}, bf16[3344,128]{1,0:T(8,128)(2,1)S(1)}, u32[]{:S(2)}, u32[]{:S(2)}) %collective-permute-start.14) | collective-permute-done | bytes 856096 | tf_op jit(solution)/shard_map/ppermute | solution.py:30
  54.2 8.0 %conditional.2 = ((bf16[4096,128]{1,0:T(8,128)(2,1)}, bf16[4096,128]{1,0:T(8,128)(2,1)}, bf16[4096,128]{1,0:T(8,128)(2,1)S(1)}, bf16[4096,128]{1,0:T(8,128)(2,1)})) conditional(s32[]{:T(128)} %bitcast.5, (s32[1]{0:T(128)}, s32[8,64]{1,0:T(8,128)S(1)}, bf16[64,128,128]{2,1,0:T(8,128)(2,1)S(1)}, bf16[2064,128]{1,0:T(8,128)(2,1)S(1)}, ...), branch_computations={%region_0.0_spmd, %region_1.0_spmd} | conditional | flops 8388608 | bytes 67109104 | solution.py:455
  54.2 8.0 %branch_0_fun.2 = (bf16[4096,128]{1,0:T(8,128)(2,1)}, bf16[4096,128]{1,0:T(8,128)(2,1)}, bf16[4096,128]{1,0:T(8,128)(2,1)S(1)}, bf16[4096,128]{1,0:T(8,128)(2,1)}) custom-call(s32[1]{0:T(128)} %get-tuple-element.88.live, s32[8,64]{1,0:T(8,128)S(1)} %get-tuple-element.89.tables, bf16[64,128,128]{2,1,0:T(8,128)(2,1)S(1)} %get-tuple-element.90.tiles_ref, ...), custom_call_target="tpu_custom_call" | custom-call | tf_op jit(solution)/shard_map/cond/branch_0_fun/pallas_call | solution.py:211
  65.5 3.4 %collective-permute-start.21 = (bf16[1024,128]{1,0:T(8,128)(2,1)S(1)}, bf16[1024,128]{1,0:T(8,128)(2,1)S(1)}, u32[]{:S(2)}, u32[]{:S(2)}) collective-permute-start(bf16[1024,128]{1,0:T(8,128)(2,1)S(1)} %get-tuple-element.211), channel_id=1, source_target_pairs={{0,4},{1,5},{2,6},{3,7},{4,0},{5,1},{6,2},{7,3},{8,12},{9,13},{10,... | collective-permute-start | bytes 786440 | tf_op jit(solution)/shard_map/ppermute | solution.py:43
  72.0 9.2 %collective-permute-done.22.refs_4_ = bf16[1024,128]{1,0:T(8,128)(2,1)S(1)} collective-permute-done((bf16[1024,128]{1,0:T(8,128)(2,1)S(1)}, bf16[1024,128]{1,0:T(8,128)(2,1)S(1)}, u32[]{:S(2)}, u32[]{:S(2)}) %collective-permute-start.22) | collective-permute-done | bytes 262176 | tf_op jit(solution)/shard_map/ppermute | solution.py:43
  83.1 3.5 %shard_map.114 = (bf16[2048,256]{1,0:T(8,128)(2,1)}, bf16[1024,128]{1,0:T(8,128)(2,1)S(1)}, f32[136,256]{1,0:T(8,128)}) custom-call(bf16[4096,128]{1,0:T(8,128)(2,1)S(1)} %get-tuple-element.178.refs_0_, bf16[4096,128]{1,0:T(8,128)(2,1)} %copy-done.3, bf16[1024,128]{1,0:T(8,128)(2,1)} %copy-done.20, bf16[1024,128]{1,0:T(8,128)(2,1)} %copy-done.19, ...), custom_call_target="tpu_custom_call" | custom-call | tf_op jit(solution)/shard_map/pallas_call | solution.py:408
  87.6 3.3 %collective-permute-start.24 = (bf16[1024,128]{1,0:T(8,128)(2,1)S(1)}, bf16[1024,128]{1,0:T(8,128)(2,1)S(1)}, u32[]{:S(2)}, u32[]{:S(2)}) collective-permute-start(bf16[1024,128]{1,0:T(8,128)(2,1)S(1)} %get-tuple-element.182.refs_8_), channel_id=1, source_target_pairs={{0,4},{1,5},{2,6},{3,7},{4,0},{5,1},{6,2},{7,3},{8,12},{9,13},{10,... | collective-permute-start | bytes 786440 | tf_op jit(solution)/shard_map/ppermute | solution.py:43
  93.6 4.9 %collective-permute-done.25.refs_12_.refs_11_ = bf16[1024,128]{1,0:T(8,128)(2,1)S(1)} collective-permute-done((bf16[1024,128]{1,0:T(8,128)(2,1)S(1)}, bf16[1024,128]{1,0:T(8,128)(2,1)S(1)}, u32[]{:S(2)}, u32[]{:S(2)}) %collective-permute-start.25) | collective-permute-done | bytes 262176 | tf_op jit(solution)/shard_map/ppermute | solution.py:43
  98.5 4.8 %collective-permute-done.24.refs_11_.refs_10_ = bf16[1024,128]{1,0:T(8,128)(2,1)S(1)} collective-permute-done((bf16[1024,128]{1,0:T(8,128)(2,1)S(1)}, bf16[1024,128]{1,0:T(8,128)(2,1)S(1)}, u32[]{:S(2)}, u32[]{:S(2)}) %collective-permute-start.24) | collective-permute-done | bytes 262176 | tf_op jit(solution)/shard_map/ppermute | solution.py:43
  103.8 3.6 %shard_map.115 = (bf16[2048,256]{1,0:T(8,128)(2,1)}, bf16[1024,128]{1,0:T(8,128)(2,1)S(1)}, f32[136,256]{1,0:T(8,128)}) custom-call(bf16[4096,128]{1,0:T(8,128)(2,1)S(1)} %copy-done.4, bf16[4096,128]{1,0:T(8,128)(2,1)} %copy-done.2, bf16[1024,128]{1,0:T(8,128)(2,1)} %copy-done.17, bf16[1024,128]{1,0:T(8,128)(2,1)} %copy-done.16, ...), custom_call_target="tpu_custom_call", output_to_operand_aliasing={{0}: (8, {})} | custom-call | tf_op jit(solution)/shard_map/pallas_call | solution.py:408
  108.5 3.6 %collective-permute-start.33 = (bf16[1024,128]{1,0:T(8,128)(2,1)S(1)}, bf16[1024,128]{1,0:T(8,128)(2,1)S(1)}, u32[]{:S(2)}, u32[]{:S(2)}) collective-permute-start(bf16[1024,128]{1,0:T(8,128)(2,1)S(1)} %get-tuple-element.186.refs_12_), channel_id=1, source_target_pairs={{0,4},{1,5},{2,6},{3,7},{4,0},{5,1},{6,2},{7,3},{8,12},{9,13},{10,... | collective-permute-start | bytes 786440 | tf_op jit(solution)/shard_map/ppermute | solution.py:43
  118.5 5.8 %collective-permute-done.33.refs_14_ = bf16[1024,128]{1,0:T(8,128)(2,1)S(1)} collective-permute-done((bf16[1024,128]{1,0:T(8,128)(2,1)S(1)}, bf16[1024,128]{1,0:T(8,128)(2,1)S(1)}, u32[]{:S(2)}, u32[]{:S(2)}) %collective-permute-start.33) | collective-permute-done | bytes 262176 | tf_op jit(solution)/shard_map/ppermute | solution.py:43
  128.0 8.1 %shard_map.116 = (bf16[8192,128]{1,0:T(8,128)(2,1)S(1)}, bf16[3328,128]{1,0:T(8,128)(2,1)}, bf16[3328,128]{1,0:T(8,128)(2,1)}, bf16[3328,128]{1,0:T(8,128)(2,1)}, f32[136,256]{1,0:T(8,128)}) custom-call(s32[1]{0:T(128)} %bitcast.10.live, s32[8,64]{1,0:T(8,128)S(1)} %get-tuple-element.175.tables, bf16[64,128,128]{2,1,0:T(8,128)(2,1)S(1)} %bitcast.13, ...), custom_call_target="tpu_custom_call" | custom-call | tf_op jit(solution)/shard_map/pallas_call | solution.py:211
  145.8 4.0 %collective-permute-done.41 = f32[136,256]{1,0:T(8,128)S(1)} collective-permute-done((f32[136,256]{1,0:T(8,128)}, f32[136,256]{1,0:T(8,128)S(1)}, u32[]{:S(2)}, u32[]{:S(2)}) %collective-permute-start.41) | collective-permute-done | bytes 139296 | tf_op jit(solution)/shard_map/ppermute | solution.py:43
  151.5 8.9 %collective-permute-done.46 = bf16[3328,128]{1,0:T(8,128)(2,1)S(1)} collective-permute-done((bf16[3328,128]{1,0:T(8,128)(2,1)}, bf16[3328,128]{1,0:T(8,128)(2,1)S(1)}, u32[]{:S(2)}, u32[]{:S(2)}) %collective-permute-start.46) | collective-permute-done | bytes 852000 | tf_op jit(solution)/shard_map/ppermute | solution.py:30
  160.4 6.6 %conditional.3 = ((f32[2048,128]{1,0:T(8,128)}, bf16[2320,128]{1,0:T(8,128)(2,1)}, bf16[2320,128]{1,0:T(8,128)(2,1)}, bf16[2320,128]{1,0:T(8,128)(2,1)})) conditional(s32[]{:T(128)} %bitcast.5, (s32[78]{0:T(128)S(1)}, s32[3]{0:T(128)S(1)}, bf16[8192,128]{1,0:T(8,128)(2,1)S(1)}, bf16[272,128]{1,0:T(8,128)(2,1)S(1)}, bf16[3328,128]{1,0:T(8,128)(2,1)S(1)}, ...), branch_computations={%region_2.0_spmd, %region_3.0_spmd} | conditional | flops 11358208 | bytes 48513184 | solution.py:495
  162.5 4.5 %branch_0_fun.3 = (f32[2048,128]{1,0:T(8,128)}, bf16[2320,128]{1,0:T(8,128)(2,1)}, bf16[2320,128]{1,0:T(8,128)(2,1)}, bf16[2320,128]{1,0:T(8,128)(2,1)}) custom-call(s32[78]{0:T(128)S(1)} %get-tuple-element.105.lists, s32[3]{0:T(128)S(1)} %get-tuple-element.106.counts, bf16[8192,128]{1,0:T(8,128)(2,1)S(1)} %get-tuple-element.107.own, ...), custom_call_target="tpu_custom_call" | custom-call | tf_op jit(solution)/shard_map/cond/branch_0_fun/pallas_call | solution.py:333
  167.0 3.0 %collective-permute-start.47 = (bf16[2320,128]{1,0:T(8,128)(2,1)}, bf16[2320,128]{1,0:T(8,128)(2,1)S(1)}, u32[]{:S(2)}, u32[]{:S(2)}) collective-permute-start(bf16[2320,128]{1,0:T(8,128)(2,1)} %get-tuple-element.194), channel_id=1, source_target_pairs={{0,96},{1,25},{2,98},{3,27},{4,100},{5,29},{6,102},{7,31},{8,104},... | collective-permute-start | bytes 1781768 | tf_op jit(solution)/shard_map/ppermute | solution.py:30
  171.4 12.9 %collective-permute-done.47.refs_1_ = bf16[2320,128]{1,0:T(8,128)(2,1)S(1)} collective-permute-done((bf16[2320,128]{1,0:T(8,128)(2,1)}, bf16[2320,128]{1,0:T(8,128)(2,1)S(1)}, u32[]{:S(2)}, u32[]{:S(2)}) %collective-permute-start.47) | collective-permute-done | bytes 593952 | tf_op jit(solution)/shard_map/ppermute | solution.py:30
  184.2 3.8 %collective-permute-done.49.refs_3_ = bf16[2320,128]{1,0:T(8,128)(2,1)S(1)} collective-permute-done((bf16[2320,128]{1,0:T(8,128)(2,1)}, bf16[2320,128]{1,0:T(8,128)(2,1)S(1)}, u32[]{:S(2)}, u32[]{:S(2)}) %collective-permute-start.49) | collective-permute-done | bytes 593952 | tf_op jit(solution)/shard_map/ppermute | solution.py:30
  (122 shorter events, 61.8 us)
Async XLA Ops:
  3.6 15.6 %collective-permute-start.8 = (bf16[2064,128]{1,0:T(8,128)(2,1)S(1)}, bf16[2064,128]{1,0:T(8,128)(2,1)S(1)}, u32[]{:S(2)}, u32[]{:S(2)}) collective-permute-start(bf16[2064,128]{1,0:T(8,128)(2,1)S(1)} %get-tuple-element.170.refs_0_), channel_id=1, source_target_pairs={{0,32},{1,9},{2,34},{3,11},{4,36},{5,13},{6,38},{7,15},{8,40},{9,1... | collective-permute-start | bytes 1585160 | tf_op jit(solution)/shard_map/ppermute | solution.py:30
  5.2 15.7 %collective-permute-start.7 = (bf16[2064,128]{1,0:T(8,128)(2,1)S(1)}, bf16[2064,128]{1,0:T(8,128)(2,1)S(1)}, u32[]{:S(2)}, u32[]{:S(2)}) collective-permute-start(bf16[2064,128]{1,0:T(8,128)(2,1)S(1)} %get-tuple-element.170.refs_0_), channel_id=1, source_target_pairs={{0,64},{1,17},{2,66},{3,19},{4,68},{5,21},{6,70},{7,23},{8,72},{9,... | collective-permute-start | bytes 1585160 | tf_op jit(solution)/shard_map/ppermute | solution.py:30
  8.0 13.0 %collective-permute-start.6 = (bf16[2064,128]{1,0:T(8,128)(2,1)S(1)}, bf16[2064,128]{1,0:T(8,128)(2,1)S(1)}, u32[]{:S(2)}, u32[]{:S(2)}) collective-permute-start(bf16[2064,128]{1,0:T(8,128)(2,1)S(1)} %get-tuple-element.170.refs_0_), channel_id=1, source_target_pairs={{0,96},{1,25},{2,98},{3,27},{4,100},{5,29},{6,102},{7,31},{8,104},... | collective-permute-start | bytes 1585160 | tf_op jit(solution)/shard_map/ppermute | solution.py:30
  24.4 23.8 %collective-permute-start.12 = (bf16[3344,128]{1,0:T(8,128)(2,1)}, bf16[3344,128]{1,0:T(8,128)(2,1)S(1)}, u32[]{:S(2)}, u32[]{:S(2)}) collective-permute-start(bf16[3344,128]{1,0:T(8,128)(2,1)} %get-tuple-element.173), channel_id=1, source_target_pairs={{0,24},{1,97},{2,26},{3,99},{4,28},{5,101},{6,30},{7,103},{8,0},{9... | collective-permute-start | bytes 2568200 | tf_op jit(solution)/shard_map/ppermute | solution.py:30
  28.6 19.7 %collective-permute-start.13 = (bf16[3344,128]{1,0:T(8,128)(2,1)}, bf16[3344,128]{1,0:T(8,128)(2,1)S(1)}, u32[]{:S(2)}, u32[]{:S(2)}) collective-permute-start(bf16[3344,128]{1,0:T(8,128)(2,1)} %get-tuple-element.174), channel_id=1, source_target_pairs={{0,16},{1,65},{2,18},{3,67},{4,20},{5,69},{6,22},{7,71},{8,24},{9,... | collective-permute-start | bytes 2568200 | tf_op jit(solution)/shard_map/ppermute | solution.py:30
  29.4 22.8 %collective-permute-start.14 = (bf16[3344,128]{1,0:T(8,128)(2,1)}, bf16[3344,128]{1,0:T(8,128)(2,1)S(1)}, u32[]{:S(2)}, u32[]{:S(2)}) collective-permute-start(bf16[3344,128]{1,0:T(8,128)(2,1)} %get-tuple-element.172.refs_0_), channel_id=1, source_target_pairs={{0,8},{1,33},{2,10},{3,35},{4,12},{5,37},{6,14},{7,39},{8,16},{9,4... | collective-permute-start | bytes 2568200 | tf_op jit(solution)/shard_map/ppermute | solution.py:30
  65.4 15.8 %collective-permute-start.22 = (bf16[1024,128]{1,0:T(8,128)(2,1)S(1)}, bf16[1024,128]{1,0:T(8,128)(2,1)S(1)}, u32[]{:S(2)}, u32[]{:S(2)}) collective-permute-start(bf16[1024,128]{1,0:T(8,128)(2,1)S(1)} %get-tuple-element.210), channel_id=1, source_target_pairs={{0,2},{1,3},{2,4},{3,5},{4,6},{5,7},{6,0},{7,1},{8,10},{9,11},{10,... | collective-permute-start | bytes 786440 | tf_op jit(solution)/shard_map/ppermute | solution.py:43
  65.5 16.2 %collective-permute-start.21 = (bf16[1024,128]{1,0:T(8,128)(2,1)S(1)}, bf16[1024,128]{1,0:T(8,128)(2,1)S(1)}, u32[]{:S(2)}, u32[]{:S(2)}) collective-permute-start(bf16[1024,128]{1,0:T(8,128)(2,1)S(1)} %get-tuple-element.211), channel_id=1, source_target_pairs={{0,4},{1,5},{2,6},{3,7},{4,0},{5,1},{6,2},{7,3},{8,12},{9,13},{10,... | collective-permute-start | bytes 786440 | tf_op jit(solution)/shard_map/ppermute | solution.py:43
  68.9 13.5 %collective-permute-start.20 = (bf16[1024,128]{1,0:T(8,128)(2,1)S(1)}, bf16[1024,128]{1,0:T(8,128)(2,1)S(1)}, u32[]{:S(2)}, u32[]{:S(2)}) collective-permute-start(bf16[1024,128]{1,0:T(8,128)(2,1)S(1)} %get-tuple-element.212), channel_id=1, source_target_pairs={{0,6},{1,7},{2,0},{3,1},{4,2},{5,3},{6,4},{7,5},{8,14},{9,15},{10,... | collective-permute-start | bytes 786440 | tf_op jit(solution)/shard_map/ppermute | solution.py:43
  69.5 21.4 %collective-permute-start.18 = (bf16[1024,128]{1,0:T(8,128)(2,1)S(1)}, bf16[1024,128]{1,0:T(8,128)(2,1)S(1)}, u32[]{:S(2)}, u32[]{:S(2)}) collective-permute-start(bf16[1024,128]{1,0:T(8,128)(2,1)S(1)} %get-tuple-element.213), channel_id=1, source_target_pairs={{0,2},{1,3},{2,4},{3,5},{4,6},{5,7},{6,0},{7,1},{8,10},{9,11},{10,... | collective-permute-start | bytes 786440 | tf_op jit(solution)/shard_map/ppermute | solution.py:43
  71.2 21.7 %collective-permute-start.17 = (bf16[1024,128]{1,0:T(8,128)(2,1)S(1)}, bf16[1024,128]{1,0:T(8,128)(2,1)S(1)}, u32[]{:S(2)}, u32[]{:S(2)}) collective-permute-start(bf16[1024,128]{1,0:T(8,128)(2,1)S(1)} %get-tuple-element.214), channel_id=1, source_target_pairs={{0,4},{1,5},{2,6},{3,7},{4,0},{5,1},{6,2},{7,3},{8,12},{9,13},{10,... | collective-permute-start | bytes 786440 | tf_op jit(solution)/shard_map/ppermute | solution.py:43
  81.2 12.5 %collective-permute-start.16 = (bf16[1024,128]{1,0:T(8,128)(2,1)S(1)}, bf16[1024,128]{1,0:T(8,128)(2,1)S(1)}, u32[]{:S(2)}, u32[]{:S(2)}) collective-permute-start(bf16[1024,128]{1,0:T(8,128)(2,1)S(1)} %get-tuple-element.215), channel_id=1, source_target_pairs={{0,6},{1,7},{2,0},{3,1},{4,2},{5,3},{6,4},{7,5},{8,14},{9,15},{10,... | collective-permute-start | bytes 786440 | tf_op jit(solution)/shard_map/ppermute | solution.py:43
  86.6 12.0 %collective-permute-start.25 = (bf16[1024,128]{1,0:T(8,128)(2,1)S(1)}, bf16[1024,128]{1,0:T(8,128)(2,1)S(1)}, u32[]{:S(2)}, u32[]{:S(2)}) collective-permute-start(bf16[1024,128]{1,0:T(8,128)(2,1)S(1)} %get-tuple-element.182.refs_8_), channel_id=1, source_target_pairs={{0,2},{1,3},{2,4},{3,5},{4,6},{5,7},{6,0},{7,1},{8,10},{9,11},{10,... | collective-permute-start | bytes 786440 | tf_op jit(solution)/shard_map/ppermute | solution.py:43
  87.6 15.8 %collective-permute-start.24 = (bf16[1024,128]{1,0:T(8,128)(2,1)S(1)}, bf16[1024,128]{1,0:T(8,128)(2,1)S(1)}, u32[]{:S(2)}, u32[]{:S(2)}) collective-permute-start(bf16[1024,128]{1,0:T(8,128)(2,1)S(1)} %get-tuple-element.182.refs_8_), channel_id=1, source_target_pairs={{0,4},{1,5},{2,6},{3,7},{4,0},{5,1},{6,2},{7,3},{8,12},{9,13},{10,... | collective-permute-start | bytes 786440 | tf_op jit(solution)/shard_map/ppermute | solution.py:43
  90.8 13.0 %collective-permute-start.23 = (bf16[1024,128]{1,0:T(8,128)(2,1)S(1)}, bf16[1024,128]{1,0:T(8,128)(2,1)S(1)}, u32[]{:S(2)}, u32[]{:S(2)}) collective-permute-start(bf16[1024,128]{1,0:T(8,128)(2,1)S(1)} %get-tuple-element.182.refs_8_), channel_id=1, source_target_pairs={{0,6},{1,7},{2,0},{3,1},{4,2},{5,3},{6,4},{7,5},{8,14},{9,15},{10,... | collective-permute-start | bytes 786440 | tf_op jit(solution)/shard_map/ppermute | solution.py:43
  92.9 15.6 %collective-permute-start.26 = (bf16[1024,128]{1,0:T(8,128)(2,1)S(1)}, bf16[1024,128]{1,0:T(8,128)(2,1)S(1)}, u32[]{:S(2)}, u32[]{:S(2)}) collective-permute-start(bf16[1024,128]{1,0:T(8,128)(2,1)S(1)} %get-tuple-element.182.refs_8_), channel_id=1, source_target_pairs={{0,1},{1,0},{2,3},{3,2},{4,5},{5,4},{6,7},{7,6},{8,9},{9,8},{10,11... | collective-permute-start | bytes 786440 | tf_op jit(solution)/shard_map/ppermute | solution.py:48
  108.5 15.8 %collective-permute-start.33 = (bf16[1024,128]{1,0:T(8,128)(2,1)S(1)}, bf16[1024,128]{1,0:T(8,128)(2,1)S(1)}, u32[]{:S(2)}, u32[]{:S(2)}) collective-permute-start(bf16[1024,128]{1,0:T(8,128)(2,1)S(1)} %get-tuple-element.186.refs_12_), channel_id=1, source_target_pairs={{0,4},{1,5},{2,6},{3,7},{4,0},{5,1},{6,2},{7,3},{8,12},{9,13},{10,... | collective-permute-start | bytes 786440 | tf_op jit(solution)/shard_map/ppermute | solution.py:43
  112.0 12.2 %collective-permute-start.31 = (bf16[1024,128]{1,0:T(8,128)(2,1)S(1)}, bf16[1024,128]{1,0:T(8,128)(2,1)S(1)}, u32[]{:S(2)}, u32[]{:S(2)}) collective-permute-start(bf16[1024,128]{1,0:T(8,128)(2,1)S(1)} %get-tuple-element.186.refs_12_), channel_id=1, source_target_pairs={{0,6},{1,7},{2,0},{3,1},{4,2},{5,3},{6,4},{7,5},{8,14},{9,15},{10,... | collective-permute-start | bytes 786440 | tf_op jit(solution)/shard_map/ppermute | solution.py:43
  136.2 15.3 %collective-permute-start.44 = (bf16[3328,128]{1,0:T(8,128)(2,1)}, bf16[3328,128]{1,0:T(8,128)(2,1)S(1)}, u32[]{:S(2)}, u32[]{:S(2)}) collective-permute-start(bf16[3328,128]{1,0:T(8,128)(2,1)} %get-tuple-element.190), channel_id=1, source_target_pairs={{0,24},{1,97},{2,26},{3,99},{4,28},{5,101},{6,30},{7,103},{8,0},{9... | collective-permute-start | bytes 2555912 | tf_op jit(solution)/shard_map/ppermute | solution.py:30
  136.9 14.6 %collective-permute-start.45 = (bf16[3328,128]{1,0:T(8,128)(2,1)}, bf16[3328,128]{1,0:T(8,128)(2,1)S(1)}, u32[]{:S(2)}, u32[]{:S(2)}) collective-permute-start(bf16[3328,128]{1,0:T(8,128)(2,1)} %get-tuple-element.191), channel_id=1, source_target_pairs={{0,16},{1,65},{2,18},{3,67},{4,20},{5,69},{6,22},{7,71},{8,24},{9,... | collective-permute-start | bytes 2555912 | tf_op jit(solution)/shard_map/ppermute | solution.py:30
  137.1 23.3 %collective-permute-start.46 = (bf16[3328,128]{1,0:T(8,128)(2,1)}, bf16[3328,128]{1,0:T(8,128)(2,1)S(1)}, u32[]{:S(2)}, u32[]{:S(2)}) collective-permute-start(bf16[3328,128]{1,0:T(8,128)(2,1)} %get-tuple-element.192), channel_id=1, source_target_pairs={{0,8},{1,33},{2,10},{3,35},{4,12},{5,37},{6,14},{7,39},{8,16},{9,4... | collective-permute-start | bytes 2555912 | tf_op jit(solution)/shard_map/ppermute | solution.py:30
  167.0 17.2 %collective-permute-start.47 = (bf16[2320,128]{1,0:T(8,128)(2,1)}, bf16[2320,128]{1,0:T(8,128)(2,1)S(1)}, u32[]{:S(2)}, u32[]{:S(2)}) collective-permute-start(bf16[2320,128]{1,0:T(8,128)(2,1)} %get-tuple-element.194), channel_id=1, source_target_pairs={{0,96},{1,25},{2,98},{3,27},{4,100},{5,29},{6,102},{7,31},{8,104},... | collective-permute-start | bytes 1781768 | tf_op jit(solution)/shard_map/ppermute | solution.py:30
  170.1 14.2 %collective-permute-start.48 = (bf16[2320,128]{1,0:T(8,128)(2,1)}, bf16[2320,128]{1,0:T(8,128)(2,1)S(1)}, u32[]{:S(2)}, u32[]{:S(2)}) collective-permute-start(bf16[2320,128]{1,0:T(8,128)(2,1)} %get-tuple-element.195), channel_id=1, source_target_pairs={{0,64},{1,17},{2,66},{3,19},{4,68},{5,21},{6,70},{7,23},{8,72},{9,... | collective-permute-start | bytes 1781768 | tf_op jit(solution)/shard_map/ppermute | solution.py:30
  171.4 16.7 %collective-permute-start.49 = (bf16[2320,128]{1,0:T(8,128)(2,1)}, bf16[2320,128]{1,0:T(8,128)(2,1)S(1)}, u32[]{:S(2)}, u32[]{:S(2)}) collective-permute-start(bf16[2320,128]{1,0:T(8,128)(2,1)} %get-tuple-element.196), channel_id=1, source_target_pairs={{0,32},{1,9},{2,34},{3,11},{4,36},{5,13},{6,38},{7,15},{8,40},{9,1... | collective-permute-start | bytes 1781768 | tf_op jit(solution)/shard_map/ppermute | solution.py:30
  (40 other events, 230.8 us)

commit v5 on v4

--- a/solution.py
+++ b/solution.py
@@ -73,12 +73,7 @@
     return pl.ds(pl.multiple_of(place * T, T), T)
 
 
-def prepare_kernel(
-    at_row, at_col, live_ref, rows_ref, cols_ref, features, payload, meta, tables, sem
-):
-    nodes = features.shape[0]
-    copy = pltpu.make_async_copy(features, payload.at[pl.ds(0, nodes)], sem)
-    copy.start()
+def prepare_kernel(at_row, at_col, live_ref, rows_ref, cols_ref, meta, tables):
     live = live_ref[0]
     x, z = at_row[0] >> 2, at_row[0] & 3
     y, core = at_col[0] >> 1, at_col[0] & 1
@@ -124,24 +119,20 @@
     line = lax.broadcasted_iota(I32, (META, T), 0)
     lines = [wanted, amounts, jnp.broadcast_to(over, (1, T)), jnp.zeros((META - 3, T), F32)]
     meta[...] = jnp.concatenate(lines, axis=0).astype(BF16)
-    payload[pl.ds(nodes, META)] = meta[...]
-    copy.wait()
-
-
-def prepare(at_row, at_col, live, rows, cols, features):
+
+
+def prepare(at_row, at_col, live, rows, cols):
     slots = cols.shape[-1]
     return pl.pallas_call(
         prepare_kernel,
         out_shape=[
-            jax.ShapeDtypeStruct((features.shape[0] + META, T), BF16),
             jax.ShapeDtypeStruct((META, T), BF16),
             jax.ShapeDtypeStruct((8, slots), I32),
         ],
-        in_specs=[SMEM] * 3 + [VMEM] * 2 + [ANY],
-        out_specs=[VMEM] * 3,
-        scratch_shapes=[pltpu.SemaphoreType.DMA],
-        compiler_params=PARAMS,
-    )(at_row, at_col, live, rows.reshape(1, slots), cols.reshape(1, slots), features)
+        in_specs=[SMEM] * 3 + [VMEM] * 2,
+        out_specs=[VMEM] * 2,
+        compiler_params=PARAMS,
+    )(at_row, at_col, live, rows.reshape(1, slots), cols.reshape(1, slots))
 
 
 def products_kernel(live, tables, tiles_ref, *refs, spans, outs, contract, in_row, out_row):
@@ -192,10 +183,11 @@
     for ref, blocks in zip(out_refs, outs):
 
         def out(k, carry, ref=ref, start=start):
-            ref[block(k)] = total[start + k].astype(BF16)
+            for at in range(2):
+                ref[block(k * 2 + at)] = total[start + k * 2 + at].astype(BF16)
             return carry
 
-        lax.fori_loop(0, blocks, out, 0)
+        lax.fori_loop(0, blocks // 2, out, 0)
         start += blocks
 
 
@@ -225,28 +217,26 @@
 
 
 def pack_kernel(*refs):
-    pieces, metas, sends, (lists, counts), (held, words, table, sems) = (
+    pieces, metas, sends, (said, lists, counts), (held, words, table, sems) = (
         refs[:4],
-        refs[4:7],
-        refs[7:10],
-        refs[10:12],
-        refs[12:],
+        refs[4:8],
+        refs[8:11],
+        refs[11:14],
+        refs[14:],
     )
-    nodes = held.shape[1] - META
     copies = [pltpu.make_async_copy(p, held.at[k], sems.at[k]) for k, p in enumerate(pieces)]
     for copy in copies:
         copy.start()
     for n in range(3):
-        words[pl.ds(n * 8, 8)] = metas[n][...].astype(F32)[:8].astype(I32)
+        words[pl.ds(n * 8, 8)] = metas[n + 1][...].astype(F32)[:8].astype(I32)
     fetch = pltpu.make_async_copy(words, table, sems.at[4])
     fetch.start()
+    over = functools.reduce(jnp.maximum, [ref[...].astype(F32)[2:3] for ref in metas])
+    said[...] = jnp.broadcast_to(over, (8, T))
     fetch.wait()
     for copy in copies:
         copy.wait()
-    said = [held[k, pl.ds(nodes, META)].astype(F32) for k in range(4)]
-    said = functools.reduce(jnp.maximum, said).astype(BF16)
     for n in range(3):
-        sends[n][pl.ds(CAP * T, META)] = said
         group = 3 - n
         amount = table[n * 8 + 1, group]
         counts[n] = amount
@@ -263,10 +253,11 @@
 def pack(pieces, metas):
     return pl.pallas_call(
         pack_kernel,
-        out_shape=[jax.ShapeDtypeStruct((CAP * T + META, T), BF16)] * 3
+        out_shape=[jax.ShapeDtypeStruct((CAP * T, T), BF16)] * 3
+        + [jax.ShapeDtypeStruct((8, T), F32)]
         + [jax.ShapeDtypeStruct((3 * CAP,), I32), jax.ShapeDtypeStruct((3,), I32)],
-        in_specs=[ANY] * 4 + [VMEM] * 3,
-        out_specs=[VMEM] * 3 + [SMEM] * 2,
+        in_specs=[ANY] * 4 + [VMEM] * 4,
+        out_specs=[VMEM] * 4 + [SMEM] * 2,
         scratch_shapes=[
             pltpu.VMEM((4,) + pieces[0].shape, BF16),
             pltpu.VMEM((24, T), I32),
@@ -277,55 +268,40 @@
     )(*pieces, *metas)
 
 
-def flag_kernel(*refs):
-    sources, out, held, sems = refs[:4], refs[4], refs[5], refs[6]
-    copies = [
-        pltpu.make_async_copy(ref.at[pl.ds(CAP * T, META)], held.at[k], sems.at[k])
-        for k, ref in enumerate(sources)
-    ]
+def combine_kernel(lists, counts, own_ref, sums, *refs):
+    part_refs, outs, (own, parts, total, sems) = refs[:3], refs[3:7], refs[7:]
+    copies = [pltpu.make_async_copy(own_ref, own, sems.at[3])]
+    for n, ref in enumerate(part_refs):
+        copies.append(pltpu.make_async_copy(ref, parts.at[n], sems.at[n]))
     for copy in copies:
         copy.start()
-    for copy in copies:
+    for ref in outs[1:]:
+        ref[pl.ds(16 * T, sums.shape[0])] = sums[...]
+    copies[0].wait()
+
+    def widen(k, carry):
+        for at in range(4):
+            total[k * 4 + at] = own[block(k * 4 + at)].astype(F32)
+        return carry
+
+    lax.fori_loop(0, 16, widen, 0)
+    for copy in copies[1:]:
         copy.wait()
-    said = functools.reduce(jnp.maximum, [held[k].astype(F32) for k in range(4)])
-    out[0] = jnp.max(said[2:3]).astype(I32)
-
-
-def overflow(sources):
-    return pl.pallas_call(
-        flag_kernel,
-        out_shape=jax.ShapeDtypeStruct((1,), I32),
-        in_specs=[ANY] * 4,
-        out_specs=SMEM,
-        scratch_shapes=[pltpu.VMEM((4, META, T), BF16), pltpu.SemaphoreType.DMA((4,))],
-        compiler_params=PARAMS,
-    )(*sources)
-
-
-def combine_kernel(lists, counts, own, sums, *refs):
-    parts, outs, (total,) = refs[:3], refs[3:7], refs[7:]
-
-    def widen(k, carry):
-        total[k] = own[block(k)].astype(F32)
-        return carry
-
-    lax.fori_loop(0, 64, widen, 0)
-    for n, part in enumerate(parts):
-
-        def add(k, carry, n=n, part=part):
-            total[lists[n * CAP + k]] += part[block(k)].astype(F32)
+    for n in range(3):
+
+        def add(k, carry, n=n):
+            total[lists[n * CAP + k]] += parts[n, block(k)].astype(F32)
             return carry
 
         lax.fori_loop(0, counts[n], add, 0)
     for n, ref in enumerate(outs):
 
         def out(k, carry, n=n, ref=ref):
-            ref[block(k)] = total[n * 16 + k].astype(ref.dtype)
+            for at in range(4):
+                ref[block(k * 4 + at)] = total[n * 16 + k * 4 + at].astype(ref.dtype)
             return carry
 
-        lax.fori_loop(0, 16, out, 0)
-        if n:
-            ref[pl.ds(16 * T, sums.shape[0])] = sums[...]
+        lax.fori_loop(0, 4, out, 0)
 
 
 def combine(lists, counts, own, sums, parts):
@@ -334,9 +310,14 @@
         combine_kernel,
         out_shape=[jax.ShapeDtypeStruct((rows, T), F32)]
         + [jax.ShapeDtypeStruct((rows + sums.shape[0], T), BF16)] * 3,
-        in_specs=[SMEM] * 2 + [VMEM] * 5,
+        in_specs=[SMEM] * 2 + [ANY, VMEM] + [ANY] * 3,
         out_specs=[VMEM] * 4,
-        scratch_shapes=[pltpu.VMEM((64, T, T), F32)],
+        scratch_shapes=[
+            pltpu.VMEM(own.shape, BF16),
+            pltpu.VMEM((3,) + parts[0].shape, BF16),
+            pltpu.VMEM((64, T, T), F32),
+            pltpu.SemaphoreType.DMA((4,)),
+        ],
         compiler_params=PARAMS,
     )(lists, counts, own, sums, *parts)
 
@@ -432,18 +413,15 @@
     scaling = 1.0 / math.sqrt(nodes_here * lax.axis_size("row") * lax.axis_size("col"))
     at_row, at_col = lax.axis_index("row"), lax.axis_index("col")
     live = live_tiles.reshape(1)
-    payload, meta, tables = prepare(
-        at_row.reshape(1), at_col.reshape(1), live, tile_rows, tile_cols, features
-    )
-
-    pieces = ring_gather(payload, along_inner)
-    *sends, lists, counts = pack(pieces, ring_gather(meta, along_outer)[1:])
+    meta, tables = prepare(at_row.reshape(1), at_col.reshape(1), live, tile_rows, tile_cols)
+
+    pieces = ring_gather(features, along_inner)
+    *sends, said, lists, counts = pack(pieces, ring_gather(meta, along_outer))
     named = ring_swap([None] + sends, along_outer)[1:]
-    flags = [sends[0]] + named
-    full = overflow(flags)[0] > 0
+    full = functools.reduce(jnp.maximum, ring_gather(said, along_inner))[0, 0] > 0.5
 
     def forward_all(pieces, named):
-        whole = jnp.concatenate([p[:nodes_here] for p in pieces])
+        whole = jnp.concatenate(pieces)
         whole = ring_gather(whole, along_outer)
         spans = (4 * nodes_here,) * 4
         return products(live, tables, 2, 0, tiles, whole, spans, (32,) * 4, (1,))
@@ -469,9 +447,9 @@
             parts, grad_hidden, weight, offset.reshape(1, -1), part, before
         )
         here = ring_gather(projected, along_y)
-        before = (hidden, sums, *here[1:])
         own += here
         others += [other_core(piece) for piece in here]
+        before = (hidden, sums, others[0])
 
     sums = total_of(ring_gather(sums + other_core(sums), along_outer))
 

time: 193 us -> 184 us (0.953)
  waiting for transfers between devices: 95 us -> 74.7 us
  starting transfers between devices: 48.9 us -> 61.8 us
  Pallas kernels: 37.8 us -> 33.8 us
  other arithmetic: 3.65 us -> 6.72 us
    ppermute x15, waiting for transfers between devices: 40.5 us -> 26.5 us  [along_y(): return lax.ppermute(value, 'col', pairs)]
    ppermute x15, starting transfers between devices: 16.9 us -> 24.2 us  [along_y(): return lax.ppermute(value, 'col', pairs)]
    ppermute x18 -> x21, waiting for transfers between devices: 50.9 us -> 44.9 us  [along_xz(): return lax.ppermute(value, ('row', 'col'), pairs)]
    ppermute x18 -> x21, starting transfers between devices: 29.7 us -> 34.2 us  [along_xz(): return lax.ppermute(value, ('row', 'col'), pairs)]
    convert_element_type x2, other arithmetic: 0.41 us -> 2.78 us  [on_device(): far.append((keep[at].astype(F32) + got[at].astype(F32)).astype(BF16))]
    pallas_call x3 -> x2, Pallas kernels: 7.16 us -> 5.25 us  [the longest x1 3.68 us: pack(): pl.pallas_call(pack_kernel, out_shape=[jax.ShapeDtypeStruct((CAP * T, T),...]
  transfers between devices with their start and end apart: 44 -> 47, of which waited for: 26 -> 22; matrix products, arithmetic and copies ran while one was open for 2% -> 4% of each run, Pallas kernels for 4% -> 5%
where the time goes in v5:
time: 184 us
  waiting for transfers between devices  74.7 us (41%)
  starting transfers between devices  61.8 us (34%)
  Pallas kernels  33.8 us (18%)
  other arithmetic  6.72 us (4%)
  local copies, waits for them, and re-layouts  4.54 us (2%)
  between operations  2.19 us (1%)
    ppermute x21, waiting for transfers between devices, along_xz(): return lax.ppermute(value, ('row', 'col'), pairs)  44.9 us
    ppermute x21, starting transfers between devices, along_xz(): return lax.ppermute(value, ('row', 'col'), pairs)  34.2 us
    ppermute x15, waiting for transfers between devices, along_y(): return lax.ppermute(value, 'col', pairs)  26.5 us
    ppermute x15, starting transfers between devices, along_y(): return lax.ppermute(value, 'col', pairs)  24.2 us
    pallas_call x2, Pallas kernels, products(): pl.pallas_call(kernel, out_shape=[jax.ShapeDtypeStruct((n * T, T), BF16)...  16 us
    pallas_call x2, Pallas kernels, dense(): pl.pallas_call(dense_kernel, grid=(steps,), out_shape=[jax.ShapeDtypeStru...  7.08 us
    pallas_call x1, Pallas kernels, pack(): pl.pallas_call(pack_kernel, out_shape=[jax.ShapeDtypeStruct((CAP * T, T),...  3.68 us
  transfers between devices with their start and end apart: 47, of which 22 were waited for; matrix products, arithmetic and copies ran while one was open for 4% of the time, Pallas kernels for 5%

profile of v5, /device:TPU:0, one launch (start us, length us, event | category | flops | bytes accessed | tf_op | source)
XLA Modules:
  0.0 183.7 jit_solution(17240671256389322832)
XLA Ops:
  10.6 3.6 %collective-permute-start.10 = (bf16[16,128]{1,0:T(8,128)(2,1)}, bf16[16,128]{1,0:T(8,128)(2,1)S(1)}, u32[]{:S(2)}, u32[]{:S(2)}) collective-permute-start(bf16[16,128]{1,0:T(8,128)(2,1)} %get-tuple-element.170.refs_4_), channel_id=1, source_target_pairs={{0,16},{1,65},{2,18},{3,67},{4,20},{5,69},{6,22},{7,71},{8,24},{9,... | collective-permute-start | bytes 12296 | tf_op jit(solution)/shard_map/ppermute | solution.py:30
  19.3 3.7 %shard_map.112 = (bf16[3328,128]{1,0:T(8,128)(2,1)}, bf16[3328,128]{1,0:T(8,128)(2,1)}, bf16[3328,128]{1,0:T(8,128)(2,1)}, f32[8,128]{1,0:T(8,128)}, s32[78]{0:T(128)S(1)}, /*index=5*/s32[3]{0:T(128)S(1)}) custom-call(bf16[2048,128]{1,0:T(8,128)(2,1)} %refs_0_.1, bf16[2048,128]{1,0:T(8,128)(2,1)} %collective-permute-done.6.refs_1_, ...), custom_call_target="tpu_custom_call" | custom-call | tf_op jit(solution)/shard_map/pallas_call | solution.py:254
  23.0 3.0 %collective-permute-start.15 = (bf16[3328,128]{1,0:T(8,128)(2,1)}, bf16[3328,128]{1,0:T(8,128)(2,1)S(1)}, u32[]{:S(2)}, u32[]{:S(2)}) collective-permute-start(bf16[3328,128]{1,0:T(8,128)(2,1)} %get-tuple-element.173), channel_id=1, source_target_pairs={{0,24},{1,97},{2,26},{3,99},{4,28},{5,101},{6,30},{7,103},{8,0},{9... | collective-permute-start | bytes 2555912 | tf_op jit(solution)/shard_map/ppermute | solution.py:30
  32.2 5.7 %collective-permute-done.14 = f32[8,128]{1,0:T(8,128)S(1)} collective-permute-done((f32[8,128]{1,0:T(8,128)}, f32[8,128]{1,0:T(8,128)S(1)}, u32[]{:S(2)}, u32[]{:S(2)}) %collective-permute-start.14) | collective-permute-done | bytes 4128 | tf_op jit(solution)/shard_map/ppermute | solution.py:30
  37.9 3.9 %collective-permute-done.12 = f32[8,128]{1,0:T(8,128)S(1)} collective-permute-done((f32[8,128]{1,0:T(8,128)}, f32[8,128]{1,0:T(8,128)S(1)}, u32[]{:S(2)}, u32[]{:S(2)}) %collective-permute-start.12) | collective-permute-done | bytes 4128 | tf_op jit(solution)/shard_map/ppermute | solution.py:30
  45.8 3.8 %collective-permute-done.17 = bf16[3328,128]{1,0:T(8,128)(2,1)S(1)} collective-permute-done((bf16[3328,128]{1,0:T(8,128)(2,1)}, bf16[3328,128]{1,0:T(8,128)(2,1)S(1)}, u32[]{:S(2)}, u32[]{:S(2)}) %collective-permute-start.17) | collective-permute-done | bytes 852000 | tf_op jit(solution)/shard_map/ppermute | solution.py:30
  49.6 8.1 %conditional.2 = ((bf16[4096,128]{1,0:T(8,128)(2,1)}, bf16[4096,128]{1,0:T(8,128)(2,1)}, bf16[4096,128]{1,0:T(8,128)(2,1)}, bf16[4096,128]{1,0:T(8,128)(2,1)})) conditional(s32[]{:T(128)} %bitcast.5, (s32[1]{0:T(128)}, s32[8,64]{1,0:T(8,128)S(1)}, bf16[64,128,128]{2,1,0:T(8,128)(2,1)S(1)}, bf16[2048,128]{1,0:T(8,128)(2,1)}, ...), branch_computations={%region_0.0_spmd, %region_1.0_spmd} | conditional | bytes 62914800 | solution.py:433
  49.6 8.1 %branch_0_fun.2 = (bf16[4096,128]{1,0:T(8,128)(2,1)}, bf16[4096,128]{1,0:T(8,128)(2,1)}, bf16[4096,128]{1,0:T(8,128)(2,1)}, bf16[4096,128]{1,0:T(8,128)(2,1)}) custom-call(s32[1]{0:T(128)} %get-tuple-element.88.live, s32[8,64]{1,0:T(8,128)S(1)} %get-tuple-element.89.tables, bf16[64,128,128]{2,1,0:T(8,128)(2,1)S(1)} %get-tuple-element.90.tiles_ref, ...), custom_call_target="tpu_custom_call" | custom-call | tf_op jit(solution)/shard_map/cond/branch_0_fun/pallas_call | solution.py:203
  62.8 3.2 %collective-permute-start.24 = (bf16[1024,128]{1,0:T(8,128)(2,1)S(1)}, bf16[1024,128]{1,0:T(8,128)(2,1)S(1)}, u32[]{:S(2)}, u32[]{:S(2)}) collective-permute-start(bf16[1024,128]{1,0:T(8,128)(2,1)S(1)} %get-tuple-element.211), channel_id=1, source_target_pairs={{0,4},{1,5},{2,6},{3,7},{4,0},{5,1},{6,2},{7,3},{8,12},{9,13},{10,... | collective-permute-start | bytes 786440 | tf_op jit(solution)/shard_map/ppermute | solution.py:43
  73.6 5.1 %collective-permute-done.24.refs_3_ = bf16[1024,128]{1,0:T(8,128)(2,1)S(1)} collective-permute-done((bf16[1024,128]{1,0:T(8,128)(2,1)S(1)}, bf16[1024,128]{1,0:T(8,128)(2,1)S(1)}, u32[]{:S(2)}, u32[]{:S(2)}) %collective-permute-start.24) | collective-permute-done | bytes 262176 | tf_op jit(solution)/shard_map/ppermute | solution.py:43
  80.1 3.5 %shard_map.113 = (bf16[2048,256]{1,0:T(8,128)(2,1)}, bf16[1024,128]{1,0:T(8,128)(2,1)S(1)}, f32[136,256]{1,0:T(8,128)}) custom-call(bf16[4096,128]{1,0:T(8,128)(2,1)S(1)} %copy-done.3, bf16[4096,128]{1,0:T(8,128)(2,1)} %copy-done.2, bf16[1024,128]{1,0:T(8,128)(2,1)} %copy-done.19, bf16[1024,128]{1,0:T(8,128)(2,1)} %copy-done.18, ...), custom_call_target="tpu_custom_call" | custom-call | tf_op jit(solution)/shard_map/pallas_call | solution.py:389
  84.4 7.6 %collective-permute-start.29 = (bf16[1024,128]{1,0:T(8,128)(2,1)S(1)}, bf16[1024,128]{1,0:T(8,128)(2,1)S(1)}, u32[]{:S(2)}, u32[]{:S(2)}) collective-permute-start(bf16[1024,128]{1,0:T(8,128)(2,1)S(1)} %get-tuple-element.182.refs_8_), channel_id=1, source_target_pairs={{0,4},{1,5},{2,6},{3,7},{4,0},{5,1},{6,2},{7,3},{8,12},{9,13},{10,... | collective-permute-start | bytes 786440 | tf_op jit(solution)/shard_map/ppermute | solution.py:43
  92.9 3.6 %shard_map.114 = (bf16[2048,256]{1,0:T(8,128)(2,1)}, bf16[1024,128]{1,0:T(8,128)(2,1)S(1)}, f32[136,256]{1,0:T(8,128)}) custom-call(bf16[4096,128]{1,0:T(8,128)(2,1)S(1)} %copy-done.5, bf16[4096,128]{1,0:T(8,128)(2,1)} %copy-done.4, bf16[1024,128]{1,0:T(8,128)(2,1)} %copy-done.16, bf16[1024,128]{1,0:T(8,128)(2,1)} %copy-done.15, ...), custom_call_target="tpu_custom_call", output_to_operand_aliasing={{0}: (8, {})} | custom-call | tf_op jit(solution)/shard_map/pallas_call | solution.py:389
  97.0 3.7 %collective-permute-done.29.refs_10_ = bf16[1024,128]{1,0:T(8,128)(2,1)S(1)} collective-permute-done((bf16[1024,128]{1,0:T(8,128)(2,1)S(1)}, bf16[1024,128]{1,0:T(8,128)(2,1)S(1)}, u32[]{:S(2)}, u32[]{:S(2)}) %collective-permute-start.29) | collective-permute-done | bytes 262176 | tf_op jit(solution)/shard_map/ppermute | solution.py:43
  100.8 3.5 %collective-permute-start.36 = (bf16[1024,128]{1,0:T(8,128)(2,1)S(1)}, bf16[1024,128]{1,0:T(8,128)(2,1)S(1)}, u32[]{:S(2)}, u32[]{:S(2)}) collective-permute-start(bf16[1024,128]{1,0:T(8,128)(2,1)S(1)} %get-tuple-element.186.refs_12_), channel_id=1, source_target_pairs={{0,4},{1,5},{2,6},{3,7},{4,0},{5,1},{6,2},{7,3},{8,12},{9,13},{10,... | collective-permute-start | bytes 786440 | tf_op jit(solution)/shard_map/ppermute | solution.py:43
  109.5 6.8 %collective-permute-done.38.refs_15_ = bf16[1024,128]{1,0:T(8,128)(2,1)S(1)} collective-permute-done((bf16[1024,128]{1,0:T(8,128)(2,1)S(1)}, bf16[1024,128]{1,0:T(8,128)(2,1)S(1)}, u32[]{:S(2)}, u32[]{:S(2)}) %collective-permute-start.38) | collective-permute-done | bytes 262176 | tf_op jit(solution)/shard_map/ppermute | solution.py:43
  123.0 7.8 %shard_map.115 = (bf16[8192,128]{1,0:T(8,128)(2,1)S(1)}, bf16[3328,128]{1,0:T(8,128)(2,1)}, bf16[3328,128]{1,0:T(8,128)(2,1)}, bf16[3328,128]{1,0:T(8,128)(2,1)}, f32[136,256]{1,0:T(8,128)}) custom-call(s32[1]{0:T(128)} %bitcast.10.live, s32[8,64]{1,0:T(8,128)S(1)} %get-tuple-element.172.tables, bf16[64,128,128]{2,1,0:T(8,128)(2,1)S(1)} %bitcast.13, ...), custom_call_target="tpu_custom_call" | custom-call | tf_op jit(solution)/shard_map/pallas_call | solution.py:203
  137.5 3.5 %collective-permute-done.45 = f32[136,256]{1,0:T(8,128)S(1)} collective-permute-done((f32[136,256]{1,0:T(8,128)}, f32[136,256]{1,0:T(8,128)S(1)}, u32[]{:S(2)}, u32[]{:S(2)}) %collective-permute-start.45) | collective-permute-done | bytes 139296 | tf_op jit(solution)/shard_map/ppermute | solution.py:43
  141.0 3.3 %collective-permute-done.44 = f32[136,256]{1,0:T(8,128)S(1)} collective-permute-done((f32[136,256]{1,0:T(8,128)}, f32[136,256]{1,0:T(8,128)S(1)}, u32[]{:S(2)}, u32[]{:S(2)}) %collective-permute-start.44) | collective-permute-done | bytes 139296 | tf_op jit(solution)/shard_map/ppermute | solution.py:43
  146.0 8.6 %collective-permute-done.49 = bf16[3328,128]{1,0:T(8,128)(2,1)S(1)} collective-permute-done((bf16[3328,128]{1,0:T(8,128)(2,1)}, bf16[3328,128]{1,0:T(8,128)(2,1)S(1)}, u32[]{:S(2)}, u32[]{:S(2)}) %collective-permute-start.49) | collective-permute-done | bytes 852000 | tf_op jit(solution)/shard_map/ppermute | solution.py:30
  154.6 4.1 %conditional.3 = ((f32[2048,128]{1,0:T(8,128)S(1)}, bf16[2320,128]{1,0:T(8,128)(2,1)S(1)}, bf16[2320,128]{1,0:T(8,128)(2,1)S(1)}, bf16[2320,128]{1,0:T(8,128)(2,1)S(1)})) conditional(s32[]{:T(128)} %bitcast.5, (s32[78]{0:T(128)S(1)}, s32[3]{0:T(128)S(1)}, bf16[8192,128]{1,0:T(8,128)(2,1)S(1)}, bf16[272,128]{1,0:T(8,128)(2,1)S(1)}, ...), branch_computations={%region_2.0_spmd, %region_3.0_spmd} | conditional | flops 11358208 | bytes 48513184 | solution.py:473
  158.7 3.7 %collective-permute-start.50 = (bf16[2320,128]{1,0:T(8,128)(2,1)S(1)}, bf16[2320,128]{1,0:T(8,128)(2,1)S(1)}, u32[]{:S(2)}, u32[]{:S(2)}) collective-permute-start(bf16[2320,128]{1,0:T(8,128)(2,1)S(1)} %get-tuple-element.194), channel_id=1, source_target_pairs={{0,96},{1,25},{2,98},{3,27},{4,100},{5,29},{6,102},{7,31},{8,104},... | collective-permute-start | bytes 1781768 | tf_op jit(solution)/shard_map/ppermute | solution.py:30
  165.1 5.8 %collective-permute-done.50.refs_1_ = bf16[2320,128]{1,0:T(8,128)(2,1)S(1)} collective-permute-done((bf16[2320,128]{1,0:T(8,128)(2,1)S(1)}, bf16[2320,128]{1,0:T(8,128)(2,1)S(1)}, u32[]{:S(2)}, u32[]{:S(2)}) %collective-permute-start.50) | collective-permute-done | bytes 593952 | tf_op jit(solution)/shard_map/ppermute | solution.py:30
  174.0 6.3 %collective-permute-done.52.refs_3_ = bf16[2320,128]{1,0:T(8,128)(2,1)S(1)} collective-permute-done((bf16[2320,128]{1,0:T(8,128)(2,1)S(1)}, bf16[2320,128]{1,0:T(8,128)(2,1)S(1)}, u32[]{:S(2)}, u32[]{:S(2)}) %collective-permute-start.52) | collective-permute-done | bytes 593952 | tf_op jit(solution)/shard_map/ppermute | solution.py:30
  (127 shorter events, 73.6 us)
Async XLA Ops:
  0.6 18.1 %collective-permute-start.8 = (bf16[2048,128]{1,0:T(8,128)(2,1)}, bf16[2048,128]{1,0:T(8,128)(2,1)S(1)}, u32[]{:S(2)}, u32[]{:S(2)}) collective-permute-start(bf16[2048,128]{1,0:T(8,128)(2,1)} %refs_0_.1), channel_id=1, source_target_pairs={{0,32},{1,9},{2,34},{3,11},{4,36},{5,13},{6,38},{7,15},{8,40},{9,1... | collective-permute-start | bytes 1572872 | tf_op jit(solution)/shard_map/ppermute | solution.py:30
  2.3 16.4 %collective-permute-start.7 = (bf16[2048,128]{1,0:T(8,128)(2,1)}, bf16[2048,128]{1,0:T(8,128)(2,1)S(1)}, u32[]{:S(2)}, u32[]{:S(2)}) collective-permute-start(bf16[2048,128]{1,0:T(8,128)(2,1)} %refs_0_.1), channel_id=1, source_target_pairs={{0,64},{1,17},{2,66},{3,19},{4,68},{5,21},{6,70},{7,23},{8,72},{9,... | collective-permute-start | bytes 1572872 | tf_op jit(solution)/shard_map/ppermute | solution.py:30
  5.0 13.7 %collective-permute-start.6 = (bf16[2048,128]{1,0:T(8,128)(2,1)}, bf16[2048,128]{1,0:T(8,128)(2,1)}, u32[]{:S(2)}, u32[]{:S(2)}) collective-permute-start(bf16[2048,128]{1,0:T(8,128)(2,1)} %refs_0_.1), channel_id=1, source_target_pairs={{0,96},{1,25},{2,98},{3,27},{4,100},{5,29},{6,102},{7,31},{8,104},... | collective-permute-start | bytes 1572872 | tf_op jit(solution)/shard_map/ppermute | solution.py:30
  23.0 22.8 %collective-permute-start.15 = (bf16[3328,128]{1,0:T(8,128)(2,1)}, bf16[3328,128]{1,0:T(8,128)(2,1)S(1)}, u32[]{:S(2)}, u32[]{:S(2)}) collective-permute-start(bf16[3328,128]{1,0:T(8,128)(2,1)} %get-tuple-element.173), channel_id=1, source_target_pairs={{0,24},{1,97},{2,26},{3,99},{4,28},{5,101},{6,30},{7,103},{8,0},{9... | collective-permute-start | bytes 2555912 | tf_op jit(solution)/shard_map/ppermute | solution.py:30
  26.0 19.7 %collective-permute-start.16 = (bf16[3328,128]{1,0:T(8,128)(2,1)}, bf16[3328,128]{1,0:T(8,128)(2,1)S(1)}, u32[]{:S(2)}, u32[]{:S(2)}) collective-permute-start(bf16[3328,128]{1,0:T(8,128)(2,1)} %get-tuple-element.174), channel_id=1, source_target_pairs={{0,16},{1,65},{2,18},{3,67},{4,20},{5,69},{6,22},{7,71},{8,24},{9,... | collective-permute-start | bytes 2555912 | tf_op jit(solution)/shard_map/ppermute | solution.py:30
  26.6 22.9 %collective-permute-start.17 = (bf16[3328,128]{1,0:T(8,128)(2,1)}, bf16[3328,128]{1,0:T(8,128)(2,1)S(1)}, u32[]{:S(2)}, u32[]{:S(2)}) collective-permute-start(bf16[3328,128]{1,0:T(8,128)(2,1)} %get-tuple-element.175), channel_id=1, source_target_pairs={{0,8},{1,33},{2,10},{3,35},{4,12},{5,37},{6,14},{7,39},{8,16},{9,4... | collective-permute-start | bytes 2555912 | tf_op jit(solution)/shard_map/ppermute | solution.py:30
  62.8 15.9 %collective-permute-start.24 = (bf16[1024,128]{1,0:T(8,128)(2,1)S(1)}, bf16[1024,128]{1,0:T(8,128)(2,1)S(1)}, u32[]{:S(2)}, u32[]{:S(2)}) collective-permute-start(bf16[1024,128]{1,0:T(8,128)(2,1)S(1)} %get-tuple-element.211), channel_id=1, source_target_pairs={{0,4},{1,5},{2,6},{3,7},{4,0},{5,1},{6,2},{7,3},{8,12},{9,13},{10,... | collective-permute-start | bytes 786440 | tf_op jit(solution)/shard_map/ppermute | solution.py:43
  66.1 13.3 %collective-permute-start.23 = (bf16[1024,128]{1,0:T(8,128)(2,1)S(1)}, bf16[1024,128]{1,0:T(8,128)(2,1)S(1)}, u32[]{:S(2)}, u32[]{:S(2)}) collective-permute-start(bf16[1024,128]{1,0:T(8,128)(2,1)S(1)} %get-tuple-element.212), channel_id=1, source_target_pairs={{0,6},{1,7},{2,0},{3,1},{4,2},{5,3},{6,4},{7,5},{8,14},{9,15},{10,... | collective-permute-start | bytes 786440 | tf_op jit(solution)/shard_map/ppermute | solution.py:43
  69.7 14.7 %collective-permute-start.21 = (bf16[1024,128]{1,0:T(8,128)(2,1)}, bf16[1024,128]{1,0:T(8,128)(2,1)S(1)}, u32[]{:S(2)}, u32[]{:S(2)}) collective-permute-start(bf16[1024,128]{1,0:T(8,128)(2,1)} %get-tuple-element.213), channel_id=1, source_target_pairs={{0,2},{1,3},{2,4},{3,5},{4,6},{5,7},{6,0},{7,1},{8,10},{9,11},{10,... | collective-permute-start | bytes 786440 | tf_op jit(solution)/shard_map/ppermute | solution.py:43
  69.7 22.3 %collective-permute-start.20 = (bf16[1024,128]{1,0:T(8,128)(2,1)S(1)}, bf16[1024,128]{1,0:T(8,128)(2,1)S(1)}, u32[]{:S(2)}, u32[]{:S(2)}) collective-permute-start(bf16[1024,128]{1,0:T(8,128)(2,1)S(1)} %get-tuple-element.214), channel_id=1, source_target_pairs={{0,4},{1,5},{2,6},{3,7},{4,0},{5,1},{6,2},{7,3},{8,12},{9,13},{10,... | collective-permute-start | bytes 786440 | tf_op jit(solution)/shard_map/ppermute | solution.py:43
  72.0 20.2 %collective-permute-start.19 = (bf16[1024,128]{1,0:T(8,128)(2,1)S(1)}, bf16[1024,128]{1,0:T(8,128)(2,1)S(1)}, u32[]{:S(2)}, u32[]{:S(2)}) collective-permute-start(bf16[1024,128]{1,0:T(8,128)(2,1)S(1)} %get-tuple-element.215), channel_id=1, source_target_pairs={{0,6},{1,7},{2,0},{3,1},{4,2},{5,3},{6,4},{7,5},{8,14},{9,15},{10,... | collective-permute-start | bytes 786440 | tf_op jit(solution)/shard_map/ppermute | solution.py:43
  83.7 12.8 %collective-permute-start.31 = (bf16[1024,128]{1,0:T(8,128)(2,1)S(1)}, bf16[1024,128]{1,0:T(8,128)(2,1)S(1)}, u32[]{:S(2)}, u32[]{:S(2)}) collective-permute-start(bf16[1024,128]{1,0:T(8,128)(2,1)S(1)} %get-tuple-element.182.refs_8_), channel_id=1, source_target_pairs={{0,2},{1,3},{2,4},{3,5},{4,6},{5,7},{6,0},{7,1},{8,10},{9,11},{10,... | collective-permute-start | bytes 786440 | tf_op jit(solution)/shard_map/ppermute | solution.py:43
  84.4 16.3 %collective-permute-start.29 = (bf16[1024,128]{1,0:T(8,128)(2,1)S(1)}, bf16[1024,128]{1,0:T(8,128)(2,1)S(1)}, u32[]{:S(2)}, u32[]{:S(2)}) collective-permute-start(bf16[1024,128]{1,0:T(8,128)(2,1)S(1)} %get-tuple-element.182.refs_8_), channel_id=1, source_target_pairs={{0,4},{1,5},{2,6},{3,7},{4,0},{5,1},{6,2},{7,3},{8,12},{9,13},{10,... | collective-permute-start | bytes 786440 | tf_op jit(solution)/shard_map/ppermute | solution.py:43
  100.7 15.5 %collective-permute-start.38 = (bf16[1024,128]{1,0:T(8,128)(2,1)S(1)}, bf16[1024,128]{1,0:T(8,128)(2,1)S(1)}, u32[]{:S(2)}, u32[]{:S(2)}) collective-permute-start(bf16[1024,128]{1,0:T(8,128)(2,1)S(1)} %get-tuple-element.186.refs_12_), channel_id=1, source_target_pairs={{0,2},{1,3},{2,4},{3,5},{4,6},{5,7},{6,0},{7,1},{8,10},{9,11},{10,... | collective-permute-start | bytes 786440 | tf_op jit(solution)/shard_map/ppermute | solution.py:43
  100.8 15.4 %collective-permute-start.36 = (bf16[1024,128]{1,0:T(8,128)(2,1)S(1)}, bf16[1024,128]{1,0:T(8,128)(2,1)S(1)}, u32[]{:S(2)}, u32[]{:S(2)}) collective-permute-start(bf16[1024,128]{1,0:T(8,128)(2,1)S(1)} %get-tuple-element.186.refs_12_), channel_id=1, source_target_pairs={{0,4},{1,5},{2,6},{3,7},{4,0},{5,1},{6,2},{7,3},{8,12},{9,13},{10,... | collective-permute-start | bytes 786440 | tf_op jit(solution)/shard_map/ppermute | solution.py:43
  104.3 13.5 %collective-permute-start.34 = (bf16[1024,128]{1,0:T(8,128)(2,1)S(1)}, bf16[1024,128]{1,0:T(8,128)(2,1)S(1)}, u32[]{:S(2)}, u32[]{:S(2)}) collective-permute-start(bf16[1024,128]{1,0:T(8,128)(2,1)S(1)} %get-tuple-element.186.refs_12_), channel_id=1, source_target_pairs={{0,6},{1,7},{2,0},{3,1},{4,2},{5,3},{6,4},{7,5},{8,14},{9,15},{10,... | collective-permute-start | bytes 786440 | tf_op jit(solution)/shard_map/ppermute | solution.py:43
  106.5 11.5 %collective-permute-start.43 = (f32[136,256]{1,0:T(8,128)S(1)}, f32[136,256]{1,0:T(8,128)S(1)}, u32[]{:S(2)}, u32[]{:S(2)}) collective-permute-start(f32[136,256]{1,0:T(8,128)S(1)} %add.54), channel_id=1, source_target_pairs={{0,8},{1,33},{2,10},{3,35},{4,12},{5,37},{6,14},{7,39},{8,16},{9,4... | collective-permute-start | bytes 417800 | tf_op jit(solution)/shard_map/ppermute | solution.py:30
  106.6 11.8 %collective-permute-start.42 = (f32[136,256]{1,0:T(8,128)S(1)}, f32[136,256]{1,0:T(8,128)S(1)}, u32[]{:S(2)}, u32[]{:S(2)}) collective-permute-start(f32[136,256]{1,0:T(8,128)S(1)} %add.54), channel_id=1, source_target_pairs={{0,16},{1,65},{2,18},{3,67},{4,20},{5,69},{6,22},{7,71},{8,24},{9,... | collective-permute-start | bytes 417800 | tf_op jit(solution)/shard_map/ppermute | solution.py:30
  130.9 15.1 %collective-permute-start.47 = (bf16[3328,128]{1,0:T(8,128)(2,1)}, bf16[3328,128]{1,0:T(8,128)(2,1)}, u32[]{:S(2)}, u32[]{:S(2)}) collective-permute-start(bf16[3328,128]{1,0:T(8,128)(2,1)} %get-tuple-element.190), channel_id=1, source_target_pairs={{0,24},{1,97},{2,26},{3,99},{4,28},{5,101},{6,30},{7,103},{8,0},{9... | collective-permute-start | bytes 2555912 | tf_op jit(solution)/shard_map/ppermute | solution.py:30
  131.0 15.0 %collective-permute-start.48 = (bf16[3328,128]{1,0:T(8,128)(2,1)}, bf16[3328,128]{1,0:T(8,128)(2,1)S(1)}, u32[]{:S(2)}, u32[]{:S(2)}) collective-permute-start(bf16[3328,128]{1,0:T(8,128)(2,1)} %get-tuple-element.191), channel_id=1, source_target_pairs={{0,16},{1,65},{2,18},{3,67},{4,20},{5,69},{6,22},{7,71},{8,24},{9,... | collective-permute-start | bytes 2555912 | tf_op jit(solution)/shard_map/ppermute | solution.py:30
  132.2 22.4 %collective-permute-start.49 = (bf16[3328,128]{1,0:T(8,128)(2,1)}, bf16[3328,128]{1,0:T(8,128)(2,1)S(1)}, u32[]{:S(2)}, u32[]{:S(2)}) collective-permute-start(bf16[3328,128]{1,0:T(8,128)(2,1)} %get-tuple-element.192), channel_id=1, source_target_pairs={{0,8},{1,33},{2,10},{3,35},{4,12},{5,37},{6,14},{7,39},{8,16},{9,4... | collective-permute-start | bytes 2555912 | tf_op jit(solution)/shard_map/ppermute | solution.py:30
  158.7 12.3 %collective-permute-start.50 = (bf16[2320,128]{1,0:T(8,128)(2,1)S(1)}, bf16[2320,128]{1,0:T(8,128)(2,1)S(1)}, u32[]{:S(2)}, u32[]{:S(2)}) collective-permute-start(bf16[2320,128]{1,0:T(8,128)(2,1)S(1)} %get-tuple-element.194), channel_id=1, source_target_pairs={{0,96},{1,25},{2,98},{3,27},{4,100},{5,29},{6,102},{7,31},{8,104},... | collective-permute-start | bytes 1781768 | tf_op jit(solution)/shard_map/ppermute | solution.py:30
  162.5 11.5 %collective-permute-start.51 = (bf16[2320,128]{1,0:T(8,128)(2,1)S(1)}, bf16[2320,128]{1,0:T(8,128)(2,1)S(1)}, u32[]{:S(2)}, u32[]{:S(2)}) collective-permute-start(bf16[2320,128]{1,0:T(8,128)(2,1)S(1)} %get-tuple-element.195), channel_id=1, source_target_pairs={{0,64},{1,17},{2,66},{3,19},{4,68},{5,21},{6,70},{7,23},{8,72},{9,... | collective-permute-start | bytes 1781768 | tf_op jit(solution)/shard_map/ppermute | solution.py:30
  165.1 15.1 %collective-permute-start.52 = (bf16[2320,128]{1,0:T(8,128)(2,1)S(1)}, bf16[2320,128]{1,0:T(8,128)(2,1)S(1)}, u32[]{:S(2)}, u32[]{:S(2)}) collective-permute-start(bf16[2320,128]{1,0:T(8,128)(2,1)S(1)} %get-tuple-element.196), channel_id=1, source_target_pairs={{0,32},{1,9},{2,34},{3,11},{4,36},{5,13},{6,38},{7,15},{8,40},{9,1... | collective-permute-start | bytes 1781768 | tf_op jit(solution)/shard_map/ppermute | solution.py:30
  (42 other events, 296.3 us)

commit v6 on v5

--- a/solution.py
+++ b/solution.py
@@ -53,16 +53,13 @@
 
 
 def ring_gather(value, along):
-    return [value, along(value, ahead(-1)), along(value, ahead(2)), along(value, ahead(1))]
+    after, before, across = [along(value, ahead(step)) for step in (-1, 1, 2)]
+    return [value, after, across, before]
 
 
 def ring_swap(pieces, along):
-    return [
-        pieces[0],
-        along(pieces[3], ahead(-1)),
-        along(pieces[2], ahead(2)),
-        along(pieces[1], ahead(1)),
-    ]
+    after, before = along(pieces[3], ahead(-1)), along(pieces[1], ahead(1))
+    return [pieces[0], after, along(pieces[2], ahead(2)), before]
 
 
 def total_of(pieces):
@@ -110,8 +107,10 @@
     place = jnp.where(outer == 0, code.astype(F32), far)
     place = count(same & first_c, column(place))
     place = jnp.where(valid, place, 0.0).astype(I32)
-    pad = jnp.zeros((5, slots), I32)
-    tables[...] = jnp.concatenate([row_place, place, dense_place, pad], axis=0)
+    second = (rows >> 3) & 1
+    source = (1 - second) * 64 + ((row_place & 64) >> 1) + (row_place & 31)
+    pad = jnp.zeros((4, slots), I32)
+    tables[...] = jnp.concatenate([row_place, place, dense_place, source, pad], axis=0)
 
     key = column(jnp.where(first & (rank < CAP), outer_f * LANES + rank, -1.0))
     wanted = count(key == lane, column(code.astype(F32)))
@@ -135,12 +134,11 @@
     )(at_row, at_col, live, rows.reshape(1, slots), cols.reshape(1, slots))
 
 
-def products_kernel(live, tables, tiles_ref, *refs, spans, outs, contract, in_row, out_row):
+def products_kernel(
+    live, tables, tiles_ref, *refs, spans, outs, contract, in_row, out_row, tailed
+):
     n = len(spans)
-    sources, out_refs, (tiles, held, total, sems) = refs[:n], refs[n:-4], refs[-4:]
-    if len(out_refs) > len(outs):
-        out_refs[-1][...] = out_refs[0][...]
-        out_refs = out_refs[1:-1]
+    sources, out_refs, (tiles, held, total, tails, sems) = refs[:n], refs[n:-5], refs[-5:]
     copies = [pltpu.make_async_copy(tiles_ref, tiles, sems.at[n])]
     start = 0
     for k, (ref, rows) in enumerate(zip(sources, spans)):
@@ -150,6 +148,9 @@
             )
         )
         start += rows
+    for k in range(tailed):
+        tail = sources[k].at[pl.ds(spans[k], tails.shape[1])]
+        copies.append(pltpu.make_async_copy(tail, tails.at[k], sems.at[n + 1 + k]))
     for copy in copies:
         copy.start()
 
@@ -162,6 +163,11 @@
     lax.fori_loop(0, total.shape[0] // 4, clear, 0)
     for copy in copies:
         copy.wait()
+    if tailed:
+        summed = jnp.sum(tails[...].astype(F32), axis=0)
+        lines = summed.shape[0] // 2
+        out_refs[-1][:, :T] = summed[:lines]
+        out_refs[-1][:, T:] = summed[lines:]
 
     def group(number, carry):
         products = []
@@ -191,7 +197,8 @@
         start += blocks
 
 
-def products(live, tables, in_row, out_row, tiles, sources, spans, outs, contract, passed=()):
+def products(live, tables, in_row, out_row, tiles, sources, spans, outs, contract, tailed=0):
+    lines = sources[0].shape[0] - spans[0] if tailed else 16
     kernel = functools.partial(
         products_kernel,
         spans=spans,
@@ -199,39 +206,45 @@
         contract=contract,
         in_row=in_row,
         out_row=out_row,
+        tailed=tailed,
     )
     return pl.pallas_call(
         kernel,
         out_shape=[jax.ShapeDtypeStruct((n * T, T), BF16) for n in outs]
-        + [jax.ShapeDtypeStruct(p.shape, p.dtype) for p in passed],
-        in_specs=[SMEM] * 2 + [ANY] * (1 + len(sources)) + [VMEM] * len(passed),
-        out_specs=[VMEM] * (len(outs) + len(passed)),
+        + ([jax.ShapeDtypeStruct((lines // 2, 2 * T), F32)] if tailed else []),
+        in_specs=[SMEM] * 2 + [ANY] * (1 + len(sources)),
+        out_specs=[VMEM] * (len(outs) + (tailed > 0)),
         scratch_shapes=[
             pltpu.VMEM(tiles.shape, BF16),
             pltpu.VMEM((sum(spans), T), BF16),
             pltpu.VMEM((sum(outs), T, T), F32),
-            pltpu.SemaphoreType.DMA((len(spans) + 1,)),
+            pltpu.VMEM((max(tailed, 1), lines, T), BF16),
+            pltpu.SemaphoreType.DMA((len(spans) + 1 + tailed,)),
         ],
         compiler_params=PARAMS,
-    )(live, tables, tiles, *sources, *passed)
+    )(live, tables, tiles, *sources)
 
 
 def pack_kernel(*refs):
-    pieces, metas, sends, (said, lists, counts), (held, words, table, sems) = (
+    pieces, metas, sends, (said, lists, counts), (held, heard, words, table, sems) = (
         refs[:4],
         refs[4:8],
         refs[8:11],
         refs[11:14],
         refs[14:],
     )
+    fetches = [pltpu.make_async_copy(p, heard.at[k], sems.at[k + 4]) for k, p in enumerate(metas)]
     copies = [pltpu.make_async_copy(p, held.at[k], sems.at[k]) for k, p in enumerate(pieces)]
-    for copy in copies:
+    for copy in fetches + copies:
         copy.start()
+    for copy in fetches:
+        copy.wait()
+    told = [heard[k].astype(F32)[:8] for k in range(4)]
     for n in range(3):
-        words[pl.ds(n * 8, 8)] = metas[n + 1][...].astype(F32)[:8].astype(I32)
-    fetch = pltpu.make_async_copy(words, table, sems.at[4])
+        words[pl.ds(n * 8, 8)] = told[n + 1].astype(I32)
+    fetch = pltpu.make_async_copy(words, table, sems.at[8])
     fetch.start()
-    over = functools.reduce(jnp.maximum, [ref[...].astype(F32)[2:3] for ref in metas])
+    over = functools.reduce(jnp.maximum, told)[2:3]
     said[...] = jnp.broadcast_to(over, (8, T))
     fetch.wait()
     for copy in copies:
@@ -256,13 +269,14 @@
         out_shape=[jax.ShapeDtypeStruct((CAP * T, T), BF16)] * 3
         + [jax.ShapeDtypeStruct((8, T), F32)]
         + [jax.ShapeDtypeStruct((3 * CAP,), I32), jax.ShapeDtypeStruct((3,), I32)],
-        in_specs=[ANY] * 4 + [VMEM] * 4,
+        in_specs=[ANY] * 8,
         out_specs=[VMEM] * 4 + [SMEM] * 2,
         scratch_shapes=[
             pltpu.VMEM((4,) + pieces[0].shape, BF16),
+            pltpu.VMEM((4, META, T), BF16),
             pltpu.VMEM((24, T), I32),
             pltpu.SMEM((24, T), I32),
-            pltpu.SemaphoreType.DMA((5,)),
+            pltpu.SemaphoreType.DMA((9,)),
         ],
         compiler_params=PARAMS,
     )(*pieces, *metas)
@@ -352,12 +366,14 @@
     )(*pieces, sums)
 
 
-def dense_kernel(*refs):
-    parts, (grad, weight, offset), (hidden, projected, sums) = refs[:5], refs[5:8], refs[-3:]
+def dense_kernel(*refs, step):
+    parts, (grad, weight, offset), rest = refs[:5], refs[5:8], refs[8:]
+    hidden, projected, sums = rest[-3:]
+    second = len(rest) > 3
 
     @pl.when(pl.program_id(0) == 0)
     def _():
-        sums[...] = refs[9][...] if len(refs) > 11 else jnp.zeros_like(sums)
+        sums[...] = rest[1][...] if second else jnp.zeros_like(sums)
 
     mixed = total_of([ref[...] for ref in parts])
     high = mixed.astype(BF16)
@@ -368,7 +384,7 @@
     s = jax.nn.sigmoid(pre)
     hidden[...] = (pre * s).astype(BF16)
     slope = (grad[...].astype(F32) * s * (1.0 + pre * (1.0 - s))).astype(BF16)
-    projected[...] = lax.dot_general(
+    projected[pl.ds(pl.multiple_of(pl.program_id(0) * step, step), step)] = lax.dot_general(
         slope, w, (((1,), (1,)), ((), ())), preferred_element_type=F32
     ).astype(BF16)
     over_rows = (((0,), (0,)), ((), ()))
@@ -377,31 +393,38 @@
     ) + lax.dot_general(low, slope, over_rows, preferred_element_type=F32)
     sums[T:] += jnp.sum(slope.astype(F32).reshape(-1, 8, slope.shape[1]), axis=0)
 
+    @pl.when((pl.program_id(0) == pl.num_programs(0) - 1) & second)
+    def _():
+        lines = sums.shape[0]
+        for k in range(2 if second else 0):
+            part = sums[:, k * T : (k + 1) * T].astype(BF16)
+            projected[pl.ds(projected.shape[0] - (2 - k) * lines, lines)] = part
+
 
 def dense(parts, grad, weight, offset, part, before):
     width, rows = weight.shape[1], grad.shape[0]
     step = 512
     steps = rows // 2 // step
     shift = part * steps
+    tail = 2 * (T + 8) if before else 0
     half = pl.BlockSpec((step, T), lambda i: (i, 0))
     full = pl.BlockSpec((step, width), lambda i: (i + shift, 0))
-    whole = pl.BlockSpec((T + 8, width), lambda i: (0, 0))
+
+    def whole(*shape):
+        return pl.BlockSpec(shape, lambda i: (0, 0))
+
     return pl.pallas_call(
-        dense_kernel,
+        functools.partial(dense_kernel, step=step),
         grid=(steps,),
         out_shape=[
             jax.ShapeDtypeStruct((rows, width), BF16),
-            jax.ShapeDtypeStruct((rows // 2, T), BF16),
+            jax.ShapeDtypeStruct((rows // 2 + tail, T), BF16),
             jax.ShapeDtypeStruct((T + 8, width), F32),
         ],
         in_specs=[half] * 5
-        + [
-            full,
-            pl.BlockSpec((T, width), lambda i: (0, 0)),
-            pl.BlockSpec((1, width), lambda i: (0, 0)),
-        ]
-        + ([ANY, whole] + [ANY] * (len(before) - 2) if before else []),
-        out_specs=[full, half, whole],
+        + [full, whole(T, width), whole(1, width)]
+        + ([ANY, whole(T + 8, width), ANY] if before else []),
+        out_specs=[full, whole(rows // 2 + tail, T), whole(T + 8, width)],
         input_output_aliases={8: 0} if before else {},
         compiler_params=PARAMS,
     )(*parts, grad, weight, offset, *before)
@@ -447,22 +470,21 @@
             parts, grad_hidden, weight, offset.reshape(1, -1), part, before
         )
         here = ring_gather(projected, along_y)
-        own += here
-        others += [other_core(piece) for piece in here]
-        before = (hidden, sums, others[0])
-
-    sums = total_of(ring_gather(sums + other_core(sums), along_outer))
-
-    gathered, spans, outs = others + own, (part_rows,) * 16, (64,) + (CAP,) * 3
+        own.append(here)
+        others.append([other_core(piece) for piece in here])
+        before = (hidden, sums, others[0][0])
+
+    gathered = others[1] + own[1] + others[0] + own[0]
+    spans, outs = (part_rows,) * 16, (64,) + (CAP,) * 3
     here, *parts, sums = products(
-        live, tables, 0, 1, tiles, gathered, spans, outs, (0,), (sums,)
+        live, tables, 3, 1, tiles, gathered, spans, outs, (0,), tailed=8
     )
-    sums = total_of(ring_gather(sums, along_y))
+    sums = total_of(ring_gather(sums, along_outer))
     rounded = jnp.concatenate([sums[:, :T], sums[:, T:]]).astype(BF16)
     parts = ring_swap([None] + parts, along_outer)[1:]
 
     def backward_all(here, rounded, parts, gathered):
-        outs = products(live, tables, 0, 2, tiles, gathered, spans, (64,) * 4, (0,))
+        outs = products(live, tables, 3, 2, tiles, gathered, spans, (64,) * 4, (0,))
         mine = total_of(ring_swap(outs, along_outer)).reshape(4, nodes_here, T)
         far = [jnp.concatenate([mine[d].astype(BF16), rounded]) for d in (1, 2, 3)]
         return [mine[0]] + far

time: 184 us -> 188 us (1.022)
  waiting for transfers between devices: 74.7 us -> 81.7 us
  other arithmetic: 6.72 us -> 4.23 us
    ppermute x21, waiting for transfers between devices: 44.9 us -> 52.9 us  [along_xz(): return lax.ppermute(value, ('row', 'col'), pairs)]
    ppermute x21, starting transfers between devices: 34.2 us -> 39.8 us  [along_xz(): return lax.ppermute(value, ('row', 'col'), pairs)]
    ppermute x15 -> x12, starting transfers between devices: 24.2 us -> 18.8 us  [along_y(): return lax.ppermute(value, 'col', pairs)]
    ppermute x15 -> x12, waiting for transfers between devices: 26.5 us -> 23.4 us  [along_y(): return lax.ppermute(value, 'col', pairs)]
    pallas_call x2, Pallas kernels: 16 us -> 13.6 us  [products(): pl.pallas_call(kernel, out_shape=[jax.ShapeDtypeStruct((n * T, T), BF16)...]
    ppermute x11 -> x10, waiting for transfers between devices: 3.31 us -> 5.4 us  [other_core(): return lax.ppermute(value, 'col', pairs)]
  transfers between devices with their start and end apart: 47 -> 43, of which waited for: 22 -> 21; matrix products, arithmetic and copies ran while one was open for 4% -> 3% of each run, Pallas kernels for 5% -> 5%
where the time goes in v6:
time: 188 us
  waiting for transfers between devices  81.7 us (43%)
  starting transfers between devices  60.2 us (32%)
  Pallas kernels  33.5 us (18%)
  local copies, waits for them, and re-layouts  6.08 us (3%)
  other arithmetic  4.23 us (2%)
  between operations  2.16 us (1%)
    ppermute x21, waiting for transfers between devices, along_xz(): return lax.ppermute(value, ('row', 'col'), pairs)  52.9 us
    ppermute x21, starting transfers between devices, along_xz(): return lax.ppermute(value, ('row', 'col'), pairs)  39.8 us
    ppermute x12, waiting for transfers between devices, along_y(): return lax.ppermute(value, 'col', pairs)  23.4 us
    ppermute x12, starting transfers between devices, along_y(): return lax.ppermute(value, 'col', pairs)  18.8 us
    pallas_call x2, Pallas kernels, products(): pl.pallas_call(kernel, out_shape=[jax.ShapeDtypeStruct((n * T, T), BF16)...  13.6 us
    pallas_call x2, Pallas kernels, dense(): pl.pallas_call(functools.partial(dense_kernel, step=step), grid=(steps,),...  7.19 us
    ppermute x10, waiting for transfers between devices, other_core(): return lax.ppermute(value, 'col', pairs)  5.4 us
    pallas_call x1, Pallas kernels, combine(): pl.pallas_call(combine_kernel, out_shape=[jax.ShapeDtypeStruct((rows, T),...  4.67 us
  transfers between devices with their start and end apart: 43, of which 21 were waited for; matrix products, arithmetic and copies ran while one was open for 3% of the time, Pallas kernels for 5%

profile of v6, /device:TPU:0, one launch (start us, length us, event | category | flops | bytes accessed | tf_op | source)
XLA Modules:
  0.0 187.9 jit_solution(16256151015122968371)
XLA Ops:
  2.3 2.7 %collective-permute-start.7 = (bf16[2048,128]{1,0:T(8,128)(2,1)}, bf16[2048,128]{1,0:T(8,128)(2,1)S(1)}, u32[]{:S(2)}, u32[]{:S(2)}) collective-permute-start(bf16[2048,128]{1,0:T(8,128)(2,1)} %refs_0_.1), channel_id=1, source_target_pairs={{0,64},{1,17},{2,66},{3,19},{4,68},{5,21},{6,70},{7,23},{8,72},{9,... | collective-permute-start | bytes 1572872 | tf_op jit(solution)/shard_map/ppermute | solution.py:30
  10.6 3.6 %collective-permute-start.10 = (bf16[16,128]{1,0:T(8,128)(2,1)}, bf16[16,128]{1,0:T(8,128)(2,1)S(1)}, u32[]{:S(2)}, u32[]{:S(2)}) collective-permute-start(bf16[16,128]{1,0:T(8,128)(2,1)} %get-tuple-element.169.refs_4_), channel_id=1, source_target_pairs={{0,16},{1,65},{2,18},{3,67},{4,20},{5,69},{6,22},{7,71},{8,24},{9,... | collective-permute-start | bytes 12296 | tf_op jit(solution)/shard_map/ppermute | solution.py:30
  19.3 3.5 %shard_map.112 = (bf16[3328,128]{1,0:T(8,128)(2,1)}, bf16[3328,128]{1,0:T(8,128)(2,1)}, bf16[3328,128]{1,0:T(8,128)(2,1)}, f32[8,128]{1,0:T(8,128)}, s32[78]{0:T(128)S(1)}, /*index=5*/s32[3]{0:T(128)S(1)}) custom-call(bf16[2048,128]{1,0:T(8,128)(2,1)} %refs_0_.1, bf16[2048,128]{1,0:T(8,128)(2,1)} %collective-permute-done.6.refs_1_, ...), custom_call_target="tpu_custom_call" | custom-call | tf_op jit(solution)/shard_map/pallas_call | solution.py:267
  22.8 2.9 %collective-permute-start.15 = (bf16[3328,128]{1,0:T(8,128)(2,1)}, bf16[3328,128]{1,0:T(8,128)(2,1)S(1)}, u32[]{:S(2)}, u32[]{:S(2)}) collective-permute-start(bf16[3328,128]{1,0:T(8,128)(2,1)} %get-tuple-element.172), channel_id=1, source_target_pairs={{0,24},{1,97},{2,26},{3,99},{4,28},{5,101},{6,30},{7,103},{8,0},{9... | collective-permute-start | bytes 2555912 | tf_op jit(solution)/shard_map/ppermute | solution.py:30
  29.1 2.8 %collective-permute-start.13 = (f32[8,128]{1,0:T(8,128)}, f32[8,128]{1,0:T(8,128)S(1)}, u32[]{:S(2)}, u32[]{:S(2)}) collective-permute-start(f32[8,128]{1,0:T(8,128)} %get-tuple-element.170), channel_id=1, source_target_pairs={{0,64},{1,17},{2,66},{3,19},{4,68},{5,21},{6,70},{7,23},{8,72},{9,... | collective-permute-start | bytes 12296 | tf_op jit(solution)/shard_map/ppermute | solution.py:30
  31.9 5.8 %collective-permute-done.14 = f32[8,128]{1,0:T(8,128)S(1)} collective-permute-done((f32[8,128]{1,0:T(8,128)}, f32[8,128]{1,0:T(8,128)S(1)}, u32[]{:S(2)}, u32[]{:S(2)}) %collective-permute-start.14) | collective-permute-done | bytes 4128 | tf_op jit(solution)/shard_map/ppermute | solution.py:30
  37.7 3.9 %collective-permute-done.12 = f32[8,128]{1,0:T(8,128)S(1)} collective-permute-done((f32[8,128]{1,0:T(8,128)}, f32[8,128]{1,0:T(8,128)S(1)}, u32[]{:S(2)}, u32[]{:S(2)}) %collective-permute-start.12) | collective-permute-done | bytes 4128 | tf_op jit(solution)/shard_map/ppermute | solution.py:30
  45.5 3.8 %collective-permute-done.17 = bf16[3328,128]{1,0:T(8,128)(2,1)S(1)} collective-permute-done((bf16[3328,128]{1,0:T(8,128)(2,1)}, bf16[3328,128]{1,0:T(8,128)(2,1)S(1)}, u32[]{:S(2)}, u32[]{:S(2)}) %collective-permute-start.17) | collective-permute-done | bytes 852000 | tf_op jit(solution)/shard_map/ppermute | solution.py:30
  49.3 6.8 %conditional.2 = ((bf16[4096,128]{1,0:T(8,128)(2,1)}, bf16[4096,128]{1,0:T(8,128)(2,1)}, bf16[4096,128]{1,0:T(8,128)(2,1)}, bf16[4096,128]{1,0:T(8,128)(2,1)})) conditional(s32[]{:T(128)} %bitcast.5, (s32[1]{0:T(128)}, s32[8,64]{1,0:T(8,128)S(1)}, bf16[64,128,128]{2,1,0:T(8,128)(2,1)S(1)}, bf16[2048,128]{1,0:T(8,128)(2,1)}, ...), branch_computations={%region_0.0_spmd, %region_1.0_spmd} | conditional | bytes 62914800 | solution.py:456
  49.3 6.8 %branch_0_fun.2 = (bf16[4096,128]{1,0:T(8,128)(2,1)}, bf16[4096,128]{1,0:T(8,128)(2,1)}, bf16[4096,128]{1,0:T(8,128)(2,1)}, bf16[4096,128]{1,0:T(8,128)(2,1)}) custom-call(s32[1]{0:T(128)} %get-tuple-element.88.live, s32[8,64]{1,0:T(8,128)S(1)} %get-tuple-element.89.tables, bf16[64,128,128]{2,1,0:T(8,128)(2,1)S(1)} %get-tuple-element.90.tiles_ref, ...), custom_call_target="tpu_custom_call" | custom-call | tf_op jit(solution)/shard_map/cond/branch_0_fun/pallas_call | solution.py:211
  72.5 5.1 %collective-permute-done.24.refs_3_ = bf16[1024,128]{1,0:T(8,128)(2,1)S(1)} collective-permute-done((bf16[1024,128]{1,0:T(8,128)(2,1)S(1)}, bf16[1024,128]{1,0:T(8,128)(2,1)S(1)}, u32[]{:S(2)}, u32[]{:S(2)}) %collective-permute-start.24) | collective-permute-done | bytes 262176 | tf_op jit(solution)/shard_map/ppermute | solution.py:43
  78.5 3.5 %shard_map.113 = (bf16[2048,256]{1,0:T(8,128)(2,1)}, bf16[1024,128]{1,0:T(8,128)(2,1)S(1)}, f32[136,256]{1,0:T(8,128)}) custom-call(bf16[4096,128]{1,0:T(8,128)(2,1)S(1)} %copy-done.3, bf16[4096,128]{1,0:T(8,128)(2,1)} %copy-done.2, bf16[1024,128]{1,0:T(8,128)(2,1)} %copy-done.22, bf16[1024,128]{1,0:T(8,128)(2,1)} %copy-done.21, ...), custom_call_target="tpu_custom_call" | custom-call | tf_op jit(solution)/shard_map/pallas_call | solution.py:416
  89.5 3.7 %shard_map.114 = (bf16[2048,256]{1,0:T(8,128)(2,1)}, bf16[1296,128]{1,0:T(8,128)(2,1)S(1)}, f32[136,256]{1,0:T(8,128)}) custom-call(bf16[4096,128]{1,0:T(8,128)(2,1)S(1)} %copy-done.5, bf16[4096,128]{1,0:T(8,128)(2,1)} %copy-done.4, bf16[1024,128]{1,0:T(8,128)(2,1)} %copy-done.19, bf16[1024,128]{1,0:T(8,128)(2,1)} %copy-done.18, ...), custom_call_target="tpu_custom_call", output_to_operand_aliasing={{0}: (8, {})} | custom-call | tf_op jit(solution)/shard_map/pallas_call | solution.py:416
  101.6 5.2 %collective-permute-done.32.refs_7_ = bf16[1296,128]{1,0:T(8,128)(2,1)S(1)} collective-permute-done((bf16[1296,128]{1,0:T(8,128)(2,1)S(1)}, bf16[1296,128]{1,0:T(8,128)(2,1)S(1)}, u32[]{:S(2)}, u32[]{:S(2)}) %collective-permute-start.32) | collective-permute-done | bytes 331808 | tf_op jit(solution)/shard_map/ppermute | solution.py:43
  106.9 6.6 %collective-permute-done.30.refs_6_ = bf16[1296,128]{1,0:T(8,128)(2,1)S(1)} collective-permute-done((bf16[1296,128]{1,0:T(8,128)(2,1)S(1)}, bf16[1296,128]{1,0:T(8,128)(2,1)S(1)}, u32[]{:S(2)}, u32[]{:S(2)}) %collective-permute-start.30) | collective-permute-done | bytes 331808 | tf_op jit(solution)/shard_map/ppermute | solution.py:43
  116.7 6.8 %shard_map.115 = (bf16[8192,128]{1,0:T(8,128)(2,1)S(1)}, bf16[3328,128]{1,0:T(8,128)(2,1)}, bf16[3328,128]{1,0:T(8,128)(2,1)}, bf16[3328,128]{1,0:T(8,128)(2,1)}, f32[136,256]{1,0:T(8,128)}) custom-call(s32[1]{0:T(128)} %bitcast.10.live, s32[8,64]{1,0:T(8,128)S(1)} %get-tuple-element.171.tables, bf16[64,128,128]{2,1,0:T(8,128)(2,1)S(1)} %bitcast.13, ...), custom_call_target="tpu_custom_call" | custom-call | tf_op jit(solution)/shard_map/pallas_call | solution.py:211
  124.4 3.8 %collective-permute-start.43 = (bf16[3328,128]{1,0:T(8,128)(2,1)}, bf16[3328,128]{1,0:T(8,128)(2,1)S(1)}, u32[]{:S(2)}, u32[]{:S(2)}) collective-permute-start(bf16[3328,128]{1,0:T(8,128)(2,1)} %get-tuple-element.188), channel_id=1, source_target_pairs={{0,24},{1,97},{2,26},{3,99},{4,28},{5,101},{6,30},{7,103},{8,0},{9... | collective-permute-start | bytes 2555912 | tf_op jit(solution)/shard_map/ppermute | solution.py:30
  134.4 18.9 %collective-permute-done.41 = f32[136,256]{1,0:T(8,128)S(1)} collective-permute-done((f32[136,256]{1,0:T(8,128)}, f32[136,256]{1,0:T(8,128)S(1)}, u32[]{:S(2)}, u32[]{:S(2)}) %collective-permute-start.41) | collective-permute-done | bytes 139296 | tf_op jit(solution)/shard_map/ppermute | solution.py:30
  154.9 6.8 %conditional.3 = ((f32[2048,128]{1,0:T(8,128)}, bf16[2320,128]{1,0:T(8,128)(2,1)}, bf16[2320,128]{1,0:T(8,128)(2,1)}, bf16[2320,128]{1,0:T(8,128)(2,1)})) conditional(s32[]{:T(128)} %bitcast.5, (s32[78]{0:T(128)S(1)}, s32[3]{0:T(128)S(1)}, bf16[8192,128]{1,0:T(8,128)(2,1)S(1)}, bf16[272,128]{1,0:T(8,128)(2,1)S(1)}, bf16[3328,128]{1,0:T(8,128)(2,1)S(1)}, ...), branch_computations={%region_2.0_spmd, %region_3.0_spmd} | conditional | flops 11358208 | bytes 48513184 | solution.py:495
  157.0 4.7 %branch_0_fun.3 = (f32[2048,128]{1,0:T(8,128)}, bf16[2320,128]{1,0:T(8,128)(2,1)}, bf16[2320,128]{1,0:T(8,128)(2,1)}, bf16[2320,128]{1,0:T(8,128)(2,1)}) custom-call(s32[78]{0:T(128)S(1)} %get-tuple-element.105.lists, s32[3]{0:T(128)S(1)} %get-tuple-element.106.counts, bf16[8192,128]{1,0:T(8,128)(2,1)S(1)} %get-tuple-element.107.own_ref, ...), custom_call_target="tpu_custom_call" | custom-call | tf_op jit(solution)/shard_map/cond/branch_0_fun/pallas_call | solution.py:323
  161.7 4.4 %collective-permute-start.46 = (bf16[2320,128]{1,0:T(8,128)(2,1)}, bf16[2320,128]{1,0:T(8,128)(2,1)S(1)}, u32[]{:S(2)}, u32[]{:S(2)}) collective-permute-start(bf16[2320,128]{1,0:T(8,128)(2,1)} %get-tuple-element.192), channel_id=1, source_target_pairs={{0,96},{1,25},{2,98},{3,27},{4,100},{5,29},{6,102},{7,31},{8,104},... | collective-permute-start | bytes 1781768 | tf_op jit(solution)/shard_map/ppermute | solution.py:30
  168.5 11.8 %collective-permute-done.46.refs_1_ = bf16[2320,128]{1,0:T(8,128)(2,1)S(1)} collective-permute-done((bf16[2320,128]{1,0:T(8,128)(2,1)}, bf16[2320,128]{1,0:T(8,128)(2,1)S(1)}, u32[]{:S(2)}, u32[]{:S(2)}) %collective-permute-start.46) | collective-permute-done | bytes 593952 | tf_op jit(solution)/shard_map/ppermute | solution.py:30
  180.3 3.8 %collective-permute-done.48.refs_3_ = bf16[2320,128]{1,0:T(8,128)(2,1)S(1)} collective-permute-done((bf16[2320,128]{1,0:T(8,128)(2,1)}, bf16[2320,128]{1,0:T(8,128)(2,1)S(1)}, u32[]{:S(2)}, u32[]{:S(2)}) %collective-permute-start.48) | collective-permute-done | bytes 593952 | tf_op jit(solution)/shard_map/ppermute | solution.py:30
  185.0 3.0 %shard_map.116 = (f32[2048,128]{1,0:T(8,128)}, f32[128,256]{1,0:T(8,128)}, f32[1,256]{1,0:T(1,128)}) custom-call(f32[2048,128]{1,0:T(8,128)} %get-tuple-element.191.refs_0_, bf16[2320,128]{1,0:T(8,128)(2,1)} %copy-done.14, bf16[2320,128]{1,0:T(8,128)(2,1)} %copy-done.15, bf16[2320,128]{1,0:T(8,128)(2,1)} %copy-done.16, f32[136,256]{1,0:T(8,128)} %get-tuple-element.201.refs_4_), custom_call_target="tpu_custom_call" | custom-call | tf_op jit(solution)/shard_map/pallas_call | solution.py:356
  (123 shorter events, 68.5 us)
Async XLA Ops:
  0.6 18.1 %collective-permute-start.8 = (bf16[2048,128]{1,0:T(8,128)(2,1)}, bf16[2048,128]{1,0:T(8,128)(2,1)S(1)}, u32[]{:S(2)}, u32[]{:S(2)}) collective-permute-start(bf16[2048,128]{1,0:T(8,128)(2,1)} %refs_0_.1), channel_id=1, source_target_pairs={{0,32},{1,9},{2,34},{3,11},{4,36},{5,13},{6,38},{7,15},{8,40},{9,1... | collective-permute-start | bytes 1572872 | tf_op jit(solution)/shard_map/ppermute | solution.py:30
  2.3 16.4 %collective-permute-start.7 = (bf16[2048,128]{1,0:T(8,128)(2,1)}, bf16[2048,128]{1,0:T(8,128)(2,1)S(1)}, u32[]{:S(2)}, u32[]{:S(2)}) collective-permute-start(bf16[2048,128]{1,0:T(8,128)(2,1)} %refs_0_.1), channel_id=1, source_target_pairs={{0,64},{1,17},{2,66},{3,19},{4,68},{5,21},{6,70},{7,23},{8,72},{9,... | collective-permute-start | bytes 1572872 | tf_op jit(solution)/shard_map/ppermute | solution.py:30
  5.0 13.7 %collective-permute-start.6 = (bf16[2048,128]{1,0:T(8,128)(2,1)}, bf16[2048,128]{1,0:T(8,128)(2,1)}, u32[]{:S(2)}, u32[]{:S(2)}) collective-permute-start(bf16[2048,128]{1,0:T(8,128)(2,1)} %refs_0_.1), channel_id=1, source_target_pairs={{0,96},{1,25},{2,98},{3,27},{4,100},{5,29},{6,102},{7,31},{8,104},... | collective-permute-start | bytes 1572872 | tf_op jit(solution)/shard_map/ppermute | solution.py:30
  22.8 22.6 %collective-permute-start.15 = (bf16[3328,128]{1,0:T(8,128)(2,1)}, bf16[3328,128]{1,0:T(8,128)(2,1)S(1)}, u32[]{:S(2)}, u32[]{:S(2)}) collective-permute-start(bf16[3328,128]{1,0:T(8,128)(2,1)} %get-tuple-element.172), channel_id=1, source_target_pairs={{0,24},{1,97},{2,26},{3,99},{4,28},{5,101},{6,30},{7,103},{8,0},{9... | collective-permute-start | bytes 2555912 | tf_op jit(solution)/shard_map/ppermute | solution.py:30
  25.7 19.7 %collective-permute-start.16 = (bf16[3328,128]{1,0:T(8,128)(2,1)}, bf16[3328,128]{1,0:T(8,128)(2,1)S(1)}, u32[]{:S(2)}, u32[]{:S(2)}) collective-permute-start(bf16[3328,128]{1,0:T(8,128)(2,1)} %get-tuple-element.173), channel_id=1, source_target_pairs={{0,16},{1,65},{2,18},{3,67},{4,20},{5,69},{6,22},{7,71},{8,24},{9,... | collective-permute-start | bytes 2555912 | tf_op jit(solution)/shard_map/ppermute | solution.py:30
  26.3 22.9 %collective-permute-start.17 = (bf16[3328,128]{1,0:T(8,128)(2,1)}, bf16[3328,128]{1,0:T(8,128)(2,1)S(1)}, u32[]{:S(2)}, u32[]{:S(2)}) collective-permute-start(bf16[3328,128]{1,0:T(8,128)(2,1)} %get-tuple-element.174), channel_id=1, source_target_pairs={{0,8},{1,33},{2,10},{3,35},{4,12},{5,37},{6,14},{7,39},{8,16},{9,4... | collective-permute-start | bytes 2555912 | tf_op jit(solution)/shard_map/ppermute | solution.py:30
  63.4 14.2 %collective-permute-start.24 = (bf16[1024,128]{1,0:T(8,128)(2,1)S(1)}, bf16[1024,128]{1,0:T(8,128)(2,1)S(1)}, u32[]{:S(2)}, u32[]{:S(2)}) collective-permute-start(bf16[1024,128]{1,0:T(8,128)(2,1)S(1)} %get-tuple-element.209), channel_id=1, source_target_pairs={{0,4},{1,5},{2,6},{3,7},{4,0},{5,1},{6,2},{7,3},{8,12},{9,13},{10,... | collective-permute-start | bytes 786440 | tf_op jit(solution)/shard_map/ppermute | solution.py:43
  66.4 17.9 %collective-permute-start.21 = (bf16[1024,128]{1,0:T(8,128)(2,1)S(1)}, bf16[1024,128]{1,0:T(8,128)(2,1)S(1)}, u32[]{:S(2)}, u32[]{:S(2)}) collective-permute-start(bf16[1024,128]{1,0:T(8,128)(2,1)S(1)} %get-tuple-element.211), channel_id=1, source_target_pairs={{0,2},{1,3},{2,4},{3,5},{4,6},{5,7},{6,0},{7,1},{8,10},{9,11},{10,... | collective-permute-start | bytes 786440 | tf_op jit(solution)/shard_map/ppermute | solution.py:43
  67.1 21.4 %collective-permute-start.20 = (bf16[1024,128]{1,0:T(8,128)(2,1)S(1)}, bf16[1024,128]{1,0:T(8,128)(2,1)S(1)}, u32[]{:S(2)}, u32[]{:S(2)}) collective-permute-start(bf16[1024,128]{1,0:T(8,128)(2,1)S(1)} %get-tuple-element.212), channel_id=1, source_target_pairs={{0,4},{1,5},{2,6},{3,7},{4,0},{5,1},{6,2},{7,3},{8,12},{9,13},{10,... | collective-permute-start | bytes 786440 | tf_op jit(solution)/shard_map/ppermute | solution.py:43
  71.7 17.2 %collective-permute-start.19 = (bf16[1024,128]{1,0:T(8,128)(2,1)S(1)}, bf16[1024,128]{1,0:T(8,128)(2,1)S(1)}, u32[]{:S(2)}, u32[]{:S(2)}) collective-permute-start(bf16[1024,128]{1,0:T(8,128)(2,1)S(1)} %get-tuple-element.213), channel_id=1, source_target_pairs={{0,6},{1,7},{2,0},{3,1},{4,2},{5,3},{6,4},{7,5},{8,14},{9,15},{10,... | collective-permute-start | bytes 786440 | tf_op jit(solution)/shard_map/ppermute | solution.py:43
  82.1 15.2 %collective-permute-start.38 = (bf16[1024,128]{1,0:T(8,128)(2,1)S(1)}, bf16[1024,128]{1,0:T(8,128)(2,1)S(1)}, u32[]{:S(2)}, u32[]{:S(2)}) collective-permute-start(bf16[1024,128]{1,0:T(8,128)(2,1)S(1)} %get-tuple-element.181.refs_12_), channel_id=1, source_target_pairs={{0,2},{1,3},{2,4},{3,5},{4,6},{5,7},{6,0},{7,1},{8,10},{9,11},{10,... | collective-permute-start | bytes 786440 | tf_op jit(solution)/shard_map/ppermute | solution.py:43
  84.3 15.5 %collective-permute-start.36 = (bf16[1024,128]{1,0:T(8,128)(2,1)S(1)}, bf16[1024,128]{1,0:T(8,128)(2,1)S(1)}, u32[]{:S(2)}, u32[]{:S(2)}) collective-permute-start(bf16[1024,128]{1,0:T(8,128)(2,1)S(1)} %get-tuple-element.181.refs_12_), channel_id=1, source_target_pairs={{0,4},{1,5},{2,6},{3,7},{4,0},{5,1},{6,2},{7,3},{8,12},{9,13},{10,... | collective-permute-start | bytes 786440 | tf_op jit(solution)/shard_map/ppermute | solution.py:43
  95.0 18.5 %collective-permute-start.30 = (bf16[1296,128]{1,0:T(8,128)(2,1)S(1)}, bf16[1296,128]{1,0:T(8,128)(2,1)S(1)}, u32[]{:S(2)}, u32[]{:S(2)}) collective-permute-start(bf16[1296,128]{1,0:T(8,128)(2,1)S(1)} %get-tuple-element.185.refs_4_), channel_id=1, source_target_pairs={{0,4},{1,5},{2,6},{3,7},{4,0},{5,1},{6,2},{7,3},{8,12},{9,13},{10,... | collective-permute-start | bytes 995336 | tf_op jit(solution)/shard_map/ppermute | solution.py:43
  97.3 16.2 %collective-permute-start.28 = (bf16[1296,128]{1,0:T(8,128)(2,1)S(1)}, bf16[1296,128]{1,0:T(8,128)(2,1)S(1)}, u32[]{:S(2)}, u32[]{:S(2)}) collective-permute-start(bf16[1296,128]{1,0:T(8,128)(2,1)S(1)} %get-tuple-element.185.refs_4_), channel_id=1, source_target_pairs={{0,6},{1,7},{2,0},{3,1},{4,2},{5,3},{6,4},{7,5},{8,14},{9,15},{10,... | collective-permute-start | bytes 995336 | tf_op jit(solution)/shard_map/ppermute | solution.py:43
  100.1 13.9 %collective-permute-start.37 = (bf16[1024,128]{1,0:T(8,128)(2,1)S(1)}, bf16[1024,128]{1,0:T(8,128)(2,1)S(1)}, u32[]{:S(2)}, u32[]{:S(2)}) collective-permute-start(bf16[1024,128]{1,0:T(8,128)(2,1)S(1)} %collective-permute-done.36.refs_14_), channel_id=1, source_target_pairs={{0,1},{1,0},{2,3},{3,2},{4,5},{5,4},{6,7},{7,6},{8,9},{9,8},{10,11... | collective-permute-start | bytes 786440 | tf_op jit(solution)/shard_map/ppermute | solution.py:48
  101.5 14.5 %collective-permute-start.27 = (bf16[1296,128]{1,0:T(8,128)(2,1)S(1)}, bf16[1296,128]{1,0:T(8,128)(2,1)S(1)}, u32[]{:S(2)}, u32[]{:S(2)}) collective-permute-start(bf16[1296,128]{1,0:T(8,128)(2,1)S(1)} %get-tuple-element.185.refs_4_), channel_id=1, source_target_pairs={{0,1},{1,0},{2,3},{3,2},{4,5},{5,4},{6,7},{7,6},{8,9},{9,8},{10,11... | collective-permute-start | bytes 995336 | tf_op jit(solution)/shard_map/ppermute | solution.py:48
  124.4 30.5 %collective-permute-start.43 = (bf16[3328,128]{1,0:T(8,128)(2,1)}, bf16[3328,128]{1,0:T(8,128)(2,1)S(1)}, u32[]{:S(2)}, u32[]{:S(2)}) collective-permute-start(bf16[3328,128]{1,0:T(8,128)(2,1)} %get-tuple-element.188), channel_id=1, source_target_pairs={{0,24},{1,97},{2,26},{3,99},{4,28},{5,101},{6,30},{7,103},{8,0},{9... | collective-permute-start | bytes 2555912 | tf_op jit(solution)/shard_map/ppermute | solution.py:30
  128.2 26.7 %collective-permute-start.44 = (bf16[3328,128]{1,0:T(8,128)(2,1)}, bf16[3328,128]{1,0:T(8,128)(2,1)S(1)}, u32[]{:S(2)}, u32[]{:S(2)}) collective-permute-start(bf16[3328,128]{1,0:T(8,128)(2,1)} %get-tuple-element.189), channel_id=1, source_target_pairs={{0,16},{1,65},{2,18},{3,67},{4,20},{5,69},{6,22},{7,71},{8,24},{9,... | collective-permute-start | bytes 2555912 | tf_op jit(solution)/shard_map/ppermute | solution.py:30
  129.6 25.3 %collective-permute-start.45 = (bf16[3328,128]{1,0:T(8,128)(2,1)}, bf16[3328,128]{1,0:T(8,128)(2,1)S(1)}, u32[]{:S(2)}, u32[]{:S(2)}) collective-permute-start(bf16[3328,128]{1,0:T(8,128)(2,1)} %get-tuple-element.190), channel_id=1, source_target_pairs={{0,8},{1,33},{2,10},{3,35},{4,12},{5,37},{6,14},{7,39},{8,16},{9,4... | collective-permute-start | bytes 2555912 | tf_op jit(solution)/shard_map/ppermute | solution.py:30
  131.0 22.3 %collective-permute-start.41 = (f32[136,256]{1,0:T(8,128)}, f32[136,256]{1,0:T(8,128)S(1)}, u32[]{:S(2)}, u32[]{:S(2)}) collective-permute-start(f32[136,256]{1,0:T(8,128)} %get-tuple-element.187), channel_id=1, source_target_pairs={{0,16},{1,65},{2,18},{3,67},{4,20},{5,69},{6,22},{7,71},{8,24},{9,... | collective-permute-start | bytes 417800 | tf_op jit(solution)/shard_map/ppermute | solution.py:30
  131.7 21.5 %collective-permute-start.40 = (f32[136,256]{1,0:T(8,128)}, f32[136,256]{1,0:T(8,128)S(1)}, u32[]{:S(2)}, u32[]{:S(2)}) collective-permute-start(f32[136,256]{1,0:T(8,128)} %get-tuple-element.187), channel_id=1, source_target_pairs={{0,24},{1,97},{2,26},{3,99},{4,28},{5,101},{6,30},{7,103},{8,0},{9... | collective-permute-start | bytes 417800 | tf_op jit(solution)/shard_map/ppermute | solution.py:30
  161.7 18.6 %collective-permute-start.46 = (bf16[2320,128]{1,0:T(8,128)(2,1)}, bf16[2320,128]{1,0:T(8,128)(2,1)S(1)}, u32[]{:S(2)}, u32[]{:S(2)}) collective-permute-start(bf16[2320,128]{1,0:T(8,128)(2,1)} %get-tuple-element.192), channel_id=1, source_target_pairs={{0,96},{1,25},{2,98},{3,27},{4,100},{5,29},{6,102},{7,31},{8,104},... | collective-permute-start | bytes 1781768 | tf_op jit(solution)/shard_map/ppermute | solution.py:30
  166.1 14.2 %collective-permute-start.47 = (bf16[2320,128]{1,0:T(8,128)(2,1)}, bf16[2320,128]{1,0:T(8,128)(2,1)S(1)}, u32[]{:S(2)}, u32[]{:S(2)}) collective-permute-start(bf16[2320,128]{1,0:T(8,128)(2,1)} %get-tuple-element.193), channel_id=1, source_target_pairs={{0,64},{1,17},{2,66},{3,19},{4,68},{5,21},{6,70},{7,23},{8,72},{9,... | collective-permute-start | bytes 1781768 | tf_op jit(solution)/shard_map/ppermute | solution.py:30
  168.5 15.7 %collective-permute-start.48 = (bf16[2320,128]{1,0:T(8,128)(2,1)}, bf16[2320,128]{1,0:T(8,128)(2,1)S(1)}, u32[]{:S(2)}, u32[]{:S(2)}) collective-permute-start(bf16[2320,128]{1,0:T(8,128)(2,1)} %get-tuple-element.194), channel_id=1, source_target_pairs={{0,32},{1,9},{2,34},{3,11},{4,36},{5,13},{6,38},{7,15},{8,40},{9,1... | collective-permute-start | bytes 1781768 | tf_op jit(solution)/shard_map/ppermute | solution.py:30
  (41 other events, 269.0 us)

commit v7 on v6

--- a/solution.py
+++ b/solution.py
@@ -11,7 +11,7 @@
 
 T = 128
 F32, BF16, I32 = jnp.float32, jnp.bfloat16, jnp.int32
-VMEM_BYTES = 56 * 1024 * 1024
+MIB = 1024 * 1024
 GROUP = 4
 META = 16
 CAP = 26
@@ -19,7 +19,10 @@
 SMEM = pl.BlockSpec(memory_space=pltpu.SMEM)
 VMEM = pl.BlockSpec(memory_space=pltpu.VMEM)
 ANY = pl.BlockSpec(memory_space=pl.ANY)
-PARAMS = pltpu.CompilerParams(vmem_limit_bytes=VMEM_BYTES)
+
+
+def room(mib):
+    return pltpu.CompilerParams(vmem_limit_bytes=mib * MIB)
 
 
 def along_xz(value, to, x_core):
@@ -53,13 +56,13 @@
 
 
 def ring_gather(value, along):
-    after, before, across = [along(value, ahead(step)) for step in (-1, 1, 2)]
+    across, after, before = [along(value, ahead(step)) for step in (2, -1, 1)]
     return [value, after, across, before]
 
 
 def ring_swap(pieces, along):
-    after, before = along(pieces[3], ahead(-1)), along(pieces[1], ahead(1))
-    return [pieces[0], after, along(pieces[2], ahead(2)), before]
+    across = along(pieces[2], ahead(2))
+    return [pieces[0], along(pieces[3], ahead(-1)), across, along(pieces[1], ahead(1))]
 
 
 def total_of(pieces):
@@ -130,7 +133,7 @@
         ],
         in_specs=[SMEM] * 3 + [VMEM] * 2,
         out_specs=[VMEM] * 2,
-        compiler_params=PARAMS,
+        compiler_params=room(4),
     )(at_row, at_col, live, rows.reshape(1, slots), cols.reshape(1, slots))
 
 
@@ -168,6 +171,8 @@
         lines = summed.shape[0] // 2
         out_refs[-1][:, :T] = summed[:lines]
         out_refs[-1][:, T:] = summed[lines:]
+        for ref, blocks in zip(out_refs[1:-1], outs[1:]):
+            ref[pl.ds(blocks * T, 2 * lines)] = summed.astype(BF16)
 
     def group(number, carry):
         products = []
@@ -208,9 +213,11 @@
         out_row=out_row,
         tailed=tailed,
     )
+    need = tiles.size * 2 + sum(spans) * T * 2 + sum(outs) * T * T * 6
+    extra = [lines if tailed and n else 0 for n in range(len(outs))]
     return pl.pallas_call(
         kernel,
-        out_shape=[jax.ShapeDtypeStruct((n * T, T), BF16) for n in outs]
+        out_shape=[jax.ShapeDtypeStruct((n * T + e, T), BF16) for n, e in zip(outs, extra)]
         + ([jax.ShapeDtypeStruct((lines // 2, 2 * T), F32)] if tailed else []),
         in_specs=[SMEM] * 2 + [ANY] * (1 + len(sources)),
         out_specs=[VMEM] * (len(outs) + (tailed > 0)),
@@ -221,7 +228,7 @@
             pltpu.VMEM((max(tailed, 1), lines, T), BF16),
             pltpu.SemaphoreType.DMA((len(spans) + 1 + tailed,)),
         ],
-        compiler_params=PARAMS,
+        compiler_params=room(need // MIB + 5),
     )(live, tables, tiles, *sources)
 
 
@@ -278,19 +285,17 @@
             pltpu.SMEM((24, T), I32),
             pltpu.SemaphoreType.DMA((9,)),
         ],
-        compiler_params=PARAMS,
+        compiler_params=room(10),
     )(*pieces, *metas)
 
 
 def combine_kernel(lists, counts, own_ref, sums, *refs):
-    part_refs, outs, (own, parts, total, sems) = refs[:3], refs[3:7], refs[7:]
+    part_refs, outs, summed, (own, parts, total, sems) = refs[:3], refs[3:7], refs[7], refs[8:]
     copies = [pltpu.make_async_copy(own_ref, own, sems.at[3])]
     for n, ref in enumerate(part_refs):
         copies.append(pltpu.make_async_copy(ref, parts.at[n], sems.at[n]))
     for copy in copies:
         copy.start()
-    for ref in outs[1:]:
-        ref[pl.ds(16 * T, sums.shape[0])] = sums[...]
     copies[0].wait()
 
     def widen(k, carry):
@@ -301,6 +306,13 @@
     lax.fori_loop(0, 16, widen, 0)
     for copy in copies[1:]:
         copy.wait()
+    lines = sums.shape[0]
+    for k in range(2):
+        tail = pl.ds(CAP * T + k * lines, lines)
+        line = sums[:, k * T : (k + 1) * T] + total_of([parts[n, tail] for n in range(3)])
+        summed[:, k * T : (k + 1) * T] = line
+        for ref in outs[1:]:
+            ref[pl.ds(16 * T + k * lines, lines)] = line.astype(BF16)
     for n in range(3):
 
         def add(k, carry, n=n):
@@ -323,16 +335,17 @@
     return pl.pallas_call(
         combine_kernel,
         out_shape=[jax.ShapeDtypeStruct((rows, T), F32)]
-        + [jax.ShapeDtypeStruct((rows + sums.shape[0], T), BF16)] * 3,
+        + [jax.ShapeDtypeStruct((rows + 2 * sums.shape[0], T), BF16)] * 3
+        + [jax.ShapeDtypeStruct(sums.shape, F32)],
         in_specs=[SMEM] * 2 + [ANY, VMEM] + [ANY] * 3,
-        out_specs=[VMEM] * 4,
+        out_specs=[VMEM] * 5,
         scratch_shapes=[
             pltpu.VMEM(own.shape, BF16),
             pltpu.VMEM((3,) + parts[0].shape, BF16),
             pltpu.VMEM((64, T, T), F32),
             pltpu.SemaphoreType.DMA((4,)),
         ],
-        compiler_params=PARAMS,
+        compiler_params=room(16),
     )(lists, counts, own, sums, *parts)
 
 
@@ -362,7 +375,7 @@
         ],
         in_specs=[VMEM] * 5,
         out_specs=[VMEM] * 3,
-        compiler_params=PARAMS,
+        compiler_params=room(10),
     )(*pieces, sums)
 
 
@@ -426,7 +439,7 @@
         + ([ANY, whole(T + 8, width), ANY] if before else []),
         out_specs=[full, whole(rows // 2 + tail, T), whole(T + 8, width)],
         input_output_aliases={8: 0} if before else {},
-        compiler_params=PARAMS,
+        compiler_params=room(14),
     )(*parts, grad, weight, offset, *before)
 
 
@@ -479,20 +492,22 @@
     here, *parts, sums = products(
         live, tables, 3, 1, tiles, gathered, spans, outs, (0,), tailed=8
     )
-    sums = total_of(ring_gather(sums, along_outer))
-    rounded = jnp.concatenate([sums[:, :T], sums[:, T:]]).astype(BF16)
     parts = ring_swap([None] + parts, along_outer)[1:]
 
-    def backward_all(here, rounded, parts, gathered):
+    def backward_all(here, sums, parts, gathered):
         outs = products(live, tables, 3, 2, tiles, gathered, spans, (64,) * 4, (0,))
         mine = total_of(ring_swap(outs, along_outer)).reshape(4, nodes_here, T)
-        far = [jnp.concatenate([mine[d].astype(BF16), rounded]) for d in (1, 2, 3)]
-        return [mine[0]] + far
-
-    def backward_named(here, rounded, parts, gathered):
-        return list(combine(lists, counts, here, rounded, parts))
-
-    outs = lax.cond(full, backward_all, backward_named, here, rounded, parts, gathered)
+        tail = total_of([p[CAP * T :] for p in parts])
+        lines = sums.shape[0]
+        sums = sums + jnp.concatenate([tail[:lines], tail[lines:]], axis=1)
+        tail = jnp.concatenate([sums[:, :T], sums[:, T:]]).astype(BF16)
+        far = [jnp.concatenate([mine[d].astype(BF16), tail]) for d in (1, 2, 3)]
+        return [mine[0]] + far + [sums]
+
+    def backward_named(here, sums, parts, gathered):
+        return list(combine(lists, counts, here, sums, parts))
+
+    *outs, sums = lax.cond(full, backward_all, backward_named, here, sums, parts, gathered)
     outs = ring_swap(outs, along_inner)
     grad_features, grad_weight, grad_offset = finish(outs, sums, scaling)
     return (hidden, grad_features, grad_weight, grad_offset.reshape(-1))

time: 188 us -> 176 us (0.936)
  starting transfers between devices: 60.2 us -> 36.5 us
  waiting for transfers between devices: 81.7 us -> 105 us
  Pallas kernels: 33.5 us -> 27.6 us
  local copies, waits for them, and re-layouts: 6.08 us -> 1.87 us
  other arithmetic: 4.23 us -> 1.68 us
    ppermute x21 -> x18, starting transfers between devices: 39.8 us -> 20.7 us  [along_xz(): return lax.ppermute(value, ('row', 'col'), pairs)]
    ppermute x21 -> x18, waiting for transfers between devices: 52.9 us -> 65.8 us  [along_xz(): return lax.ppermute(value, ('row', 'col'), pairs)]
    ppermute x12, waiting for transfers between devices: 23.4 us -> 35.2 us  [along_y(): return lax.ppermute(value, 'col', pairs)]
    ppermute x12, starting transfers between devices: 18.8 us -> 13.7 us  [along_y(): return lax.ppermute(value, 'col', pairs)]
    pallas_call x2, Pallas kernels: 7.19 us -> 4.46 us  [dense(): pl.pallas_call(functools.partial(dense_kernel, step=step), grid=(steps,),...]
    unnamed x38 -> x30, local copies, waits for them, and re-layouts: 3.48 us -> 1.35 us
    cond x6 -> x0, local copies, waits for them, and re-layouts: 2.07 us -> none
  transfers between devices with their start and end apart: 43 -> 40, of which waited for: 21 -> 24; matrix products, arithmetic and copies ran while one was open for 3% -> 1% of each run, Pallas kernels for 5% -> 3%
where the time goes in v7:
time: 176 us; the launch traced here: 175 us
  waiting for transfers between devices  105 us (60%)
  starting transfers between devices  36.5 us (21%)
  Pallas kernels  27.6 us (16%)
  between operations  2.17 us (1%)
  local copies, waits for them, and re-layouts  1.87 us (1%)
    ppermute x18, waiting for transfers between devices, along_xz(): return lax.ppermute(value, ('row', 'col'), pairs)  65.8 us
    ppermute x12, waiting for transfers between devices, along_y(): return lax.ppermute(value, 'col', pairs)  35.2 us
    ppermute x18, starting transfers between devices, along_xz(): return lax.ppermute(value, ('row', 'col'), pairs)  20.7 us
    pallas_call x2, Pallas kernels, products(): pl.pallas_call(kernel, out_shape=[jax.ShapeDtypeStruct((n * T + e, T), BF...  14.6 us
    ppermute x12, starting transfers between devices, along_y(): return lax.ppermute(value, 'col', pairs)  13.7 us
    pallas_call x2, Pallas kernels, dense(): pl.pallas_call(functools.partial(dense_kernel, step=step), grid=(steps,),...  4.46 us
    ppermute x10, waiting for transfers between devices, other_core(): return lax.ppermute(value, 'col', pairs)  3.87 us
    pallas_call x1, Pallas kernels, combine(): pl.pallas_call(combine_kernel, out_shape=[jax.ShapeDtypeStruct((rows, T),...  3.54 us
  transfers between devices with their start and end apart: 40, of which 24 were waited for; matrix products, arithmetic and copies ran while one was open for 1% of the time, Pallas kernels for 3%

profile of v7, /device:TPU:0, one launch (start us, length us, event | category | flops | bytes accessed | tf_op | source)
XLA Modules:
  0.0 174.7 jit_solution(1958594374215621878)
XLA Ops:
  0.6 2.9 %collective-permute-start.6 = (bf16[2048,128]{1,0:T(8,128)(2,1)}, bf16[2048,128]{1,0:T(8,128)(2,1)S(1)}, u32[]{:S(2)}, u32[]{:S(2)}) collective-permute-start(bf16[2048,128]{1,0:T(8,128)(2,1)} %refs_0_.1), channel_id=1, source_target_pairs={{0,96},{1,25},{2,98},{3,27},{4,100},{5,29},{6,102},{7,31},{8,104},... | collective-permute-start | bytes 1572872 | tf_op jit(solution)/shard_map/ppermute | solution.py:33
  7.5 4.1 %collective-permute-start.9 = (bf16[16,128]{1,0:T(8,128)(2,1)S(1)}, bf16[16,128]{1,0:T(8,128)(2,1)S(1)}, u32[]{:S(2)}, u32[]{:S(2)}) collective-permute-start(bf16[16,128]{1,0:T(8,128)(2,1)S(1)} %get-tuple-element.179.refs_4_), channel_id=1, source_target_pairs={{0,24},{1,97},{2,26},{3,99},{4,28},{5,101},{6,30},{7,103},{8,0},{9... | collective-permute-start | bytes 12296 | tf_op jit(solution)/shard_map/ppermute | solution.py:33
  13.5 3.3 %collective-permute-done.10.refs_6_ = bf16[16,128]{1,0:T(8,128)(2,1)S(1)} collective-permute-done((bf16[16,128]{1,0:T(8,128)(2,1)S(1)}, bf16[16,128]{1,0:T(8,128)(2,1)S(1)}, u32[]{:S(2)}, u32[]{:S(2)}) %collective-permute-start.10) | collective-permute-done | bytes 4128 | tf_op jit(solution)/shard_map/ppermute | solution.py:33
  22.5 4.3 %collective-permute-start.15 = (bf16[3328,128]{1,0:T(8,128)(2,1)S(1)}, bf16[3328,128]{1,0:T(8,128)(2,1)S(1)}, u32[]{:S(2)}, u32[]{:S(2)}) collective-permute-start(bf16[3328,128]{1,0:T(8,128)(2,1)S(1)} %get-tuple-element.182), channel_id=1, source_target_pairs={{0,24},{1,97},{2,26},{3,99},{4,28},{5,101},{6,30},{7,103},{8,0},{9... | collective-permute-start | bytes 2555912 | tf_op jit(solution)/shard_map/ppermute | solution.py:33
  29.7 8.2 %collective-permute-done.14 = f32[8,128]{1,0:T(8,128)S(1)} collective-permute-done((f32[8,128]{1,0:T(8,128)S(1)}, f32[8,128]{1,0:T(8,128)S(1)}, u32[]{:S(2)}, u32[]{:S(2)}) %collective-permute-start.14) | collective-permute-done | bytes 4128 | tf_op jit(solution)/shard_map/ppermute | solution.py:33
  37.9 3.7 %collective-permute-done.12 = f32[8,128]{1,0:T(8,128)S(1)} collective-permute-done((f32[8,128]{1,0:T(8,128)S(1)}, f32[8,128]{1,0:T(8,128)S(1)}, u32[]{:S(2)}, u32[]{:S(2)}) %collective-permute-start.12) | collective-permute-done | bytes 4128 | tf_op jit(solution)/shard_map/ppermute | solution.py:33
  42.8 3.3 %collective-permute-done.15 = bf16[3328,128]{1,0:T(8,128)(2,1)S(1)} collective-permute-done((bf16[3328,128]{1,0:T(8,128)(2,1)S(1)}, bf16[3328,128]{1,0:T(8,128)(2,1)S(1)}, u32[]{:S(2)}, u32[]{:S(2)}) %collective-permute-start.15) | collective-permute-done | bytes 852000 | tf_op jit(solution)/shard_map/ppermute | solution.py:33
  46.2 3.6 %collective-permute-done.17 = bf16[3328,128]{1,0:T(8,128)(2,1)S(1)} collective-permute-done((bf16[3328,128]{1,0:T(8,128)(2,1)S(1)}, bf16[3328,128]{1,0:T(8,128)(2,1)S(1)}, u32[]{:S(2)}, u32[]{:S(2)}) %collective-permute-start.17) | collective-permute-done | bytes 852000 | tf_op jit(solution)/shard_map/ppermute | solution.py:33
  49.8 8.0 %conditional.2 = ((bf16[4096,128]{1,0:T(8,128)(2,1)}, bf16[4096,128]{1,0:T(8,128)(2,1)}, bf16[4096,128]{1,0:T(8,128)(2,1)}, bf16[4096,128]{1,0:T(8,128)(2,1)})) conditional(s32[]{:T(128)} %bitcast.5, (s32[1]{0:T(128)}, s32[8,64]{1,0:T(8,128)S(1)}, bf16[64,128,128]{2,1,0:T(8,128)(2,1)S(1)}, bf16[2048,128]{1,0:T(8,128)(2,1)}, ...), branch_computations={%region_0.0_spmd, %region_1.0_spmd} | conditional | bytes 29360256 | solution.py:469
  49.8 8.0 %branch_0_fun.2 = (bf16[4096,128]{1,0:T(8,128)(2,1)}, bf16[4096,128]{1,0:T(8,128)(2,1)}, bf16[4096,128]{1,0:T(8,128)(2,1)}, bf16[4096,128]{1,0:T(8,128)(2,1)}) custom-call(s32[1]{0:T(128)} %get-tuple-element.94.live, s32[8,64]{1,0:T(8,128)S(1)} %get-tuple-element.95.tables, bf16[64,128,128]{2,1,0:T(8,128)(2,1)S(1)} %get-tuple-element.96.tiles_ref, ...), custom_call_target="tpu_custom_call" | custom-call | tf_op jit(solution)/shard_map/cond/branch_0_fun/pallas_call | solution.py:218
  70.8 6.3 %collective-permute-done.23.refs_2_ = bf16[1024,128]{1,0:T(8,128)(2,1)S(1)} collective-permute-done((bf16[1024,128]{1,0:T(8,128)(2,1)S(1)}, bf16[1024,128]{1,0:T(8,128)(2,1)S(1)}, u32[]{:S(2)}, u32[]{:S(2)}) %collective-permute-start.23) | collective-permute-done | bytes 262176 | tf_op jit(solution)/shard_map/ppermute | solution.py:46
  77.1 4.3 %collective-permute-done.25.refs_4_ = bf16[1024,128]{1,0:T(8,128)(2,1)S(1)} collective-permute-done((bf16[1024,128]{1,0:T(8,128)(2,1)S(1)}, bf16[1024,128]{1,0:T(8,128)(2,1)S(1)}, u32[]{:S(2)}, u32[]{:S(2)}) %collective-permute-start.25) | collective-permute-done | bytes 262176 | tf_op jit(solution)/shard_map/ppermute | solution.py:46
  84.1 4.3 %collective-permute-done.19.refs_2_ = bf16[1024,128]{1,0:T(8,128)(2,1)S(1)} collective-permute-done((bf16[1024,128]{1,0:T(8,128)(2,1)S(1)}, bf16[1024,128]{1,0:T(8,128)(2,1)S(1)}, u32[]{:S(2)}, u32[]{:S(2)}) %collective-permute-start.19) | collective-permute-done | bytes 262176 | tf_op jit(solution)/shard_map/ppermute | solution.py:46
  88.4 4.7 %collective-permute-start.38 = (bf16[1024,128]{1,0:T(8,128)(2,1)S(1)}, bf16[1024,128]{1,0:T(8,128)(2,1)S(1)}, u32[]{:S(2)}, u32[]{:S(2)}) collective-permute-start(bf16[1024,128]{1,0:T(8,128)(2,1)S(1)} %get-tuple-element.191.refs_12_), channel_id=1, source_target_pairs={{0,2},{1,3},{2,4},{3,5},{4,6},{5,7},{6,0},{7,1},{8,10},{9,11},{10,... | collective-permute-start | bytes 786440 | tf_op jit(solution)/shard_map/ppermute | solution.py:46
  99.7 5.1 %collective-permute-done.38.refs_15_ = bf16[1024,128]{1,0:T(8,128)(2,1)S(1)} collective-permute-done((bf16[1024,128]{1,0:T(8,128)(2,1)S(1)}, bf16[1024,128]{1,0:T(8,128)(2,1)S(1)}, u32[]{:S(2)}, u32[]{:S(2)}) %collective-permute-start.38) | collective-permute-done | bytes 262176 | tf_op jit(solution)/shard_map/ppermute | solution.py:46
  105.4 7.8 %collective-permute-done.28.refs_5_ = bf16[1296,128]{1,0:T(8,128)(2,1)S(1)} collective-permute-done((bf16[1296,128]{1,0:T(8,128)(2,1)S(1)}, bf16[1296,128]{1,0:T(8,128)(2,1)S(1)}, u32[]{:S(2)}, u32[]{:S(2)}) %collective-permute-start.28) | collective-permute-done | bytes 331808 | tf_op jit(solution)/shard_map/ppermute | solution.py:46
  113.7 3.2 %collective-permute-done.32.refs_7_ = bf16[1296,128]{1,0:T(8,128)(2,1)S(1)} collective-permute-done((bf16[1296,128]{1,0:T(8,128)(2,1)S(1)}, bf16[1296,128]{1,0:T(8,128)(2,1)S(1)}, u32[]{:S(2)}, u32[]{:S(2)}) %collective-permute-start.32) | collective-permute-done | bytes 331808 | tf_op jit(solution)/shard_map/ppermute | solution.py:46
  118.9 6.7 %shard_map.115 = (bf16[8192,128]{1,0:T(8,128)(2,1)S(1)}, bf16[3600,128]{1,0:T(8,128)(2,1)S(1)}, bf16[3600,128]{1,0:T(8,128)(2,1)S(1)}, bf16[3600,128]{1,0:T(8,128)(2,1)S(1)}, f32[136,256]{1,0:T(8,128)S(1)}) custom-call(s32[1]{0:T(128)} %bitcast.10.live, s32[8,64]{1,0:T(8,128)S(1)} %get-tuple-element.181.tables, bf16[64,128,128]{2,1,0:T(8,128)(2,1)S(1)} %bitcast.17, ...), custom_call_target="tpu_custom_call" | custom-call | tf_op jit(solution)/shard_map/pallas_call | solution.py:218
  127.8 11.4 %collective-permute-done.40 = bf16[3600,128]{1,0:T(8,128)(2,1)S(1)} collective-permute-done((bf16[3600,128]{1,0:T(8,128)(2,1)S(1)}, bf16[3600,128]{1,0:T(8,128)(2,1)S(1)}, u32[]{:S(2)}, u32[]{:S(2)}) %collective-permute-start.40) | collective-permute-done | bytes 921632 | tf_op jit(solution)/shard_map/ppermute | solution.py:33
  140.9 9.8 %collective-permute-done.42 = bf16[3600,128]{1,0:T(8,128)(2,1)S(1)} collective-permute-done((bf16[3600,128]{1,0:T(8,128)(2,1)S(1)}, bf16[3600,128]{1,0:T(8,128)(2,1)S(1)}, u32[]{:S(2)}, u32[]{:S(2)}) %collective-permute-start.42) | collective-permute-done | bytes 921632 | tf_op jit(solution)/shard_map/ppermute | solution.py:33
  150.6 3.6 %conditional.3 = ((f32[2048,128]{1,0:T(8,128)}, bf16[2320,128]{1,0:T(8,128)(2,1)S(1)}, bf16[2320,128]{1,0:T(8,128)(2,1)S(1)}, bf16[2320,128]{1,0:T(8,128)(2,1)}, f32[136,256]{1,0:T(8,128)})) conditional(s32[]{:T(128)} %bitcast.5, (s32[78]{0:T(128)S(1)}, s32[3]{0:T(128)S(1)}, bf16[8192,128]{1,0:T(8,128)(2,1)S(1)}, f32[136,256]{1,0:T(8,128)S(1)}, ...), branch_computations={%region_2.0_spmd, %region_3.0_spmd} | conditional | flops 12824576 | bytes 61940020 | solution.py:510
  150.6 3.5 %branch_0_fun.3 = (f32[2048,128]{1,0:T(8,128)}, bf16[2320,128]{1,0:T(8,128)(2,1)S(1)}, bf16[2320,128]{1,0:T(8,128)(2,1)S(1)}, bf16[2320,128]{1,0:T(8,128)(2,1)}, f32[136,256]{1,0:T(8,128)}) custom-call(s32[78]{0:T(128)S(1)} %get-tuple-element.111.lists, s32[3]{0:T(128)S(1)} %get-tuple-element.112.counts, bf16[8192,128]{1,0:T(8,128)(2,1)S(1)} %get-tuple-element.113.own_ref, ...), custom_call_target="tpu_custom_call" | custom-call | tf_op jit(solution)/shard_map/cond/branch_0_fun/pallas_call | solution.py:335
  156.3 8.1 %collective-permute-done.43.refs_1_ = bf16[2320,128]{1,0:T(8,128)(2,1)S(1)} collective-permute-done((bf16[2320,128]{1,0:T(8,128)(2,1)}, bf16[2320,128]{1,0:T(8,128)(2,1)S(1)}, u32[]{:S(2)}, u32[]{:S(2)}) %collective-permute-start.43) | collective-permute-done | bytes 593952 | tf_op jit(solution)/shard_map/ppermute | solution.py:33
  165.9 6.3 %collective-permute-done.45.refs_3_ = bf16[2320,128]{1,0:T(8,128)(2,1)S(1)} collective-permute-done((bf16[2320,128]{1,0:T(8,128)(2,1)S(1)}, bf16[2320,128]{1,0:T(8,128)(2,1)S(1)}, u32[]{:S(2)}, u32[]{:S(2)}) %collective-permute-start.45) | collective-permute-done | bytes 593952 | tf_op jit(solution)/shard_map/ppermute | solution.py:33
  (100 shorter events, 49.6 us)
Async XLA Ops:
  0.6 18.9 %collective-permute-start.6 = (bf16[2048,128]{1,0:T(8,128)(2,1)}, bf16[2048,128]{1,0:T(8,128)(2,1)S(1)}, u32[]{:S(2)}, u32[]{:S(2)}) collective-permute-start(bf16[2048,128]{1,0:T(8,128)(2,1)} %refs_0_.1), channel_id=1, source_target_pairs={{0,96},{1,25},{2,98},{3,27},{4,100},{5,29},{6,102},{7,31},{8,104},... | collective-permute-start | bytes 1572872 | tf_op jit(solution)/shard_map/ppermute | solution.py:33
  3.5 16.0 %collective-permute-start.7 = (bf16[2048,128]{1,0:T(8,128)(2,1)}, bf16[2048,128]{1,0:T(8,128)(2,1)S(1)}, u32[]{:S(2)}, u32[]{:S(2)}) collective-permute-start(bf16[2048,128]{1,0:T(8,128)(2,1)} %refs_0_.1), channel_id=1, source_target_pairs={{0,64},{1,17},{2,66},{3,19},{4,68},{5,21},{6,70},{7,23},{8,72},{9,... | collective-permute-start | bytes 1572872 | tf_op jit(solution)/shard_map/ppermute | solution.py:33
  4.3 15.9 %collective-permute-start.8 = (bf16[2048,128]{1,0:T(8,128)(2,1)}, bf16[2048,128]{1,0:T(8,128)(2,1)}, u32[]{:S(2)}, u32[]{:S(2)}) collective-permute-start(bf16[2048,128]{1,0:T(8,128)(2,1)} %refs_0_.1), channel_id=1, source_target_pairs={{0,32},{1,9},{2,34},{3,11},{4,36},{5,13},{6,38},{7,15},{8,40},{9,1... | collective-permute-start | bytes 1572872 | tf_op jit(solution)/shard_map/ppermute | solution.py:33
  22.5 23.7 %collective-permute-start.15 = (bf16[3328,128]{1,0:T(8,128)(2,1)S(1)}, bf16[3328,128]{1,0:T(8,128)(2,1)S(1)}, u32[]{:S(2)}, u32[]{:S(2)}) collective-permute-start(bf16[3328,128]{1,0:T(8,128)(2,1)S(1)} %get-tuple-element.182), channel_id=1, source_target_pairs={{0,24},{1,97},{2,26},{3,99},{4,28},{5,101},{6,30},{7,103},{8,0},{9... | collective-permute-start | bytes 2555912 | tf_op jit(solution)/shard_map/ppermute | solution.py:33
  26.7 19.4 %collective-permute-start.16 = (bf16[3328,128]{1,0:T(8,128)(2,1)S(1)}, bf16[3328,128]{1,0:T(8,128)(2,1)S(1)}, u32[]{:S(2)}, u32[]{:S(2)}) collective-permute-start(bf16[3328,128]{1,0:T(8,128)(2,1)S(1)} %get-tuple-element.183), channel_id=1, source_target_pairs={{0,16},{1,65},{2,18},{3,67},{4,20},{5,69},{6,22},{7,71},{8,24},{9,... | collective-permute-start | bytes 2555912 | tf_op jit(solution)/shard_map/ppermute | solution.py:33
  26.7 23.0 %collective-permute-start.17 = (bf16[3328,128]{1,0:T(8,128)(2,1)S(1)}, bf16[3328,128]{1,0:T(8,128)(2,1)S(1)}, u32[]{:S(2)}, u32[]{:S(2)}) collective-permute-start(bf16[3328,128]{1,0:T(8,128)(2,1)S(1)} %get-tuple-element.184), channel_id=1, source_target_pairs={{0,8},{1,33},{2,10},{3,35},{4,12},{5,37},{6,14},{7,39},{8,16},{9,4... | collective-permute-start | bytes 2555912 | tf_op jit(solution)/shard_map/ppermute | solution.py:33
  62.2 14.9 %collective-permute-start.23 = (bf16[1024,128]{1,0:T(8,128)(2,1)S(1)}, bf16[1024,128]{1,0:T(8,128)(2,1)S(1)}, u32[]{:S(2)}, u32[]{:S(2)}) collective-permute-start(bf16[1024,128]{1,0:T(8,128)(2,1)S(1)} %get-tuple-element.225), channel_id=1, source_target_pairs={{0,6},{1,7},{2,0},{3,1},{4,2},{5,3},{6,4},{7,5},{8,14},{9,15},{10,... | collective-permute-start | bytes 786440 | tf_op jit(solution)/shard_map/ppermute | solution.py:46
  65.0 12.1 %collective-permute-start.24 = (bf16[1024,128]{1,0:T(8,128)(2,1)S(1)}, bf16[1024,128]{1,0:T(8,128)(2,1)S(1)}, u32[]{:S(2)}, u32[]{:S(2)}) collective-permute-start(bf16[1024,128]{1,0:T(8,128)(2,1)S(1)} %get-tuple-element.224), channel_id=1, source_target_pairs={{0,4},{1,5},{2,6},{3,7},{4,0},{5,1},{6,2},{7,3},{8,12},{9,13},{10,... | collective-permute-start | bytes 786440 | tf_op jit(solution)/shard_map/ppermute | solution.py:46
  66.0 15.4 %collective-permute-start.25 = (bf16[1024,128]{1,0:T(8,128)(2,1)S(1)}, bf16[1024,128]{1,0:T(8,128)(2,1)S(1)}, u32[]{:S(2)}, u32[]{:S(2)}) collective-permute-start(bf16[1024,128]{1,0:T(8,128)(2,1)S(1)} %get-tuple-element.223), channel_id=1, source_target_pairs={{0,2},{1,3},{2,4},{3,5},{4,6},{5,7},{6,0},{7,1},{8,10},{9,11},{10,... | collective-permute-start | bytes 786440 | tf_op jit(solution)/shard_map/ppermute | solution.py:46
  67.3 21.1 %collective-permute-start.19 = (bf16[1024,128]{1,0:T(8,128)(2,1)S(1)}, bf16[1024,128]{1,0:T(8,128)(2,1)S(1)}, u32[]{:S(2)}, u32[]{:S(2)}) collective-permute-start(bf16[1024,128]{1,0:T(8,128)(2,1)S(1)} %get-tuple-element.228), channel_id=1, source_target_pairs={{0,6},{1,7},{2,0},{3,1},{4,2},{5,3},{6,4},{7,5},{8,14},{9,15},{10,... | collective-permute-start | bytes 786440 | tf_op jit(solution)/shard_map/ppermute | solution.py:46
  69.5 18.9 %collective-permute-start.20 = (bf16[1024,128]{1,0:T(8,128)(2,1)S(1)}, bf16[1024,128]{1,0:T(8,128)(2,1)S(1)}, u32[]{:S(2)}, u32[]{:S(2)}) collective-permute-start(bf16[1024,128]{1,0:T(8,128)(2,1)S(1)} %get-tuple-element.227), channel_id=1, source_target_pairs={{0,4},{1,5},{2,6},{3,7},{4,0},{5,1},{6,2},{7,3},{8,12},{9,13},{10,... | collective-permute-start | bytes 786440 | tf_op jit(solution)/shard_map/ppermute | solution.py:46
  77.1 18.2 %collective-permute-start.21 = (bf16[1024,128]{1,0:T(8,128)(2,1)S(1)}, bf16[1024,128]{1,0:T(8,128)(2,1)S(1)}, u32[]{:S(2)}, u32[]{:S(2)}) collective-permute-start(bf16[1024,128]{1,0:T(8,128)(2,1)S(1)} %get-tuple-element.226), channel_id=1, source_target_pairs={{0,2},{1,3},{2,4},{3,5},{4,6},{5,7},{6,0},{7,1},{8,10},{9,11},{10,... | collective-permute-start | bytes 786440 | tf_op jit(solution)/shard_map/ppermute | solution.py:46
  83.6 11.7 %collective-permute-start.26 = (bf16[1024,128]{1,0:T(8,128)(2,1)S(1)}, bf16[1024,128]{1,0:T(8,128)(2,1)S(1)}, u32[]{:S(2)}, u32[]{:S(2)}) collective-permute-start(bf16[1024,128]{1,0:T(8,128)(2,1)S(1)} %get-tuple-element.191.refs_12_), channel_id=1, source_target_pairs={{0,1},{1,0},{2,3},{3,2},{4,5},{5,4},{6,7},{7,6},{8,9},{9,8},{10,11... | collective-permute-start | bytes 786440 | tf_op jit(solution)/shard_map/ppermute | solution.py:51
  83.6 16.0 %collective-permute-start.34 = (bf16[1024,128]{1,0:T(8,128)(2,1)S(1)}, bf16[1024,128]{1,0:T(8,128)(2,1)S(1)}, u32[]{:S(2)}, u32[]{:S(2)}) collective-permute-start(bf16[1024,128]{1,0:T(8,128)(2,1)S(1)} %get-tuple-element.191.refs_12_), channel_id=1, source_target_pairs={{0,6},{1,7},{2,0},{3,1},{4,2},{5,3},{6,4},{7,5},{8,14},{9,15},{10,... | collective-permute-start | bytes 786440 | tf_op jit(solution)/shard_map/ppermute | solution.py:46
  88.4 16.5 %collective-permute-start.38 = (bf16[1024,128]{1,0:T(8,128)(2,1)S(1)}, bf16[1024,128]{1,0:T(8,128)(2,1)S(1)}, u32[]{:S(2)}, u32[]{:S(2)}) collective-permute-start(bf16[1024,128]{1,0:T(8,128)(2,1)S(1)} %get-tuple-element.191.refs_12_), channel_id=1, source_target_pairs={{0,2},{1,3},{2,4},{3,5},{4,6},{5,7},{6,0},{7,1},{8,10},{9,11},{10,... | collective-permute-start | bytes 786440 | tf_op jit(solution)/shard_map/ppermute | solution.py:46
  97.6 15.6 %collective-permute-start.28 = (bf16[1296,128]{1,0:T(8,128)(2,1)S(1)}, bf16[1296,128]{1,0:T(8,128)(2,1)S(1)}, u32[]{:S(2)}, u32[]{:S(2)}) collective-permute-start(bf16[1296,128]{1,0:T(8,128)(2,1)S(1)} %get-tuple-element.195.refs_4_), channel_id=1, source_target_pairs={{0,6},{1,7},{2,0},{3,1},{4,2},{5,3},{6,4},{7,5},{8,14},{9,15},{10,... | collective-permute-start | bytes 995336 | tf_op jit(solution)/shard_map/ppermute | solution.py:46
  97.6 15.6 %collective-permute-start.30 = (bf16[1296,128]{1,0:T(8,128)(2,1)S(1)}, bf16[1296,128]{1,0:T(8,128)(2,1)S(1)}, u32[]{:S(2)}, u32[]{:S(2)}) collective-permute-start(bf16[1296,128]{1,0:T(8,128)(2,1)S(1)} %get-tuple-element.195.refs_4_), channel_id=1, source_target_pairs={{0,4},{1,5},{2,6},{3,7},{4,0},{5,1},{6,2},{7,3},{8,12},{9,13},{10,... | collective-permute-start | bytes 995336 | tf_op jit(solution)/shard_map/ppermute | solution.py:46
  99.6 17.3 %collective-permute-start.32 = (bf16[1296,128]{1,0:T(8,128)(2,1)S(1)}, bf16[1296,128]{1,0:T(8,128)(2,1)S(1)}, u32[]{:S(2)}, u32[]{:S(2)}) collective-permute-start(bf16[1296,128]{1,0:T(8,128)(2,1)S(1)} %get-tuple-element.195.refs_4_), channel_id=1, source_target_pairs={{0,2},{1,3},{2,4},{3,5},{4,6},{5,7},{6,0},{7,1},{8,10},{9,11},{10,... | collective-permute-start | bytes 995336 | tf_op jit(solution)/shard_map/ppermute | solution.py:46
  104.9 12.0 %collective-permute-start.37 = (bf16[1024,128]{1,0:T(8,128)(2,1)S(1)}, bf16[1024,128]{1,0:T(8,128)(2,1)S(1)}, u32[]{:S(2)}, u32[]{:S(2)}) collective-permute-start(bf16[1024,128]{1,0:T(8,128)(2,1)S(1)} %collective-permute-done.36.refs_14_), channel_id=1, source_target_pairs={{0,1},{1,0},{2,3},{3,2},{4,5},{5,4},{6,7},{7,6},{8,9},{9,8},{10,11... | collective-permute-start | bytes 786440 | tf_op jit(solution)/shard_map/ppermute | solution.py:51
  104.9 14.0 %collective-permute-start.27 = (bf16[1296,128]{1,0:T(8,128)(2,1)S(1)}, bf16[1296,128]{1,0:T(8,128)(2,1)S(1)}, u32[]{:S(2)}, u32[]{:S(2)}) collective-permute-start(bf16[1296,128]{1,0:T(8,128)(2,1)S(1)} %get-tuple-element.195.refs_4_), channel_id=1, source_target_pairs={{0,1},{1,0},{2,3},{3,2},{4,5},{5,4},{6,7},{7,6},{8,9},{9,8},{10,11... | collective-permute-start | bytes 995336 | tf_op jit(solution)/shard_map/ppermute | solution.py:51
  125.7 13.5 %collective-permute-start.40 = (bf16[3600,128]{1,0:T(8,128)(2,1)S(1)}, bf16[3600,128]{1,0:T(8,128)(2,1)S(1)}, u32[]{:S(2)}, u32[]{:S(2)}) collective-permute-start(bf16[3600,128]{1,0:T(8,128)(2,1)S(1)} %get-tuple-element.198), channel_id=1, source_target_pairs={{0,24},{1,97},{2,26},{3,99},{4,28},{5,101},{6,30},{7,103},{8,0},{9... | collective-permute-start | bytes 2764808 | tf_op jit(solution)/shard_map/ppermute | solution.py:33
  125.8 15.1 %collective-permute-start.41 = (bf16[3600,128]{1,0:T(8,128)(2,1)S(1)}, bf16[3600,128]{1,0:T(8,128)(2,1)S(1)}, u32[]{:S(2)}, u32[]{:S(2)}) collective-permute-start(bf16[3600,128]{1,0:T(8,128)(2,1)S(1)} %get-tuple-element.199), channel_id=1, source_target_pairs={{0,16},{1,65},{2,18},{3,67},{4,20},{5,69},{6,22},{7,71},{8,24},{9,... | collective-permute-start | bytes 2764808 | tf_op jit(solution)/shard_map/ppermute | solution.py:33
  127.0 23.7 %collective-permute-start.42 = (bf16[3600,128]{1,0:T(8,128)(2,1)S(1)}, bf16[3600,128]{1,0:T(8,128)(2,1)S(1)}, u32[]{:S(2)}, u32[]{:S(2)}) collective-permute-start(bf16[3600,128]{1,0:T(8,128)(2,1)S(1)} %get-tuple-element.200), channel_id=1, source_target_pairs={{0,8},{1,33},{2,10},{3,35},{4,12},{5,37},{6,14},{7,39},{8,16},{9,4... | collective-permute-start | bytes 2764808 | tf_op jit(solution)/shard_map/ppermute | solution.py:33
  155.4 16.8 %collective-permute-start.45 = (bf16[2320,128]{1,0:T(8,128)(2,1)S(1)}, bf16[2320,128]{1,0:T(8,128)(2,1)S(1)}, u32[]{:S(2)}, u32[]{:S(2)}) collective-permute-start(bf16[2320,128]{1,0:T(8,128)(2,1)S(1)} %get-tuple-element.204), channel_id=1, source_target_pairs={{0,32},{1,9},{2,34},{3,11},{4,36},{5,13},{6,38},{7,15},{8,40},{9,1... | collective-permute-start | bytes 1781768 | tf_op jit(solution)/shard_map/ppermute | solution.py:33
  (31 other events, 386.8 us)

commit v8 on v7

--- a/solution.py
+++ b/solution.py
@@ -12,7 +12,7 @@
 T = 128
 F32, BF16, I32 = jnp.float32, jnp.bfloat16, jnp.int32
 MIB = 1024 * 1024
-GROUP = 4
+GROUP = 16
 META = 16
 CAP = 26
 LANES = 32
@@ -42,7 +42,10 @@
 
 
 def along_y(value, to):
-    pairs = [(y * 2 + k, to(y) % 4 * 2 + k) for y in range(4) for k in range(2)]
+    pairs = []
+    for y in range(4):
+        pairs.append((y * 2, to(y) % 4 * 2))
+        pairs.append((y * 2 + 1, (2 * y - to(y)) % 4 * 2 + 1))
     return lax.ppermute(value, "col", pairs)
 
 
@@ -80,8 +83,11 @@
     rows, cols = rows_ref[...], cols_ref[...]
     slots = cols.shape[1]
 
-    same_core = jnp.where(((rows >> 4) & 1) == core, 64, 0)
-    row_place = same_core + ((rows >> 3) & 1) * 32 + (((rows >> 5) - y) & 3) * 8 + (rows & 7)
+    far_core = (rows >> 4) & 1
+    same_core = jnp.where(far_core == core, 64, 0)
+    dy = (rows >> 5) - y
+    dy = jnp.where(far_core == 0, dy, -dy) & 3
+    row_place = same_core + ((rows >> 3) & 1) * 32 + dy * 8 + (rows & 7)
     dx, dz = ((cols >> 6) - x) & 3, ((cols >> 4) - z) & 3
     outer, inner = jnp.where(core == 0, dz, dx), jnp.where(core == 0, dx, dz)
     code = inner * 16 + (cols & 15)
@@ -260,10 +266,12 @@
         group = 3 - n
         amount = table[n * 8 + 1, group]
         counts[n] = amount
+        for k in range(4):
+            lists[n * LANES + amount + k] = 64
 
         def step(k, carry, n=n, group=group):
             code = table[n * 8, group * LANES + k]
-            lists[n * CAP + k] = code
+            lists[n * LANES + k] = code
             sends[n][block(k)] = held[code >> 4, block(code & 15)]
             return carry
 
@@ -275,7 +283,7 @@
         pack_kernel,
         out_shape=[jax.ShapeDtypeStruct((CAP * T, T), BF16)] * 3
         + [jax.ShapeDtypeStruct((8, T), F32)]
-        + [jax.ShapeDtypeStruct((3 * CAP,), I32), jax.ShapeDtypeStruct((3,), I32)],
+        + [jax.ShapeDtypeStruct((3 * LANES,), I32), jax.ShapeDtypeStruct((3,), I32)],
         in_specs=[ANY] * 8,
         out_specs=[VMEM] * 4 + [SMEM] * 2,
         scratch_shapes=[
@@ -316,10 +324,12 @@
     for n in range(3):
 
         def add(k, carry, n=n):
-            total[lists[n * CAP + k]] += parts[n, block(k)].astype(F32)
+            for at in range(4):
+                slot = k * 4 + at
+                total[lists[n * LANES + slot]] += parts[n, block(slot)].astype(F32)
             return carry
 
-        lax.fori_loop(0, counts[n], add, 0)
+        lax.fori_loop(0, (counts[n] + 3) // 4, add, 0)
     for n, ref in enumerate(outs):
 
         def out(k, carry, n=n, ref=ref):
@@ -342,7 +352,7 @@
         scratch_shapes=[
             pltpu.VMEM(own.shape, BF16),
             pltpu.VMEM((3,) + parts[0].shape, BF16),
-            pltpu.VMEM((64, T, T), F32),
+            pltpu.VMEM((65, T, T), F32),
             pltpu.SemaphoreType.DMA((4,)),
         ],
         compiler_params=room(16),
@@ -350,9 +360,14 @@
 
 
 def finish_kernel(*refs, scaling):
-    pieces, sums, (nodes, weight, offset) = refs[:4], refs[4], refs[5:]
+    pieces, sums, (nodes, weight, offset), (held, sems) = refs[:4], refs[4], refs[5:8], refs[8:]
     rows = nodes.shape[0]
-    nodes[...] = total_of([ref[pl.ds(0, rows)] for ref in pieces])
+    copies = []
+    for k in range(4):
+        part = pl.ds(k * rows // 4, rows // 4)
+        held[part] = total_of([ref[part] for ref in pieces])
+        copies.append(pltpu.make_async_copy(held.at[part], nodes.at[part], sems.at[k]))
+        copies[k].start()
     lines = sums.shape[0]
     for k in range(2):
         part = pl.ds(k * T, T)
@@ -362,6 +377,8 @@
         total = total * scaling
         weight[:, part] = total[:T]
         offset[:, part] = jnp.sum(total[T:], axis=0, keepdims=True)
+    for copy in copies:
+        copy.wait()
 
 
 def finish(pieces, sums, scaling):
@@ -374,7 +391,8 @@
             jax.ShapeDtypeStruct((1, width), F32),
         ],
         in_specs=[VMEM] * 5,
-        out_specs=[VMEM] * 3,
+        out_specs=[ANY] + [VMEM] * 2,
+        scratch_shapes=[pltpu.VMEM(pieces[0].shape, F32), pltpu.SemaphoreType.DMA((4,))],
         compiler_params=room(10),
     )(*pieces, sums)
 

time: 176 us -> 172 us (0.977)
  starting transfers between devices: 36.5 us -> 40.6 us
  waiting for transfers between devices: 105 us -> 101 us
  Pallas kernels: 27.6 us -> 24.2 us
    ppermute x12, waiting for transfers between devices: 35.2 us -> 30.9 us  [along_y(): return lax.ppermute(value, 'col', pairs)]
    pallas_call x2, Pallas kernels: 14.6 us -> 10.8 us  [products(): pl.pallas_call(kernel, out_shape=[jax.ShapeDtypeStruct((n * T + e, T), BF...]
    ppermute x12, starting transfers between devices: 13.7 us -> 16.9 us  [along_y(): return lax.ppermute(value, 'col', pairs)]
  transfers between devices with their start and end apart: 40 -> 40, of which waited for: 24 -> 22; matrix products, arithmetic and copies ran while one was open for 1% -> 1% of each run, Pallas kernels for 3% -> 3%
where the time goes in v8:
time: 172 us
  waiting for transfers between devices  101 us (59%)
  starting transfers between devices  40.6 us (24%)
  Pallas kernels  24.2 us (14%)
  between operations  2.34 us (1%)
  local copies, waits for them, and re-layouts  1.87 us (1%)
    ppermute x18, waiting for transfers between devices, along_xz(): return lax.ppermute(value, ('row', 'col'), pairs)  66.1 us
    ppermute x12, waiting for transfers between devices, along_y(): return lax.ppermute(value, 'col', pairs)  30.9 us
    ppermute x18, starting transfers between devices, along_xz(): return lax.ppermute(value, ('row', 'col'), pairs)  21.5 us
    ppermute x12, starting transfers between devices, along_y(): return lax.ppermute(value, 'col', pairs)  16.9 us
    pallas_call x2, Pallas kernels, products(): pl.pallas_call(kernel, out_shape=[jax.ShapeDtypeStruct((n * T + e, T), BF...  10.8 us
    pallas_call x2, Pallas kernels, dense(): pl.pallas_call(functools.partial(dense_kernel, step=step), grid=(steps,),...  4.49 us
    ppermute x10, waiting for transfers between devices, other_core(): return lax.ppermute(value, 'col', pairs)  3.87 us
    pallas_call x1, Pallas kernels, combine(): pl.pallas_call(combine_kernel, out_shape=[jax.ShapeDtypeStruct((rows, T),...  3.45 us
  transfers between devices with their start and end apart: 40, of which 22 were waited for; matrix products, arithmetic and copies ran while one was open for 1% of the time, Pallas kernels for 3%

profile of v8, /device:TPU:0, one launch (start us, length us, event | category | flops | bytes accessed | tf_op | source)
XLA Modules:
  0.0 171.5 jit_solution(14493222186562617283)
XLA Ops:
  7.5 4.1 %collective-permute-start.9 = (bf16[16,128]{1,0:T(8,128)(2,1)S(1)}, bf16[16,128]{1,0:T(8,128)(2,1)S(1)}, u32[]{:S(2)}, u32[]{:S(2)}) collective-permute-start(bf16[16,128]{1,0:T(8,128)(2,1)S(1)} %get-tuple-element.179.refs_4_), channel_id=1, source_target_pairs={{0,24},{1,97},{2,26},{3,99},{4,28},{5,101},{6,30},{7,103},{8,0},{9... | collective-permute-start | bytes 12296 | tf_op jit(solution)/shard_map/ppermute | solution.py:33
  13.5 3.3 %collective-permute-done.10.refs_6_ = bf16[16,128]{1,0:T(8,128)(2,1)S(1)} collective-permute-done((bf16[16,128]{1,0:T(8,128)(2,1)S(1)}, bf16[16,128]{1,0:T(8,128)(2,1)S(1)}, u32[]{:S(2)}, u32[]{:S(2)}) %collective-permute-start.10) | collective-permute-done | bytes 4128 | tf_op jit(solution)/shard_map/ppermute | solution.py:33
  22.4 4.1 %collective-permute-start.15 = (bf16[3328,128]{1,0:T(8,128)(2,1)S(1)}, bf16[3328,128]{1,0:T(8,128)(2,1)S(1)}, u32[]{:S(2)}, u32[]{:S(2)}) collective-permute-start(bf16[3328,128]{1,0:T(8,128)(2,1)S(1)} %get-tuple-element.182), channel_id=1, source_target_pairs={{0,24},{1,97},{2,26},{3,99},{4,28},{5,101},{6,30},{7,103},{8,0},{9... | collective-permute-start | bytes 2555912 | tf_op jit(solution)/shard_map/ppermute | solution.py:33
  29.8 8.1 %collective-permute-done.14 = f32[8,128]{1,0:T(8,128)S(1)} collective-permute-done((f32[8,128]{1,0:T(8,128)S(1)}, f32[8,128]{1,0:T(8,128)S(1)}, u32[]{:S(2)}, u32[]{:S(2)}) %collective-permute-start.14) | collective-permute-done | bytes 4128 | tf_op jit(solution)/shard_map/ppermute | solution.py:33
  37.9 3.7 %collective-permute-done.12 = f32[8,128]{1,0:T(8,128)S(1)} collective-permute-done((f32[8,128]{1,0:T(8,128)S(1)}, f32[8,128]{1,0:T(8,128)S(1)}, u32[]{:S(2)}, u32[]{:S(2)}) %collective-permute-start.12) | collective-permute-done | bytes 4128 | tf_op jit(solution)/shard_map/ppermute | solution.py:33
  42.8 3.2 %collective-permute-done.15 = bf16[3328,128]{1,0:T(8,128)(2,1)S(1)} collective-permute-done((bf16[3328,128]{1,0:T(8,128)(2,1)S(1)}, bf16[3328,128]{1,0:T(8,128)(2,1)S(1)}, u32[]{:S(2)}, u32[]{:S(2)}) %collective-permute-start.15) | collective-permute-done | bytes 852000 | tf_op jit(solution)/shard_map/ppermute | solution.py:33
  46.0 3.6 %collective-permute-done.17 = bf16[3328,128]{1,0:T(8,128)(2,1)S(1)} collective-permute-done((bf16[3328,128]{1,0:T(8,128)(2,1)S(1)}, bf16[3328,128]{1,0:T(8,128)(2,1)S(1)}, u32[]{:S(2)}, u32[]{:S(2)}) %collective-permute-start.17) | collective-permute-done | bytes 852000 | tf_op jit(solution)/shard_map/ppermute | solution.py:33
  49.6 6.2 %conditional.2 = ((bf16[4096,128]{1,0:T(8,128)(2,1)}, bf16[4096,128]{1,0:T(8,128)(2,1)}, bf16[4096,128]{1,0:T(8,128)(2,1)}, bf16[4096,128]{1,0:T(8,128)(2,1)})) conditional(s32[]{:T(128)} %bitcast.5, (s32[1]{0:T(128)}, s32[8,64]{1,0:T(8,128)S(1)}, bf16[64,128,128]{2,1,0:T(8,128)(2,1)S(1)}, bf16[2048,128]{1,0:T(8,128)(2,1)}, ...), branch_computations={%region_0.0_spmd, %region_1.0_spmd} | conditional | bytes 29360256 | solution.py:487
  49.6 6.2 %branch_0_fun.2 = (bf16[4096,128]{1,0:T(8,128)(2,1)}, bf16[4096,128]{1,0:T(8,128)(2,1)}, bf16[4096,128]{1,0:T(8,128)(2,1)}, bf16[4096,128]{1,0:T(8,128)(2,1)}) custom-call(s32[1]{0:T(128)} %get-tuple-element.94.live, s32[8,64]{1,0:T(8,128)S(1)} %get-tuple-element.95.tables, bf16[64,128,128]{2,1,0:T(8,128)(2,1)S(1)} %get-tuple-element.96.tiles_ref, ...), custom_call_target="tpu_custom_call" | custom-call | tf_op jit(solution)/shard_map/cond/branch_0_fun/pallas_call | solution.py:224
  60.3 3.4 %collective-permute-start.23 = (bf16[1024,128]{1,0:T(8,128)(2,1)S(1)}, bf16[1024,128]{1,0:T(8,128)(2,1)S(1)}, u32[]{:S(2)}, u32[]{:S(2)}) collective-permute-start(bf16[1024,128]{1,0:T(8,128)(2,1)S(1)} %get-tuple-element.225), channel_id=1, source_target_pairs={{0,6},{1,3},{2,0},{3,5},{4,2},{5,7},{6,4},{7,1},{8,14},{9,11},{10,... | collective-permute-start | bytes 786440 | tf_op jit(solution)/shard_map/ppermute | solution.py:49
  64.9 3.0 %collective-permute-start.19 = (bf16[1024,128]{1,0:T(8,128)(2,1)S(1)}, bf16[1024,128]{1,0:T(8,128)(2,1)S(1)}, u32[]{:S(2)}, u32[]{:S(2)}) collective-permute-start(bf16[1024,128]{1,0:T(8,128)(2,1)S(1)} %get-tuple-element.228), channel_id=1, source_target_pairs={{0,6},{1,3},{2,0},{3,5},{4,2},{5,7},{6,4},{7,1},{8,14},{9,11},{10,... | collective-permute-start | bytes 786440 | tf_op jit(solution)/shard_map/ppermute | solution.py:49
  69.5 5.9 %collective-permute-done.23.refs_2_ = bf16[1024,128]{1,0:T(8,128)(2,1)S(1)} collective-permute-done((bf16[1024,128]{1,0:T(8,128)(2,1)S(1)}, bf16[1024,128]{1,0:T(8,128)(2,1)S(1)}, u32[]{:S(2)}, u32[]{:S(2)}) %collective-permute-start.23) | collective-permute-done | bytes 262176 | tf_op jit(solution)/shard_map/ppermute | solution.py:49
  75.5 4.5 %collective-permute-done.25.refs_4_ = bf16[1024,128]{1,0:T(8,128)(2,1)S(1)} collective-permute-done((bf16[1024,128]{1,0:T(8,128)(2,1)S(1)}, bf16[1024,128]{1,0:T(8,128)(2,1)S(1)}, u32[]{:S(2)}, u32[]{:S(2)}) %collective-permute-start.25) | collective-permute-done | bytes 262176 | tf_op jit(solution)/shard_map/ppermute | solution.py:49
  82.8 4.0 %collective-permute-done.19.refs_2_ = bf16[1024,128]{1,0:T(8,128)(2,1)S(1)} collective-permute-done((bf16[1024,128]{1,0:T(8,128)(2,1)S(1)}, bf16[1024,128]{1,0:T(8,128)(2,1)S(1)}, u32[]{:S(2)}, u32[]{:S(2)}) %collective-permute-start.19) | collective-permute-done | bytes 262176 | tf_op jit(solution)/shard_map/ppermute | solution.py:49
  86.8 5.0 %collective-permute-start.38 = (bf16[1024,128]{1,0:T(8,128)(2,1)S(1)}, bf16[1024,128]{1,0:T(8,128)(2,1)S(1)}, u32[]{:S(2)}, u32[]{:S(2)}) collective-permute-start(bf16[1024,128]{1,0:T(8,128)(2,1)S(1)} %get-tuple-element.191.refs_12_), channel_id=1, source_target_pairs={{0,2},{1,7},{2,4},{3,1},{4,6},{5,3},{6,0},{7,5},{8,10},{9,15},{10,... | collective-permute-start | bytes 786440 | tf_op jit(solution)/shard_map/ppermute | solution.py:49
  96.3 3.7 %collective-permute-done.34.refs_13_ = bf16[1024,128]{1,0:T(8,128)(2,1)S(1)} collective-permute-done((bf16[1024,128]{1,0:T(8,128)(2,1)S(1)}, bf16[1024,128]{1,0:T(8,128)(2,1)S(1)}, u32[]{:S(2)}, u32[]{:S(2)}) %collective-permute-start.34) | collective-permute-done | bytes 262176 | tf_op jit(solution)/shard_map/ppermute | solution.py:49
  102.9 9.1 %collective-permute-done.28.refs_5_ = bf16[1296,128]{1,0:T(8,128)(2,1)S(1)} collective-permute-done((bf16[1296,128]{1,0:T(8,128)(2,1)S(1)}, bf16[1296,128]{1,0:T(8,128)(2,1)S(1)}, u32[]{:S(2)}, u32[]{:S(2)}) %collective-permute-start.28) | collective-permute-done | bytes 331808 | tf_op jit(solution)/shard_map/ppermute | solution.py:49
  116.0 4.6 %shard_map.115 = (bf16[8192,128]{1,0:T(8,128)(2,1)S(1)}, bf16[3600,128]{1,0:T(8,128)(2,1)S(1)}, bf16[3600,128]{1,0:T(8,128)(2,1)S(1)}, bf16[3600,128]{1,0:T(8,128)(2,1)S(1)}, f32[136,256]{1,0:T(8,128)S(1)}) custom-call(s32[1]{0:T(128)} %bitcast.10.live, s32[8,64]{1,0:T(8,128)S(1)} %get-tuple-element.181.tables, bf16[64,128,128]{2,1,0:T(8,128)(2,1)S(1)} %bitcast.17, ...), custom_call_target="tpu_custom_call" | custom-call | tf_op jit(solution)/shard_map/pallas_call | solution.py:224
  123.4 19.9 %collective-permute-done.40 = bf16[3600,128]{1,0:T(8,128)(2,1)S(1)} collective-permute-done((bf16[3600,128]{1,0:T(8,128)(2,1)S(1)}, bf16[3600,128]{1,0:T(8,128)(2,1)S(1)}, u32[]{:S(2)}, u32[]{:S(2)}) %collective-permute-start.40) | collective-permute-done | bytes 921632 | tf_op jit(solution)/shard_map/ppermute | solution.py:33
  143.3 3.7 %collective-permute-done.42 = bf16[3600,128]{1,0:T(8,128)(2,1)S(1)} collective-permute-done((bf16[3600,128]{1,0:T(8,128)(2,1)S(1)}, bf16[3600,128]{1,0:T(8,128)(2,1)S(1)}, u32[]{:S(2)}, u32[]{:S(2)}) %collective-permute-start.42) | collective-permute-done | bytes 921632 | tf_op jit(solution)/shard_map/ppermute | solution.py:33
  147.0 3.5 %conditional.3 = ((f32[2048,128]{1,0:T(8,128)}, bf16[2320,128]{1,0:T(8,128)(2,1)S(1)}, bf16[2320,128]{1,0:T(8,128)(2,1)S(1)}, bf16[2320,128]{1,0:T(8,128)(2,1)}, f32[136,256]{1,0:T(8,128)})) conditional(s32[]{:T(128)} %bitcast.5, (s32[96]{0:T(128)S(1)}, s32[3]{0:T(128)S(1)}, bf16[8192,128]{1,0:T(8,128)(2,1)S(1)}, f32[136,256]{1,0:T(8,128)S(1)}, ...), branch_computations={%region_2.0_spmd, %region_3.0_spmd} | conditional | flops 12824576 | bytes 61940020 | solution.py:528
  147.0 3.4 %branch_0_fun.3 = (f32[2048,128]{1,0:T(8,128)}, bf16[2320,128]{1,0:T(8,128)(2,1)S(1)}, bf16[2320,128]{1,0:T(8,128)(2,1)S(1)}, bf16[2320,128]{1,0:T(8,128)(2,1)}, f32[136,256]{1,0:T(8,128)}) custom-call(s32[96]{0:T(128)S(1)} %get-tuple-element.111.lists, s32[3]{0:T(128)S(1)} %get-tuple-element.112.counts, bf16[8192,128]{1,0:T(8,128)(2,1)S(1)} %get-tuple-element.113.own_ref, ...), custom_call_target="tpu_custom_call" | custom-call | tf_op jit(solution)/shard_map/cond/branch_0_fun/pallas_call | solution.py:345
  152.5 8.1 %collective-permute-done.43.refs_1_ = bf16[2320,128]{1,0:T(8,128)(2,1)S(1)} collective-permute-done((bf16[2320,128]{1,0:T(8,128)(2,1)}, bf16[2320,128]{1,0:T(8,128)(2,1)S(1)}, u32[]{:S(2)}, u32[]{:S(2)}) %collective-permute-start.43) | collective-permute-done | bytes 593952 | tf_op jit(solution)/shard_map/ppermute | solution.py:33
  162.1 6.3 %collective-permute-done.45.refs_3_ = bf16[2320,128]{1,0:T(8,128)(2,1)S(1)} collective-permute-done((bf16[2320,128]{1,0:T(8,128)(2,1)S(1)}, bf16[2320,128]{1,0:T(8,128)(2,1)S(1)}, u32[]{:S(2)}, u32[]{:S(2)}) %collective-permute-start.45) | collective-permute-done | bytes 593952 | tf_op jit(solution)/shard_map/ppermute | solution.py:33
  (100 shorter events, 48.1 us)
Async XLA Ops:
  0.6 18.9 %collective-permute-start.6 = (bf16[2048,128]{1,0:T(8,128)(2,1)}, bf16[2048,128]{1,0:T(8,128)(2,1)S(1)}, u32[]{:S(2)}, u32[]{:S(2)}) collective-permute-start(bf16[2048,128]{1,0:T(8,128)(2,1)} %refs_0_.1), channel_id=1, source_target_pairs={{0,96},{1,25},{2,98},{3,27},{4,100},{5,29},{6,102},{7,31},{8,104},... | collective-permute-start | bytes 1572872 | tf_op jit(solution)/shard_map/ppermute | solution.py:33
  3.5 16.0 %collective-permute-start.7 = (bf16[2048,128]{1,0:T(8,128)(2,1)}, bf16[2048,128]{1,0:T(8,128)(2,1)S(1)}, u32[]{:S(2)}, u32[]{:S(2)}) collective-permute-start(bf16[2048,128]{1,0:T(8,128)(2,1)} %refs_0_.1), channel_id=1, source_target_pairs={{0,64},{1,17},{2,66},{3,19},{4,68},{5,21},{6,70},{7,23},{8,72},{9,... | collective-permute-start | bytes 1572872 | tf_op jit(solution)/shard_map/ppermute | solution.py:33
  4.3 15.9 %collective-permute-start.8 = (bf16[2048,128]{1,0:T(8,128)(2,1)}, bf16[2048,128]{1,0:T(8,128)(2,1)}, u32[]{:S(2)}, u32[]{:S(2)}) collective-permute-start(bf16[2048,128]{1,0:T(8,128)(2,1)} %refs_0_.1), channel_id=1, source_target_pairs={{0,32},{1,9},{2,34},{3,11},{4,36},{5,13},{6,38},{7,15},{8,40},{9,1... | collective-permute-start | bytes 1572872 | tf_op jit(solution)/shard_map/ppermute | solution.py:33
  22.4 23.5 %collective-permute-start.15 = (bf16[3328,128]{1,0:T(8,128)(2,1)S(1)}, bf16[3328,128]{1,0:T(8,128)(2,1)S(1)}, u32[]{:S(2)}, u32[]{:S(2)}) collective-permute-start(bf16[3328,128]{1,0:T(8,128)(2,1)S(1)} %get-tuple-element.182), channel_id=1, source_target_pairs={{0,24},{1,97},{2,26},{3,99},{4,28},{5,101},{6,30},{7,103},{8,0},{9... | collective-permute-start | bytes 2555912 | tf_op jit(solution)/shard_map/ppermute | solution.py:33
  26.5 19.4 %collective-permute-start.16 = (bf16[3328,128]{1,0:T(8,128)(2,1)S(1)}, bf16[3328,128]{1,0:T(8,128)(2,1)S(1)}, u32[]{:S(2)}, u32[]{:S(2)}) collective-permute-start(bf16[3328,128]{1,0:T(8,128)(2,1)S(1)} %get-tuple-element.183), channel_id=1, source_target_pairs={{0,16},{1,65},{2,18},{3,67},{4,20},{5,69},{6,22},{7,71},{8,24},{9,... | collective-permute-start | bytes 2555912 | tf_op jit(solution)/shard_map/ppermute | solution.py:33
  26.5 23.0 %collective-permute-start.17 = (bf16[3328,128]{1,0:T(8,128)(2,1)S(1)}, bf16[3328,128]{1,0:T(8,128)(2,1)S(1)}, u32[]{:S(2)}, u32[]{:S(2)}) collective-permute-start(bf16[3328,128]{1,0:T(8,128)(2,1)S(1)} %get-tuple-element.184), channel_id=1, source_target_pairs={{0,8},{1,33},{2,10},{3,35},{4,12},{5,37},{6,14},{7,39},{8,16},{9,4... | collective-permute-start | bytes 2555912 | tf_op jit(solution)/shard_map/ppermute | solution.py:33
  60.3 15.2 %collective-permute-start.23 = (bf16[1024,128]{1,0:T(8,128)(2,1)S(1)}, bf16[1024,128]{1,0:T(8,128)(2,1)S(1)}, u32[]{:S(2)}, u32[]{:S(2)}) collective-permute-start(bf16[1024,128]{1,0:T(8,128)(2,1)S(1)} %get-tuple-element.225), channel_id=1, source_target_pairs={{0,6},{1,3},{2,0},{3,5},{4,2},{5,7},{6,4},{7,1},{8,14},{9,11},{10,... | collective-permute-start | bytes 786440 | tf_op jit(solution)/shard_map/ppermute | solution.py:49
  63.7 11.8 %collective-permute-start.24 = (bf16[1024,128]{1,0:T(8,128)(2,1)S(1)}, bf16[1024,128]{1,0:T(8,128)(2,1)S(1)}, u32[]{:S(2)}, u32[]{:S(2)}) collective-permute-start(bf16[1024,128]{1,0:T(8,128)(2,1)S(1)} %get-tuple-element.224), channel_id=1, source_target_pairs={{0,4},{1,5},{2,6},{3,7},{4,0},{5,1},{6,2},{7,3},{8,12},{9,13},{10,... | collective-permute-start | bytes 786440 | tf_op jit(solution)/shard_map/ppermute | solution.py:49
  64.4 15.6 %collective-permute-start.25 = (bf16[1024,128]{1,0:T(8,128)(2,1)S(1)}, bf16[1024,128]{1,0:T(8,128)(2,1)S(1)}, u32[]{:S(2)}, u32[]{:S(2)}) collective-permute-start(bf16[1024,128]{1,0:T(8,128)(2,1)S(1)} %get-tuple-element.223), channel_id=1, source_target_pairs={{0,2},{1,7},{2,4},{3,1},{4,6},{5,3},{6,0},{7,5},{8,10},{9,15},{10,... | collective-permute-start | bytes 786440 | tf_op jit(solution)/shard_map/ppermute | solution.py:49
  64.9 21.9 %collective-permute-start.19 = (bf16[1024,128]{1,0:T(8,128)(2,1)S(1)}, bf16[1024,128]{1,0:T(8,128)(2,1)S(1)}, u32[]{:S(2)}, u32[]{:S(2)}) collective-permute-start(bf16[1024,128]{1,0:T(8,128)(2,1)S(1)} %get-tuple-element.228), channel_id=1, source_target_pairs={{0,6},{1,3},{2,0},{3,5},{4,2},{5,7},{6,4},{7,1},{8,14},{9,11},{10,... | collective-permute-start | bytes 786440 | tf_op jit(solution)/shard_map/ppermute | solution.py:49
  67.9 18.9 %collective-permute-start.20 = (bf16[1024,128]{1,0:T(8,128)(2,1)S(1)}, bf16[1024,128]{1,0:T(8,128)(2,1)S(1)}, u32[]{:S(2)}, u32[]{:S(2)}) collective-permute-start(bf16[1024,128]{1,0:T(8,128)(2,1)S(1)} %get-tuple-element.227), channel_id=1, source_target_pairs={{0,4},{1,5},{2,6},{3,7},{4,0},{5,1},{6,2},{7,3},{8,12},{9,13},{10,... | collective-permute-start | bytes 786440 | tf_op jit(solution)/shard_map/ppermute | solution.py:49
  75.5 16.4 %collective-permute-start.21 = (bf16[1024,128]{1,0:T(8,128)(2,1)S(1)}, bf16[1024,128]{1,0:T(8,128)(2,1)S(1)}, u32[]{:S(2)}, u32[]{:S(2)}) collective-permute-start(bf16[1024,128]{1,0:T(8,128)(2,1)S(1)} %get-tuple-element.226), channel_id=1, source_target_pairs={{0,2},{1,7},{2,4},{3,1},{4,6},{5,3},{6,0},{7,5},{8,10},{9,15},{10,... | collective-permute-start | bytes 786440 | tf_op jit(solution)/shard_map/ppermute | solution.py:49
  82.2 17.8 %collective-permute-start.34 = (bf16[1024,128]{1,0:T(8,128)(2,1)S(1)}, bf16[1024,128]{1,0:T(8,128)(2,1)S(1)}, u32[]{:S(2)}, u32[]{:S(2)}) collective-permute-start(bf16[1024,128]{1,0:T(8,128)(2,1)S(1)} %get-tuple-element.191.refs_12_), channel_id=1, source_target_pairs={{0,6},{1,3},{2,0},{3,5},{4,2},{5,7},{6,4},{7,1},{8,14},{9,11},{10,... | collective-permute-start | bytes 786440 | tf_op jit(solution)/shard_map/ppermute | solution.py:49
  86.8 13.2 %collective-permute-start.36 = (bf16[1024,128]{1,0:T(8,128)(2,1)S(1)}, bf16[1024,128]{1,0:T(8,128)(2,1)S(1)}, u32[]{:S(2)}, u32[]{:S(2)}) collective-permute-start(bf16[1024,128]{1,0:T(8,128)(2,1)S(1)} %get-tuple-element.191.refs_12_), channel_id=1, source_target_pairs={{0,4},{1,5},{2,6},{3,7},{4,0},{5,1},{6,2},{7,3},{8,12},{9,13},{10,... | collective-permute-start | bytes 786440 | tf_op jit(solution)/shard_map/ppermute | solution.py:49
  86.8 15.5 %collective-permute-start.38 = (bf16[1024,128]{1,0:T(8,128)(2,1)S(1)}, bf16[1024,128]{1,0:T(8,128)(2,1)S(1)}, u32[]{:S(2)}, u32[]{:S(2)}) collective-permute-start(bf16[1024,128]{1,0:T(8,128)(2,1)S(1)} %get-tuple-element.191.refs_12_), channel_id=1, source_target_pairs={{0,2},{1,7},{2,4},{3,1},{4,6},{5,3},{6,0},{7,5},{8,10},{9,15},{10,... | collective-permute-start | bytes 786440 | tf_op jit(solution)/shard_map/ppermute | solution.py:49
  94.2 17.8 %collective-permute-start.28 = (bf16[1296,128]{1,0:T(8,128)(2,1)S(1)}, bf16[1296,128]{1,0:T(8,128)(2,1)S(1)}, u32[]{:S(2)}, u32[]{:S(2)}) collective-permute-start(bf16[1296,128]{1,0:T(8,128)(2,1)S(1)} %get-tuple-element.195.refs_4_), channel_id=1, source_target_pairs={{0,6},{1,3},{2,0},{3,5},{4,2},{5,7},{6,4},{7,1},{8,14},{9,11},{10,... | collective-permute-start | bytes 995336 | tf_op jit(solution)/shard_map/ppermute | solution.py:49
  94.3 17.7 %collective-permute-start.30 = (bf16[1296,128]{1,0:T(8,128)(2,1)S(1)}, bf16[1296,128]{1,0:T(8,128)(2,1)S(1)}, u32[]{:S(2)}, u32[]{:S(2)}) collective-permute-start(bf16[1296,128]{1,0:T(8,128)(2,1)S(1)} %get-tuple-element.195.refs_4_), channel_id=1, source_target_pairs={{0,4},{1,5},{2,6},{3,7},{4,0},{5,1},{6,2},{7,3},{8,12},{9,13},{10,... | collective-permute-start | bytes 995336 | tf_op jit(solution)/shard_map/ppermute | solution.py:49
  100.0 13.9 %collective-permute-start.32 = (bf16[1296,128]{1,0:T(8,128)(2,1)S(1)}, bf16[1296,128]{1,0:T(8,128)(2,1)S(1)}, u32[]{:S(2)}, u32[]{:S(2)}) collective-permute-start(bf16[1296,128]{1,0:T(8,128)(2,1)S(1)} %get-tuple-element.195.refs_4_), channel_id=1, source_target_pairs={{0,2},{1,7},{2,4},{3,1},{4,6},{5,3},{6,0},{7,5},{8,10},{9,15},{10,... | collective-permute-start | bytes 995336 | tf_op jit(solution)/shard_map/ppermute | solution.py:49
  102.4 13.5 %collective-permute-start.27 = (bf16[1296,128]{1,0:T(8,128)(2,1)S(1)}, bf16[1296,128]{1,0:T(8,128)(2,1)S(1)}, u32[]{:S(2)}, u32[]{:S(2)}) collective-permute-start(bf16[1296,128]{1,0:T(8,128)(2,1)S(1)} %get-tuple-element.195.refs_4_), channel_id=1, source_target_pairs={{0,1},{1,0},{2,3},{3,2},{4,5},{5,4},{6,7},{7,6},{8,9},{9,8},{10,11... | collective-permute-start | bytes 995336 | tf_op jit(solution)/shard_map/ppermute | solution.py:54
  120.6 22.7 %collective-permute-start.40 = (bf16[3600,128]{1,0:T(8,128)(2,1)S(1)}, bf16[3600,128]{1,0:T(8,128)(2,1)S(1)}, u32[]{:S(2)}, u32[]{:S(2)}) collective-permute-start(bf16[3600,128]{1,0:T(8,128)(2,1)S(1)} %get-tuple-element.198), channel_id=1, source_target_pairs={{0,24},{1,97},{2,26},{3,99},{4,28},{5,101},{6,30},{7,103},{8,0},{9... | collective-permute-start | bytes 2764808 | tf_op jit(solution)/shard_map/ppermute | solution.py:33
  122.5 20.9 %collective-permute-start.41 = (bf16[3600,128]{1,0:T(8,128)(2,1)S(1)}, bf16[3600,128]{1,0:T(8,128)(2,1)S(1)}, u32[]{:S(2)}, u32[]{:S(2)}) collective-permute-start(bf16[3600,128]{1,0:T(8,128)(2,1)S(1)} %get-tuple-element.199), channel_id=1, source_target_pairs={{0,16},{1,65},{2,18},{3,67},{4,20},{5,69},{6,22},{7,71},{8,24},{9,... | collective-permute-start | bytes 2764808 | tf_op jit(solution)/shard_map/ppermute | solution.py:33
  122.5 24.5 %collective-permute-start.42 = (bf16[3600,128]{1,0:T(8,128)(2,1)S(1)}, bf16[3600,128]{1,0:T(8,128)(2,1)S(1)}, u32[]{:S(2)}, u32[]{:S(2)}) collective-permute-start(bf16[3600,128]{1,0:T(8,128)(2,1)S(1)} %get-tuple-element.200), channel_id=1, source_target_pairs={{0,8},{1,33},{2,10},{3,35},{4,12},{5,37},{6,14},{7,39},{8,16},{9,4... | collective-permute-start | bytes 2764808 | tf_op jit(solution)/shard_map/ppermute | solution.py:33
  150.5 11.6 %collective-permute-start.44 = (bf16[2320,128]{1,0:T(8,128)(2,1)S(1)}, bf16[2320,128]{1,0:T(8,128)(2,1)S(1)}, u32[]{:S(2)}, u32[]{:S(2)}) collective-permute-start(bf16[2320,128]{1,0:T(8,128)(2,1)S(1)} %get-tuple-element.203), channel_id=1, source_target_pairs={{0,64},{1,17},{2,66},{3,19},{4,68},{5,21},{6,70},{7,23},{8,72},{9,... | collective-permute-start | bytes 1781768 | tf_op jit(solution)/shard_map/ppermute | solution.py:33
  152.4 16.0 %collective-permute-start.45 = (bf16[2320,128]{1,0:T(8,128)(2,1)S(1)}, bf16[2320,128]{1,0:T(8,128)(2,1)S(1)}, u32[]{:S(2)}, u32[]{:S(2)}) collective-permute-start(bf16[2320,128]{1,0:T(8,128)(2,1)S(1)} %get-tuple-element.204), channel_id=1, source_target_pairs={{0,32},{1,9},{2,34},{3,11},{4,36},{5,13},{6,38},{7,15},{8,40},{9,1... | collective-permute-start | bytes 1781768 | tf_op jit(solution)/shard_map/ppermute | solution.py:33
  (31 other events, 358.8 us)

commit v9 on v8

--- a/solution.py
+++ b/solution.py
@@ -360,14 +360,9 @@
 
 
 def finish_kernel(*refs, scaling):
-    pieces, sums, (nodes, weight, offset), (held, sems) = refs[:4], refs[4], refs[5:8], refs[8:]
+    pieces, sums, (nodes, weight, offset) = refs[:4], refs[4], refs[5:]
     rows = nodes.shape[0]
-    copies = []
-    for k in range(4):
-        part = pl.ds(k * rows // 4, rows // 4)
-        held[part] = total_of([ref[part] for ref in pieces])
-        copies.append(pltpu.make_async_copy(held.at[part], nodes.at[part], sems.at[k]))
-        copies[k].start()
+    nodes[...] = total_of([ref[pl.ds(0, rows)] for ref in pieces])
     lines = sums.shape[0]
     for k in range(2):
         part = pl.ds(k * T, T)
@@ -377,8 +372,6 @@
         total = total * scaling
         weight[:, part] = total[:T]
         offset[:, part] = jnp.sum(total[T:], axis=0, keepdims=True)
-    for copy in copies:
-        copy.wait()
 
 
 def finish(pieces, sums, scaling):
@@ -391,8 +384,7 @@
             jax.ShapeDtypeStruct((1, width), F32),
         ],
         in_specs=[VMEM] * 5,
-        out_specs=[ANY] + [VMEM] * 2,
-        scratch_shapes=[pltpu.VMEM(pieces[0].shape, F32), pltpu.SemaphoreType.DMA((4,))],
+        out_specs=[VMEM] * 3,
         compiler_params=room(10),
     )(*pieces, sums)
 
@@ -474,17 +466,14 @@
     named = ring_swap([None] + sends, along_outer)[1:]
     full = functools.reduce(jnp.maximum, ring_gather(said, along_inner))[0, 0] > 0.5
 
-    def forward_all(pieces, named):
-        whole = jnp.concatenate(pieces)
-        whole = ring_gather(whole, along_outer)
+    def forward_all(outs, pieces):
+        whole = ring_gather(jnp.concatenate(pieces), along_outer)
         spans = (4 * nodes_here,) * 4
         return products(live, tables, 2, 0, tiles, whole, spans, (32,) * 4, (1,))
 
-    def forward_named(pieces, named):
-        spans = (nodes_here,) * 4 + (CAP * T,) * 3
-        return products(live, tables, 1, 0, tiles, pieces + named, spans, (32,) * 4, (1,))
-
-    outs = lax.cond(full, forward_all, forward_named, pieces, named)
+    spans = (nodes_here,) * 4 + (CAP * T,) * 3
+    outs = products(live, tables, 1, 0, tiles, pieces + named, spans, (32,) * 4, (1,))
+    outs = lax.cond(full, forward_all, lambda outs, pieces: outs, outs, pieces)
 
     part_rows = nodes_here // 2
     halves = []
@@ -512,20 +501,14 @@
     )
     parts = ring_swap([None] + parts, along_outer)[1:]
 
-    def backward_all(here, sums, parts, gathered):
-        outs = products(live, tables, 3, 2, tiles, gathered, spans, (64,) * 4, (0,))
-        mine = total_of(ring_swap(outs, along_outer)).reshape(4, nodes_here, T)
-        tail = total_of([p[CAP * T :] for p in parts])
-        lines = sums.shape[0]
-        sums = sums + jnp.concatenate([tail[:lines], tail[lines:]], axis=1)
-        tail = jnp.concatenate([sums[:, :T], sums[:, T:]]).astype(BF16)
-        far = [jnp.concatenate([mine[d].astype(BF16), tail]) for d in (1, 2, 3)]
-        return [mine[0]] + far + [sums]
-
-    def backward_named(here, sums, parts, gathered):
-        return list(combine(lists, counts, here, sums, parts))
-
-    *outs, sums = lax.cond(full, backward_all, backward_named, here, sums, parts, gathered)
+    def backward_all(outs, gathered):
+        mine = products(live, tables, 3, 2, tiles, gathered, spans, (64,) * 4, (0,))
+        mine = total_of(ring_swap(mine, along_outer)).reshape(4, nodes_here, T)
+        far = [outs[d].at[:nodes_here].set(mine[d].astype(BF16)) for d in (1, 2, 3)]
+        return [mine[0]] + far
+
+    *outs, sums = combine(lists, counts, here, sums, parts)
+    outs = lax.cond(full, backward_all, lambda outs, gathered: outs, outs, gathered)
     outs = ring_swap(outs, along_inner)
     grad_features, grad_weight, grad_offset = finish(outs, sums, scaling)
     return (hidden, grad_features, grad_weight, grad_offset.reshape(-1))

time: 172 us -> 172 us (level)
  starting transfers between devices: 40.6 us -> 62.5 us
  waiting for transfers between devices: 101 us -> 80.8 us
    ppermute x12, waiting for transfers between devices: 30.9 us -> 18.5 us  [along_y(): return lax.ppermute(value, 'col', pairs)]
    ppermute x18, starting transfers between devices: 21.5 us -> 30.3 us  [along_xz(): return lax.ppermute(value, ('row', 'col'), pairs)]
    ppermute x18, waiting for transfers between devices: 66.1 us -> 57.6 us  [along_xz(): return lax.ppermute(value, ('row', 'col'), pairs)]
    ppermute x10, starting transfers between devices: 2.19 us -> 9.03 us  [other_core(): return lax.ppermute(value, 'col', pairs)]
    ppermute x12, starting transfers between devices: 16.9 us -> 23.1 us  [along_y(): return lax.ppermute(value, 'col', pairs)]
  transfers between devices with their start and end apart: 40 -> 40, of which waited for: 22 -> 21; matrix products, arithmetic and copies ran while one was open for 1% -> 1% of each run, Pallas kernels for 3% -> 3%
where the time goes in v9:
time: 172 us
  waiting for transfers between devices  80.8 us (47%)
  starting transfers between devices  62.5 us (36%)
  Pallas kernels  23.1 us (13%)
  between operations  2.12 us (1%)
  local copies, waits for them, and re-layouts  1.84 us (1%)
    ppermute x18, waiting for transfers between devices, along_xz(): return lax.ppermute(value, ('row', 'col'), pairs)  57.6 us
    ppermute x18, starting transfers between devices, along_xz(): return lax.ppermute(value, ('row', 'col'), pairs)  30.3 us
    ppermute x12, starting transfers between devices, along_y(): return lax.ppermute(value, 'col', pairs)  23.1 us
    ppermute x12, waiting for transfers between devices, along_y(): return lax.ppermute(value, 'col', pairs)  18.5 us
    pallas_call x2, Pallas kernels, products(): pl.pallas_call(kernel, out_shape=[jax.ShapeDtypeStruct((n * T + e, T), BF...  9.54 us
    ppermute x10, starting transfers between devices, other_core(): return lax.ppermute(value, 'col', pairs)  9.03 us
    ppermute x10, waiting for transfers between devices, other_core(): return lax.ppermute(value, 'col', pairs)  4.63 us
    pallas_call x2, Pallas kernels, dense(): pl.pallas_call(functools.partial(dense_kernel, step=step), grid=(steps,),...  4.51 us
  transfers between devices with their start and end apart: 40, of which 21 were waited for; matrix products, arithmetic and copies ran while one was open for 1% of the time, Pallas kernels for 3%

profile of v9, /device:TPU:0, one launch (start us, length us, event | category | flops | bytes accessed | tf_op | source)
XLA Modules:
  0.0 172.0 jit_solution(16388400868495310925)
XLA Ops:
  2.3 2.7 %collective-permute-start.7 = (bf16[2048,128]{1,0:T(8,128)(2,1)}, bf16[2048,128]{1,0:T(8,128)(2,1)S(1)}, u32[]{:S(2)}, u32[]{:S(2)}) collective-permute-start(bf16[2048,128]{1,0:T(8,128)(2,1)} %refs_0_.3), channel_id=1, source_target_pairs={{0,64},{1,17},{2,66},{3,19},{4,68},{5,21},{6,70},{7,23},{8,72},{9,... | collective-permute-start | bytes 1572872 | tf_op jit(solution)/shard_map/ppermute | solution.py:33
  10.7 3.6 %collective-permute-start.10 = (bf16[16,128]{1,0:T(8,128)(2,1)S(1)}, bf16[16,128]{1,0:T(8,128)(2,1)S(1)}, u32[]{:S(2)}, u32[]{:S(2)}) collective-permute-start(bf16[16,128]{1,0:T(8,128)(2,1)S(1)} %get-tuple-element.181.refs_4_), channel_id=1, source_target_pairs={{0,16},{1,65},{2,18},{3,67},{4,20},{5,69},{6,22},{7,71},{8,24},{9,... | collective-permute-start | bytes 12296 | tf_op jit(solution)/shard_map/ppermute | solution.py:33
  20.7 3.7 %collective-permute-start.15 = (bf16[3328,128]{1,0:T(8,128)(2,1)S(1)}, bf16[3328,128]{1,0:T(8,128)(2,1)S(1)}, u32[]{:S(2)}, u32[]{:S(2)}) collective-permute-start(bf16[3328,128]{1,0:T(8,128)(2,1)S(1)} %get-tuple-element.184), channel_id=1, source_target_pairs={{0,24},{1,97},{2,26},{3,99},{4,28},{5,101},{6,30},{7,103},{8,0},{9... | collective-permute-start | bytes 2555912 | tf_op jit(solution)/shard_map/ppermute | solution.py:33
  29.9 6.4 %collective-permute-done.14 = f32[8,128]{1,0:T(8,128)S(1)} collective-permute-done((f32[8,128]{1,0:T(8,128)S(1)}, f32[8,128]{1,0:T(8,128)S(1)}, u32[]{:S(2)}, u32[]{:S(2)}) %collective-permute-start.14) | collective-permute-done | bytes 4128 | tf_op jit(solution)/shard_map/ppermute | solution.py:33
  36.3 3.7 %collective-permute-done.12 = f32[8,128]{1,0:T(8,128)S(1)} collective-permute-done((f32[8,128]{1,0:T(8,128)S(1)}, f32[8,128]{1,0:T(8,128)S(1)}, u32[]{:S(2)}, u32[]{:S(2)}) %collective-permute-start.12) | collective-permute-done | bytes 4128 | tf_op jit(solution)/shard_map/ppermute | solution.py:33
  41.1 2.8 %collective-permute-done.15.refs_4_ = bf16[3328,128]{1,0:T(8,128)(2,1)S(1)} collective-permute-done((bf16[3328,128]{1,0:T(8,128)(2,1)S(1)}, bf16[3328,128]{1,0:T(8,128)(2,1)S(1)}, u32[]{:S(2)}, u32[]{:S(2)}) %collective-permute-start.15) | collective-permute-done | bytes 852000 | tf_op jit(solution)/shard_map/ppermute | solution.py:33
  43.9 3.6 %collective-permute-done.17.refs_6_ = bf16[3328,128]{1,0:T(8,128)(2,1)S(1)} collective-permute-done((bf16[3328,128]{1,0:T(8,128)(2,1)S(1)}, bf16[3328,128]{1,0:T(8,128)(2,1)S(1)}, u32[]{:S(2)}, u32[]{:S(2)}) %collective-permute-start.17) | collective-permute-done | bytes 852000 | tf_op jit(solution)/shard_map/ppermute | solution.py:33
  47.6 5.3 %shard_map.113 = (bf16[4096,128]{1,0:T(8,128)(2,1)}, bf16[4096,128]{1,0:T(8,128)(2,1)}, bf16[4096,128]{1,0:T(8,128)(2,1)}, bf16[4096,128]{1,0:T(8,128)(2,1)}) custom-call(s32[1]{0:T(128)} %bitcast.10.live, s32[8,64]{1,0:T(8,128)S(1)} %get-tuple-element.183.tables, bf16[64,128,128]{2,1,0:T(8,128)(2,1)S(1)} %bitcast.16, bf16[2048,128]{1,0:T(8,128)(2,1)} %refs_0_.3, ...), custom_call_target="tpu_custom_call" | custom-call | tf_op jit(solution)/shard_map/pallas_call | solution.py:224
  58.9 3.2 %collective-permute-start.24 = (bf16[1024,128]{1,0:T(8,128)(2,1)S(1)}, bf16[1024,128]{1,0:T(8,128)(2,1)S(1)}, u32[]{:S(2)}, u32[]{:S(2)}) collective-permute-start(bf16[1024,128]{1,0:T(8,128)(2,1)S(1)} %get-tuple-element.221), channel_id=1, source_target_pairs={{0,4},{1,5},{2,6},{3,7},{4,0},{5,1},{6,2},{7,3},{8,12},{9,13},{10,... | collective-permute-start | bytes 786440 | tf_op jit(solution)/shard_map/ppermute | solution.py:49
  68.9 5.1 %collective-permute-done.24.refs_3_ = bf16[1024,128]{1,0:T(8,128)(2,1)S(1)} collective-permute-done((bf16[1024,128]{1,0:T(8,128)(2,1)S(1)}, bf16[1024,128]{1,0:T(8,128)(2,1)S(1)}, u32[]{:S(2)}, u32[]{:S(2)}) %collective-permute-start.24) | collective-permute-done | bytes 262176 | tf_op jit(solution)/shard_map/ppermute | solution.py:49
  78.3 7.9 %collective-permute-start.36 = (bf16[1024,128]{1,0:T(8,128)(2,1)S(1)}, bf16[1024,128]{1,0:T(8,128)(2,1)S(1)}, u32[]{:S(2)}, u32[]{:S(2)}) collective-permute-start(bf16[1024,128]{1,0:T(8,128)(2,1)S(1)} %get-tuple-element.193.refs_12_), channel_id=1, source_target_pairs={{0,4},{1,5},{2,6},{3,7},{4,0},{5,1},{6,2},{7,3},{8,12},{9,13},{10,... | collective-permute-start | bytes 786440 | tf_op jit(solution)/shard_map/ppermute | solution.py:49
  90.9 2.4 %collective-permute-start.28 = (bf16[1296,128]{1,0:T(8,128)(2,1)S(1)}, bf16[1296,128]{1,0:T(8,128)(2,1)S(1)}, u32[]{:S(2)}, u32[]{:S(2)}) collective-permute-start(bf16[1296,128]{1,0:T(8,128)(2,1)S(1)} %get-tuple-element.197.refs_4_), channel_id=1, source_target_pairs={{0,6},{1,3},{2,0},{3,5},{4,2},{5,7},{6,4},{7,1},{8,14},{9,11},{10,... | collective-permute-start | bytes 995336 | tf_op jit(solution)/shard_map/ppermute | solution.py:49
  93.3 4.4 %collective-permute-done.36.refs_14_ = bf16[1024,128]{1,0:T(8,128)(2,1)S(1)} collective-permute-done((bf16[1024,128]{1,0:T(8,128)(2,1)S(1)}, bf16[1024,128]{1,0:T(8,128)(2,1)S(1)}, u32[]{:S(2)}, u32[]{:S(2)}) %collective-permute-start.36) | collective-permute-done | bytes 262176 | tf_op jit(solution)/shard_map/ppermute | solution.py:49
  99.4 3.9 %collective-permute-done.32.refs_7_ = bf16[1296,128]{1,0:T(8,128)(2,1)S(1)} collective-permute-done((bf16[1296,128]{1,0:T(8,128)(2,1)S(1)}, bf16[1296,128]{1,0:T(8,128)(2,1)S(1)}, u32[]{:S(2)}, u32[]{:S(2)}) %collective-permute-start.32) | collective-permute-done | bytes 331808 | tf_op jit(solution)/shard_map/ppermute | solution.py:49
  103.3 6.7 %collective-permute-start.33 = (bf16[1296,128]{1,0:T(8,128)(2,1)S(1)}, bf16[1296,128]{1,0:T(8,128)(2,1)S(1)}, u32[]{:S(2)}, u32[]{:S(2)}) collective-permute-start(bf16[1296,128]{1,0:T(8,128)(2,1)S(1)} %collective-permute-done.32.refs_7_), channel_id=1, source_target_pairs={{0,1},{1,0},{2,3},{3,2},{4,5},{5,4},{6,7},{7,6},{8,9},{9,8},{10,11... | collective-permute-start | bytes 995336 | tf_op jit(solution)/shard_map/ppermute | solution.py:54
  114.4 4.3 %shard_map.116 = (bf16[8192,128]{1,0:T(8,128)(2,1)S(1)}, bf16[3600,128]{1,0:T(8,128)(2,1)S(1)}, bf16[3600,128]{1,0:T(8,128)(2,1)S(1)}, bf16[3600,128]{1,0:T(8,128)(2,1)S(1)}, f32[136,256]{1,0:T(8,128)S(1)}) custom-call(s32[1]{0:T(128)} %bitcast.11.live, s32[8,64]{1,0:T(8,128)S(1)} %get-tuple-element.183.tables, bf16[64,128,128]{2,1,0:T(8,128)(2,1)S(1)} %bitcast.18, ...), custom_call_target="tpu_custom_call" | custom-call | tf_op jit(solution)/shard_map/pallas_call | solution.py:224
  121.8 10.4 %collective-permute-done.40.refs_0_ = bf16[3600,128]{1,0:T(8,128)(2,1)S(1)} collective-permute-done((bf16[3600,128]{1,0:T(8,128)(2,1)S(1)}, bf16[3600,128]{1,0:T(8,128)(2,1)S(1)}, u32[]{:S(2)}, u32[]{:S(2)}) %collective-permute-start.40) | collective-permute-done | bytes 921632 | tf_op jit(solution)/shard_map/ppermute | solution.py:33
  132.2 3.1 %collective-permute-done.41.refs_1_ = bf16[3600,128]{1,0:T(8,128)(2,1)S(1)} collective-permute-done((bf16[3600,128]{1,0:T(8,128)(2,1)S(1)}, bf16[3600,128]{1,0:T(8,128)(2,1)S(1)}, u32[]{:S(2)}, u32[]{:S(2)}) %collective-permute-start.41) | collective-permute-done | bytes 921632 | tf_op jit(solution)/shard_map/ppermute | solution.py:33
  135.3 9.8 %collective-permute-done.42.refs_2_ = bf16[3600,128]{1,0:T(8,128)(2,1)S(1)} collective-permute-done((bf16[3600,128]{1,0:T(8,128)(2,1)S(1)}, bf16[3600,128]{1,0:T(8,128)(2,1)S(1)}, u32[]{:S(2)}, u32[]{:S(2)}) %collective-permute-start.42) | collective-permute-done | bytes 921632 | tf_op jit(solution)/shard_map/ppermute | solution.py:33
  145.1 3.9 %shard_map.117 = (f32[2048,128]{1,0:T(8,128)}, bf16[2320,128]{1,0:T(8,128)(2,1)}, bf16[2320,128]{1,0:T(8,128)(2,1)}, bf16[2320,128]{1,0:T(8,128)(2,1)}, f32[136,256]{1,0:T(8,128)S(1)}) custom-call(s32[96]{0:T(128)S(1)} %get-tuple-element.195.lists, s32[3]{0:T(128)S(1)} %get-tuple-element.196.counts, bf16[8192,128]{1,0:T(8,128)(2,1)S(1)} %get-tuple-element.198.own_ref, ...), custom_call_target="tpu_custom_call" | custom-call | tf_op jit(solution)/shard_map/pallas_call | solution.py:345
  149.0 2.5 %collective-permute-start.43 = (bf16[2320,128]{1,0:T(8,128)(2,1)}, bf16[2320,128]{1,0:T(8,128)(2,1)S(1)}, u32[]{:S(2)}, u32[]{:S(2)}) collective-permute-start(bf16[2320,128]{1,0:T(8,128)(2,1)} %get-tuple-element.208), channel_id=1, source_target_pairs={{0,96},{1,25},{2,98},{3,27},{4,100},{5,29},{6,102},{7,31},{8,104},... | collective-permute-start | bytes 1781768 | tf_op jit(solution)/shard_map/ppermute | solution.py:33
  154.0 11.7 %collective-permute-done.43.refs_1_ = bf16[2320,128]{1,0:T(8,128)(2,1)S(1)} collective-permute-done((bf16[2320,128]{1,0:T(8,128)(2,1)}, bf16[2320,128]{1,0:T(8,128)(2,1)S(1)}, u32[]{:S(2)}, u32[]{:S(2)}) %collective-permute-start.43) | collective-permute-done | bytes 593952 | tf_op jit(solution)/shard_map/ppermute | solution.py:33
  165.7 3.8 %collective-permute-done.45.refs_3_ = bf16[2320,128]{1,0:T(8,128)(2,1)S(1)} collective-permute-done((bf16[2320,128]{1,0:T(8,128)(2,1)}, bf16[2320,128]{1,0:T(8,128)(2,1)S(1)}, u32[]{:S(2)}, u32[]{:S(2)}) %collective-permute-start.45) | collective-permute-done | bytes 593952 | tf_op jit(solution)/shard_map/ppermute | solution.py:33
  169.5 2.5 %shard_map.118 = (f32[2048,128]{1,0:T(8,128)}, f32[128,256]{1,0:T(8,128)}, f32[1,256]{1,0:T(1,128)}) custom-call(f32[2048,128]{1,0:T(8,128)} %get-tuple-element.207.refs_0_, bf16[2320,128]{1,0:T(8,128)(2,1)S(1)} %collective-permute-done.43.refs_1_, bf16[2320,128]{1,0:T(8,128)(2,1)S(1)} %collective-permute-done.44.refs_2_, ...), custom_call_target="tpu_custom_call" | custom-call | tf_op jit(solution)/shard_map/pallas_call | solution.py:379
  (88 shorter events, 52.6 us)
Async XLA Ops:
  0.6 17.8 %collective-permute-start.8 = (bf16[2048,128]{1,0:T(8,128)(2,1)}, bf16[2048,128]{1,0:T(8,128)(2,1)S(1)}, u32[]{:S(2)}, u32[]{:S(2)}) collective-permute-start(bf16[2048,128]{1,0:T(8,128)(2,1)} %refs_0_.3), channel_id=1, source_target_pairs={{0,32},{1,9},{2,34},{3,11},{4,36},{5,13},{6,38},{7,15},{8,40},{9,1... | collective-permute-start | bytes 1572872 | tf_op jit(solution)/shard_map/ppermute | solution.py:33
  2.3 16.1 %collective-permute-start.7 = (bf16[2048,128]{1,0:T(8,128)(2,1)}, bf16[2048,128]{1,0:T(8,128)(2,1)S(1)}, u32[]{:S(2)}, u32[]{:S(2)}) collective-permute-start(bf16[2048,128]{1,0:T(8,128)(2,1)} %refs_0_.3), channel_id=1, source_target_pairs={{0,64},{1,17},{2,66},{3,19},{4,68},{5,21},{6,70},{7,23},{8,72},{9,... | collective-permute-start | bytes 1572872 | tf_op jit(solution)/shard_map/ppermute | solution.py:33
  5.0 13.4 %collective-permute-start.6 = (bf16[2048,128]{1,0:T(8,128)(2,1)}, bf16[2048,128]{1,0:T(8,128)(2,1)}, u32[]{:S(2)}, u32[]{:S(2)}) collective-permute-start(bf16[2048,128]{1,0:T(8,128)(2,1)} %refs_0_.3), channel_id=1, source_target_pairs={{0,96},{1,25},{2,98},{3,27},{4,100},{5,29},{6,102},{7,31},{8,104},... | collective-permute-start | bytes 1572872 | tf_op jit(solution)/shard_map/ppermute | solution.py:33
  20.7 23.1 %collective-permute-start.15 = (bf16[3328,128]{1,0:T(8,128)(2,1)S(1)}, bf16[3328,128]{1,0:T(8,128)(2,1)S(1)}, u32[]{:S(2)}, u32[]{:S(2)}) collective-permute-start(bf16[3328,128]{1,0:T(8,128)(2,1)S(1)} %get-tuple-element.184), channel_id=1, source_target_pairs={{0,24},{1,97},{2,26},{3,99},{4,28},{5,101},{6,30},{7,103},{8,0},{9... | collective-permute-start | bytes 2555912 | tf_op jit(solution)/shard_map/ppermute | solution.py:33
  24.5 19.4 %collective-permute-start.16 = (bf16[3328,128]{1,0:T(8,128)(2,1)S(1)}, bf16[3328,128]{1,0:T(8,128)(2,1)S(1)}, u32[]{:S(2)}, u32[]{:S(2)}) collective-permute-start(bf16[3328,128]{1,0:T(8,128)(2,1)S(1)} %get-tuple-element.185), channel_id=1, source_target_pairs={{0,16},{1,65},{2,18},{3,67},{4,20},{5,69},{6,22},{7,71},{8,24},{9,... | collective-permute-start | bytes 2555912 | tf_op jit(solution)/shard_map/ppermute | solution.py:33
  24.5 23.1 %collective-permute-start.17 = (bf16[3328,128]{1,0:T(8,128)(2,1)S(1)}, bf16[3328,128]{1,0:T(8,128)(2,1)S(1)}, u32[]{:S(2)}, u32[]{:S(2)}) collective-permute-start(bf16[3328,128]{1,0:T(8,128)(2,1)S(1)} %get-tuple-element.186), channel_id=1, source_target_pairs={{0,8},{1,33},{2,10},{3,35},{4,12},{5,37},{6,14},{7,39},{8,16},{9,4... | collective-permute-start | bytes 2555912 | tf_op jit(solution)/shard_map/ppermute | solution.py:33
  58.9 15.1 %collective-permute-start.24 = (bf16[1024,128]{1,0:T(8,128)(2,1)S(1)}, bf16[1024,128]{1,0:T(8,128)(2,1)S(1)}, u32[]{:S(2)}, u32[]{:S(2)}) collective-permute-start(bf16[1024,128]{1,0:T(8,128)(2,1)S(1)} %get-tuple-element.221), channel_id=1, source_target_pairs={{0,4},{1,5},{2,6},{3,7},{4,0},{5,1},{6,2},{7,3},{8,12},{9,13},{10,... | collective-permute-start | bytes 786440 | tf_op jit(solution)/shard_map/ppermute | solution.py:49
  62.1 12.4 %collective-permute-start.23 = (bf16[1024,128]{1,0:T(8,128)(2,1)S(1)}, bf16[1024,128]{1,0:T(8,128)(2,1)S(1)}, u32[]{:S(2)}, u32[]{:S(2)}) collective-permute-start(bf16[1024,128]{1,0:T(8,128)(2,1)S(1)} %get-tuple-element.222), channel_id=1, source_target_pairs={{0,6},{1,3},{2,0},{3,5},{4,2},{5,7},{6,4},{7,1},{8,14},{9,11},{10,... | collective-permute-start | bytes 786440 | tf_op jit(solution)/shard_map/ppermute | solution.py:49
  63.0 15.3 %collective-permute-start.21 = (bf16[1024,128]{1,0:T(8,128)(2,1)S(1)}, bf16[1024,128]{1,0:T(8,128)(2,1)S(1)}, u32[]{:S(2)}, u32[]{:S(2)}) collective-permute-start(bf16[1024,128]{1,0:T(8,128)(2,1)S(1)} %get-tuple-element.223), channel_id=1, source_target_pairs={{0,2},{1,7},{2,4},{3,1},{4,6},{5,3},{6,0},{7,5},{8,10},{9,15},{10,... | collective-permute-start | bytes 786440 | tf_op jit(solution)/shard_map/ppermute | solution.py:49
  64.4 21.8 %collective-permute-start.20 = (bf16[1024,128]{1,0:T(8,128)(2,1)S(1)}, bf16[1024,128]{1,0:T(8,128)(2,1)S(1)}, u32[]{:S(2)}, u32[]{:S(2)}) collective-permute-start(bf16[1024,128]{1,0:T(8,128)(2,1)S(1)} %get-tuple-element.224), channel_id=1, source_target_pairs={{0,4},{1,5},{2,6},{3,7},{4,0},{5,1},{6,2},{7,3},{8,12},{9,13},{10,... | collective-permute-start | bytes 786440 | tf_op jit(solution)/shard_map/ppermute | solution.py:49
  66.7 19.6 %collective-permute-start.19 = (bf16[1024,128]{1,0:T(8,128)(2,1)S(1)}, bf16[1024,128]{1,0:T(8,128)(2,1)S(1)}, u32[]{:S(2)}, u32[]{:S(2)}) collective-permute-start(bf16[1024,128]{1,0:T(8,128)(2,1)S(1)} %get-tuple-element.225), channel_id=1, source_target_pairs={{0,6},{1,3},{2,0},{3,5},{4,2},{5,7},{6,4},{7,1},{8,14},{9,11},{10,... | collective-permute-start | bytes 786440 | tf_op jit(solution)/shard_map/ppermute | solution.py:49
  77.2 13.7 %collective-permute-start.38 = (bf16[1024,128]{1,0:T(8,128)(2,1)S(1)}, bf16[1024,128]{1,0:T(8,128)(2,1)S(1)}, u32[]{:S(2)}, u32[]{:S(2)}) collective-permute-start(bf16[1024,128]{1,0:T(8,128)(2,1)S(1)} %get-tuple-element.193.refs_12_), channel_id=1, source_target_pairs={{0,2},{1,7},{2,4},{3,1},{4,6},{5,3},{6,0},{7,5},{8,10},{9,15},{10,... | collective-permute-start | bytes 786440 | tf_op jit(solution)/shard_map/ppermute | solution.py:49
  78.3 19.3 %collective-permute-start.36 = (bf16[1024,128]{1,0:T(8,128)(2,1)S(1)}, bf16[1024,128]{1,0:T(8,128)(2,1)S(1)}, u32[]{:S(2)}, u32[]{:S(2)}) collective-permute-start(bf16[1024,128]{1,0:T(8,128)(2,1)S(1)} %get-tuple-element.193.refs_12_), channel_id=1, source_target_pairs={{0,4},{1,5},{2,6},{3,7},{4,0},{5,1},{6,2},{7,3},{8,12},{9,13},{10,... | collective-permute-start | bytes 786440 | tf_op jit(solution)/shard_map/ppermute | solution.py:49
  88.6 14.7 %collective-permute-start.32 = (bf16[1296,128]{1,0:T(8,128)(2,1)S(1)}, bf16[1296,128]{1,0:T(8,128)(2,1)S(1)}, u32[]{:S(2)}, u32[]{:S(2)}) collective-permute-start(bf16[1296,128]{1,0:T(8,128)(2,1)S(1)} %get-tuple-element.197.refs_4_), channel_id=1, source_target_pairs={{0,2},{1,7},{2,4},{3,1},{4,6},{5,3},{6,0},{7,5},{8,10},{9,15},{10,... | collective-permute-start | bytes 995336 | tf_op jit(solution)/shard_map/ppermute | solution.py:49
  90.6 21.3 %collective-permute-start.30 = (bf16[1296,128]{1,0:T(8,128)(2,1)S(1)}, bf16[1296,128]{1,0:T(8,128)(2,1)S(1)}, u32[]{:S(2)}, u32[]{:S(2)}) collective-permute-start(bf16[1296,128]{1,0:T(8,128)(2,1)S(1)} %get-tuple-element.197.refs_4_), channel_id=1, source_target_pairs={{0,4},{1,5},{2,6},{3,7},{4,0},{5,1},{6,2},{7,3},{8,12},{9,13},{10,... | collective-permute-start | bytes 995336 | tf_op jit(solution)/shard_map/ppermute | solution.py:49
  90.9 21.1 %collective-permute-start.28 = (bf16[1296,128]{1,0:T(8,128)(2,1)S(1)}, bf16[1296,128]{1,0:T(8,128)(2,1)S(1)}, u32[]{:S(2)}, u32[]{:S(2)}) collective-permute-start(bf16[1296,128]{1,0:T(8,128)(2,1)S(1)} %get-tuple-element.197.refs_4_), channel_id=1, source_target_pairs={{0,6},{1,3},{2,0},{3,5},{4,2},{5,7},{6,4},{7,1},{8,14},{9,11},{10,... | collective-permute-start | bytes 995336 | tf_op jit(solution)/shard_map/ppermute | solution.py:49
  98.4 14.1 %collective-permute-start.37 = (bf16[1024,128]{1,0:T(8,128)(2,1)S(1)}, bf16[1024,128]{1,0:T(8,128)(2,1)S(1)}, u32[]{:S(2)}, u32[]{:S(2)}) collective-permute-start(bf16[1024,128]{1,0:T(8,128)(2,1)S(1)} %collective-permute-done.36.refs_14_), channel_id=1, source_target_pairs={{0,1},{1,0},{2,3},{3,2},{4,5},{5,4},{6,7},{7,6},{8,9},{9,8},{10,11... | collective-permute-start | bytes 786440 | tf_op jit(solution)/shard_map/ppermute | solution.py:54
  99.2 15.2 %collective-permute-start.27 = (bf16[1296,128]{1,0:T(8,128)(2,1)S(1)}, bf16[1296,128]{1,0:T(8,128)(2,1)S(1)}, u32[]{:S(2)}, u32[]{:S(2)}) collective-permute-start(bf16[1296,128]{1,0:T(8,128)(2,1)S(1)} %get-tuple-element.197.refs_4_), channel_id=1, source_target_pairs={{0,1},{1,0},{2,3},{3,2},{4,5},{5,4},{6,7},{7,6},{8,9},{9,8},{10,11... | collective-permute-start | bytes 995336 | tf_op jit(solution)/shard_map/ppermute | solution.py:54
  118.7 13.5 %collective-permute-start.40 = (bf16[3600,128]{1,0:T(8,128)(2,1)S(1)}, bf16[3600,128]{1,0:T(8,128)(2,1)S(1)}, u32[]{:S(2)}, u32[]{:S(2)}) collective-permute-start(bf16[3600,128]{1,0:T(8,128)(2,1)S(1)} %get-tuple-element.200), channel_id=1, source_target_pairs={{0,24},{1,97},{2,26},{3,99},{4,28},{5,101},{6,30},{7,103},{8,0},{9... | collective-permute-start | bytes 2764808 | tf_op jit(solution)/shard_map/ppermute | solution.py:33
  120.2 15.0 %collective-permute-start.41 = (bf16[3600,128]{1,0:T(8,128)(2,1)S(1)}, bf16[3600,128]{1,0:T(8,128)(2,1)S(1)}, u32[]{:S(2)}, u32[]{:S(2)}) collective-permute-start(bf16[3600,128]{1,0:T(8,128)(2,1)S(1)} %get-tuple-element.201), channel_id=1, source_target_pairs={{0,16},{1,65},{2,18},{3,67},{4,20},{5,69},{6,22},{7,71},{8,24},{9,... | collective-permute-start | bytes 2764808 | tf_op jit(solution)/shard_map/ppermute | solution.py:33
  120.8 24.3 %collective-permute-start.42 = (bf16[3600,128]{1,0:T(8,128)(2,1)S(1)}, bf16[3600,128]{1,0:T(8,128)(2,1)S(1)}, u32[]{:S(2)}, u32[]{:S(2)}) collective-permute-start(bf16[3600,128]{1,0:T(8,128)(2,1)S(1)} %get-tuple-element.202), channel_id=1, source_target_pairs={{0,8},{1,33},{2,10},{3,35},{4,12},{5,37},{6,14},{7,39},{8,16},{9,4... | collective-permute-start | bytes 2764808 | tf_op jit(solution)/shard_map/ppermute | solution.py:33
  149.0 16.7 %collective-permute-start.43 = (bf16[2320,128]{1,0:T(8,128)(2,1)}, bf16[2320,128]{1,0:T(8,128)(2,1)S(1)}, u32[]{:S(2)}, u32[]{:S(2)}) collective-permute-start(bf16[2320,128]{1,0:T(8,128)(2,1)} %get-tuple-element.208), channel_id=1, source_target_pairs={{0,96},{1,25},{2,98},{3,27},{4,100},{5,29},{6,102},{7,31},{8,104},... | collective-permute-start | bytes 1781768 | tf_op jit(solution)/shard_map/ppermute | solution.py:33
  151.5 14.2 %collective-permute-start.44 = (bf16[2320,128]{1,0:T(8,128)(2,1)}, bf16[2320,128]{1,0:T(8,128)(2,1)S(1)}, u32[]{:S(2)}, u32[]{:S(2)}) collective-permute-start(bf16[2320,128]{1,0:T(8,128)(2,1)} %get-tuple-element.209), channel_id=1, source_target_pairs={{0,64},{1,17},{2,66},{3,19},{4,68},{5,21},{6,70},{7,23},{8,72},{9,... | collective-permute-start | bytes 1781768 | tf_op jit(solution)/shard_map/ppermute | solution.py:33
  153.2 16.4 %collective-permute-start.45 = (bf16[2320,128]{1,0:T(8,128)(2,1)}, bf16[2320,128]{1,0:T(8,128)(2,1)S(1)}, u32[]{:S(2)}, u32[]{:S(2)}) collective-permute-start(bf16[2320,128]{1,0:T(8,128)(2,1)} %get-tuple-element.210), channel_id=1, source_target_pairs={{0,32},{1,9},{2,34},{3,11},{4,36},{5,13},{6,38},{7,15},{8,40},{9,1... | collective-permute-start | bytes 1781768 | tf_op jit(solution)/shard_map/ppermute | solution.py:33
  (25 other events, 232.3 us)

commit v10 on v9

--- a/solution.py
+++ b/solution.py
@@ -64,8 +64,8 @@
 
 
 def ring_swap(pieces, along):
-    across = along(pieces[2], ahead(2))
-    return [pieces[0], along(pieces[3], ahead(-1)), across, along(pieces[1], ahead(1))]
+    after, before = along(pieces[3], ahead(-1)), along(pieces[1], ahead(1))
+    return [pieces[0], after, along(pieces[2], ahead(2)), before]
 
 
 def total_of(pieces):
@@ -76,11 +76,19 @@
     return pl.ds(pl.multiple_of(place * T, T), T)
 
 
-def prepare_kernel(at_row, at_col, live_ref, rows_ref, cols_ref, meta, tables):
+def prepare_kernel(at_row, at_col, live_ref, rows_ref, cols_ref, meta, tables, slots_held, sems):
+    copies = [
+        pltpu.make_async_copy(ref, slots_held.at[k], sems.at[k])
+        for k, ref in enumerate((rows_ref, cols_ref))
+    ]
+    for copy in copies:
+        copy.start()
+    for copy in copies:
+        copy.wait()
     live = live_ref[0]
     x, z = at_row[0] >> 2, at_row[0] & 3
     y, core = at_col[0] >> 1, at_col[0] & 1
-    rows, cols = rows_ref[...], cols_ref[...]
+    rows, cols = slots_held[0], slots_held[1]
     slots = cols.shape[1]
 
     far_core = (rows >> 4) & 1
@@ -137,8 +145,9 @@
             jax.ShapeDtypeStruct((META, T), BF16),
             jax.ShapeDtypeStruct((8, slots), I32),
         ],
-        in_specs=[SMEM] * 3 + [VMEM] * 2,
+        in_specs=[SMEM] * 3 + [ANY] * 2,
         out_specs=[VMEM] * 2,
+        scratch_shapes=[pltpu.VMEM((2, 1, slots), I32), pltpu.SemaphoreType.DMA((2,))],
         compiler_params=room(4),
     )(at_row, at_col, live, rows.reshape(1, slots), cols.reshape(1, slots))
 
@@ -297,14 +306,8 @@
     )(*pieces, *metas)
 
 
-def combine_kernel(lists, counts, own_ref, sums, *refs):
-    part_refs, outs, summed, (own, parts, total, sems) = refs[:3], refs[3:7], refs[7], refs[8:]
-    copies = [pltpu.make_async_copy(own_ref, own, sems.at[3])]
-    for n, ref in enumerate(part_refs):
-        copies.append(pltpu.make_async_copy(ref, parts.at[n], sems.at[n]))
-    for copy in copies:
-        copy.start()
-    copies[0].wait()
+def combine_kernel(lists, counts, own, sums, *refs):
+    parts, outs, summed, total = refs[:3], refs[3:7], refs[7], refs[8]
 
     def widen(k, carry):
         for at in range(4):
@@ -312,12 +315,10 @@
         return carry
 
     lax.fori_loop(0, 16, widen, 0)
-    for copy in copies[1:]:
-        copy.wait()
     lines = sums.shape[0]
     for k in range(2):
         tail = pl.ds(CAP * T + k * lines, lines)
-        line = sums[:, k * T : (k + 1) * T] + total_of([parts[n, tail] for n in range(3)])
+        line = sums[:, k * T : (k + 1) * T] + total_of([part[tail] for part in parts])
         summed[:, k * T : (k + 1) * T] = line
         for ref in outs[1:]:
             ref[pl.ds(16 * T + k * lines, lines)] = line.astype(BF16)
@@ -326,7 +327,7 @@
         def add(k, carry, n=n):
             for at in range(4):
                 slot = k * 4 + at
-                total[lists[n * LANES + slot]] += parts[n, block(slot)].astype(F32)
+                total[lists[n * LANES + slot]] += parts[n][block(slot)].astype(F32)
             return carry
 
         lax.fori_loop(0, (counts[n] + 3) // 4, add, 0)
@@ -347,14 +348,9 @@
         out_shape=[jax.ShapeDtypeStruct((rows, T), F32)]
         + [jax.ShapeDtypeStruct((rows + 2 * sums.shape[0], T), BF16)] * 3
         + [jax.ShapeDtypeStruct(sums.shape, F32)],
-        in_specs=[SMEM] * 2 + [ANY, VMEM] + [ANY] * 3,
+        in_specs=[SMEM] * 2 + [VMEM] * 5,
         out_specs=[VMEM] * 5,
-        scratch_shapes=[
-            pltpu.VMEM(own.shape, BF16),
-            pltpu.VMEM((3,) + parts[0].shape, BF16),
-            pltpu.VMEM((65, T, T), F32),
-            pltpu.SemaphoreType.DMA((4,)),
-        ],
+        scratch_shapes=[pltpu.VMEM((65, T, T), F32)],
         compiler_params=room(16),
     )(lists, counts, own, sums, *parts)
 
@@ -426,7 +422,7 @@
 
 def dense(parts, grad, weight, offset, part, before):
     width, rows = weight.shape[1], grad.shape[0]
-    step = 512
+    step = 1024
     steps = rows // 2 // step
     shift = part * steps
     tail = 2 * (T + 8) if before else 0
@@ -449,7 +445,7 @@
         + ([ANY, whole(T + 8, width), ANY] if before else []),
         out_specs=[full, whole(rows // 2 + tail, T), whole(T + 8, width)],
         input_output_aliases={8: 0} if before else {},
-        compiler_params=room(14),
+        compiler_params=room(20),
     )(*parts, grad, weight, offset, *before)
 
 

time: 172 us -> 171 us (level)
  Pallas kernels: 23.1 us -> 20.6 us
  transfers between devices with their start and end apart: 40 -> 40, of which waited for: 21 -> 22; matrix products, arithmetic and copies ran while one was open for 1% -> 1% of each run, Pallas kernels for 3% -> 2%
where the time goes in v10:
time: 171 us
  waiting for transfers between devices  81.8 us (48%)
  starting transfers between devices  62.5 us (37%)
  Pallas kernels  20.6 us (12%)
  between operations  2.11 us (1%)
  local copies, waits for them, and re-layouts  1.84 us (1%)
    ppermute x18, waiting for transfers between devices, along_xz(): return lax.ppermute(value, ('row', 'col'), pairs)  59.1 us
    ppermute x18, starting transfers between devices, along_xz(): return lax.ppermute(value, ('row', 'col'), pairs)  28.8 us
    ppermute x12, starting transfers between devices, along_y(): return lax.ppermute(value, 'col', pairs)  24.7 us
    ppermute x12, waiting for transfers between devices, along_y(): return lax.ppermute(value, 'col', pairs)  18.1 us
    ppermute x10, starting transfers between devices, other_core(): return lax.ppermute(value, 'col', pairs)  9.04 us
    pallas_call x2, Pallas kernels, products(): pl.pallas_call(kernel, out_shape=[jax.ShapeDtypeStruct((n * T + e, T), BF...  8.89 us
    ppermute x10, waiting for transfers between devices, other_core(): return lax.ppermute(value, 'col', pairs)  4.63 us
    pallas_call x2, Pallas kernels, dense(): pl.pallas_call(functools.partial(dense_kernel, step=step), grid=(steps,),...  3.73 us
  transfers between devices with their start and end apart: 40, of which 22 were waited for; matrix products, arithmetic and copies ran while one was open for 1% of the time, Pallas kernels for 2%

profile of v10, /device:TPU:0, one launch (start us, length us, event | category | flops | bytes accessed | tf_op | source)
XLA Modules:
  0.0 170.6 jit_solution(12351318577388445817)
XLA Ops:
  2.3 2.7 %collective-permute-start.7 = (bf16[2048,128]{1,0:T(8,128)(2,1)}, bf16[2048,128]{1,0:T(8,128)(2,1)S(1)}, u32[]{:S(2)}, u32[]{:S(2)}) collective-permute-start(bf16[2048,128]{1,0:T(8,128)(2,1)} %refs_0_.3), channel_id=1, source_target_pairs={{0,64},{1,17},{2,66},{3,19},{4,68},{5,21},{6,70},{7,23},{8,72},{9,... | collective-permute-start | bytes 1572872 | tf_op jit(solution)/shard_map/ppermute | solution.py:33
  10.7 3.6 %collective-permute-start.10 = (bf16[16,128]{1,0:T(8,128)(2,1)S(1)}, bf16[16,128]{1,0:T(8,128)(2,1)S(1)}, u32[]{:S(2)}, u32[]{:S(2)}) collective-permute-start(bf16[16,128]{1,0:T(8,128)(2,1)S(1)} %get-tuple-element.181.refs_4_), channel_id=1, source_target_pairs={{0,16},{1,65},{2,18},{3,67},{4,20},{5,69},{6,22},{7,71},{8,24},{9,... | collective-permute-start | bytes 12296 | tf_op jit(solution)/shard_map/ppermute | solution.py:33
  20.7 3.8 %collective-permute-start.15 = (bf16[3328,128]{1,0:T(8,128)(2,1)S(1)}, bf16[3328,128]{1,0:T(8,128)(2,1)S(1)}, u32[]{:S(2)}, u32[]{:S(2)}) collective-permute-start(bf16[3328,128]{1,0:T(8,128)(2,1)S(1)} %get-tuple-element.184), channel_id=1, source_target_pairs={{0,24},{1,97},{2,26},{3,99},{4,28},{5,101},{6,30},{7,103},{8,0},{9... | collective-permute-start | bytes 2555912 | tf_op jit(solution)/shard_map/ppermute | solution.py:33
  29.8 6.5 %collective-permute-done.14 = f32[8,128]{1,0:T(8,128)S(1)} collective-permute-done((f32[8,128]{1,0:T(8,128)S(1)}, f32[8,128]{1,0:T(8,128)S(1)}, u32[]{:S(2)}, u32[]{:S(2)}) %collective-permute-start.14) | collective-permute-done | bytes 4128 | tf_op jit(solution)/shard_map/ppermute | solution.py:33
  36.4 3.7 %collective-permute-done.12 = f32[8,128]{1,0:T(8,128)S(1)} collective-permute-done((f32[8,128]{1,0:T(8,128)S(1)}, f32[8,128]{1,0:T(8,128)S(1)}, u32[]{:S(2)}, u32[]{:S(2)}) %collective-permute-start.12) | collective-permute-done | bytes 4128 | tf_op jit(solution)/shard_map/ppermute | solution.py:33
  41.3 2.6 %collective-permute-done.15.refs_4_ = bf16[3328,128]{1,0:T(8,128)(2,1)S(1)} collective-permute-done((bf16[3328,128]{1,0:T(8,128)(2,1)S(1)}, bf16[3328,128]{1,0:T(8,128)(2,1)S(1)}, u32[]{:S(2)}, u32[]{:S(2)}) %collective-permute-start.15) | collective-permute-done | bytes 852000 | tf_op jit(solution)/shard_map/ppermute | solution.py:33
  43.9 3.6 %collective-permute-done.17.refs_6_ = bf16[3328,128]{1,0:T(8,128)(2,1)S(1)} collective-permute-done((bf16[3328,128]{1,0:T(8,128)(2,1)S(1)}, bf16[3328,128]{1,0:T(8,128)(2,1)S(1)}, u32[]{:S(2)}, u32[]{:S(2)}) %collective-permute-start.17) | collective-permute-done | bytes 852000 | tf_op jit(solution)/shard_map/ppermute | solution.py:33
  47.5 5.0 %shard_map.113 = (bf16[4096,128]{1,0:T(8,128)(2,1)}, bf16[4096,128]{1,0:T(8,128)(2,1)}, bf16[4096,128]{1,0:T(8,128)(2,1)}, bf16[4096,128]{1,0:T(8,128)(2,1)}) custom-call(s32[1]{0:T(128)} %bitcast.10.live, s32[8,64]{1,0:T(8,128)S(1)} %get-tuple-element.183.tables, bf16[64,128,128]{2,1,0:T(8,128)(2,1)S(1)} %bitcast.16, bf16[2048,128]{1,0:T(8,128)(2,1)} %refs_0_.3, ...), custom_call_target="tpu_custom_call" | custom-call | tf_op jit(solution)/shard_map/pallas_call | solution.py:233
  57.0 2.5 %collective-permute-start.25 = (bf16[1024,128]{1,0:T(8,128)(2,1)S(1)}, bf16[1024,128]{1,0:T(8,128)(2,1)S(1)}, u32[]{:S(2)}, u32[]{:S(2)}) collective-permute-start(bf16[1024,128]{1,0:T(8,128)(2,1)S(1)} %get-tuple-element.220), channel_id=1, source_target_pairs={{0,2},{1,7},{2,4},{3,1},{4,6},{5,3},{6,0},{7,5},{8,10},{9,15},{10,... | collective-permute-start | bytes 786440 | tf_op jit(solution)/shard_map/ppermute | solution.py:49
  59.5 2.7 %collective-permute-start.24 = (bf16[1024,128]{1,0:T(8,128)(2,1)S(1)}, bf16[1024,128]{1,0:T(8,128)(2,1)S(1)}, u32[]{:S(2)}, u32[]{:S(2)}) collective-permute-start(bf16[1024,128]{1,0:T(8,128)(2,1)S(1)} %get-tuple-element.221), channel_id=1, source_target_pairs={{0,4},{1,5},{2,6},{3,7},{4,0},{5,1},{6,2},{7,3},{8,12},{9,13},{10,... | collective-permute-start | bytes 786440 | tf_op jit(solution)/shard_map/ppermute | solution.py:49
  65.9 3.1 %collective-permute-start.19 = (bf16[1024,128]{1,0:T(8,128)(2,1)S(1)}, bf16[1024,128]{1,0:T(8,128)(2,1)S(1)}, u32[]{:S(2)}, u32[]{:S(2)}) collective-permute-start(bf16[1024,128]{1,0:T(8,128)(2,1)S(1)} %get-tuple-element.225), channel_id=1, source_target_pairs={{0,6},{1,3},{2,0},{3,5},{4,2},{5,7},{6,4},{7,1},{8,14},{9,11},{10,... | collective-permute-start | bytes 786440 | tf_op jit(solution)/shard_map/ppermute | solution.py:49
  69.0 5.1 %collective-permute-done.24.refs_3_ = bf16[1024,128]{1,0:T(8,128)(2,1)S(1)} collective-permute-done((bf16[1024,128]{1,0:T(8,128)(2,1)S(1)}, bf16[1024,128]{1,0:T(8,128)(2,1)S(1)}, u32[]{:S(2)}, u32[]{:S(2)}) %collective-permute-start.24) | collective-permute-done | bytes 262176 | tf_op jit(solution)/shard_map/ppermute | solution.py:49
  78.5 7.8 %collective-permute-start.36 = (bf16[1024,128]{1,0:T(8,128)(2,1)S(1)}, bf16[1024,128]{1,0:T(8,128)(2,1)S(1)}, u32[]{:S(2)}, u32[]{:S(2)}) collective-permute-start(bf16[1024,128]{1,0:T(8,128)(2,1)S(1)} %get-tuple-element.193.refs_12_), channel_id=1, source_target_pairs={{0,4},{1,5},{2,6},{3,7},{4,0},{5,1},{6,2},{7,3},{8,12},{9,13},{10,... | collective-permute-start | bytes 786440 | tf_op jit(solution)/shard_map/ppermute | solution.py:49
  92.9 4.8 %collective-permute-done.36.refs_14_ = bf16[1024,128]{1,0:T(8,128)(2,1)S(1)} collective-permute-done((bf16[1024,128]{1,0:T(8,128)(2,1)S(1)}, bf16[1024,128]{1,0:T(8,128)(2,1)S(1)}, u32[]{:S(2)}, u32[]{:S(2)}) %collective-permute-start.36) | collective-permute-done | bytes 262176 | tf_op jit(solution)/shard_map/ppermute | solution.py:49
  99.4 3.7 %collective-permute-done.32.refs_7_ = bf16[1296,128]{1,0:T(8,128)(2,1)S(1)} collective-permute-done((bf16[1296,128]{1,0:T(8,128)(2,1)S(1)}, bf16[1296,128]{1,0:T(8,128)(2,1)S(1)}, u32[]{:S(2)}, u32[]{:S(2)}) %collective-permute-start.32) | collective-permute-done | bytes 331808 | tf_op jit(solution)/shard_map/ppermute | solution.py:49
  103.1 7.1 %collective-permute-start.33 = (bf16[1296,128]{1,0:T(8,128)(2,1)S(1)}, bf16[1296,128]{1,0:T(8,128)(2,1)S(1)}, u32[]{:S(2)}, u32[]{:S(2)}) collective-permute-start(bf16[1296,128]{1,0:T(8,128)(2,1)S(1)} %collective-permute-done.32.refs_7_), channel_id=1, source_target_pairs={{0,1},{1,0},{2,3},{3,2},{4,5},{5,4},{6,7},{7,6},{8,9},{9,8},{10,11... | collective-permute-start | bytes 995336 | tf_op jit(solution)/shard_map/ppermute | solution.py:54
  114.5 3.9 %shard_map.116 = (bf16[8192,128]{1,0:T(8,128)(2,1)S(1)}, bf16[3600,128]{1,0:T(8,128)(2,1)S(1)}, bf16[3600,128]{1,0:T(8,128)(2,1)S(1)}, bf16[3600,128]{1,0:T(8,128)(2,1)S(1)}, f32[136,256]{1,0:T(8,128)S(1)}) custom-call(s32[1]{0:T(128)} %bitcast.11.live, s32[8,64]{1,0:T(8,128)S(1)} %get-tuple-element.183.tables, bf16[64,128,128]{2,1,0:T(8,128)(2,1)S(1)} %bitcast.18, ...), custom_call_target="tpu_custom_call" | custom-call | tf_op jit(solution)/shard_map/pallas_call | solution.py:233
  120.7 11.2 %collective-permute-done.40.refs_0_ = bf16[3600,128]{1,0:T(8,128)(2,1)S(1)} collective-permute-done((bf16[3600,128]{1,0:T(8,128)(2,1)S(1)}, bf16[3600,128]{1,0:T(8,128)(2,1)S(1)}, u32[]{:S(2)}, u32[]{:S(2)}) %collective-permute-start.40) | collective-permute-done | bytes 921632 | tf_op jit(solution)/shard_map/ppermute | solution.py:33
  131.9 2.9 %collective-permute-done.41.refs_1_ = bf16[3600,128]{1,0:T(8,128)(2,1)S(1)} collective-permute-done((bf16[3600,128]{1,0:T(8,128)(2,1)S(1)}, bf16[3600,128]{1,0:T(8,128)(2,1)S(1)}, u32[]{:S(2)}, u32[]{:S(2)}) %collective-permute-start.41) | collective-permute-done | bytes 921632 | tf_op jit(solution)/shard_map/ppermute | solution.py:33
  134.8 9.8 %collective-permute-done.42.refs_2_ = bf16[3600,128]{1,0:T(8,128)(2,1)S(1)} collective-permute-done((bf16[3600,128]{1,0:T(8,128)(2,1)S(1)}, bf16[3600,128]{1,0:T(8,128)(2,1)S(1)}, u32[]{:S(2)}, u32[]{:S(2)}) %collective-permute-start.42) | collective-permute-done | bytes 921632 | tf_op jit(solution)/shard_map/ppermute | solution.py:33
  144.6 3.0 %shard_map.117 = (f32[2048,128]{1,0:T(8,128)}, bf16[2320,128]{1,0:T(8,128)(2,1)}, bf16[2320,128]{1,0:T(8,128)(2,1)}, bf16[2320,128]{1,0:T(8,128)(2,1)}, f32[136,256]{1,0:T(8,128)S(1)}) custom-call(s32[96]{0:T(128)S(1)} %get-tuple-element.195.lists, s32[3]{0:T(128)S(1)} %get-tuple-element.196.counts, bf16[8192,128]{1,0:T(8,128)(2,1)S(1)} %get-tuple-element.198.own, ...), custom_call_target="tpu_custom_call" | custom-call | tf_op jit(solution)/shard_map/pallas_call | solution.py:346
  147.6 2.5 %collective-permute-start.43 = (bf16[2320,128]{1,0:T(8,128)(2,1)}, bf16[2320,128]{1,0:T(8,128)(2,1)S(1)}, u32[]{:S(2)}, u32[]{:S(2)}) collective-permute-start(bf16[2320,128]{1,0:T(8,128)(2,1)} %get-tuple-element.208), channel_id=1, source_target_pairs={{0,96},{1,25},{2,98},{3,27},{4,100},{5,29},{6,102},{7,31},{8,104},... | collective-permute-start | bytes 1781768 | tf_op jit(solution)/shard_map/ppermute | solution.py:33
  151.8 12.5 %collective-permute-done.43.refs_1_ = bf16[2320,128]{1,0:T(8,128)(2,1)S(1)} collective-permute-done((bf16[2320,128]{1,0:T(8,128)(2,1)}, bf16[2320,128]{1,0:T(8,128)(2,1)S(1)}, u32[]{:S(2)}, u32[]{:S(2)}) %collective-permute-start.43) | collective-permute-done | bytes 593952 | tf_op jit(solution)/shard_map/ppermute | solution.py:33
  164.3 3.8 %collective-permute-done.45.refs_3_ = bf16[2320,128]{1,0:T(8,128)(2,1)S(1)} collective-permute-done((bf16[2320,128]{1,0:T(8,128)(2,1)}, bf16[2320,128]{1,0:T(8,128)(2,1)S(1)}, u32[]{:S(2)}, u32[]{:S(2)}) %collective-permute-start.45) | collective-permute-done | bytes 593952 | tf_op jit(solution)/shard_map/ppermute | solution.py:33
  (88 shorter events, 50.6 us)
Async XLA Ops:
  0.6 17.8 %collective-permute-start.8 = (bf16[2048,128]{1,0:T(8,128)(2,1)}, bf16[2048,128]{1,0:T(8,128)(2,1)S(1)}, u32[]{:S(2)}, u32[]{:S(2)}) collective-permute-start(bf16[2048,128]{1,0:T(8,128)(2,1)} %refs_0_.3), channel_id=1, source_target_pairs={{0,32},{1,9},{2,34},{3,11},{4,36},{5,13},{6,38},{7,15},{8,40},{9,1... | collective-permute-start | bytes 1572872 | tf_op jit(solution)/shard_map/ppermute | solution.py:33
  2.3 16.2 %collective-permute-start.7 = (bf16[2048,128]{1,0:T(8,128)(2,1)}, bf16[2048,128]{1,0:T(8,128)(2,1)S(1)}, u32[]{:S(2)}, u32[]{:S(2)}) collective-permute-start(bf16[2048,128]{1,0:T(8,128)(2,1)} %refs_0_.3), channel_id=1, source_target_pairs={{0,64},{1,17},{2,66},{3,19},{4,68},{5,21},{6,70},{7,23},{8,72},{9,... | collective-permute-start | bytes 1572872 | tf_op jit(solution)/shard_map/ppermute | solution.py:33
  5.0 13.5 %collective-permute-start.6 = (bf16[2048,128]{1,0:T(8,128)(2,1)}, bf16[2048,128]{1,0:T(8,128)(2,1)}, u32[]{:S(2)}, u32[]{:S(2)}) collective-permute-start(bf16[2048,128]{1,0:T(8,128)(2,1)} %refs_0_.3), channel_id=1, source_target_pairs={{0,96},{1,25},{2,98},{3,27},{4,100},{5,29},{6,102},{7,31},{8,104},... | collective-permute-start | bytes 1572872 | tf_op jit(solution)/shard_map/ppermute | solution.py:33
  20.7 23.2 %collective-permute-start.15 = (bf16[3328,128]{1,0:T(8,128)(2,1)S(1)}, bf16[3328,128]{1,0:T(8,128)(2,1)S(1)}, u32[]{:S(2)}, u32[]{:S(2)}) collective-permute-start(bf16[3328,128]{1,0:T(8,128)(2,1)S(1)} %get-tuple-element.184), channel_id=1, source_target_pairs={{0,24},{1,97},{2,26},{3,99},{4,28},{5,101},{6,30},{7,103},{8,0},{9... | collective-permute-start | bytes 2555912 | tf_op jit(solution)/shard_map/ppermute | solution.py:33
  24.5 19.4 %collective-permute-start.16 = (bf16[3328,128]{1,0:T(8,128)(2,1)S(1)}, bf16[3328,128]{1,0:T(8,128)(2,1)S(1)}, u32[]{:S(2)}, u32[]{:S(2)}) collective-permute-start(bf16[3328,128]{1,0:T(8,128)(2,1)S(1)} %get-tuple-element.185), channel_id=1, source_target_pairs={{0,16},{1,65},{2,18},{3,67},{4,20},{5,69},{6,22},{7,71},{8,24},{9,... | collective-permute-start | bytes 2555912 | tf_op jit(solution)/shard_map/ppermute | solution.py:33
  24.5 23.1 %collective-permute-start.17 = (bf16[3328,128]{1,0:T(8,128)(2,1)S(1)}, bf16[3328,128]{1,0:T(8,128)(2,1)S(1)}, u32[]{:S(2)}, u32[]{:S(2)}) collective-permute-start(bf16[3328,128]{1,0:T(8,128)(2,1)S(1)} %get-tuple-element.186), channel_id=1, source_target_pairs={{0,8},{1,33},{2,10},{3,35},{4,12},{5,37},{6,14},{7,39},{8,16},{9,4... | collective-permute-start | bytes 2555912 | tf_op jit(solution)/shard_map/ppermute | solution.py:33
  59.5 14.5 %collective-permute-start.24 = (bf16[1024,128]{1,0:T(8,128)(2,1)S(1)}, bf16[1024,128]{1,0:T(8,128)(2,1)S(1)}, u32[]{:S(2)}, u32[]{:S(2)}) collective-permute-start(bf16[1024,128]{1,0:T(8,128)(2,1)S(1)} %get-tuple-element.221), channel_id=1, source_target_pairs={{0,4},{1,5},{2,6},{3,7},{4,0},{5,1},{6,2},{7,3},{8,12},{9,13},{10,... | collective-permute-start | bytes 786440 | tf_op jit(solution)/shard_map/ppermute | solution.py:49
  62.2 12.4 %collective-permute-start.23 = (bf16[1024,128]{1,0:T(8,128)(2,1)S(1)}, bf16[1024,128]{1,0:T(8,128)(2,1)S(1)}, u32[]{:S(2)}, u32[]{:S(2)}) collective-permute-start(bf16[1024,128]{1,0:T(8,128)(2,1)S(1)} %get-tuple-element.222), channel_id=1, source_target_pairs={{0,6},{1,3},{2,0},{3,5},{4,2},{5,7},{6,4},{7,1},{8,14},{9,11},{10,... | collective-permute-start | bytes 786440 | tf_op jit(solution)/shard_map/ppermute | solution.py:49
  63.7 14.8 %collective-permute-start.21 = (bf16[1024,128]{1,0:T(8,128)(2,1)S(1)}, bf16[1024,128]{1,0:T(8,128)(2,1)S(1)}, u32[]{:S(2)}, u32[]{:S(2)}) collective-permute-start(bf16[1024,128]{1,0:T(8,128)(2,1)S(1)} %get-tuple-element.223), channel_id=1, source_target_pairs={{0,2},{1,7},{2,4},{3,1},{4,6},{5,3},{6,0},{7,5},{8,10},{9,15},{10,... | collective-permute-start | bytes 786440 | tf_op jit(solution)/shard_map/ppermute | solution.py:49
  64.5 21.8 %collective-permute-start.20 = (bf16[1024,128]{1,0:T(8,128)(2,1)S(1)}, bf16[1024,128]{1,0:T(8,128)(2,1)S(1)}, u32[]{:S(2)}, u32[]{:S(2)}) collective-permute-start(bf16[1024,128]{1,0:T(8,128)(2,1)S(1)} %get-tuple-element.224), channel_id=1, source_target_pairs={{0,4},{1,5},{2,6},{3,7},{4,0},{5,1},{6,2},{7,3},{8,12},{9,13},{10,... | collective-permute-start | bytes 786440 | tf_op jit(solution)/shard_map/ppermute | solution.py:49
  65.9 20.4 %collective-permute-start.19 = (bf16[1024,128]{1,0:T(8,128)(2,1)S(1)}, bf16[1024,128]{1,0:T(8,128)(2,1)S(1)}, u32[]{:S(2)}, u32[]{:S(2)}) collective-permute-start(bf16[1024,128]{1,0:T(8,128)(2,1)S(1)} %get-tuple-element.225), channel_id=1, source_target_pairs={{0,6},{1,3},{2,0},{3,5},{4,2},{5,7},{6,4},{7,1},{8,14},{9,11},{10,... | collective-permute-start | bytes 786440 | tf_op jit(solution)/shard_map/ppermute | solution.py:49
  76.7 13.8 %collective-permute-start.38 = (bf16[1024,128]{1,0:T(8,128)(2,1)S(1)}, bf16[1024,128]{1,0:T(8,128)(2,1)S(1)}, u32[]{:S(2)}, u32[]{:S(2)}) collective-permute-start(bf16[1024,128]{1,0:T(8,128)(2,1)S(1)} %get-tuple-element.193.refs_12_), channel_id=1, source_target_pairs={{0,2},{1,7},{2,4},{3,1},{4,6},{5,3},{6,0},{7,5},{8,10},{9,15},{10,... | collective-permute-start | bytes 786440 | tf_op jit(solution)/shard_map/ppermute | solution.py:49
  78.5 19.2 %collective-permute-start.36 = (bf16[1024,128]{1,0:T(8,128)(2,1)S(1)}, bf16[1024,128]{1,0:T(8,128)(2,1)S(1)}, u32[]{:S(2)}, u32[]{:S(2)}) collective-permute-start(bf16[1024,128]{1,0:T(8,128)(2,1)S(1)} %get-tuple-element.193.refs_12_), channel_id=1, source_target_pairs={{0,4},{1,5},{2,6},{3,7},{4,0},{5,1},{6,2},{7,3},{8,12},{9,13},{10,... | collective-permute-start | bytes 786440 | tf_op jit(solution)/shard_map/ppermute | solution.py:49
  88.2 14.8 %collective-permute-start.32 = (bf16[1296,128]{1,0:T(8,128)(2,1)S(1)}, bf16[1296,128]{1,0:T(8,128)(2,1)S(1)}, u32[]{:S(2)}, u32[]{:S(2)}) collective-permute-start(bf16[1296,128]{1,0:T(8,128)(2,1)S(1)} %get-tuple-element.197.refs_4_), channel_id=1, source_target_pairs={{0,2},{1,7},{2,4},{3,1},{4,6},{5,3},{6,0},{7,5},{8,10},{9,15},{10,... | collective-permute-start | bytes 995336 | tf_op jit(solution)/shard_map/ppermute | solution.py:49
  90.3 21.7 %collective-permute-start.30 = (bf16[1296,128]{1,0:T(8,128)(2,1)S(1)}, bf16[1296,128]{1,0:T(8,128)(2,1)S(1)}, u32[]{:S(2)}, u32[]{:S(2)}) collective-permute-start(bf16[1296,128]{1,0:T(8,128)(2,1)S(1)} %get-tuple-element.197.refs_4_), channel_id=1, source_target_pairs={{0,4},{1,5},{2,6},{3,7},{4,0},{5,1},{6,2},{7,3},{8,12},{9,13},{10,... | collective-permute-start | bytes 995336 | tf_op jit(solution)/shard_map/ppermute | solution.py:49
  90.5 21.5 %collective-permute-start.28 = (bf16[1296,128]{1,0:T(8,128)(2,1)S(1)}, bf16[1296,128]{1,0:T(8,128)(2,1)S(1)}, u32[]{:S(2)}, u32[]{:S(2)}) collective-permute-start(bf16[1296,128]{1,0:T(8,128)(2,1)S(1)} %get-tuple-element.197.refs_4_), channel_id=1, source_target_pairs={{0,6},{1,3},{2,0},{3,5},{4,2},{5,7},{6,4},{7,1},{8,14},{9,11},{10,... | collective-permute-start | bytes 995336 | tf_op jit(solution)/shard_map/ppermute | solution.py:49
  98.6 13.9 %collective-permute-start.37 = (bf16[1024,128]{1,0:T(8,128)(2,1)S(1)}, bf16[1024,128]{1,0:T(8,128)(2,1)S(1)}, u32[]{:S(2)}, u32[]{:S(2)}) collective-permute-start(bf16[1024,128]{1,0:T(8,128)(2,1)S(1)} %collective-permute-done.36.refs_14_), channel_id=1, source_target_pairs={{0,1},{1,0},{2,3},{3,2},{4,5},{5,4},{6,7},{7,6},{8,9},{9,8},{10,11... | collective-permute-start | bytes 786440 | tf_op jit(solution)/shard_map/ppermute | solution.py:54
  99.3 15.2 %collective-permute-start.27 = (bf16[1296,128]{1,0:T(8,128)(2,1)S(1)}, bf16[1296,128]{1,0:T(8,128)(2,1)S(1)}, u32[]{:S(2)}, u32[]{:S(2)}) collective-permute-start(bf16[1296,128]{1,0:T(8,128)(2,1)S(1)} %get-tuple-element.197.refs_4_), channel_id=1, source_target_pairs={{0,1},{1,0},{2,3},{3,2},{4,5},{5,4},{6,7},{7,6},{8,9},{9,8},{10,11... | collective-permute-start | bytes 995336 | tf_op jit(solution)/shard_map/ppermute | solution.py:54
  118.4 13.5 %collective-permute-start.40 = (bf16[3600,128]{1,0:T(8,128)(2,1)S(1)}, bf16[3600,128]{1,0:T(8,128)(2,1)S(1)}, u32[]{:S(2)}, u32[]{:S(2)}) collective-permute-start(bf16[3600,128]{1,0:T(8,128)(2,1)S(1)} %get-tuple-element.200), channel_id=1, source_target_pairs={{0,24},{1,97},{2,26},{3,99},{4,28},{5,101},{6,30},{7,103},{8,0},{9... | collective-permute-start | bytes 2764808 | tf_op jit(solution)/shard_map/ppermute | solution.py:33
  119.8 15.0 %collective-permute-start.41 = (bf16[3600,128]{1,0:T(8,128)(2,1)S(1)}, bf16[3600,128]{1,0:T(8,128)(2,1)S(1)}, u32[]{:S(2)}, u32[]{:S(2)}) collective-permute-start(bf16[3600,128]{1,0:T(8,128)(2,1)S(1)} %get-tuple-element.201), channel_id=1, source_target_pairs={{0,16},{1,65},{2,18},{3,67},{4,20},{5,69},{6,22},{7,71},{8,24},{9,... | collective-permute-start | bytes 2764808 | tf_op jit(solution)/shard_map/ppermute | solution.py:33
  120.7 23.9 %collective-permute-start.42 = (bf16[3600,128]{1,0:T(8,128)(2,1)S(1)}, bf16[3600,128]{1,0:T(8,128)(2,1)S(1)}, u32[]{:S(2)}, u32[]{:S(2)}) collective-permute-start(bf16[3600,128]{1,0:T(8,128)(2,1)S(1)} %get-tuple-element.202), channel_id=1, source_target_pairs={{0,8},{1,33},{2,10},{3,35},{4,12},{5,37},{6,14},{7,39},{8,16},{9,4... | collective-permute-start | bytes 2764808 | tf_op jit(solution)/shard_map/ppermute | solution.py:33
  147.6 16.7 %collective-permute-start.43 = (bf16[2320,128]{1,0:T(8,128)(2,1)}, bf16[2320,128]{1,0:T(8,128)(2,1)S(1)}, u32[]{:S(2)}, u32[]{:S(2)}) collective-permute-start(bf16[2320,128]{1,0:T(8,128)(2,1)} %get-tuple-element.208), channel_id=1, source_target_pairs={{0,96},{1,25},{2,98},{3,27},{4,100},{5,29},{6,102},{7,31},{8,104},... | collective-permute-start | bytes 1781768 | tf_op jit(solution)/shard_map/ppermute | solution.py:33
  150.1 14.2 %collective-permute-start.44 = (bf16[2320,128]{1,0:T(8,128)(2,1)}, bf16[2320,128]{1,0:T(8,128)(2,1)S(1)}, u32[]{:S(2)}, u32[]{:S(2)}) collective-permute-start(bf16[2320,128]{1,0:T(8,128)(2,1)} %get-tuple-element.209), channel_id=1, source_target_pairs={{0,64},{1,17},{2,66},{3,19},{4,68},{5,21},{6,70},{7,23},{8,72},{9,... | collective-permute-start | bytes 1781768 | tf_op jit(solution)/shard_map/ppermute | solution.py:33
  151.2 16.9 %collective-permute-start.45 = (bf16[2320,128]{1,0:T(8,128)(2,1)}, bf16[2320,128]{1,0:T(8,128)(2,1)S(1)}, u32[]{:S(2)}, u32[]{:S(2)}) collective-permute-start(bf16[2320,128]{1,0:T(8,128)(2,1)} %get-tuple-element.210), channel_id=1, source_target_pairs={{0,32},{1,9},{2,34},{3,11},{4,36},{5,13},{6,38},{7,15},{8,40},{9,1... | collective-permute-start | bytes 1781768 | tf_op jit(solution)/shard_map/ppermute | solution.py:33
  (25 other events, 236.2 us)

commit v11 on v10

--- a/solution.py
+++ b/solution.py
@@ -14,7 +14,7 @@
 MIB = 1024 * 1024
 GROUP = 16
 META = 16
-CAP = 26
+CAP = 24
 LANES = 32
 SMEM = pl.BlockSpec(memory_space=pltpu.SMEM)
 VMEM = pl.BlockSpec(memory_space=pltpu.VMEM)

time: 171 us -> 168 us (0.982)
  starting transfers between devices: 62.5 us -> 58.3 us
    ppermute x12, starting transfers between devices: 24.7 us -> 18.3 us  [along_y(): return lax.ppermute(value, 'col', pairs)]
    ppermute x18, waiting for transfers between devices: 59.1 us -> 55.1 us  [along_xz(): return lax.ppermute(value, ('row', 'col'), pairs)]
    ppermute x12, waiting for transfers between devices: 18.1 us -> 22.1 us  [along_y(): return lax.ppermute(value, 'col', pairs)]
    pallas_call x2, Pallas kernels: 8.89 us -> 10.8 us  [products(): pl.pallas_call(kernel, out_shape=[jax.ShapeDtypeStruct((n * T + e, T), BF...]
where the time goes in v11:
time: 168 us
  waiting for transfers between devices  81.8 us (49%)
  starting transfers between devices  58.3 us (35%)
  Pallas kernels  22.2 us (13%)
  between operations  2.12 us (1%)
  local copies, waits for them, and re-layouts  1.84 us (1%)
  other arithmetic  1.68 us (1%)
    ppermute x18, waiting for transfers between devices, along_xz(): return lax.ppermute(value, ('row', 'col'), pairs)  55.1 us
    ppermute x18, starting transfers between devices, along_xz(): return lax.ppermute(value, ('row', 'col'), pairs)  29.3 us
    ppermute x12, waiting for transfers between devices, along_y(): return lax.ppermute(value, 'col', pairs)  22.1 us
    ppermute x12, starting transfers between devices, along_y(): return lax.ppermute(value, 'col', pairs)  18.3 us
    pallas_call x2, Pallas kernels, products(): pl.pallas_call(kernel, out_shape=[jax.ShapeDtypeStruct((n * T + e, T), BF...  10.8 us
    ppermute x10, starting transfers between devices, other_core(): return lax.ppermute(value, 'col', pairs)  10.7 us
    ppermute x10, waiting for transfers between devices, other_core(): return lax.ppermute(value, 'col', pairs)  4.63 us
    pallas_call x2, Pallas kernels, dense(): pl.pallas_call(functools.partial(dense_kernel, step=step), grid=(steps,),...  3.73 us
  transfers between devices with their start and end apart: 40, of which 22 were waited for; matrix products, arithmetic and copies ran while one was open for 1% of the time, Pallas kernels for 2%

profile of v11, /device:TPU:0, one launch (start us, length us, event | category | flops | bytes accessed | tf_op | source)
XLA Modules:
  0.0 167.9 jit_solution(5514979966977941040)
XLA Ops:
  2.3 2.7 %collective-permute-start.7 = (bf16[2048,128]{1,0:T(8,128)(2,1)}, bf16[2048,128]{1,0:T(8,128)(2,1)S(1)}, u32[]{:S(2)}, u32[]{:S(2)}) collective-permute-start(bf16[2048,128]{1,0:T(8,128)(2,1)} %refs_0_.3), channel_id=1, source_target_pairs={{0,64},{1,17},{2,66},{3,19},{4,68},{5,21},{6,70},{7,23},{8,72},{9,... | collective-permute-start | bytes 1572872 | tf_op jit(solution)/shard_map/ppermute | solution.py:33
  10.7 3.6 %collective-permute-start.10 = (bf16[16,128]{1,0:T(8,128)(2,1)S(1)}, bf16[16,128]{1,0:T(8,128)(2,1)S(1)}, u32[]{:S(2)}, u32[]{:S(2)}) collective-permute-start(bf16[16,128]{1,0:T(8,128)(2,1)S(1)} %get-tuple-element.181.refs_4_), channel_id=1, source_target_pairs={{0,16},{1,65},{2,18},{3,67},{4,20},{5,69},{6,22},{7,71},{8,24},{9,... | collective-permute-start | bytes 12296 | tf_op jit(solution)/shard_map/ppermute | solution.py:33
  20.5 3.9 %collective-permute-start.15 = (bf16[3072,128]{1,0:T(8,128)(2,1)S(1)}, bf16[3072,128]{1,0:T(8,128)(2,1)S(1)}, u32[]{:S(2)}, u32[]{:S(2)}) collective-permute-start(bf16[3072,128]{1,0:T(8,128)(2,1)S(1)} %get-tuple-element.184), channel_id=1, source_target_pairs={{0,24},{1,97},{2,26},{3,99},{4,28},{5,101},{6,30},{7,103},{8,0},{9... | collective-permute-start | bytes 2359304 | tf_op jit(solution)/shard_map/ppermute | solution.py:33
  27.6 2.4 %collective-permute-start.13 = (f32[8,128]{1,0:T(8,128)S(1)}, f32[8,128]{1,0:T(8,128)S(1)}, u32[]{:S(2)}, u32[]{:S(2)}) collective-permute-start(f32[8,128]{1,0:T(8,128)S(1)} %get-tuple-element.182), channel_id=1, source_target_pairs={{0,64},{1,17},{2,66},{3,19},{4,68},{5,21},{6,70},{7,23},{8,72},{9,... | collective-permute-start | bytes 12296 | tf_op jit(solution)/shard_map/ppermute | solution.py:33
  30.0 5.6 %collective-permute-done.14 = f32[8,128]{1,0:T(8,128)S(1)} collective-permute-done((f32[8,128]{1,0:T(8,128)S(1)}, f32[8,128]{1,0:T(8,128)S(1)}, u32[]{:S(2)}, u32[]{:S(2)}) %collective-permute-start.14) | collective-permute-done | bytes 4128 | tf_op jit(solution)/shard_map/ppermute | solution.py:33
  35.6 3.7 %collective-permute-done.12 = f32[8,128]{1,0:T(8,128)S(1)} collective-permute-done((f32[8,128]{1,0:T(8,128)S(1)}, f32[8,128]{1,0:T(8,128)S(1)}, u32[]{:S(2)}, u32[]{:S(2)}) %collective-permute-start.12) | collective-permute-done | bytes 4128 | tf_op jit(solution)/shard_map/ppermute | solution.py:33
  42.4 3.6 %collective-permute-done.17.refs_6_ = bf16[3072,128]{1,0:T(8,128)(2,1)S(1)} collective-permute-done((bf16[3072,128]{1,0:T(8,128)(2,1)S(1)}, bf16[3072,128]{1,0:T(8,128)(2,1)S(1)}, u32[]{:S(2)}, u32[]{:S(2)}) %collective-permute-start.17) | collective-permute-done | bytes 786464 | tf_op jit(solution)/shard_map/ppermute | solution.py:33
  46.1 5.9 %shard_map.113 = (bf16[4096,128]{1,0:T(8,128)(2,1)}, bf16[4096,128]{1,0:T(8,128)(2,1)}, bf16[4096,128]{1,0:T(8,128)(2,1)}, bf16[4096,128]{1,0:T(8,128)(2,1)}) custom-call(s32[1]{0:T(128)} %bitcast.10.live, s32[8,64]{1,0:T(8,128)S(1)} %get-tuple-element.183.tables, bf16[64,128,128]{2,1,0:T(8,128)(2,1)S(1)} %bitcast.16, bf16[2048,128]{1,0:T(8,128)(2,1)} %refs_0_.3, ...), custom_call_target="tpu_custom_call" | custom-call | tf_op jit(solution)/shard_map/pallas_call | solution.py:233
  58.2 2.4 %collective-permute-start.24 = (bf16[1024,128]{1,0:T(8,128)(2,1)S(1)}, bf16[1024,128]{1,0:T(8,128)(2,1)S(1)}, u32[]{:S(2)}, u32[]{:S(2)}) collective-permute-start(bf16[1024,128]{1,0:T(8,128)(2,1)S(1)} %get-tuple-element.221), channel_id=1, source_target_pairs={{0,4},{1,5},{2,6},{3,7},{4,0},{5,1},{6,2},{7,3},{8,12},{9,13},{10,... | collective-permute-start | bytes 786440 | tf_op jit(solution)/shard_map/ppermute | solution.py:49
  67.3 5.1 %collective-permute-done.24.refs_3_ = bf16[1024,128]{1,0:T(8,128)(2,1)S(1)} collective-permute-done((bf16[1024,128]{1,0:T(8,128)(2,1)S(1)}, bf16[1024,128]{1,0:T(8,128)(2,1)S(1)}, u32[]{:S(2)}, u32[]{:S(2)}) %collective-permute-start.24) | collective-permute-done | bytes 262176 | tf_op jit(solution)/shard_map/ppermute | solution.py:49
  76.7 3.4 %collective-permute-done.21.refs_4_ = bf16[1024,128]{1,0:T(8,128)(2,1)S(1)} collective-permute-done((bf16[1024,128]{1,0:T(8,128)(2,1)S(1)}, bf16[1024,128]{1,0:T(8,128)(2,1)S(1)}, u32[]{:S(2)}, u32[]{:S(2)}) %collective-permute-start.21) | collective-permute-done | bytes 262176 | tf_op jit(solution)/shard_map/ppermute | solution.py:49
  80.1 4.9 %collective-permute-start.36 = (bf16[1024,128]{1,0:T(8,128)(2,1)S(1)}, bf16[1024,128]{1,0:T(8,128)(2,1)S(1)}, u32[]{:S(2)}, u32[]{:S(2)}) collective-permute-start(bf16[1024,128]{1,0:T(8,128)(2,1)S(1)} %get-tuple-element.193.refs_12_), channel_id=1, source_target_pairs={{0,4},{1,5},{2,6},{3,7},{4,0},{5,1},{6,2},{7,3},{8,12},{9,13},{10,... | collective-permute-start | bytes 786440 | tf_op jit(solution)/shard_map/ppermute | solution.py:49
  89.2 2.4 %collective-permute-start.28 = (bf16[1296,128]{1,0:T(8,128)(2,1)S(1)}, bf16[1296,128]{1,0:T(8,128)(2,1)S(1)}, u32[]{:S(2)}, u32[]{:S(2)}) collective-permute-start(bf16[1296,128]{1,0:T(8,128)(2,1)S(1)} %get-tuple-element.197.refs_4_), channel_id=1, source_target_pairs={{0,6},{1,3},{2,0},{3,5},{4,2},{5,7},{6,4},{7,1},{8,14},{9,11},{10,... | collective-permute-start | bytes 995336 | tf_op jit(solution)/shard_map/ppermute | solution.py:49
  91.7 4.8 %collective-permute-done.36.refs_14_ = bf16[1024,128]{1,0:T(8,128)(2,1)S(1)} collective-permute-done((bf16[1024,128]{1,0:T(8,128)(2,1)S(1)}, bf16[1024,128]{1,0:T(8,128)(2,1)S(1)}, u32[]{:S(2)}, u32[]{:S(2)}) %collective-permute-start.36) | collective-permute-done | bytes 262176 | tf_op jit(solution)/shard_map/ppermute | solution.py:49
  98.1 3.3 %collective-permute-done.32.refs_7_ = bf16[1296,128]{1,0:T(8,128)(2,1)S(1)} collective-permute-done((bf16[1296,128]{1,0:T(8,128)(2,1)S(1)}, bf16[1296,128]{1,0:T(8,128)(2,1)S(1)}, u32[]{:S(2)}, u32[]{:S(2)}) %collective-permute-start.32) | collective-permute-done | bytes 331808 | tf_op jit(solution)/shard_map/ppermute | solution.py:49
  101.4 7.9 %collective-permute-start.33 = (bf16[1296,128]{1,0:T(8,128)(2,1)S(1)}, bf16[1296,128]{1,0:T(8,128)(2,1)S(1)}, u32[]{:S(2)}, u32[]{:S(2)}) collective-permute-start(bf16[1296,128]{1,0:T(8,128)(2,1)S(1)} %collective-permute-done.32.refs_7_), channel_id=1, source_target_pairs={{0,1},{1,0},{2,3},{3,2},{4,5},{5,4},{6,7},{7,6},{8,9},{9,8},{10,11... | collective-permute-start | bytes 995336 | tf_op jit(solution)/shard_map/ppermute | solution.py:54
  113.2 4.9 %shard_map.116 = (bf16[8192,128]{1,0:T(8,128)(2,1)S(1)}, bf16[3344,128]{1,0:T(8,128)(2,1)S(1)}, bf16[3344,128]{1,0:T(8,128)(2,1)S(1)}, bf16[3344,128]{1,0:T(8,128)(2,1)S(1)}, f32[136,256]{1,0:T(8,128)S(1)}) custom-call(s32[1]{0:T(128)} %bitcast.11.live, s32[8,64]{1,0:T(8,128)S(1)} %get-tuple-element.183.tables, bf16[64,128,128]{2,1,0:T(8,128)(2,1)S(1)} %bitcast.18, ...), custom_call_target="tpu_custom_call" | custom-call | tf_op jit(solution)/shard_map/pallas_call | solution.py:233
  120.2 10.7 %collective-permute-done.40.refs_0_ = bf16[3344,128]{1,0:T(8,128)(2,1)S(1)} collective-permute-done((bf16[3344,128]{1,0:T(8,128)(2,1)S(1)}, bf16[3344,128]{1,0:T(8,128)(2,1)S(1)}, u32[]{:S(2)}, u32[]{:S(2)}) %collective-permute-start.40) | collective-permute-done | bytes 856096 | tf_op jit(solution)/shard_map/ppermute | solution.py:33
  132.6 9.1 %collective-permute-done.42.refs_2_ = bf16[3344,128]{1,0:T(8,128)(2,1)S(1)} collective-permute-done((bf16[3344,128]{1,0:T(8,128)(2,1)S(1)}, bf16[3344,128]{1,0:T(8,128)(2,1)S(1)}, u32[]{:S(2)}, u32[]{:S(2)}) %collective-permute-start.42) | collective-permute-done | bytes 856096 | tf_op jit(solution)/shard_map/ppermute | solution.py:33
  141.7 2.9 %shard_map.117 = (f32[2048,128]{1,0:T(8,128)}, bf16[2320,128]{1,0:T(8,128)(2,1)}, bf16[2320,128]{1,0:T(8,128)(2,1)}, bf16[2320,128]{1,0:T(8,128)(2,1)}, f32[136,256]{1,0:T(8,128)S(1)}) custom-call(s32[96]{0:T(128)S(1)} %get-tuple-element.195.lists, s32[3]{0:T(128)S(1)} %get-tuple-element.196.counts, bf16[8192,128]{1,0:T(8,128)(2,1)S(1)} %get-tuple-element.198.own, ...), custom_call_target="tpu_custom_call" | custom-call | tf_op jit(solution)/shard_map/pallas_call | solution.py:346
  144.6 2.9 %collective-permute-start.43 = (bf16[2320,128]{1,0:T(8,128)(2,1)}, bf16[2320,128]{1,0:T(8,128)(2,1)S(1)}, u32[]{:S(2)}, u32[]{:S(2)}) collective-permute-start(bf16[2320,128]{1,0:T(8,128)(2,1)} %get-tuple-element.208), channel_id=1, source_target_pairs={{0,96},{1,25},{2,98},{3,27},{4,100},{5,29},{6,102},{7,31},{8,104},... | collective-permute-start | bytes 1781768 | tf_op jit(solution)/shard_map/ppermute | solution.py:33
  149.1 12.4 %collective-permute-done.43.refs_1_ = bf16[2320,128]{1,0:T(8,128)(2,1)S(1)} collective-permute-done((bf16[2320,128]{1,0:T(8,128)(2,1)}, bf16[2320,128]{1,0:T(8,128)(2,1)S(1)}, u32[]{:S(2)}, u32[]{:S(2)}) %collective-permute-start.43) | collective-permute-done | bytes 593952 | tf_op jit(solution)/shard_map/ppermute | solution.py:33
  161.6 3.9 %collective-permute-done.45.refs_3_ = bf16[2320,128]{1,0:T(8,128)(2,1)S(1)} collective-permute-done((bf16[2320,128]{1,0:T(8,128)(2,1)}, bf16[2320,128]{1,0:T(8,128)(2,1)S(1)}, u32[]{:S(2)}, u32[]{:S(2)}) %collective-permute-start.45) | collective-permute-done | bytes 593952 | tf_op jit(solution)/shard_map/ppermute | solution.py:33
  165.4 2.5 %shard_map.118 = (f32[2048,128]{1,0:T(8,128)}, f32[128,256]{1,0:T(8,128)}, f32[1,256]{1,0:T(1,128)}) custom-call(f32[2048,128]{1,0:T(8,128)} %get-tuple-element.207.refs_0_, bf16[2320,128]{1,0:T(8,128)(2,1)S(1)} %collective-permute-done.43.refs_1_, bf16[2320,128]{1,0:T(8,128)(2,1)S(1)} %collective-permute-done.44.refs_2_, ...), custom_call_target="tpu_custom_call" | custom-call | tf_op jit(solution)/shard_map/pallas_call | solution.py:375
  (88 shorter events, 51.1 us)
Async XLA Ops:
  0.6 17.8 %collective-permute-start.8 = (bf16[2048,128]{1,0:T(8,128)(2,1)}, bf16[2048,128]{1,0:T(8,128)(2,1)S(1)}, u32[]{:S(2)}, u32[]{:S(2)}) collective-permute-start(bf16[2048,128]{1,0:T(8,128)(2,1)} %refs_0_.3), channel_id=1, source_target_pairs={{0,32},{1,9},{2,34},{3,11},{4,36},{5,13},{6,38},{7,15},{8,40},{9,1... | collective-permute-start | bytes 1572872 | tf_op jit(solution)/shard_map/ppermute | solution.py:33
  2.3 16.2 %collective-permute-start.7 = (bf16[2048,128]{1,0:T(8,128)(2,1)}, bf16[2048,128]{1,0:T(8,128)(2,1)S(1)}, u32[]{:S(2)}, u32[]{:S(2)}) collective-permute-start(bf16[2048,128]{1,0:T(8,128)(2,1)} %refs_0_.3), channel_id=1, source_target_pairs={{0,64},{1,17},{2,66},{3,19},{4,68},{5,21},{6,70},{7,23},{8,72},{9,... | collective-permute-start | bytes 1572872 | tf_op jit(solution)/shard_map/ppermute | solution.py:33
  5.0 13.5 %collective-permute-start.6 = (bf16[2048,128]{1,0:T(8,128)(2,1)}, bf16[2048,128]{1,0:T(8,128)(2,1)}, u32[]{:S(2)}, u32[]{:S(2)}) collective-permute-start(bf16[2048,128]{1,0:T(8,128)(2,1)} %refs_0_.3), channel_id=1, source_target_pairs={{0,96},{1,25},{2,98},{3,27},{4,100},{5,29},{6,102},{7,31},{8,104},... | collective-permute-start | bytes 1572872 | tf_op jit(solution)/shard_map/ppermute | solution.py:33
  20.5 21.9 %collective-permute-start.15 = (bf16[3072,128]{1,0:T(8,128)(2,1)S(1)}, bf16[3072,128]{1,0:T(8,128)(2,1)S(1)}, u32[]{:S(2)}, u32[]{:S(2)}) collective-permute-start(bf16[3072,128]{1,0:T(8,128)(2,1)S(1)} %get-tuple-element.184), channel_id=1, source_target_pairs={{0,24},{1,97},{2,26},{3,99},{4,28},{5,101},{6,30},{7,103},{8,0},{9... | collective-permute-start | bytes 2359304 | tf_op jit(solution)/shard_map/ppermute | solution.py:33
  24.4 18.0 %collective-permute-start.16 = (bf16[3072,128]{1,0:T(8,128)(2,1)S(1)}, bf16[3072,128]{1,0:T(8,128)(2,1)S(1)}, u32[]{:S(2)}, u32[]{:S(2)}) collective-permute-start(bf16[3072,128]{1,0:T(8,128)(2,1)S(1)} %get-tuple-element.185), channel_id=1, source_target_pairs={{0,16},{1,65},{2,18},{3,67},{4,20},{5,69},{6,22},{7,71},{8,24},{9,... | collective-permute-start | bytes 2359304 | tf_op jit(solution)/shard_map/ppermute | solution.py:33
  24.4 21.7 %collective-permute-start.17 = (bf16[3072,128]{1,0:T(8,128)(2,1)S(1)}, bf16[3072,128]{1,0:T(8,128)(2,1)S(1)}, u32[]{:S(2)}, u32[]{:S(2)}) collective-permute-start(bf16[3072,128]{1,0:T(8,128)(2,1)S(1)} %get-tuple-element.186), channel_id=1, source_target_pairs={{0,8},{1,33},{2,10},{3,35},{4,12},{5,37},{6,14},{7,39},{8,16},{9,4... | collective-permute-start | bytes 2359304 | tf_op jit(solution)/shard_map/ppermute | solution.py:33
  58.2 14.2 %collective-permute-start.24 = (bf16[1024,128]{1,0:T(8,128)(2,1)S(1)}, bf16[1024,128]{1,0:T(8,128)(2,1)S(1)}, u32[]{:S(2)}, u32[]{:S(2)}) collective-permute-start(bf16[1024,128]{1,0:T(8,128)(2,1)S(1)} %get-tuple-element.221), channel_id=1, source_target_pairs={{0,4},{1,5},{2,6},{3,7},{4,0},{5,1},{6,2},{7,3},{8,12},{9,13},{10,... | collective-permute-start | bytes 786440 | tf_op jit(solution)/shard_map/ppermute | solution.py:49
  60.6 12.9 %collective-permute-start.23 = (bf16[1024,128]{1,0:T(8,128)(2,1)S(1)}, bf16[1024,128]{1,0:T(8,128)(2,1)S(1)}, u32[]{:S(2)}, u32[]{:S(2)}) collective-permute-start(bf16[1024,128]{1,0:T(8,128)(2,1)S(1)} %get-tuple-element.222), channel_id=1, source_target_pairs={{0,6},{1,3},{2,0},{3,5},{4,2},{5,7},{6,4},{7,1},{8,14},{9,11},{10,... | collective-permute-start | bytes 786440 | tf_op jit(solution)/shard_map/ppermute | solution.py:49
  62.7 17.4 %collective-permute-start.21 = (bf16[1024,128]{1,0:T(8,128)(2,1)S(1)}, bf16[1024,128]{1,0:T(8,128)(2,1)S(1)}, u32[]{:S(2)}, u32[]{:S(2)}) collective-permute-start(bf16[1024,128]{1,0:T(8,128)(2,1)S(1)} %get-tuple-element.223), channel_id=1, source_target_pairs={{0,2},{1,7},{2,4},{3,1},{4,6},{5,3},{6,0},{7,5},{8,10},{9,15},{10,... | collective-permute-start | bytes 786440 | tf_op jit(solution)/shard_map/ppermute | solution.py:49
  62.9 22.1 %collective-permute-start.20 = (bf16[1024,128]{1,0:T(8,128)(2,1)S(1)}, bf16[1024,128]{1,0:T(8,128)(2,1)S(1)}, u32[]{:S(2)}, u32[]{:S(2)}) collective-permute-start(bf16[1024,128]{1,0:T(8,128)(2,1)S(1)} %get-tuple-element.224), channel_id=1, source_target_pairs={{0,4},{1,5},{2,6},{3,7},{4,0},{5,1},{6,2},{7,3},{8,12},{9,13},{10,... | collective-permute-start | bytes 786440 | tf_op jit(solution)/shard_map/ppermute | solution.py:49
  66.5 18.5 %collective-permute-start.19 = (bf16[1024,128]{1,0:T(8,128)(2,1)S(1)}, bf16[1024,128]{1,0:T(8,128)(2,1)S(1)}, u32[]{:S(2)}, u32[]{:S(2)}) collective-permute-start(bf16[1024,128]{1,0:T(8,128)(2,1)S(1)} %get-tuple-element.225), channel_id=1, source_target_pairs={{0,6},{1,3},{2,0},{3,5},{4,2},{5,7},{6,4},{7,1},{8,14},{9,11},{10,... | collective-permute-start | bytes 786440 | tf_op jit(solution)/shard_map/ppermute | solution.py:49
  76.4 12.8 %collective-permute-start.38 = (bf16[1024,128]{1,0:T(8,128)(2,1)S(1)}, bf16[1024,128]{1,0:T(8,128)(2,1)S(1)}, u32[]{:S(2)}, u32[]{:S(2)}) collective-permute-start(bf16[1024,128]{1,0:T(8,128)(2,1)S(1)} %get-tuple-element.193.refs_12_), channel_id=1, source_target_pairs={{0,2},{1,7},{2,4},{3,1},{4,6},{5,3},{6,0},{7,5},{8,10},{9,15},{10,... | collective-permute-start | bytes 786440 | tf_op jit(solution)/shard_map/ppermute | solution.py:49
  80.1 16.4 %collective-permute-start.36 = (bf16[1024,128]{1,0:T(8,128)(2,1)S(1)}, bf16[1024,128]{1,0:T(8,128)(2,1)S(1)}, u32[]{:S(2)}, u32[]{:S(2)}) collective-permute-start(bf16[1024,128]{1,0:T(8,128)(2,1)S(1)} %get-tuple-element.193.refs_12_), channel_id=1, source_target_pairs={{0,4},{1,5},{2,6},{3,7},{4,0},{5,1},{6,2},{7,3},{8,12},{9,13},{10,... | collective-permute-start | bytes 786440 | tf_op jit(solution)/shard_map/ppermute | solution.py:49
  87.0 14.4 %collective-permute-start.32 = (bf16[1296,128]{1,0:T(8,128)(2,1)S(1)}, bf16[1296,128]{1,0:T(8,128)(2,1)S(1)}, u32[]{:S(2)}, u32[]{:S(2)}) collective-permute-start(bf16[1296,128]{1,0:T(8,128)(2,1)S(1)} %get-tuple-element.197.refs_4_), channel_id=1, source_target_pairs={{0,2},{1,7},{2,4},{3,1},{4,6},{5,3},{6,0},{7,5},{8,10},{9,15},{10,... | collective-permute-start | bytes 995336 | tf_op jit(solution)/shard_map/ppermute | solution.py:49
  89.0 21.7 %collective-permute-start.30 = (bf16[1296,128]{1,0:T(8,128)(2,1)S(1)}, bf16[1296,128]{1,0:T(8,128)(2,1)S(1)}, u32[]{:S(2)}, u32[]{:S(2)}) collective-permute-start(bf16[1296,128]{1,0:T(8,128)(2,1)S(1)} %get-tuple-element.197.refs_4_), channel_id=1, source_target_pairs={{0,4},{1,5},{2,6},{3,7},{4,0},{5,1},{6,2},{7,3},{8,12},{9,13},{10,... | collective-permute-start | bytes 995336 | tf_op jit(solution)/shard_map/ppermute | solution.py:49
  89.2 21.5 %collective-permute-start.28 = (bf16[1296,128]{1,0:T(8,128)(2,1)S(1)}, bf16[1296,128]{1,0:T(8,128)(2,1)S(1)}, u32[]{:S(2)}, u32[]{:S(2)}) collective-permute-start(bf16[1296,128]{1,0:T(8,128)(2,1)S(1)} %get-tuple-element.197.refs_4_), channel_id=1, source_target_pairs={{0,6},{1,3},{2,0},{3,5},{4,2},{5,7},{6,4},{7,1},{8,14},{9,11},{10,... | collective-permute-start | bytes 995336 | tf_op jit(solution)/shard_map/ppermute | solution.py:49
  97.2 14.0 %collective-permute-start.37 = (bf16[1024,128]{1,0:T(8,128)(2,1)S(1)}, bf16[1024,128]{1,0:T(8,128)(2,1)S(1)}, u32[]{:S(2)}, u32[]{:S(2)}) collective-permute-start(bf16[1024,128]{1,0:T(8,128)(2,1)S(1)} %collective-permute-done.36.refs_14_), channel_id=1, source_target_pairs={{0,1},{1,0},{2,3},{3,2},{4,5},{5,4},{6,7},{7,6},{8,9},{9,8},{10,11... | collective-permute-start | bytes 786440 | tf_op jit(solution)/shard_map/ppermute | solution.py:54
  98.0 15.2 %collective-permute-start.27 = (bf16[1296,128]{1,0:T(8,128)(2,1)S(1)}, bf16[1296,128]{1,0:T(8,128)(2,1)S(1)}, u32[]{:S(2)}, u32[]{:S(2)}) collective-permute-start(bf16[1296,128]{1,0:T(8,128)(2,1)S(1)} %get-tuple-element.197.refs_4_), channel_id=1, source_target_pairs={{0,1},{1,0},{2,3},{3,2},{4,5},{5,4},{6,7},{7,6},{8,9},{9,8},{10,11... | collective-permute-start | bytes 995336 | tf_op jit(solution)/shard_map/ppermute | solution.py:54
  118.1 12.8 %collective-permute-start.40 = (bf16[3344,128]{1,0:T(8,128)(2,1)S(1)}, bf16[3344,128]{1,0:T(8,128)(2,1)S(1)}, u32[]{:S(2)}, u32[]{:S(2)}) collective-permute-start(bf16[3344,128]{1,0:T(8,128)(2,1)S(1)} %get-tuple-element.200), channel_id=1, source_target_pairs={{0,24},{1,97},{2,26},{3,99},{4,28},{5,101},{6,30},{7,103},{8,0},{9... | collective-permute-start | bytes 2568200 | tf_op jit(solution)/shard_map/ppermute | solution.py:33
  118.2 14.4 %collective-permute-start.41 = (bf16[3344,128]{1,0:T(8,128)(2,1)S(1)}, bf16[3344,128]{1,0:T(8,128)(2,1)S(1)}, u32[]{:S(2)}, u32[]{:S(2)}) collective-permute-start(bf16[3344,128]{1,0:T(8,128)(2,1)S(1)} %get-tuple-element.201), channel_id=1, source_target_pairs={{0,16},{1,65},{2,18},{3,67},{4,20},{5,69},{6,22},{7,71},{8,24},{9,... | collective-permute-start | bytes 2568200 | tf_op jit(solution)/shard_map/ppermute | solution.py:33
  118.3 23.4 %collective-permute-start.42 = (bf16[3344,128]{1,0:T(8,128)(2,1)S(1)}, bf16[3344,128]{1,0:T(8,128)(2,1)S(1)}, u32[]{:S(2)}, u32[]{:S(2)}) collective-permute-start(bf16[3344,128]{1,0:T(8,128)(2,1)S(1)} %get-tuple-element.202), channel_id=1, source_target_pairs={{0,8},{1,33},{2,10},{3,35},{4,12},{5,37},{6,14},{7,39},{8,16},{9,4... | collective-permute-start | bytes 2568200 | tf_op jit(solution)/shard_map/ppermute | solution.py:33
  144.6 17.0 %collective-permute-start.43 = (bf16[2320,128]{1,0:T(8,128)(2,1)}, bf16[2320,128]{1,0:T(8,128)(2,1)S(1)}, u32[]{:S(2)}, u32[]{:S(2)}) collective-permute-start(bf16[2320,128]{1,0:T(8,128)(2,1)} %get-tuple-element.208), channel_id=1, source_target_pairs={{0,96},{1,25},{2,98},{3,27},{4,100},{5,29},{6,102},{7,31},{8,104},... | collective-permute-start | bytes 1781768 | tf_op jit(solution)/shard_map/ppermute | solution.py:33
  147.4 14.1 %collective-permute-start.44 = (bf16[2320,128]{1,0:T(8,128)(2,1)}, bf16[2320,128]{1,0:T(8,128)(2,1)S(1)}, u32[]{:S(2)}, u32[]{:S(2)}) collective-permute-start(bf16[2320,128]{1,0:T(8,128)(2,1)} %get-tuple-element.209), channel_id=1, source_target_pairs={{0,64},{1,17},{2,66},{3,19},{4,68},{5,21},{6,70},{7,23},{8,72},{9,... | collective-permute-start | bytes 1781768 | tf_op jit(solution)/shard_map/ppermute | solution.py:33
  148.7 16.8 %collective-permute-start.45 = (bf16[2320,128]{1,0:T(8,128)(2,1)}, bf16[2320,128]{1,0:T(8,128)(2,1)S(1)}, u32[]{:S(2)}, u32[]{:S(2)}) collective-permute-start(bf16[2320,128]{1,0:T(8,128)(2,1)} %get-tuple-element.210), channel_id=1, source_target_pairs={{0,32},{1,9},{2,34},{3,11},{4,36},{5,13},{6,38},{7,15},{8,40},{9,1... | collective-permute-start | bytes 1781768 | tf_op jit(solution)/shard_map/ppermute | solution.py:33
  (25 other events, 232.2 us)

commit v12 on v11

--- a/solution.py
+++ b/solution.py
@@ -410,7 +410,7 @@
     sums[:T] += lax.dot_general(
         high, slope, over_rows, preferred_element_type=F32
     ) + lax.dot_general(low, slope, over_rows, preferred_element_type=F32)
-    sums[T:] += jnp.sum(slope.astype(F32).reshape(-1, 8, slope.shape[1]), axis=0)
+    sums[T:] += jnp.sum(slope.astype(F32).reshape(-1, 16, slope.shape[1]), axis=0)
 
     @pl.when((pl.program_id(0) == pl.num_programs(0) - 1) & second)
     def _():
@@ -425,7 +425,7 @@
     step = 1024
     steps = rows // 2 // step
     shift = part * steps
-    tail = 2 * (T + 8) if before else 0
+    tail = 2 * (T + 16) if before else 0
     half = pl.BlockSpec((step, T), lambda i: (i, 0))
     full = pl.BlockSpec((step, width), lambda i: (i + shift, 0))
 
@@ -438,12 +438,12 @@
         out_shape=[
             jax.ShapeDtypeStruct((rows, width), BF16),
             jax.ShapeDtypeStruct((rows // 2 + tail, T), BF16),
-            jax.ShapeDtypeStruct((T + 8, width), F32),
+            jax.ShapeDtypeStruct((T + 16, width), F32),
         ],
         in_specs=[half] * 5
         + [full, whole(T, width), whole(1, width)]
-        + ([ANY, whole(T + 8, width), ANY] if before else []),
-        out_specs=[full, whole(rows // 2 + tail, T), whole(T + 8, width)],
+        + ([ANY, whole(T + 16, width), ANY] if before else []),
+        out_specs=[full, whole(rows // 2 + tail, T), whole(T + 16, width)],
         input_output_aliases={8: 0} if before else {},
         compiler_params=room(20),
     )(*parts, grad, weight, offset, *before)

time: 168 us -> 169 us (level)
    ppermute x12, starting transfers between devices: 18.3 us -> 20.4 us  [along_y(): return lax.ppermute(value, 'col', pairs)]
where the time goes in v12:
time: 169 us; the launch traced here: 168 us
  waiting for transfers between devices  82.1 us (49%)
  starting transfers between devices  58.5 us (35%)
  Pallas kernels  22.1 us (13%)
  between operations  2.11 us (1%)
  local copies, waits for them, and re-layouts  1.84 us (1%)
    ppermute x18, waiting for transfers between devices, along_xz(): return lax.ppermute(value, ('row', 'col'), pairs)  55.8 us
    ppermute x18, starting transfers between devices, along_xz(): return lax.ppermute(value, ('row', 'col'), pairs)  29.1 us
    ppermute x12, waiting for transfers between devices, along_y(): return lax.ppermute(value, 'col', pairs)  21.7 us
    ppermute x12, starting transfers between devices, along_y(): return lax.ppermute(value, 'col', pairs)  20.4 us
    pallas_call x2, Pallas kernels, products(): pl.pallas_call(kernel, out_shape=[jax.ShapeDtypeStruct((n * T + e, T), BF...  10.2 us
    ppermute x10, starting transfers between devices, other_core(): return lax.ppermute(value, 'col', pairs)  9.09 us
    ppermute x10, waiting for transfers between devices, other_core(): return lax.ppermute(value, 'col', pairs)  4.64 us
    pallas_call x2, Pallas kernels, dense(): pl.pallas_call(functools.partial(dense_kernel, step=step), grid=(steps,),...  3.73 us
  transfers between devices with their start and end apart: 40, of which 22 were waited for; matrix products, arithmetic and copies ran while one was open for 1% of the time, Pallas kernels for 2%

profile of v12, /device:TPU:0, one launch (start us, length us, event | category | flops | bytes accessed | tf_op | source)
XLA Modules:
  0.0 168.4 jit_solution(15743695398311098848)
XLA Ops:
  2.3 2.7 %collective-permute-start.7 = (bf16[2048,128]{1,0:T(8,128)(2,1)}, bf16[2048,128]{1,0:T(8,128)(2,1)S(1)}, u32[]{:S(2)}, u32[]{:S(2)}) collective-permute-start(bf16[2048,128]{1,0:T(8,128)(2,1)} %refs_0_.3), channel_id=1, source_target_pairs={{0,64},{1,17},{2,66},{3,19},{4,68},{5,21},{6,70},{7,23},{8,72},{9,... | collective-permute-start | bytes 1572872 | tf_op jit(solution)/shard_map/ppermute | solution.py:33
  10.7 3.6 %collective-permute-start.10 = (bf16[16,128]{1,0:T(8,128)(2,1)S(1)}, bf16[16,128]{1,0:T(8,128)(2,1)S(1)}, u32[]{:S(2)}, u32[]{:S(2)}) collective-permute-start(bf16[16,128]{1,0:T(8,128)(2,1)S(1)} %get-tuple-element.181.refs_4_), channel_id=1, source_target_pairs={{0,16},{1,65},{2,18},{3,67},{4,20},{5,69},{6,22},{7,71},{8,24},{9,... | collective-permute-start | bytes 12296 | tf_op jit(solution)/shard_map/ppermute | solution.py:33
  20.8 3.6 %collective-permute-start.15 = (bf16[3072,128]{1,0:T(8,128)(2,1)S(1)}, bf16[3072,128]{1,0:T(8,128)(2,1)S(1)}, u32[]{:S(2)}, u32[]{:S(2)}) collective-permute-start(bf16[3072,128]{1,0:T(8,128)(2,1)S(1)} %get-tuple-element.184), channel_id=1, source_target_pairs={{0,24},{1,97},{2,26},{3,99},{4,28},{5,101},{6,30},{7,103},{8,0},{9... | collective-permute-start | bytes 2359304 | tf_op jit(solution)/shard_map/ppermute | solution.py:33
  27.6 2.5 %collective-permute-start.13 = (f32[8,128]{1,0:T(8,128)S(1)}, f32[8,128]{1,0:T(8,128)S(1)}, u32[]{:S(2)}, u32[]{:S(2)}) collective-permute-start(f32[8,128]{1,0:T(8,128)S(1)} %get-tuple-element.182), channel_id=1, source_target_pairs={{0,64},{1,17},{2,66},{3,19},{4,68},{5,21},{6,70},{7,23},{8,72},{9,... | collective-permute-start | bytes 12296 | tf_op jit(solution)/shard_map/ppermute | solution.py:33
  30.0 5.4 %collective-permute-done.14 = f32[8,128]{1,0:T(8,128)S(1)} collective-permute-done((f32[8,128]{1,0:T(8,128)S(1)}, f32[8,128]{1,0:T(8,128)S(1)}, u32[]{:S(2)}, u32[]{:S(2)}) %collective-permute-start.14) | collective-permute-done | bytes 4128 | tf_op jit(solution)/shard_map/ppermute | solution.py:33
  35.4 3.7 %collective-permute-done.12 = f32[8,128]{1,0:T(8,128)S(1)} collective-permute-done((f32[8,128]{1,0:T(8,128)S(1)}, f32[8,128]{1,0:T(8,128)S(1)}, u32[]{:S(2)}, u32[]{:S(2)}) %collective-permute-start.12) | collective-permute-done | bytes 4128 | tf_op jit(solution)/shard_map/ppermute | solution.py:33
  42.5 3.6 %collective-permute-done.17.refs_6_ = bf16[3072,128]{1,0:T(8,128)(2,1)S(1)} collective-permute-done((bf16[3072,128]{1,0:T(8,128)(2,1)S(1)}, bf16[3072,128]{1,0:T(8,128)(2,1)S(1)}, u32[]{:S(2)}, u32[]{:S(2)}) %collective-permute-start.17) | collective-permute-done | bytes 786464 | tf_op jit(solution)/shard_map/ppermute | solution.py:33
  46.1 5.6 %shard_map.113 = (bf16[4096,128]{1,0:T(8,128)(2,1)}, bf16[4096,128]{1,0:T(8,128)(2,1)}, bf16[4096,128]{1,0:T(8,128)(2,1)}, bf16[4096,128]{1,0:T(8,128)(2,1)}) custom-call(s32[1]{0:T(128)} %bitcast.10.live, s32[8,64]{1,0:T(8,128)S(1)} %get-tuple-element.183.tables, bf16[64,128,128]{2,1,0:T(8,128)(2,1)S(1)} %bitcast.16, bf16[2048,128]{1,0:T(8,128)(2,1)} %refs_0_.3, ...), custom_call_target="tpu_custom_call" | custom-call | tf_op jit(solution)/shard_map/pallas_call | solution.py:233
  52.3 2.4 %collective-permute-done.22.refs_1_ = bf16[4096,128]{1,0:T(8,128)(2,1)S(1)} collective-permute-done((bf16[4096,128]{1,0:T(8,128)(2,1)}, bf16[4096,128]{1,0:T(8,128)(2,1)S(1)}, u32[]{:S(2)}, u32[]{:S(2)}) %collective-permute-start.22) | collective-permute-done | bytes 1048608 | tf_op jit(solution)/shard_map/ppermute | solution.py:54
  57.4 3.3 %collective-permute-start.24 = (bf16[1024,128]{1,0:T(8,128)(2,1)S(1)}, bf16[1024,128]{1,0:T(8,128)(2,1)S(1)}, u32[]{:S(2)}, u32[]{:S(2)}) collective-permute-start(bf16[1024,128]{1,0:T(8,128)(2,1)S(1)} %get-tuple-element.221), channel_id=1, source_target_pairs={{0,4},{1,5},{2,6},{3,7},{4,0},{5,1},{6,2},{7,3},{8,12},{9,13},{10,... | collective-permute-start | bytes 786440 | tf_op jit(solution)/shard_map/ppermute | solution.py:49
  63.4 2.9 %collective-permute-done.25.refs_4_ = bf16[1024,128]{1,0:T(8,128)(2,1)S(1)} collective-permute-done((bf16[1024,128]{1,0:T(8,128)(2,1)S(1)}, bf16[1024,128]{1,0:T(8,128)(2,1)S(1)}, u32[]{:S(2)}, u32[]{:S(2)}) %collective-permute-start.25) | collective-permute-done | bytes 262176 | tf_op jit(solution)/shard_map/ppermute | solution.py:49
  67.4 5.1 %collective-permute-done.24.refs_3_ = bf16[1024,128]{1,0:T(8,128)(2,1)S(1)} collective-permute-done((bf16[1024,128]{1,0:T(8,128)(2,1)S(1)}, bf16[1024,128]{1,0:T(8,128)(2,1)S(1)}, u32[]{:S(2)}, u32[]{:S(2)}) %collective-permute-start.24) | collective-permute-done | bytes 262176 | tf_op jit(solution)/shard_map/ppermute | solution.py:49
  78.1 6.6 %collective-permute-start.36 = (bf16[1024,128]{1,0:T(8,128)(2,1)S(1)}, bf16[1024,128]{1,0:T(8,128)(2,1)S(1)}, u32[]{:S(2)}, u32[]{:S(2)}) collective-permute-start(bf16[1024,128]{1,0:T(8,128)(2,1)S(1)} %get-tuple-element.193.refs_12_), channel_id=1, source_target_pairs={{0,4},{1,5},{2,6},{3,7},{4,0},{5,1},{6,2},{7,3},{8,12},{9,13},{10,... | collective-permute-start | bytes 786440 | tf_op jit(solution)/shard_map/ppermute | solution.py:49
  91.3 4.8 %collective-permute-done.36.refs_14_ = bf16[1024,128]{1,0:T(8,128)(2,1)S(1)} collective-permute-done((bf16[1024,128]{1,0:T(8,128)(2,1)S(1)}, bf16[1024,128]{1,0:T(8,128)(2,1)S(1)}, u32[]{:S(2)}, u32[]{:S(2)}) %collective-permute-start.36) | collective-permute-done | bytes 262176 | tf_op jit(solution)/shard_map/ppermute | solution.py:49
  97.7 4.1 %collective-permute-done.32.refs_7_ = bf16[1312,128]{1,0:T(8,128)(2,1)S(1)} collective-permute-done((bf16[1312,128]{1,0:T(8,128)(2,1)S(1)}, bf16[1312,128]{1,0:T(8,128)(2,1)S(1)}, u32[]{:S(2)}, u32[]{:S(2)}) %collective-permute-start.32) | collective-permute-done | bytes 335904 | tf_op jit(solution)/shard_map/ppermute | solution.py:49
  101.9 6.7 %collective-permute-start.33 = (bf16[1312,128]{1,0:T(8,128)(2,1)S(1)}, bf16[1312,128]{1,0:T(8,128)(2,1)S(1)}, u32[]{:S(2)}, u32[]{:S(2)}) collective-permute-start(bf16[1312,128]{1,0:T(8,128)(2,1)S(1)} %collective-permute-done.32.refs_7_), channel_id=1, source_target_pairs={{0,1},{1,0},{2,3},{3,2},{4,5},{5,4},{6,7},{7,6},{8,9},{9,8},{10,11... | collective-permute-start | bytes 1007624 | tf_op jit(solution)/shard_map/ppermute | solution.py:54
  113.0 4.6 %shard_map.116 = (bf16[8192,128]{1,0:T(8,128)(2,1)S(1)}, bf16[3360,128]{1,0:T(8,128)(2,1)S(1)}, bf16[3360,128]{1,0:T(8,128)(2,1)S(1)}, bf16[3360,128]{1,0:T(8,128)(2,1)S(1)}, f32[144,256]{1,0:T(8,128)S(1)}) custom-call(s32[1]{0:T(128)} %bitcast.11.live, s32[8,64]{1,0:T(8,128)S(1)} %get-tuple-element.183.tables, bf16[64,128,128]{2,1,0:T(8,128)(2,1)S(1)} %bitcast.18, ...), custom_call_target="tpu_custom_call" | custom-call | tf_op jit(solution)/shard_map/pallas_call | solution.py:233
  120.2 10.3 %collective-permute-done.40.refs_0_ = bf16[3360,128]{1,0:T(8,128)(2,1)S(1)} collective-permute-done((bf16[3360,128]{1,0:T(8,128)(2,1)S(1)}, bf16[3360,128]{1,0:T(8,128)(2,1)S(1)}, u32[]{:S(2)}, u32[]{:S(2)}) %collective-permute-start.40) | collective-permute-done | bytes 860192 | tf_op jit(solution)/shard_map/ppermute | solution.py:33
  130.5 3.2 %collective-permute-done.41.refs_1_ = bf16[3360,128]{1,0:T(8,128)(2,1)S(1)} collective-permute-done((bf16[3360,128]{1,0:T(8,128)(2,1)S(1)}, bf16[3360,128]{1,0:T(8,128)(2,1)S(1)}, u32[]{:S(2)}, u32[]{:S(2)}) %collective-permute-start.41) | collective-permute-done | bytes 860192 | tf_op jit(solution)/shard_map/ppermute | solution.py:33
  133.7 8.8 %collective-permute-done.42.refs_2_ = bf16[3360,128]{1,0:T(8,128)(2,1)S(1)} collective-permute-done((bf16[3360,128]{1,0:T(8,128)(2,1)S(1)}, bf16[3360,128]{1,0:T(8,128)(2,1)S(1)}, u32[]{:S(2)}, u32[]{:S(2)}) %collective-permute-start.42) | collective-permute-done | bytes 860192 | tf_op jit(solution)/shard_map/ppermute | solution.py:33
  142.5 3.1 %shard_map.117 = (f32[2048,128]{1,0:T(8,128)}, bf16[2336,128]{1,0:T(8,128)(2,1)}, bf16[2336,128]{1,0:T(8,128)(2,1)}, bf16[2336,128]{1,0:T(8,128)(2,1)}, f32[144,256]{1,0:T(8,128)S(1)}) custom-call(s32[96]{0:T(128)S(1)} %get-tuple-element.195.lists, s32[3]{0:T(128)S(1)} %get-tuple-element.196.counts, bf16[8192,128]{1,0:T(8,128)(2,1)S(1)} %get-tuple-element.198.own, ...), custom_call_target="tpu_custom_call" | custom-call | tf_op jit(solution)/shard_map/pallas_call | solution.py:346
  149.8 12.4 %collective-permute-done.43.refs_1_ = bf16[2336,128]{1,0:T(8,128)(2,1)S(1)} collective-permute-done((bf16[2336,128]{1,0:T(8,128)(2,1)}, bf16[2336,128]{1,0:T(8,128)(2,1)S(1)}, u32[]{:S(2)}, u32[]{:S(2)}) %collective-permute-start.43) | collective-permute-done | bytes 598048 | tf_op jit(solution)/shard_map/ppermute | solution.py:33
  162.1 3.8 %collective-permute-done.45.refs_3_ = bf16[2336,128]{1,0:T(8,128)(2,1)S(1)} collective-permute-done((bf16[2336,128]{1,0:T(8,128)(2,1)}, bf16[2336,128]{1,0:T(8,128)(2,1)S(1)}, u32[]{:S(2)}, u32[]{:S(2)}) %collective-permute-start.45) | collective-permute-done | bytes 598048 | tf_op jit(solution)/shard_map/ppermute | solution.py:33
  166.0 2.5 %shard_map.118 = (f32[2048,128]{1,0:T(8,128)}, f32[128,256]{1,0:T(8,128)}, f32[1,256]{1,0:T(1,128)}) custom-call(f32[2048,128]{1,0:T(8,128)} %get-tuple-element.207.refs_0_, bf16[2336,128]{1,0:T(8,128)(2,1)S(1)} %collective-permute-done.43.refs_1_, bf16[2336,128]{1,0:T(8,128)(2,1)S(1)} %collective-permute-done.44.refs_2_, ...), custom_call_target="tpu_custom_call" | custom-call | tf_op jit(solution)/shard_map/pallas_call | solution.py:375
  (88 shorter events, 51.2 us)
Async XLA Ops:
  0.6 17.8 %collective-permute-start.8 = (bf16[2048,128]{1,0:T(8,128)(2,1)}, bf16[2048,128]{1,0:T(8,128)(2,1)S(1)}, u32[]{:S(2)}, u32[]{:S(2)}) collective-permute-start(bf16[2048,128]{1,0:T(8,128)(2,1)} %refs_0_.3), channel_id=1, source_target_pairs={{0,32},{1,9},{2,34},{3,11},{4,36},{5,13},{6,38},{7,15},{8,40},{9,1... | collective-permute-start | bytes 1572872 | tf_op jit(solution)/shard_map/ppermute | solution.py:33
  2.3 16.2 %collective-permute-start.7 = (bf16[2048,128]{1,0:T(8,128)(2,1)}, bf16[2048,128]{1,0:T(8,128)(2,1)S(1)}, u32[]{:S(2)}, u32[]{:S(2)}) collective-permute-start(bf16[2048,128]{1,0:T(8,128)(2,1)} %refs_0_.3), channel_id=1, source_target_pairs={{0,64},{1,17},{2,66},{3,19},{4,68},{5,21},{6,70},{7,23},{8,72},{9,... | collective-permute-start | bytes 1572872 | tf_op jit(solution)/shard_map/ppermute | solution.py:33
  5.0 13.5 %collective-permute-start.6 = (bf16[2048,128]{1,0:T(8,128)(2,1)}, bf16[2048,128]{1,0:T(8,128)(2,1)}, u32[]{:S(2)}, u32[]{:S(2)}) collective-permute-start(bf16[2048,128]{1,0:T(8,128)(2,1)} %refs_0_.3), channel_id=1, source_target_pairs={{0,96},{1,25},{2,98},{3,27},{4,100},{5,29},{6,102},{7,31},{8,104},... | collective-permute-start | bytes 1572872 | tf_op jit(solution)/shard_map/ppermute | solution.py:33
  20.8 21.6 %collective-permute-start.15 = (bf16[3072,128]{1,0:T(8,128)(2,1)S(1)}, bf16[3072,128]{1,0:T(8,128)(2,1)S(1)}, u32[]{:S(2)}, u32[]{:S(2)}) collective-permute-start(bf16[3072,128]{1,0:T(8,128)(2,1)S(1)} %get-tuple-element.184), channel_id=1, source_target_pairs={{0,24},{1,97},{2,26},{3,99},{4,28},{5,101},{6,30},{7,103},{8,0},{9... | collective-permute-start | bytes 2359304 | tf_op jit(solution)/shard_map/ppermute | solution.py:33
  24.4 18.0 %collective-permute-start.16 = (bf16[3072,128]{1,0:T(8,128)(2,1)S(1)}, bf16[3072,128]{1,0:T(8,128)(2,1)S(1)}, u32[]{:S(2)}, u32[]{:S(2)}) collective-permute-start(bf16[3072,128]{1,0:T(8,128)(2,1)S(1)} %get-tuple-element.185), channel_id=1, source_target_pairs={{0,16},{1,65},{2,18},{3,67},{4,20},{5,69},{6,22},{7,71},{8,24},{9,... | collective-permute-start | bytes 2359304 | tf_op jit(solution)/shard_map/ppermute | solution.py:33
  24.4 21.7 %collective-permute-start.17 = (bf16[3072,128]{1,0:T(8,128)(2,1)S(1)}, bf16[3072,128]{1,0:T(8,128)(2,1)S(1)}, u32[]{:S(2)}, u32[]{:S(2)}) collective-permute-start(bf16[3072,128]{1,0:T(8,128)(2,1)S(1)} %get-tuple-element.186), channel_id=1, source_target_pairs={{0,8},{1,33},{2,10},{3,35},{4,12},{5,37},{6,14},{7,39},{8,16},{9,4... | collective-permute-start | bytes 2359304 | tf_op jit(solution)/shard_map/ppermute | solution.py:33
  57.4 15.1 %collective-permute-start.24 = (bf16[1024,128]{1,0:T(8,128)(2,1)S(1)}, bf16[1024,128]{1,0:T(8,128)(2,1)S(1)}, u32[]{:S(2)}, u32[]{:S(2)}) collective-permute-start(bf16[1024,128]{1,0:T(8,128)(2,1)S(1)} %get-tuple-element.221), channel_id=1, source_target_pairs={{0,4},{1,5},{2,6},{3,7},{4,0},{5,1},{6,2},{7,3},{8,12},{9,13},{10,... | collective-permute-start | bytes 786440 | tf_op jit(solution)/shard_map/ppermute | solution.py:49
  60.7 12.6 %collective-permute-start.23 = (bf16[1024,128]{1,0:T(8,128)(2,1)S(1)}, bf16[1024,128]{1,0:T(8,128)(2,1)S(1)}, u32[]{:S(2)}, u32[]{:S(2)}) collective-permute-start(bf16[1024,128]{1,0:T(8,128)(2,1)S(1)} %get-tuple-element.222), channel_id=1, source_target_pairs={{0,6},{1,3},{2,0},{3,5},{4,2},{5,7},{6,4},{7,1},{8,14},{9,11},{10,... | collective-permute-start | bytes 786440 | tf_op jit(solution)/shard_map/ppermute | solution.py:49
  61.9 16.2 %collective-permute-start.21 = (bf16[1024,128]{1,0:T(8,128)(2,1)S(1)}, bf16[1024,128]{1,0:T(8,128)(2,1)S(1)}, u32[]{:S(2)}, u32[]{:S(2)}) collective-permute-start(bf16[1024,128]{1,0:T(8,128)(2,1)S(1)} %get-tuple-element.223), channel_id=1, source_target_pairs={{0,2},{1,7},{2,4},{3,1},{4,6},{5,3},{6,0},{7,5},{8,10},{9,15},{10,... | collective-permute-start | bytes 786440 | tf_op jit(solution)/shard_map/ppermute | solution.py:49
  63.0 21.7 %collective-permute-start.20 = (bf16[1024,128]{1,0:T(8,128)(2,1)S(1)}, bf16[1024,128]{1,0:T(8,128)(2,1)S(1)}, u32[]{:S(2)}, u32[]{:S(2)}) collective-permute-start(bf16[1024,128]{1,0:T(8,128)(2,1)S(1)} %get-tuple-element.224), channel_id=1, source_target_pairs={{0,4},{1,5},{2,6},{3,7},{4,0},{5,1},{6,2},{7,3},{8,12},{9,13},{10,... | collective-permute-start | bytes 786440 | tf_op jit(solution)/shard_map/ppermute | solution.py:49
  66.3 18.3 %collective-permute-start.19 = (bf16[1024,128]{1,0:T(8,128)(2,1)S(1)}, bf16[1024,128]{1,0:T(8,128)(2,1)S(1)}, u32[]{:S(2)}, u32[]{:S(2)}) collective-permute-start(bf16[1024,128]{1,0:T(8,128)(2,1)S(1)} %get-tuple-element.225), channel_id=1, source_target_pairs={{0,6},{1,3},{2,0},{3,5},{4,2},{5,7},{6,4},{7,1},{8,14},{9,11},{10,... | collective-permute-start | bytes 786440 | tf_op jit(solution)/shard_map/ppermute | solution.py:49
  75.8 13.2 %collective-permute-start.38 = (bf16[1024,128]{1,0:T(8,128)(2,1)S(1)}, bf16[1024,128]{1,0:T(8,128)(2,1)S(1)}, u32[]{:S(2)}, u32[]{:S(2)}) collective-permute-start(bf16[1024,128]{1,0:T(8,128)(2,1)S(1)} %get-tuple-element.193.refs_12_), channel_id=1, source_target_pairs={{0,2},{1,7},{2,4},{3,1},{4,6},{5,3},{6,0},{7,5},{8,10},{9,15},{10,... | collective-permute-start | bytes 786440 | tf_op jit(solution)/shard_map/ppermute | solution.py:49
  78.1 18.0 %collective-permute-start.36 = (bf16[1024,128]{1,0:T(8,128)(2,1)S(1)}, bf16[1024,128]{1,0:T(8,128)(2,1)S(1)}, u32[]{:S(2)}, u32[]{:S(2)}) collective-permute-start(bf16[1024,128]{1,0:T(8,128)(2,1)S(1)} %get-tuple-element.193.refs_12_), channel_id=1, source_target_pairs={{0,4},{1,5},{2,6},{3,7},{4,0},{5,1},{6,2},{7,3},{8,12},{9,13},{10,... | collective-permute-start | bytes 786440 | tf_op jit(solution)/shard_map/ppermute | solution.py:49
  86.6 15.3 %collective-permute-start.32 = (bf16[1312,128]{1,0:T(8,128)(2,1)S(1)}, bf16[1312,128]{1,0:T(8,128)(2,1)S(1)}, u32[]{:S(2)}, u32[]{:S(2)}) collective-permute-start(bf16[1312,128]{1,0:T(8,128)(2,1)S(1)} %get-tuple-element.197.refs_4_), channel_id=1, source_target_pairs={{0,2},{1,7},{2,4},{3,1},{4,6},{5,3},{6,0},{7,5},{8,10},{9,15},{10,... | collective-permute-start | bytes 1007624 | tf_op jit(solution)/shard_map/ppermute | solution.py:49
  88.6 21.9 %collective-permute-start.30 = (bf16[1312,128]{1,0:T(8,128)(2,1)S(1)}, bf16[1312,128]{1,0:T(8,128)(2,1)S(1)}, u32[]{:S(2)}, u32[]{:S(2)}) collective-permute-start(bf16[1312,128]{1,0:T(8,128)(2,1)S(1)} %get-tuple-element.197.refs_4_), channel_id=1, source_target_pairs={{0,4},{1,5},{2,6},{3,7},{4,0},{5,1},{6,2},{7,3},{8,12},{9,13},{10,... | collective-permute-start | bytes 1007624 | tf_op jit(solution)/shard_map/ppermute | solution.py:49
  89.0 21.5 %collective-permute-start.28 = (bf16[1312,128]{1,0:T(8,128)(2,1)S(1)}, bf16[1312,128]{1,0:T(8,128)(2,1)S(1)}, u32[]{:S(2)}, u32[]{:S(2)}) collective-permute-start(bf16[1312,128]{1,0:T(8,128)(2,1)S(1)} %get-tuple-element.197.refs_4_), channel_id=1, source_target_pairs={{0,6},{1,3},{2,0},{3,5},{4,2},{5,7},{6,4},{7,1},{8,14},{9,11},{10,... | collective-permute-start | bytes 1007624 | tf_op jit(solution)/shard_map/ppermute | solution.py:49
  96.9 14.1 %collective-permute-start.37 = (bf16[1024,128]{1,0:T(8,128)(2,1)S(1)}, bf16[1024,128]{1,0:T(8,128)(2,1)S(1)}, u32[]{:S(2)}, u32[]{:S(2)}) collective-permute-start(bf16[1024,128]{1,0:T(8,128)(2,1)S(1)} %collective-permute-done.36.refs_14_), channel_id=1, source_target_pairs={{0,1},{1,0},{2,3},{3,2},{4,5},{5,4},{6,7},{7,6},{8,9},{9,8},{10,11... | collective-permute-start | bytes 786440 | tf_op jit(solution)/shard_map/ppermute | solution.py:54
  97.6 15.4 %collective-permute-start.27 = (bf16[1312,128]{1,0:T(8,128)(2,1)S(1)}, bf16[1312,128]{1,0:T(8,128)(2,1)S(1)}, u32[]{:S(2)}, u32[]{:S(2)}) collective-permute-start(bf16[1312,128]{1,0:T(8,128)(2,1)S(1)} %get-tuple-element.197.refs_4_), channel_id=1, source_target_pairs={{0,1},{1,0},{2,3},{3,2},{4,5},{5,4},{6,7},{7,6},{8,9},{9,8},{10,11... | collective-permute-start | bytes 1007624 | tf_op jit(solution)/shard_map/ppermute | solution.py:54
  117.6 12.8 %collective-permute-start.40 = (bf16[3360,128]{1,0:T(8,128)(2,1)S(1)}, bf16[3360,128]{1,0:T(8,128)(2,1)S(1)}, u32[]{:S(2)}, u32[]{:S(2)}) collective-permute-start(bf16[3360,128]{1,0:T(8,128)(2,1)S(1)} %get-tuple-element.200), channel_id=1, source_target_pairs={{0,24},{1,97},{2,26},{3,99},{4,28},{5,101},{6,30},{7,103},{8,0},{9... | collective-permute-start | bytes 2580488 | tf_op jit(solution)/shard_map/ppermute | solution.py:33
  119.3 14.4 %collective-permute-start.41 = (bf16[3360,128]{1,0:T(8,128)(2,1)S(1)}, bf16[3360,128]{1,0:T(8,128)(2,1)S(1)}, u32[]{:S(2)}, u32[]{:S(2)}) collective-permute-start(bf16[3360,128]{1,0:T(8,128)(2,1)S(1)} %get-tuple-element.201), channel_id=1, source_target_pairs={{0,16},{1,65},{2,18},{3,67},{4,20},{5,69},{6,22},{7,71},{8,24},{9,... | collective-permute-start | bytes 2580488 | tf_op jit(solution)/shard_map/ppermute | solution.py:33
  119.3 23.2 %collective-permute-start.42 = (bf16[3360,128]{1,0:T(8,128)(2,1)S(1)}, bf16[3360,128]{1,0:T(8,128)(2,1)S(1)}, u32[]{:S(2)}, u32[]{:S(2)}) collective-permute-start(bf16[3360,128]{1,0:T(8,128)(2,1)S(1)} %get-tuple-element.202), channel_id=1, source_target_pairs={{0,8},{1,33},{2,10},{3,35},{4,12},{5,37},{6,14},{7,39},{8,16},{9,4... | collective-permute-start | bytes 2580488 | tf_op jit(solution)/shard_map/ppermute | solution.py:33
  145.6 16.5 %collective-permute-start.43 = (bf16[2336,128]{1,0:T(8,128)(2,1)}, bf16[2336,128]{1,0:T(8,128)(2,1)S(1)}, u32[]{:S(2)}, u32[]{:S(2)}) collective-permute-start(bf16[2336,128]{1,0:T(8,128)(2,1)} %get-tuple-element.208), channel_id=1, source_target_pairs={{0,96},{1,25},{2,98},{3,27},{4,100},{5,29},{6,102},{7,31},{8,104},... | collective-permute-start | bytes 1794056 | tf_op jit(solution)/shard_map/ppermute | solution.py:33
  147.9 14.2 %collective-permute-start.44 = (bf16[2336,128]{1,0:T(8,128)(2,1)}, bf16[2336,128]{1,0:T(8,128)(2,1)S(1)}, u32[]{:S(2)}, u32[]{:S(2)}) collective-permute-start(bf16[2336,128]{1,0:T(8,128)(2,1)} %get-tuple-element.209), channel_id=1, source_target_pairs={{0,64},{1,17},{2,66},{3,19},{4,68},{5,21},{6,70},{7,23},{8,72},{9,... | collective-permute-start | bytes 1794056 | tf_op jit(solution)/shard_map/ppermute | solution.py:33
  148.8 17.2 %collective-permute-start.45 = (bf16[2336,128]{1,0:T(8,128)(2,1)}, bf16[2336,128]{1,0:T(8,128)(2,1)S(1)}, u32[]{:S(2)}, u32[]{:S(2)}) collective-permute-start(bf16[2336,128]{1,0:T(8,128)(2,1)} %get-tuple-element.210), channel_id=1, source_target_pairs={{0,32},{1,9},{2,34},{3,11},{4,36},{5,13},{6,38},{7,15},{8,40},{9,1... | collective-permute-start | bytes 1794056 | tf_op jit(solution)/shard_map/ppermute | solution.py:33
  (25 other events, 230.0 us)

commit v13 on v12

--- a/solution.py
+++ b/solution.py
@@ -153,11 +153,11 @@
 
 
 def products_kernel(
-    live, tables, tiles_ref, *refs, spans, outs, contract, in_row, out_row, tailed
+    live, tables, tiles, *refs, spans, outs, contract, in_row, out_row, tailed
 ):
     n = len(spans)
-    sources, out_refs, (tiles, held, total, tails, sems) = refs[:n], refs[n:-5], refs[-5:]
-    copies = [pltpu.make_async_copy(tiles_ref, tiles, sems.at[n])]
+    sources, out_refs, (held, total, tails, sems) = refs[:n], refs[n:-4], refs[-4:]
+    copies = []
     start = 0
     for k, (ref, rows) in enumerate(zip(sources, spans)):
         copies.append(
@@ -168,7 +168,7 @@
         start += rows
     for k in range(tailed):
         tail = sources[k].at[pl.ds(spans[k], tails.shape[1])]
-        copies.append(pltpu.make_async_copy(tail, tails.at[k], sems.at[n + 1 + k]))
+        copies.append(pltpu.make_async_copy(tail, tails.at[k], sems.at[n + k]))
     for copy in copies:
         copy.start()
 
@@ -209,11 +209,11 @@
     for ref, blocks in zip(out_refs, outs):
 
         def out(k, carry, ref=ref, start=start):
-            for at in range(2):
-                ref[block(k * 2 + at)] = total[start + k * 2 + at].astype(BF16)
+            for at in range(4):
+                ref[block(k * 4 + at)] = total[start + k * 4 + at].astype(BF16)
             return carry
 
-        lax.fori_loop(0, blocks // 2, out, 0)
+        lax.fori_loop(0, blocks // 4, out, 0)
         start += blocks
 
 
@@ -234,14 +234,13 @@
         kernel,
         out_shape=[jax.ShapeDtypeStruct((n * T + e, T), BF16) for n, e in zip(outs, extra)]
         + ([jax.ShapeDtypeStruct((lines // 2, 2 * T), F32)] if tailed else []),
-        in_specs=[SMEM] * 2 + [ANY] * (1 + len(sources)),
+        in_specs=[SMEM] * 2 + [VMEM] + [ANY] * len(sources),
         out_specs=[VMEM] * (len(outs) + (tailed > 0)),
         scratch_shapes=[
-            pltpu.VMEM(tiles.shape, BF16),
             pltpu.VMEM((sum(spans), T), BF16),
             pltpu.VMEM((sum(outs), T, T), F32),
             pltpu.VMEM((max(tailed, 1), lines, T), BF16),
-            pltpu.SemaphoreType.DMA((len(spans) + 1 + tailed,)),
+            pltpu.SemaphoreType.DMA((len(spans) + tailed,)),
         ],
         compiler_params=room(need // MIB + 5),
     )(live, tables, tiles, *sources)

time: 169 us -> 168 us (level)
    ppermute x12, starting transfers between devices: 20.4 us -> 18.2 us  [along_y(): return lax.ppermute(value, 'col', pairs)]
    ppermute x10, starting transfers between devices: 9.09 us -> 10.8 us  [other_core(): return lax.ppermute(value, 'col', pairs)]
where the time goes in v13:
time: 168 us; the launch traced here: 167 us
  waiting for transfers between devices  81.8 us (49%)
  starting transfers between devices  58.7 us (35%)
  Pallas kernels  21.2 us (13%)
  between operations  2.11 us (1%)
  local copies, waits for them, and re-layouts  1.84 us (1%)
  other arithmetic  1.68 us (1%)
    ppermute x18, waiting for transfers between devices, along_xz(): return lax.ppermute(value, ('row', 'col'), pairs)  54.9 us
    ppermute x18, starting transfers between devices, along_xz(): return lax.ppermute(value, ('row', 'col'), pairs)  29.6 us
    ppermute x12, waiting for transfers between devices, along_y(): return lax.ppermute(value, 'col', pairs)  22.2 us
    ppermute x12, starting transfers between devices, along_y(): return lax.ppermute(value, 'col', pairs)  18.2 us
    ppermute x10, starting transfers between devices, other_core(): return lax.ppermute(value, 'col', pairs)  10.8 us
    pallas_call x2, Pallas kernels, products(): pl.pallas_call(kernel, out_shape=[jax.ShapeDtypeStruct((n * T + e, T), BF...  9.64 us
    ppermute x10, waiting for transfers between devices, other_core(): return lax.ppermute(value, 'col', pairs)  4.64 us
    pallas_call x2, Pallas kernels, dense(): pl.pallas_call(functools.partial(dense_kernel, step=step), grid=(steps,),...  3.73 us
  transfers between devices with their start and end apart: 40, of which 22 were waited for; matrix products, arithmetic and copies ran while one was open for 1% of the time, Pallas kernels for 2%

profile of v13, /device:TPU:0, one launch (start us, length us, event | category | flops | bytes accessed | tf_op | source)
XLA Modules:
  0.0 167.3 jit_solution(5359288755222807414)
XLA Ops:
  2.3 2.7 %collective-permute-start.7 = (bf16[2048,128]{1,0:T(8,128)(2,1)}, bf16[2048,128]{1,0:T(8,128)(2,1)S(1)}, u32[]{:S(2)}, u32[]{:S(2)}) collective-permute-start(bf16[2048,128]{1,0:T(8,128)(2,1)} %refs_0_.3), channel_id=1, source_target_pairs={{0,64},{1,17},{2,66},{3,19},{4,68},{5,21},{6,70},{7,23},{8,72},{9,... | collective-permute-start | bytes 1572872 | tf_op jit(solution)/shard_map/ppermute | solution.py:33
  10.7 3.6 %collective-permute-start.10 = (bf16[16,128]{1,0:T(8,128)(2,1)S(1)}, bf16[16,128]{1,0:T(8,128)(2,1)S(1)}, u32[]{:S(2)}, u32[]{:S(2)}) collective-permute-start(bf16[16,128]{1,0:T(8,128)(2,1)S(1)} %get-tuple-element.181.refs_4_), channel_id=1, source_target_pairs={{0,16},{1,65},{2,18},{3,67},{4,20},{5,69},{6,22},{7,71},{8,24},{9,... | collective-permute-start | bytes 12296 | tf_op jit(solution)/shard_map/ppermute | solution.py:33
  20.6 4.0 %collective-permute-start.15 = (bf16[3072,128]{1,0:T(8,128)(2,1)S(1)}, bf16[3072,128]{1,0:T(8,128)(2,1)S(1)}, u32[]{:S(2)}, u32[]{:S(2)}) collective-permute-start(bf16[3072,128]{1,0:T(8,128)(2,1)S(1)} %get-tuple-element.184), channel_id=1, source_target_pairs={{0,24},{1,97},{2,26},{3,99},{4,28},{5,101},{6,30},{7,103},{8,0},{9... | collective-permute-start | bytes 2359304 | tf_op jit(solution)/shard_map/ppermute | solution.py:33
  29.9 5.7 %collective-permute-done.14 = f32[8,128]{1,0:T(8,128)S(1)} collective-permute-done((f32[8,128]{1,0:T(8,128)S(1)}, f32[8,128]{1,0:T(8,128)S(1)}, u32[]{:S(2)}, u32[]{:S(2)}) %collective-permute-start.14) | collective-permute-done | bytes 4128 | tf_op jit(solution)/shard_map/ppermute | solution.py:33
  35.7 3.7 %collective-permute-done.12 = f32[8,128]{1,0:T(8,128)S(1)} collective-permute-done((f32[8,128]{1,0:T(8,128)S(1)}, f32[8,128]{1,0:T(8,128)S(1)}, u32[]{:S(2)}, u32[]{:S(2)}) %collective-permute-start.12) | collective-permute-done | bytes 4128 | tf_op jit(solution)/shard_map/ppermute | solution.py:33
  42.5 3.6 %collective-permute-done.17.refs_6_ = bf16[3072,128]{1,0:T(8,128)(2,1)S(1)} collective-permute-done((bf16[3072,128]{1,0:T(8,128)(2,1)S(1)}, bf16[3072,128]{1,0:T(8,128)(2,1)S(1)}, u32[]{:S(2)}, u32[]{:S(2)}) %collective-permute-start.17) | collective-permute-done | bytes 786464 | tf_op jit(solution)/shard_map/ppermute | solution.py:33
  46.2 5.3 %shard_map.113 = (bf16[4096,128]{1,0:T(8,128)(2,1)}, bf16[4096,128]{1,0:T(8,128)(2,1)}, bf16[4096,128]{1,0:T(8,128)(2,1)}, bf16[4096,128]{1,0:T(8,128)(2,1)}) custom-call(s32[1]{0:T(128)} %bitcast.10.live, s32[8,64]{1,0:T(8,128)S(1)} %get-tuple-element.183.tables, bf16[64,128,128]{2,1,0:T(8,128)(2,1)S(1)} %bitcast.16, bf16[2048,128]{1,0:T(8,128)(2,1)} %refs_0_.3, ...), custom_call_target="tpu_custom_call" | custom-call | tf_op jit(solution)/shard_map/pallas_call | solution.py:233
  52.2 2.4 %collective-permute-done.22.refs_1_ = bf16[4096,128]{1,0:T(8,128)(2,1)S(1)} collective-permute-done((bf16[4096,128]{1,0:T(8,128)(2,1)}, bf16[4096,128]{1,0:T(8,128)(2,1)S(1)}, u32[]{:S(2)}, u32[]{:S(2)}) %collective-permute-start.22) | collective-permute-done | bytes 1048608 | tf_op jit(solution)/shard_map/ppermute | solution.py:54
  63.7 2.4 %collective-permute-done.25.refs_4_ = bf16[1024,128]{1,0:T(8,128)(2,1)S(1)} collective-permute-done((bf16[1024,128]{1,0:T(8,128)(2,1)S(1)}, bf16[1024,128]{1,0:T(8,128)(2,1)S(1)}, u32[]{:S(2)}, u32[]{:S(2)}) %collective-permute-start.25) | collective-permute-done | bytes 262176 | tf_op jit(solution)/shard_map/ppermute | solution.py:49
  66.9 5.1 %collective-permute-done.24.refs_3_ = bf16[1024,128]{1,0:T(8,128)(2,1)S(1)} collective-permute-done((bf16[1024,128]{1,0:T(8,128)(2,1)S(1)}, bf16[1024,128]{1,0:T(8,128)(2,1)S(1)}, u32[]{:S(2)}, u32[]{:S(2)}) %collective-permute-start.24) | collective-permute-done | bytes 262176 | tf_op jit(solution)/shard_map/ppermute | solution.py:49
  76.4 3.2 %collective-permute-done.21.refs_4_ = bf16[1024,128]{1,0:T(8,128)(2,1)S(1)} collective-permute-done((bf16[1024,128]{1,0:T(8,128)(2,1)S(1)}, bf16[1024,128]{1,0:T(8,128)(2,1)S(1)}, u32[]{:S(2)}, u32[]{:S(2)}) %collective-permute-start.21) | collective-permute-done | bytes 262176 | tf_op jit(solution)/shard_map/ppermute | solution.py:49
  79.6 5.0 %collective-permute-start.36 = (bf16[1024,128]{1,0:T(8,128)(2,1)S(1)}, bf16[1024,128]{1,0:T(8,128)(2,1)S(1)}, u32[]{:S(2)}, u32[]{:S(2)}) collective-permute-start(bf16[1024,128]{1,0:T(8,128)(2,1)S(1)} %get-tuple-element.193.refs_12_), channel_id=1, source_target_pairs={{0,4},{1,5},{2,6},{3,7},{4,0},{5,1},{6,2},{7,3},{8,12},{9,13},{10,... | collective-permute-start | bytes 786440 | tf_op jit(solution)/shard_map/ppermute | solution.py:49
  88.8 2.4 %collective-permute-start.28 = (bf16[1312,128]{1,0:T(8,128)(2,1)S(1)}, bf16[1312,128]{1,0:T(8,128)(2,1)S(1)}, u32[]{:S(2)}, u32[]{:S(2)}) collective-permute-start(bf16[1312,128]{1,0:T(8,128)(2,1)S(1)} %get-tuple-element.197.refs_4_), channel_id=1, source_target_pairs={{0,6},{1,3},{2,0},{3,5},{4,2},{5,7},{6,4},{7,1},{8,14},{9,11},{10,... | collective-permute-start | bytes 1007624 | tf_op jit(solution)/shard_map/ppermute | solution.py:49
  91.2 4.8 %collective-permute-done.36.refs_14_ = bf16[1024,128]{1,0:T(8,128)(2,1)S(1)} collective-permute-done((bf16[1024,128]{1,0:T(8,128)(2,1)S(1)}, bf16[1024,128]{1,0:T(8,128)(2,1)S(1)}, u32[]{:S(2)}, u32[]{:S(2)}) %collective-permute-start.36) | collective-permute-done | bytes 262176 | tf_op jit(solution)/shard_map/ppermute | solution.py:49
  97.7 3.4 %collective-permute-done.32.refs_7_ = bf16[1312,128]{1,0:T(8,128)(2,1)S(1)} collective-permute-done((bf16[1312,128]{1,0:T(8,128)(2,1)S(1)}, bf16[1312,128]{1,0:T(8,128)(2,1)S(1)}, u32[]{:S(2)}, u32[]{:S(2)}) %collective-permute-start.32) | collective-permute-done | bytes 335904 | tf_op jit(solution)/shard_map/ppermute | solution.py:49
  101.1 7.9 %collective-permute-start.33 = (bf16[1312,128]{1,0:T(8,128)(2,1)S(1)}, bf16[1312,128]{1,0:T(8,128)(2,1)S(1)}, u32[]{:S(2)}, u32[]{:S(2)}) collective-permute-start(bf16[1312,128]{1,0:T(8,128)(2,1)S(1)} %collective-permute-done.32.refs_7_), channel_id=1, source_target_pairs={{0,1},{1,0},{2,3},{3,2},{4,5},{5,4},{6,7},{7,6},{8,9},{9,8},{10,11... | collective-permute-start | bytes 1007624 | tf_op jit(solution)/shard_map/ppermute | solution.py:54
  113.0 4.3 %shard_map.116 = (bf16[8192,128]{1,0:T(8,128)(2,1)S(1)}, bf16[3360,128]{1,0:T(8,128)(2,1)S(1)}, bf16[3360,128]{1,0:T(8,128)(2,1)S(1)}, bf16[3360,128]{1,0:T(8,128)(2,1)S(1)}, f32[144,256]{1,0:T(8,128)S(1)}) custom-call(s32[1]{0:T(128)} %bitcast.11.live, s32[8,64]{1,0:T(8,128)S(1)} %get-tuple-element.183.tables, bf16[64,128,128]{2,1,0:T(8,128)(2,1)S(1)} %bitcast.18, ...), custom_call_target="tpu_custom_call" | custom-call | tf_op jit(solution)/shard_map/pallas_call | solution.py:233
  119.4 10.8 %collective-permute-done.40.refs_0_ = bf16[3360,128]{1,0:T(8,128)(2,1)S(1)} collective-permute-done((bf16[3360,128]{1,0:T(8,128)(2,1)S(1)}, bf16[3360,128]{1,0:T(8,128)(2,1)S(1)}, u32[]{:S(2)}, u32[]{:S(2)}) %collective-permute-start.40) | collective-permute-done | bytes 860192 | tf_op jit(solution)/shard_map/ppermute | solution.py:33
  131.9 9.1 %collective-permute-done.42.refs_2_ = bf16[3360,128]{1,0:T(8,128)(2,1)S(1)} collective-permute-done((bf16[3360,128]{1,0:T(8,128)(2,1)S(1)}, bf16[3360,128]{1,0:T(8,128)(2,1)S(1)}, u32[]{:S(2)}, u32[]{:S(2)}) %collective-permute-start.42) | collective-permute-done | bytes 860192 | tf_op jit(solution)/shard_map/ppermute | solution.py:33
  141.0 2.9 %shard_map.117 = (f32[2048,128]{1,0:T(8,128)}, bf16[2336,128]{1,0:T(8,128)(2,1)}, bf16[2336,128]{1,0:T(8,128)(2,1)}, bf16[2336,128]{1,0:T(8,128)(2,1)}, f32[144,256]{1,0:T(8,128)S(1)}) custom-call(s32[96]{0:T(128)S(1)} %get-tuple-element.195.lists, s32[3]{0:T(128)S(1)} %get-tuple-element.196.counts, bf16[8192,128]{1,0:T(8,128)(2,1)S(1)} %get-tuple-element.198.own, ...), custom_call_target="tpu_custom_call" | custom-call | tf_op jit(solution)/shard_map/pallas_call | solution.py:345
  143.9 2.8 %collective-permute-start.43 = (bf16[2336,128]{1,0:T(8,128)(2,1)}, bf16[2336,128]{1,0:T(8,128)(2,1)S(1)}, u32[]{:S(2)}, u32[]{:S(2)}) collective-permute-start(bf16[2336,128]{1,0:T(8,128)(2,1)} %get-tuple-element.208), channel_id=1, source_target_pairs={{0,96},{1,25},{2,98},{3,27},{4,100},{5,29},{6,102},{7,31},{8,104},... | collective-permute-start | bytes 1794056 | tf_op jit(solution)/shard_map/ppermute | solution.py:33
  149.0 12.0 %collective-permute-done.43.refs_1_ = bf16[2336,128]{1,0:T(8,128)(2,1)S(1)} collective-permute-done((bf16[2336,128]{1,0:T(8,128)(2,1)}, bf16[2336,128]{1,0:T(8,128)(2,1)S(1)}, u32[]{:S(2)}, u32[]{:S(2)}) %collective-permute-start.43) | collective-permute-done | bytes 598048 | tf_op jit(solution)/shard_map/ppermute | solution.py:33
  161.0 3.8 %collective-permute-done.45.refs_3_ = bf16[2336,128]{1,0:T(8,128)(2,1)S(1)} collective-permute-done((bf16[2336,128]{1,0:T(8,128)(2,1)}, bf16[2336,128]{1,0:T(8,128)(2,1)S(1)}, u32[]{:S(2)}, u32[]{:S(2)}) %collective-permute-start.45) | collective-permute-done | bytes 598048 | tf_op jit(solution)/shard_map/ppermute | solution.py:33
  164.8 2.5 %shard_map.118 = (f32[2048,128]{1,0:T(8,128)}, f32[128,256]{1,0:T(8,128)}, f32[1,256]{1,0:T(1,128)}) custom-call(f32[2048,128]{1,0:T(8,128)} %get-tuple-element.207.refs_0_, bf16[2336,128]{1,0:T(8,128)(2,1)S(1)} %collective-permute-done.43.refs_1_, bf16[2336,128]{1,0:T(8,128)(2,1)S(1)} %collective-permute-done.44.refs_2_, ...), custom_call_target="tpu_custom_call" | custom-call | tf_op jit(solution)/shard_map/pallas_call | solution.py:374
  (88 shorter events, 51.7 us)
Async XLA Ops:
  0.6 17.8 %collective-permute-start.8 = (bf16[2048,128]{1,0:T(8,128)(2,1)}, bf16[2048,128]{1,0:T(8,128)(2,1)S(1)}, u32[]{:S(2)}, u32[]{:S(2)}) collective-permute-start(bf16[2048,128]{1,0:T(8,128)(2,1)} %refs_0_.3), channel_id=1, source_target_pairs={{0,32},{1,9},{2,34},{3,11},{4,36},{5,13},{6,38},{7,15},{8,40},{9,1... | collective-permute-start | bytes 1572872 | tf_op jit(solution)/shard_map/ppermute | solution.py:33
  2.3 16.2 %collective-permute-start.7 = (bf16[2048,128]{1,0:T(8,128)(2,1)}, bf16[2048,128]{1,0:T(8,128)(2,1)S(1)}, u32[]{:S(2)}, u32[]{:S(2)}) collective-permute-start(bf16[2048,128]{1,0:T(8,128)(2,1)} %refs_0_.3), channel_id=1, source_target_pairs={{0,64},{1,17},{2,66},{3,19},{4,68},{5,21},{6,70},{7,23},{8,72},{9,... | collective-permute-start | bytes 1572872 | tf_op jit(solution)/shard_map/ppermute | solution.py:33
  5.0 13.5 %collective-permute-start.6 = (bf16[2048,128]{1,0:T(8,128)(2,1)}, bf16[2048,128]{1,0:T(8,128)(2,1)}, u32[]{:S(2)}, u32[]{:S(2)}) collective-permute-start(bf16[2048,128]{1,0:T(8,128)(2,1)} %refs_0_.3), channel_id=1, source_target_pairs={{0,96},{1,25},{2,98},{3,27},{4,100},{5,29},{6,102},{7,31},{8,104},... | collective-permute-start | bytes 1572872 | tf_op jit(solution)/shard_map/ppermute | solution.py:33
  20.6 22.0 %collective-permute-start.15 = (bf16[3072,128]{1,0:T(8,128)(2,1)S(1)}, bf16[3072,128]{1,0:T(8,128)(2,1)S(1)}, u32[]{:S(2)}, u32[]{:S(2)}) collective-permute-start(bf16[3072,128]{1,0:T(8,128)(2,1)S(1)} %get-tuple-element.184), channel_id=1, source_target_pairs={{0,24},{1,97},{2,26},{3,99},{4,28},{5,101},{6,30},{7,103},{8,0},{9... | collective-permute-start | bytes 2359304 | tf_op jit(solution)/shard_map/ppermute | solution.py:33
  24.5 18.0 %collective-permute-start.16 = (bf16[3072,128]{1,0:T(8,128)(2,1)S(1)}, bf16[3072,128]{1,0:T(8,128)(2,1)S(1)}, u32[]{:S(2)}, u32[]{:S(2)}) collective-permute-start(bf16[3072,128]{1,0:T(8,128)(2,1)S(1)} %get-tuple-element.185), channel_id=1, source_target_pairs={{0,16},{1,65},{2,18},{3,67},{4,20},{5,69},{6,22},{7,71},{8,24},{9,... | collective-permute-start | bytes 2359304 | tf_op jit(solution)/shard_map/ppermute | solution.py:33
  24.5 21.7 %collective-permute-start.17 = (bf16[3072,128]{1,0:T(8,128)(2,1)S(1)}, bf16[3072,128]{1,0:T(8,128)(2,1)S(1)}, u32[]{:S(2)}, u32[]{:S(2)}) collective-permute-start(bf16[3072,128]{1,0:T(8,128)(2,1)S(1)} %get-tuple-element.186), channel_id=1, source_target_pairs={{0,8},{1,33},{2,10},{3,35},{4,12},{5,37},{6,14},{7,39},{8,16},{9,4... | collective-permute-start | bytes 2359304 | tf_op jit(solution)/shard_map/ppermute | solution.py:33
  57.8 14.1 %collective-permute-start.24 = (bf16[1024,128]{1,0:T(8,128)(2,1)S(1)}, bf16[1024,128]{1,0:T(8,128)(2,1)S(1)}, u32[]{:S(2)}, u32[]{:S(2)}) collective-permute-start(bf16[1024,128]{1,0:T(8,128)(2,1)S(1)} %get-tuple-element.221), channel_id=1, source_target_pairs={{0,4},{1,5},{2,6},{3,7},{4,0},{5,1},{6,2},{7,3},{8,12},{9,13},{10,... | collective-permute-start | bytes 786440 | tf_op jit(solution)/shard_map/ppermute | solution.py:49
  60.1 13.0 %collective-permute-start.23 = (bf16[1024,128]{1,0:T(8,128)(2,1)S(1)}, bf16[1024,128]{1,0:T(8,128)(2,1)S(1)}, u32[]{:S(2)}, u32[]{:S(2)}) collective-permute-start(bf16[1024,128]{1,0:T(8,128)(2,1)S(1)} %get-tuple-element.222), channel_id=1, source_target_pairs={{0,6},{1,3},{2,0},{3,5},{4,2},{5,7},{6,4},{7,1},{8,14},{9,11},{10,... | collective-permute-start | bytes 786440 | tf_op jit(solution)/shard_map/ppermute | solution.py:49
  62.0 17.6 %collective-permute-start.21 = (bf16[1024,128]{1,0:T(8,128)(2,1)S(1)}, bf16[1024,128]{1,0:T(8,128)(2,1)S(1)}, u32[]{:S(2)}, u32[]{:S(2)}) collective-permute-start(bf16[1024,128]{1,0:T(8,128)(2,1)S(1)} %get-tuple-element.223), channel_id=1, source_target_pairs={{0,2},{1,7},{2,4},{3,1},{4,6},{5,3},{6,0},{7,5},{8,10},{9,15},{10,... | collective-permute-start | bytes 786440 | tf_op jit(solution)/shard_map/ppermute | solution.py:49
  62.4 22.2 %collective-permute-start.20 = (bf16[1024,128]{1,0:T(8,128)(2,1)S(1)}, bf16[1024,128]{1,0:T(8,128)(2,1)S(1)}, u32[]{:S(2)}, u32[]{:S(2)}) collective-permute-start(bf16[1024,128]{1,0:T(8,128)(2,1)S(1)} %get-tuple-element.224), channel_id=1, source_target_pairs={{0,4},{1,5},{2,6},{3,7},{4,0},{5,1},{6,2},{7,3},{8,12},{9,13},{10,... | collective-permute-start | bytes 786440 | tf_op jit(solution)/shard_map/ppermute | solution.py:49
  66.1 18.5 %collective-permute-start.19 = (bf16[1024,128]{1,0:T(8,128)(2,1)S(1)}, bf16[1024,128]{1,0:T(8,128)(2,1)S(1)}, u32[]{:S(2)}, u32[]{:S(2)}) collective-permute-start(bf16[1024,128]{1,0:T(8,128)(2,1)S(1)} %get-tuple-element.225), channel_id=1, source_target_pairs={{0,6},{1,3},{2,0},{3,5},{4,2},{5,7},{6,4},{7,1},{8,14},{9,11},{10,... | collective-permute-start | bytes 786440 | tf_op jit(solution)/shard_map/ppermute | solution.py:49
  76.1 12.7 %collective-permute-start.38 = (bf16[1024,128]{1,0:T(8,128)(2,1)S(1)}, bf16[1024,128]{1,0:T(8,128)(2,1)S(1)}, u32[]{:S(2)}, u32[]{:S(2)}) collective-permute-start(bf16[1024,128]{1,0:T(8,128)(2,1)S(1)} %get-tuple-element.193.refs_12_), channel_id=1, source_target_pairs={{0,2},{1,7},{2,4},{3,1},{4,6},{5,3},{6,0},{7,5},{8,10},{9,15},{10,... | collective-permute-start | bytes 786440 | tf_op jit(solution)/shard_map/ppermute | solution.py:49
  79.6 16.4 %collective-permute-start.36 = (bf16[1024,128]{1,0:T(8,128)(2,1)S(1)}, bf16[1024,128]{1,0:T(8,128)(2,1)S(1)}, u32[]{:S(2)}, u32[]{:S(2)}) collective-permute-start(bf16[1024,128]{1,0:T(8,128)(2,1)S(1)} %get-tuple-element.193.refs_12_), channel_id=1, source_target_pairs={{0,4},{1,5},{2,6},{3,7},{4,0},{5,1},{6,2},{7,3},{8,12},{9,13},{10,... | collective-permute-start | bytes 786440 | tf_op jit(solution)/shard_map/ppermute | solution.py:49
  86.6 14.6 %collective-permute-start.32 = (bf16[1312,128]{1,0:T(8,128)(2,1)S(1)}, bf16[1312,128]{1,0:T(8,128)(2,1)S(1)}, u32[]{:S(2)}, u32[]{:S(2)}) collective-permute-start(bf16[1312,128]{1,0:T(8,128)(2,1)S(1)} %get-tuple-element.197.refs_4_), channel_id=1, source_target_pairs={{0,2},{1,7},{2,4},{3,1},{4,6},{5,3},{6,0},{7,5},{8,10},{9,15},{10,... | collective-permute-start | bytes 1007624 | tf_op jit(solution)/shard_map/ppermute | solution.py:49
  88.6 21.9 %collective-permute-start.30 = (bf16[1312,128]{1,0:T(8,128)(2,1)S(1)}, bf16[1312,128]{1,0:T(8,128)(2,1)S(1)}, u32[]{:S(2)}, u32[]{:S(2)}) collective-permute-start(bf16[1312,128]{1,0:T(8,128)(2,1)S(1)} %get-tuple-element.197.refs_4_), channel_id=1, source_target_pairs={{0,4},{1,5},{2,6},{3,7},{4,0},{5,1},{6,2},{7,3},{8,12},{9,13},{10,... | collective-permute-start | bytes 1007624 | tf_op jit(solution)/shard_map/ppermute | solution.py:49
  88.8 21.7 %collective-permute-start.28 = (bf16[1312,128]{1,0:T(8,128)(2,1)S(1)}, bf16[1312,128]{1,0:T(8,128)(2,1)S(1)}, u32[]{:S(2)}, u32[]{:S(2)}) collective-permute-start(bf16[1312,128]{1,0:T(8,128)(2,1)S(1)} %get-tuple-element.197.refs_4_), channel_id=1, source_target_pairs={{0,6},{1,3},{2,0},{3,5},{4,2},{5,7},{6,4},{7,1},{8,14},{9,11},{10,... | collective-permute-start | bytes 1007624 | tf_op jit(solution)/shard_map/ppermute | solution.py:49
  96.8 14.2 %collective-permute-start.37 = (bf16[1024,128]{1,0:T(8,128)(2,1)S(1)}, bf16[1024,128]{1,0:T(8,128)(2,1)S(1)}, u32[]{:S(2)}, u32[]{:S(2)}) collective-permute-start(bf16[1024,128]{1,0:T(8,128)(2,1)S(1)} %collective-permute-done.36.refs_14_), channel_id=1, source_target_pairs={{0,1},{1,0},{2,3},{3,2},{4,5},{5,4},{6,7},{7,6},{8,9},{9,8},{10,11... | collective-permute-start | bytes 786440 | tf_op jit(solution)/shard_map/ppermute | solution.py:54
  97.6 15.4 %collective-permute-start.27 = (bf16[1312,128]{1,0:T(8,128)(2,1)S(1)}, bf16[1312,128]{1,0:T(8,128)(2,1)S(1)}, u32[]{:S(2)}, u32[]{:S(2)}) collective-permute-start(bf16[1312,128]{1,0:T(8,128)(2,1)S(1)} %get-tuple-element.197.refs_4_), channel_id=1, source_target_pairs={{0,1},{1,0},{2,3},{3,2},{4,5},{5,4},{6,7},{7,6},{8,9},{9,8},{10,11... | collective-permute-start | bytes 1007624 | tf_op jit(solution)/shard_map/ppermute | solution.py:54
  117.3 12.8 %collective-permute-start.40 = (bf16[3360,128]{1,0:T(8,128)(2,1)S(1)}, bf16[3360,128]{1,0:T(8,128)(2,1)S(1)}, u32[]{:S(2)}, u32[]{:S(2)}) collective-permute-start(bf16[3360,128]{1,0:T(8,128)(2,1)S(1)} %get-tuple-element.200), channel_id=1, source_target_pairs={{0,24},{1,97},{2,26},{3,99},{4,28},{5,101},{6,30},{7,103},{8,0},{9... | collective-permute-start | bytes 2580488 | tf_op jit(solution)/shard_map/ppermute | solution.py:33
  117.4 14.5 %collective-permute-start.41 = (bf16[3360,128]{1,0:T(8,128)(2,1)S(1)}, bf16[3360,128]{1,0:T(8,128)(2,1)S(1)}, u32[]{:S(2)}, u32[]{:S(2)}) collective-permute-start(bf16[3360,128]{1,0:T(8,128)(2,1)S(1)} %get-tuple-element.201), channel_id=1, source_target_pairs={{0,16},{1,65},{2,18},{3,67},{4,20},{5,69},{6,22},{7,71},{8,24},{9,... | collective-permute-start | bytes 2580488 | tf_op jit(solution)/shard_map/ppermute | solution.py:33
  118.2 22.8 %collective-permute-start.42 = (bf16[3360,128]{1,0:T(8,128)(2,1)S(1)}, bf16[3360,128]{1,0:T(8,128)(2,1)S(1)}, u32[]{:S(2)}, u32[]{:S(2)}) collective-permute-start(bf16[3360,128]{1,0:T(8,128)(2,1)S(1)} %get-tuple-element.202), channel_id=1, source_target_pairs={{0,8},{1,33},{2,10},{3,35},{4,12},{5,37},{6,14},{7,39},{8,16},{9,4... | collective-permute-start | bytes 2580488 | tf_op jit(solution)/shard_map/ppermute | solution.py:33
  143.9 17.1 %collective-permute-start.43 = (bf16[2336,128]{1,0:T(8,128)(2,1)}, bf16[2336,128]{1,0:T(8,128)(2,1)S(1)}, u32[]{:S(2)}, u32[]{:S(2)}) collective-permute-start(bf16[2336,128]{1,0:T(8,128)(2,1)} %get-tuple-element.208), channel_id=1, source_target_pairs={{0,96},{1,25},{2,98},{3,27},{4,100},{5,29},{6,102},{7,31},{8,104},... | collective-permute-start | bytes 1794056 | tf_op jit(solution)/shard_map/ppermute | solution.py:33
  146.7 14.2 %collective-permute-start.44 = (bf16[2336,128]{1,0:T(8,128)(2,1)}, bf16[2336,128]{1,0:T(8,128)(2,1)S(1)}, u32[]{:S(2)}, u32[]{:S(2)}) collective-permute-start(bf16[2336,128]{1,0:T(8,128)(2,1)} %get-tuple-element.209), channel_id=1, source_target_pairs={{0,64},{1,17},{2,66},{3,19},{4,68},{5,21},{6,70},{7,23},{8,72},{9,... | collective-permute-start | bytes 1794056 | tf_op jit(solution)/shard_map/ppermute | solution.py:33
  149.0 15.9 %collective-permute-start.45 = (bf16[2336,128]{1,0:T(8,128)(2,1)}, bf16[2336,128]{1,0:T(8,128)(2,1)S(1)}, u32[]{:S(2)}, u32[]{:S(2)}) collective-permute-start(bf16[2336,128]{1,0:T(8,128)(2,1)} %get-tuple-element.210), channel_id=1, source_target_pairs={{0,32},{1,9},{2,34},{3,11},{4,36},{5,13},{6,38},{7,15},{8,40},{9,1... | collective-permute-start | bytes 1794056 | tf_op jit(solution)/shard_map/ppermute | solution.py:33
  (25 other events, 231.5 us)

commit v14 on v13

--- a/solution.py
+++ b/solution.py
@@ -12,7 +12,7 @@
 T = 128
 F32, BF16, I32 = jnp.float32, jnp.bfloat16, jnp.int32
 MIB = 1024 * 1024
-GROUP = 16
+GROUP = 32
 META = 16
 CAP = 24
 LANES = 32

time: 168 us -> 168 us (level)
  waiting for transfers between devices: 81.8 us -> 83.6 us
where the time goes in v14:
time: 168 us
  waiting for transfers between devices  83.6 us (50%)
  starting transfers between devices  57.1 us (34%)
  Pallas kernels  21.4 us (13%)
  between operations  2.11 us (1%)
  local copies, waits for them, and re-layouts  1.84 us (1%)
  other arithmetic  1.68 us (1%)
    ppermute x18, waiting for transfers between devices, along_xz(): return lax.ppermute(value, ('row', 'col'), pairs)  55.4 us
    ppermute x18, starting transfers between devices, along_xz(): return lax.ppermute(value, ('row', 'col'), pairs)  29.3 us
    ppermute x12, waiting for transfers between devices, along_y(): return lax.ppermute(value, 'col', pairs)  23.5 us
    ppermute x12, starting transfers between devices, along_y(): return lax.ppermute(value, 'col', pairs)  17.1 us
    ppermute x10, starting transfers between devices, other_core(): return lax.ppermute(value, 'col', pairs)  10.7 us
    pallas_call x2, Pallas kernels, products(): pl.pallas_call(kernel, out_shape=[jax.ShapeDtypeStruct((n * T + e, T), BF...  9.66 us
    ppermute x10, waiting for transfers between devices, other_core(): return lax.ppermute(value, 'col', pairs)  4.64 us
    pallas_call x2, Pallas kernels, dense(): pl.pallas_call(functools.partial(dense_kernel, step=step), grid=(steps,),...  3.73 us
  transfers between devices with their start and end apart: 40, of which 22 were waited for; matrix products, arithmetic and copies ran while one was open for 1% of the time, Pallas kernels for 2%

profile of v14, /device:TPU:0, one launch (start us, length us, event | category | flops | bytes accessed | tf_op | source)
XLA Modules:
  0.0 167.7 jit_solution(4618939034058823058)
XLA Ops:
  2.3 2.7 %collective-permute-start.7 = (bf16[2048,128]{1,0:T(8,128)(2,1)}, bf16[2048,128]{1,0:T(8,128)(2,1)S(1)}, u32[]{:S(2)}, u32[]{:S(2)}) collective-permute-start(bf16[2048,128]{1,0:T(8,128)(2,1)} %refs_0_.3), channel_id=1, source_target_pairs={{0,64},{1,17},{2,66},{3,19},{4,68},{5,21},{6,70},{7,23},{8,72},{9,... | collective-permute-start | bytes 1572872 | tf_op jit(solution)/shard_map/ppermute | solution.py:33
  10.7 3.6 %collective-permute-start.10 = (bf16[16,128]{1,0:T(8,128)(2,1)S(1)}, bf16[16,128]{1,0:T(8,128)(2,1)S(1)}, u32[]{:S(2)}, u32[]{:S(2)}) collective-permute-start(bf16[16,128]{1,0:T(8,128)(2,1)S(1)} %get-tuple-element.181.refs_4_), channel_id=1, source_target_pairs={{0,16},{1,65},{2,18},{3,67},{4,20},{5,69},{6,22},{7,71},{8,24},{9,... | collective-permute-start | bytes 12296 | tf_op jit(solution)/shard_map/ppermute | solution.py:33
  20.7 3.7 %collective-permute-start.15 = (bf16[3072,128]{1,0:T(8,128)(2,1)S(1)}, bf16[3072,128]{1,0:T(8,128)(2,1)S(1)}, u32[]{:S(2)}, u32[]{:S(2)}) collective-permute-start(bf16[3072,128]{1,0:T(8,128)(2,1)S(1)} %get-tuple-element.184), channel_id=1, source_target_pairs={{0,24},{1,97},{2,26},{3,99},{4,28},{5,101},{6,30},{7,103},{8,0},{9... | collective-permute-start | bytes 2359304 | tf_op jit(solution)/shard_map/ppermute | solution.py:33
  30.0 5.4 %collective-permute-done.14 = f32[8,128]{1,0:T(8,128)S(1)} collective-permute-done((f32[8,128]{1,0:T(8,128)S(1)}, f32[8,128]{1,0:T(8,128)S(1)}, u32[]{:S(2)}, u32[]{:S(2)}) %collective-permute-start.14) | collective-permute-done | bytes 4128 | tf_op jit(solution)/shard_map/ppermute | solution.py:33
  35.4 3.7 %collective-permute-done.12 = f32[8,128]{1,0:T(8,128)S(1)} collective-permute-done((f32[8,128]{1,0:T(8,128)S(1)}, f32[8,128]{1,0:T(8,128)S(1)}, u32[]{:S(2)}, u32[]{:S(2)}) %collective-permute-start.12) | collective-permute-done | bytes 4128 | tf_op jit(solution)/shard_map/ppermute | solution.py:33
  42.4 3.7 %collective-permute-done.17.refs_6_ = bf16[3072,128]{1,0:T(8,128)(2,1)S(1)} collective-permute-done((bf16[3072,128]{1,0:T(8,128)(2,1)S(1)}, bf16[3072,128]{1,0:T(8,128)(2,1)S(1)}, u32[]{:S(2)}, u32[]{:S(2)}) %collective-permute-start.17) | collective-permute-done | bytes 786464 | tf_op jit(solution)/shard_map/ppermute | solution.py:33
  46.1 5.3 %shard_map.113 = (bf16[4096,128]{1,0:T(8,128)(2,1)}, bf16[4096,128]{1,0:T(8,128)(2,1)}, bf16[4096,128]{1,0:T(8,128)(2,1)}, bf16[4096,128]{1,0:T(8,128)(2,1)}) custom-call(s32[1]{0:T(128)} %bitcast.10.live, s32[8,64]{1,0:T(8,128)S(1)} %get-tuple-element.183.tables, bf16[64,128,128]{2,1,0:T(8,128)(2,1)S(1)} %bitcast.16, bf16[2048,128]{1,0:T(8,128)(2,1)} %refs_0_.3, ...), custom_call_target="tpu_custom_call" | custom-call | tf_op jit(solution)/shard_map/pallas_call | solution.py:233
  57.0 2.9 %collective-permute-start.24 = (bf16[1024,128]{1,0:T(8,128)(2,1)S(1)}, bf16[1024,128]{1,0:T(8,128)(2,1)S(1)}, u32[]{:S(2)}, u32[]{:S(2)}) collective-permute-start(bf16[1024,128]{1,0:T(8,128)(2,1)S(1)} %get-tuple-element.221), channel_id=1, source_target_pairs={{0,4},{1,5},{2,6},{3,7},{4,0},{5,1},{6,2},{7,3},{8,12},{9,13},{10,... | collective-permute-start | bytes 786440 | tf_op jit(solution)/shard_map/ppermute | solution.py:49
  63.0 5.6 %collective-permute-done.25.refs_4_ = bf16[1024,128]{1,0:T(8,128)(2,1)S(1)} collective-permute-done((bf16[1024,128]{1,0:T(8,128)(2,1)S(1)}, bf16[1024,128]{1,0:T(8,128)(2,1)S(1)}, u32[]{:S(2)}, u32[]{:S(2)}) %collective-permute-start.25) | collective-permute-done | bytes 262176 | tf_op jit(solution)/shard_map/ppermute | solution.py:49
  68.6 3.1 %collective-permute-done.24.refs_3_ = bf16[1024,128]{1,0:T(8,128)(2,1)S(1)} collective-permute-done((bf16[1024,128]{1,0:T(8,128)(2,1)S(1)}, bf16[1024,128]{1,0:T(8,128)(2,1)S(1)}, u32[]{:S(2)}, u32[]{:S(2)}) %collective-permute-start.24) | collective-permute-done | bytes 262176 | tf_op jit(solution)/shard_map/ppermute | solution.py:49
  76.6 3.1 %collective-permute-done.21.refs_4_ = bf16[1024,128]{1,0:T(8,128)(2,1)S(1)} collective-permute-done((bf16[1024,128]{1,0:T(8,128)(2,1)S(1)}, bf16[1024,128]{1,0:T(8,128)(2,1)S(1)}, u32[]{:S(2)}, u32[]{:S(2)}) %collective-permute-start.21) | collective-permute-done | bytes 262176 | tf_op jit(solution)/shard_map/ppermute | solution.py:49
  79.8 4.7 %collective-permute-start.36 = (bf16[1024,128]{1,0:T(8,128)(2,1)S(1)}, bf16[1024,128]{1,0:T(8,128)(2,1)S(1)}, u32[]{:S(2)}, u32[]{:S(2)}) collective-permute-start(bf16[1024,128]{1,0:T(8,128)(2,1)S(1)} %get-tuple-element.193.refs_12_), channel_id=1, source_target_pairs={{0,4},{1,5},{2,6},{3,7},{4,0},{5,1},{6,2},{7,3},{8,12},{9,13},{10,... | collective-permute-start | bytes 786440 | tf_op jit(solution)/shard_map/ppermute | solution.py:49
  88.5 2.6 %collective-permute-start.28 = (bf16[1312,128]{1,0:T(8,128)(2,1)S(1)}, bf16[1312,128]{1,0:T(8,128)(2,1)S(1)}, u32[]{:S(2)}, u32[]{:S(2)}) collective-permute-start(bf16[1312,128]{1,0:T(8,128)(2,1)S(1)} %get-tuple-element.197.refs_4_), channel_id=1, source_target_pairs={{0,6},{1,3},{2,0},{3,5},{4,2},{5,7},{6,4},{7,1},{8,14},{9,11},{10,... | collective-permute-start | bytes 1007624 | tf_op jit(solution)/shard_map/ppermute | solution.py:49
  91.1 4.8 %collective-permute-done.36.refs_14_ = bf16[1024,128]{1,0:T(8,128)(2,1)S(1)} collective-permute-done((bf16[1024,128]{1,0:T(8,128)(2,1)S(1)}, bf16[1024,128]{1,0:T(8,128)(2,1)S(1)}, u32[]{:S(2)}, u32[]{:S(2)}) %collective-permute-start.36) | collective-permute-done | bytes 262176 | tf_op jit(solution)/shard_map/ppermute | solution.py:49
  97.6 3.4 %collective-permute-done.32.refs_7_ = bf16[1312,128]{1,0:T(8,128)(2,1)S(1)} collective-permute-done((bf16[1312,128]{1,0:T(8,128)(2,1)S(1)}, bf16[1312,128]{1,0:T(8,128)(2,1)S(1)}, u32[]{:S(2)}, u32[]{:S(2)}) %collective-permute-start.32) | collective-permute-done | bytes 335904 | tf_op jit(solution)/shard_map/ppermute | solution.py:49
  101.0 7.9 %collective-permute-start.33 = (bf16[1312,128]{1,0:T(8,128)(2,1)S(1)}, bf16[1312,128]{1,0:T(8,128)(2,1)S(1)}, u32[]{:S(2)}, u32[]{:S(2)}) collective-permute-start(bf16[1312,128]{1,0:T(8,128)(2,1)S(1)} %collective-permute-done.32.refs_7_), channel_id=1, source_target_pairs={{0,1},{1,0},{2,3},{3,2},{4,5},{5,4},{6,7},{7,6},{8,9},{9,8},{10,11... | collective-permute-start | bytes 1007624 | tf_op jit(solution)/shard_map/ppermute | solution.py:54
  112.9 4.3 %shard_map.116 = (bf16[8192,128]{1,0:T(8,128)(2,1)S(1)}, bf16[3360,128]{1,0:T(8,128)(2,1)S(1)}, bf16[3360,128]{1,0:T(8,128)(2,1)S(1)}, bf16[3360,128]{1,0:T(8,128)(2,1)S(1)}, f32[144,256]{1,0:T(8,128)S(1)}) custom-call(s32[1]{0:T(128)} %bitcast.11.live, s32[8,64]{1,0:T(8,128)S(1)} %get-tuple-element.183.tables, bf16[64,128,128]{2,1,0:T(8,128)(2,1)S(1)} %bitcast.18, ...), custom_call_target="tpu_custom_call" | custom-call | tf_op jit(solution)/shard_map/pallas_call | solution.py:233
  119.3 10.8 %collective-permute-done.40.refs_0_ = bf16[3360,128]{1,0:T(8,128)(2,1)S(1)} collective-permute-done((bf16[3360,128]{1,0:T(8,128)(2,1)S(1)}, bf16[3360,128]{1,0:T(8,128)(2,1)S(1)}, u32[]{:S(2)}, u32[]{:S(2)}) %collective-permute-start.40) | collective-permute-done | bytes 860192 | tf_op jit(solution)/shard_map/ppermute | solution.py:33
  132.3 9.1 %collective-permute-done.42.refs_2_ = bf16[3360,128]{1,0:T(8,128)(2,1)S(1)} collective-permute-done((bf16[3360,128]{1,0:T(8,128)(2,1)S(1)}, bf16[3360,128]{1,0:T(8,128)(2,1)S(1)}, u32[]{:S(2)}, u32[]{:S(2)}) %collective-permute-start.42) | collective-permute-done | bytes 860192 | tf_op jit(solution)/shard_map/ppermute | solution.py:33
  141.4 3.0 %shard_map.117 = (f32[2048,128]{1,0:T(8,128)}, bf16[2336,128]{1,0:T(8,128)(2,1)}, bf16[2336,128]{1,0:T(8,128)(2,1)}, bf16[2336,128]{1,0:T(8,128)(2,1)}, f32[144,256]{1,0:T(8,128)S(1)}) custom-call(s32[96]{0:T(128)S(1)} %get-tuple-element.195.lists, s32[3]{0:T(128)S(1)} %get-tuple-element.196.counts, bf16[8192,128]{1,0:T(8,128)(2,1)S(1)} %get-tuple-element.198.own, ...), custom_call_target="tpu_custom_call" | custom-call | tf_op jit(solution)/shard_map/pallas_call | solution.py:345
  144.5 2.7 %collective-permute-start.43 = (bf16[2336,128]{1,0:T(8,128)(2,1)}, bf16[2336,128]{1,0:T(8,128)(2,1)S(1)}, u32[]{:S(2)}, u32[]{:S(2)}) collective-permute-start(bf16[2336,128]{1,0:T(8,128)(2,1)} %get-tuple-element.208), channel_id=1, source_target_pairs={{0,96},{1,25},{2,98},{3,27},{4,100},{5,29},{6,102},{7,31},{8,104},... | collective-permute-start | bytes 1794056 | tf_op jit(solution)/shard_map/ppermute | solution.py:33
  149.3 12.1 %collective-permute-done.43.refs_1_ = bf16[2336,128]{1,0:T(8,128)(2,1)S(1)} collective-permute-done((bf16[2336,128]{1,0:T(8,128)(2,1)}, bf16[2336,128]{1,0:T(8,128)(2,1)S(1)}, u32[]{:S(2)}, u32[]{:S(2)}) %collective-permute-start.43) | collective-permute-done | bytes 598048 | tf_op jit(solution)/shard_map/ppermute | solution.py:33
  161.4 3.8 %collective-permute-done.45.refs_3_ = bf16[2336,128]{1,0:T(8,128)(2,1)S(1)} collective-permute-done((bf16[2336,128]{1,0:T(8,128)(2,1)}, bf16[2336,128]{1,0:T(8,128)(2,1)S(1)}, u32[]{:S(2)}, u32[]{:S(2)}) %collective-permute-start.45) | collective-permute-done | bytes 598048 | tf_op jit(solution)/shard_map/ppermute | solution.py:33
  165.3 2.5 %shard_map.118 = (f32[2048,128]{1,0:T(8,128)}, f32[128,256]{1,0:T(8,128)}, f32[1,256]{1,0:T(1,128)}) custom-call(f32[2048,128]{1,0:T(8,128)} %get-tuple-element.207.refs_0_, bf16[2336,128]{1,0:T(8,128)(2,1)S(1)} %collective-permute-done.43.refs_1_, bf16[2336,128]{1,0:T(8,128)(2,1)S(1)} %collective-permute-done.44.refs_2_, ...), custom_call_target="tpu_custom_call" | custom-call | tf_op jit(solution)/shard_map/pallas_call | solution.py:374
  (88 shorter events, 51.1 us)
Async XLA Ops:
  0.6 17.8 %collective-permute-start.8 = (bf16[2048,128]{1,0:T(8,128)(2,1)}, bf16[2048,128]{1,0:T(8,128)(2,1)S(1)}, u32[]{:S(2)}, u32[]{:S(2)}) collective-permute-start(bf16[2048,128]{1,0:T(8,128)(2,1)} %refs_0_.3), channel_id=1, source_target_pairs={{0,32},{1,9},{2,34},{3,11},{4,36},{5,13},{6,38},{7,15},{8,40},{9,1... | collective-permute-start | bytes 1572872 | tf_op jit(solution)/shard_map/ppermute | solution.py:33
  2.3 16.2 %collective-permute-start.7 = (bf16[2048,128]{1,0:T(8,128)(2,1)}, bf16[2048,128]{1,0:T(8,128)(2,1)S(1)}, u32[]{:S(2)}, u32[]{:S(2)}) collective-permute-start(bf16[2048,128]{1,0:T(8,128)(2,1)} %refs_0_.3), channel_id=1, source_target_pairs={{0,64},{1,17},{2,66},{3,19},{4,68},{5,21},{6,70},{7,23},{8,72},{9,... | collective-permute-start | bytes 1572872 | tf_op jit(solution)/shard_map/ppermute | solution.py:33
  5.0 13.5 %collective-permute-start.6 = (bf16[2048,128]{1,0:T(8,128)(2,1)}, bf16[2048,128]{1,0:T(8,128)(2,1)}, u32[]{:S(2)}, u32[]{:S(2)}) collective-permute-start(bf16[2048,128]{1,0:T(8,128)(2,1)} %refs_0_.3), channel_id=1, source_target_pairs={{0,96},{1,25},{2,98},{3,27},{4,100},{5,29},{6,102},{7,31},{8,104},... | collective-permute-start | bytes 1572872 | tf_op jit(solution)/shard_map/ppermute | solution.py:33
  20.7 21.7 %collective-permute-start.15 = (bf16[3072,128]{1,0:T(8,128)(2,1)S(1)}, bf16[3072,128]{1,0:T(8,128)(2,1)S(1)}, u32[]{:S(2)}, u32[]{:S(2)}) collective-permute-start(bf16[3072,128]{1,0:T(8,128)(2,1)S(1)} %get-tuple-element.184), channel_id=1, source_target_pairs={{0,24},{1,97},{2,26},{3,99},{4,28},{5,101},{6,30},{7,103},{8,0},{9... | collective-permute-start | bytes 2359304 | tf_op jit(solution)/shard_map/ppermute | solution.py:33
  24.4 18.0 %collective-permute-start.16 = (bf16[3072,128]{1,0:T(8,128)(2,1)S(1)}, bf16[3072,128]{1,0:T(8,128)(2,1)S(1)}, u32[]{:S(2)}, u32[]{:S(2)}) collective-permute-start(bf16[3072,128]{1,0:T(8,128)(2,1)S(1)} %get-tuple-element.185), channel_id=1, source_target_pairs={{0,16},{1,65},{2,18},{3,67},{4,20},{5,69},{6,22},{7,71},{8,24},{9,... | collective-permute-start | bytes 2359304 | tf_op jit(solution)/shard_map/ppermute | solution.py:33
  24.4 21.7 %collective-permute-start.17 = (bf16[3072,128]{1,0:T(8,128)(2,1)S(1)}, bf16[3072,128]{1,0:T(8,128)(2,1)S(1)}, u32[]{:S(2)}, u32[]{:S(2)}) collective-permute-start(bf16[3072,128]{1,0:T(8,128)(2,1)S(1)} %get-tuple-element.186), channel_id=1, source_target_pairs={{0,8},{1,33},{2,10},{3,35},{4,12},{5,37},{6,14},{7,39},{8,16},{9,4... | collective-permute-start | bytes 2359304 | tf_op jit(solution)/shard_map/ppermute | solution.py:33
  55.9 12.7 %collective-permute-start.25 = (bf16[1024,128]{1,0:T(8,128)(2,1)S(1)}, bf16[1024,128]{1,0:T(8,128)(2,1)S(1)}, u32[]{:S(2)}, u32[]{:S(2)}) collective-permute-start(bf16[1024,128]{1,0:T(8,128)(2,1)S(1)} %get-tuple-element.220), channel_id=1, source_target_pairs={{0,2},{1,7},{2,4},{3,1},{4,6},{5,3},{6,0},{7,5},{8,10},{9,15},{10,... | collective-permute-start | bytes 786440 | tf_op jit(solution)/shard_map/ppermute | solution.py:49
  57.0 14.7 %collective-permute-start.24 = (bf16[1024,128]{1,0:T(8,128)(2,1)S(1)}, bf16[1024,128]{1,0:T(8,128)(2,1)S(1)}, u32[]{:S(2)}, u32[]{:S(2)}) collective-permute-start(bf16[1024,128]{1,0:T(8,128)(2,1)S(1)} %get-tuple-element.221), channel_id=1, source_target_pairs={{0,4},{1,5},{2,6},{3,7},{4,0},{5,1},{6,2},{7,3},{8,12},{9,13},{10,... | collective-permute-start | bytes 786440 | tf_op jit(solution)/shard_map/ppermute | solution.py:49
  59.9 13.0 %collective-permute-start.23 = (bf16[1024,128]{1,0:T(8,128)(2,1)S(1)}, bf16[1024,128]{1,0:T(8,128)(2,1)S(1)}, u32[]{:S(2)}, u32[]{:S(2)}) collective-permute-start(bf16[1024,128]{1,0:T(8,128)(2,1)S(1)} %get-tuple-element.222), channel_id=1, source_target_pairs={{0,6},{1,3},{2,0},{3,5},{4,2},{5,7},{6,4},{7,1},{8,14},{9,11},{10,... | collective-permute-start | bytes 786440 | tf_op jit(solution)/shard_map/ppermute | solution.py:49
  61.5 18.3 %collective-permute-start.21 = (bf16[1024,128]{1,0:T(8,128)(2,1)S(1)}, bf16[1024,128]{1,0:T(8,128)(2,1)S(1)}, u32[]{:S(2)}, u32[]{:S(2)}) collective-permute-start(bf16[1024,128]{1,0:T(8,128)(2,1)S(1)} %get-tuple-element.223), channel_id=1, source_target_pairs={{0,2},{1,7},{2,4},{3,1},{4,6},{5,3},{6,0},{7,5},{8,10},{9,15},{10,... | collective-permute-start | bytes 786440 | tf_op jit(solution)/shard_map/ppermute | solution.py:49
  62.2 22.3 %collective-permute-start.20 = (bf16[1024,128]{1,0:T(8,128)(2,1)S(1)}, bf16[1024,128]{1,0:T(8,128)(2,1)S(1)}, u32[]{:S(2)}, u32[]{:S(2)}) collective-permute-start(bf16[1024,128]{1,0:T(8,128)(2,1)S(1)} %get-tuple-element.224), channel_id=1, source_target_pairs={{0,4},{1,5},{2,6},{3,7},{4,0},{5,1},{6,2},{7,3},{8,12},{9,13},{10,... | collective-permute-start | bytes 786440 | tf_op jit(solution)/shard_map/ppermute | solution.py:49
  68.6 15.9 %collective-permute-start.19 = (bf16[1024,128]{1,0:T(8,128)(2,1)S(1)}, bf16[1024,128]{1,0:T(8,128)(2,1)S(1)}, u32[]{:S(2)}, u32[]{:S(2)}) collective-permute-start(bf16[1024,128]{1,0:T(8,128)(2,1)S(1)} %get-tuple-element.225), channel_id=1, source_target_pairs={{0,6},{1,3},{2,0},{3,5},{4,2},{5,7},{6,4},{7,1},{8,14},{9,11},{10,... | collective-permute-start | bytes 786440 | tf_op jit(solution)/shard_map/ppermute | solution.py:49
  79.8 16.1 %collective-permute-start.36 = (bf16[1024,128]{1,0:T(8,128)(2,1)S(1)}, bf16[1024,128]{1,0:T(8,128)(2,1)S(1)}, u32[]{:S(2)}, u32[]{:S(2)}) collective-permute-start(bf16[1024,128]{1,0:T(8,128)(2,1)S(1)} %get-tuple-element.193.refs_12_), channel_id=1, source_target_pairs={{0,4},{1,5},{2,6},{3,7},{4,0},{5,1},{6,2},{7,3},{8,12},{9,13},{10,... | collective-permute-start | bytes 786440 | tf_op jit(solution)/shard_map/ppermute | solution.py:49
  86.4 14.6 %collective-permute-start.32 = (bf16[1312,128]{1,0:T(8,128)(2,1)S(1)}, bf16[1312,128]{1,0:T(8,128)(2,1)S(1)}, u32[]{:S(2)}, u32[]{:S(2)}) collective-permute-start(bf16[1312,128]{1,0:T(8,128)(2,1)S(1)} %get-tuple-element.197.refs_4_), channel_id=1, source_target_pairs={{0,2},{1,7},{2,4},{3,1},{4,6},{5,3},{6,0},{7,5},{8,10},{9,15},{10,... | collective-permute-start | bytes 1007624 | tf_op jit(solution)/shard_map/ppermute | solution.py:49
  88.4 21.9 %collective-permute-start.30 = (bf16[1312,128]{1,0:T(8,128)(2,1)S(1)}, bf16[1312,128]{1,0:T(8,128)(2,1)S(1)}, u32[]{:S(2)}, u32[]{:S(2)}) collective-permute-start(bf16[1312,128]{1,0:T(8,128)(2,1)S(1)} %get-tuple-element.197.refs_4_), channel_id=1, source_target_pairs={{0,4},{1,5},{2,6},{3,7},{4,0},{5,1},{6,2},{7,3},{8,12},{9,13},{10,... | collective-permute-start | bytes 1007624 | tf_op jit(solution)/shard_map/ppermute | solution.py:49
  88.5 21.8 %collective-permute-start.28 = (bf16[1312,128]{1,0:T(8,128)(2,1)S(1)}, bf16[1312,128]{1,0:T(8,128)(2,1)S(1)}, u32[]{:S(2)}, u32[]{:S(2)}) collective-permute-start(bf16[1312,128]{1,0:T(8,128)(2,1)S(1)} %get-tuple-element.197.refs_4_), channel_id=1, source_target_pairs={{0,6},{1,3},{2,0},{3,5},{4,2},{5,7},{6,4},{7,1},{8,14},{9,11},{10,... | collective-permute-start | bytes 1007624 | tf_op jit(solution)/shard_map/ppermute | solution.py:49
  96.7 14.2 %collective-permute-start.37 = (bf16[1024,128]{1,0:T(8,128)(2,1)S(1)}, bf16[1024,128]{1,0:T(8,128)(2,1)S(1)}, u32[]{:S(2)}, u32[]{:S(2)}) collective-permute-start(bf16[1024,128]{1,0:T(8,128)(2,1)S(1)} %collective-permute-done.36.refs_14_), channel_id=1, source_target_pairs={{0,1},{1,0},{2,3},{3,2},{4,5},{5,4},{6,7},{7,6},{8,9},{9,8},{10,11... | collective-permute-start | bytes 786440 | tf_op jit(solution)/shard_map/ppermute | solution.py:54
  97.4 15.4 %collective-permute-start.27 = (bf16[1312,128]{1,0:T(8,128)(2,1)S(1)}, bf16[1312,128]{1,0:T(8,128)(2,1)S(1)}, u32[]{:S(2)}, u32[]{:S(2)}) collective-permute-start(bf16[1312,128]{1,0:T(8,128)(2,1)S(1)} %get-tuple-element.197.refs_4_), channel_id=1, source_target_pairs={{0,1},{1,0},{2,3},{3,2},{4,5},{5,4},{6,7},{7,6},{8,9},{9,8},{10,11... | collective-permute-start | bytes 1007624 | tf_op jit(solution)/shard_map/ppermute | solution.py:54
  117.2 12.8 %collective-permute-start.40 = (bf16[3360,128]{1,0:T(8,128)(2,1)S(1)}, bf16[3360,128]{1,0:T(8,128)(2,1)S(1)}, u32[]{:S(2)}, u32[]{:S(2)}) collective-permute-start(bf16[3360,128]{1,0:T(8,128)(2,1)S(1)} %get-tuple-element.200), channel_id=1, source_target_pairs={{0,24},{1,97},{2,26},{3,99},{4,28},{5,101},{6,30},{7,103},{8,0},{9... | collective-permute-start | bytes 2580488 | tf_op jit(solution)/shard_map/ppermute | solution.py:33
  117.9 14.4 %collective-permute-start.41 = (bf16[3360,128]{1,0:T(8,128)(2,1)S(1)}, bf16[3360,128]{1,0:T(8,128)(2,1)S(1)}, u32[]{:S(2)}, u32[]{:S(2)}) collective-permute-start(bf16[3360,128]{1,0:T(8,128)(2,1)S(1)} %get-tuple-element.201), channel_id=1, source_target_pairs={{0,16},{1,65},{2,18},{3,67},{4,20},{5,69},{6,22},{7,71},{8,24},{9,... | collective-permute-start | bytes 2580488 | tf_op jit(solution)/shard_map/ppermute | solution.py:33
  118.1 23.3 %collective-permute-start.42 = (bf16[3360,128]{1,0:T(8,128)(2,1)S(1)}, bf16[3360,128]{1,0:T(8,128)(2,1)S(1)}, u32[]{:S(2)}, u32[]{:S(2)}) collective-permute-start(bf16[3360,128]{1,0:T(8,128)(2,1)S(1)} %get-tuple-element.202), channel_id=1, source_target_pairs={{0,8},{1,33},{2,10},{3,35},{4,12},{5,37},{6,14},{7,39},{8,16},{9,4... | collective-permute-start | bytes 2580488 | tf_op jit(solution)/shard_map/ppermute | solution.py:33
  144.5 17.0 %collective-permute-start.43 = (bf16[2336,128]{1,0:T(8,128)(2,1)}, bf16[2336,128]{1,0:T(8,128)(2,1)S(1)}, u32[]{:S(2)}, u32[]{:S(2)}) collective-permute-start(bf16[2336,128]{1,0:T(8,128)(2,1)} %get-tuple-element.208), channel_id=1, source_target_pairs={{0,96},{1,25},{2,98},{3,27},{4,100},{5,29},{6,102},{7,31},{8,104},... | collective-permute-start | bytes 1794056 | tf_op jit(solution)/shard_map/ppermute | solution.py:33
  147.2 14.2 %collective-permute-start.44 = (bf16[2336,128]{1,0:T(8,128)(2,1)}, bf16[2336,128]{1,0:T(8,128)(2,1)S(1)}, u32[]{:S(2)}, u32[]{:S(2)}) collective-permute-start(bf16[2336,128]{1,0:T(8,128)(2,1)} %get-tuple-element.209), channel_id=1, source_target_pairs={{0,64},{1,17},{2,66},{3,19},{4,68},{5,21},{6,70},{7,23},{8,72},{9,... | collective-permute-start | bytes 1794056 | tf_op jit(solution)/shard_map/ppermute | solution.py:33
  148.7 16.6 %collective-permute-start.45 = (bf16[2336,128]{1,0:T(8,128)(2,1)}, bf16[2336,128]{1,0:T(8,128)(2,1)S(1)}, u32[]{:S(2)}, u32[]{:S(2)}) collective-permute-start(bf16[2336,128]{1,0:T(8,128)(2,1)} %get-tuple-element.210), channel_id=1, source_target_pairs={{0,32},{1,9},{2,34},{3,11},{4,36},{5,13},{6,38},{7,15},{8,40},{9,1... | collective-permute-start | bytes 1794056 | tf_op jit(solution)/shard_map/ppermute | solution.py:33
  (25 other events, 232.6 us)
